TPU v7x, 128 devices: a whole 4x4x4 slice. The times are simulated.
128 devices in a mesh: row: 8 (over x, core), col: 16 (over y, z).
Axes of the slice: x: 4, y: 4, z: 4, core: 2. Of those that a mesh axis runs over, the one named last changes fastest.
Arguments:
- embeddings: bfloat16 [65536, 384], P(('row', 'col')), may hold values from -6 to 6
- block_cluster: int32 [256], replicated, may hold values from 0 to 7, never falling along the last dimension, each value on 1 to 160 neighbouring positions
Outputs:
- nearest: float32 [65536], P(('row', 'col'))
Inputs may be any that keep to these rules, and one draw needn't show every extreme that they name: block_cluster never falls along the blocks; each cluster covers 1 to 160 consecutive blocks and one covers exactly 160.
All inputs are finite; a program needn't handle non-finite values.
Results may differ from a plain program's by a relative error of at most 0.0012.
Values may be sent and summed in bfloat16 or wider, within the bound.
No kernel may reach another device: no remote copies, remote signals or barrier semaphores. Data moves between devices by JAX's collectives and lax.ppermute only.
A program may use at most 128 MiB of HBM per device.

v0:
```python
import math

import jax
import jax.numpy as jnp
from jax import lax
from jax.sharding import PartitionSpec as P

BLK = 256


def make_fold(query, query_label, query_index, key_label, key_index):
    total = query.shape[0]
    width_d = query.shape[1]
    step = math.gcd(512, total)
    count = total // step
    query_blocks = query.reshape(count, step, width_d)
    label_blocks = query_label.reshape(count, step)
    index_blocks = query_index.reshape(count, step)

    def accumulate(carry, keys_part, offset):
        width = keys_part.shape[0]
        key_step = math.gcd(width, 2048)
        key_count = width // key_step
        part_label = key_label.reshape(key_count, key_step)
        part_index = key_index.reshape(key_count, key_step)
        part_keys = keys_part.reshape(key_count, key_step, width_d)

        def one_block(items):
            block_rows, block_label, block_index = items
            query_low = jnp.min(block_label)
            query_high = jnp.max(block_label)

            def one_keys(key_items):
                key_rows, key_lab, key_idx = key_items
                touching = (query_low <= jnp.max(key_lab)) & (jnp.min(key_lab) <= query_high)

                def scored(operands):
                    rows_in, keys_in, lab_in, idx_in = operands
                    scores = lax.dot_general(
                        rows_in,
                        keys_in,
                        (((1,), (1,)), ((), ())),
                        preferred_element_type=jnp.float32,
                    )
                    keep = (block_label[:, None] == lab_in[None, :]) & (
                        block_index[:, None] != idx_in[None, :]
                    )
                    return jnp.max(jnp.where(keep, scores, jnp.float32(-2.0)), axis=1)

                def skipped(operands):
                    return jnp.full((step,), -2.0, jnp.float32)

                return lax.cond(touching, scored, skipped, (block_rows, key_rows, key_lab, key_idx))

            return jnp.max(lax.map(one_keys, (part_keys, part_label, part_index)), axis=0)

        best = lax.map(one_block, (query_blocks, label_blocks, index_blocks))
        return jnp.maximum(carry, best.reshape(total))

    return accumulate


def body(embeddings, block_cluster):
    values = embeddings.astype(jnp.float32)
    squares = jnp.sum(values * values, axis=1, keepdims=True)
    unit = (values * lax.rsqrt(squares + 1e-06)).astype(jnp.bfloat16)
    label = jnp.repeat(block_cluster, BLK)
    total_docs = label.shape[0]
    index_all = jnp.arange(total_docs, dtype=jnp.int32)
    local_rows = unit.shape[0]
    row_count = lax.axis_size("row")
    col_count = lax.axis_size("col")
    row_pos = lax.axis_index("row")
    col_pos = lax.axis_index("col")
    group_rows = lax.all_gather(unit, "col", axis=0, tiled=True)
    group_start = row_pos * (col_count * local_rows)
    group_label = lax.dynamic_slice_in_dim(label, group_start, col_count * local_rows, 0)
    group_index = lax.dynamic_slice_in_dim(index_all, group_start, col_count * local_rows, 0)
    column_label = lax.dynamic_index_in_dim(
        label.reshape(row_count, col_count, local_rows), col_pos, 1, False
    ).reshape(row_count * local_rows)
    column_index = lax.dynamic_index_in_dim(
        index_all.reshape(row_count, col_count, local_rows), col_pos, 1, False
    ).reshape(row_count * local_rows)
    accumulate = make_fold(group_rows, group_label, group_index, column_label, column_index)
    initial = jnp.full((col_count * local_rows,), -2.0, jnp.float32)
    partial_value = accumulate(
        initial, lax.all_gather(unit, "row", axis=0, tiled=True), jnp.int32(0)
    )
    whole = lax.pmax(partial_value, "col")
    return lax.dynamic_slice_in_dim(whole, col_pos * local_rows, local_rows, 0)


def solution(mesh):
    placed = (P(("row", "col"), None), P())
    return jax.shard_map(
        body, mesh=mesh, in_specs=placed, out_specs=P(("row", "col")), check_vma=False
    )
```

profile of v0, /device:TPU:4, one launch (start us, length us, event | category | flops | bytes accessed | tf_op | source)
XLA Modules:
  0.0 413.3 jit_solution(11975550814622287753)
XLA Ops:
  12.5 26.1 %all-gather.5.cloned.1.call-done = bf16[4096,384]{1,0:T(8,128)(2,1)} async-done(((bf16[512,384]{1,0:T(8,128)(2,1)}), bf16[4096,384]{1,0:T(8,128)(2,1)}) %all-gather.5.cloned.1.call-update) | async-done | bytes 3145744 | tf_op jit(solution)/shard_map/all_gather | solution.py:88
  38.6 64.9 %all-gather.3.cloned.1.call-done = bf16[8192,384]{1,0:T(8,128)(2,1)} async-done(((bf16[512,384]{1,0:T(8,128)(2,1)}), bf16[8192,384]{1,0:T(8,128)(2,1)}) %all-gather.3.cloned.1.call-update) | async-done | bytes 6291472 | tf_op jit(solution)/shard_map/all_gather | solution.py:75
  103.5 229.8 %while.21 = (s32[]{:T(128)}, f32[16,512]{1,0:T(8,128)S(1)}, s32[16,512]{1,0:T(8,128)S(1)}, bf16[16,512,384]{2,1,0:T(8,128)(2,1)}, s32[16,512]{1,0:T(8,128)S(1)},...) while((s32[]{:T(128)}, f32[16,512]{1,0:T(8,128)S(1)}, ...), condition=%wide.region_12.13_spmd, body=%wide.region_1.12_spmd.sunk | while | flops 810554368 | bytes 2831328 | solution.py:57
  105.3 12.5 %while.22 = (s32[]{:T(128)}, f32[2,512]{1,0:T(2,128)S(1)}, s32[2,2048]{1,0:T(2,128)S(1)}, s32[]{:T(128)}, s32[]{:T(128)}, /*index=5*/s32[512]{0:T(512)S(1)}, s32...) while((s32[]{:T(128)}, f32[2,512]{1,0:T(2,128)S(1)}, ...), condition=%wide.region_10.10_spmd, body=%wide.region_4.9_spmd.sunk | while | flops 810552832 | bytes 2026211 | solution.py:55
  108.6 2.8 conditional.2
  114.9 2.8 conditional.2
  119.6 12.5 %while.22 = (s32[]{:T(128)}, f32[2,512]{1,0:T(2,128)S(1)}, s32[2,2048]{1,0:T(2,128)S(1)}, s32[]{:T(128)}, s32[]{:T(128)}, /*index=5*/s32[512]{0:T(512)S(1)}, s32...) while((s32[]{:T(128)}, f32[2,512]{1,0:T(2,128)S(1)}, ...), condition=%wide.region_10.10_spmd, body=%wide.region_4.9_spmd.sunk | while | flops 810552832 | bytes 2026211 | solution.py:55
  123.0 2.8 conditional.2
  129.2 2.8 conditional.2
  134.0 12.5 %while.22 = (s32[]{:T(128)}, f32[2,512]{1,0:T(2,128)S(1)}, s32[2,2048]{1,0:T(2,128)S(1)}, s32[]{:T(128)}, s32[]{:T(128)}, /*index=5*/s32[512]{0:T(512)S(1)}, s32...) while((s32[]{:T(128)}, f32[2,512]{1,0:T(2,128)S(1)}, ...), condition=%wide.region_10.10_spmd, body=%wide.region_4.9_spmd.sunk | while | flops 810552832 | bytes 2026211 | solution.py:55
  137.3 2.8 conditional.2
  143.6 2.8 conditional.2
  148.4 12.5 %while.22 = (s32[]{:T(128)}, f32[2,512]{1,0:T(2,128)S(1)}, s32[2,2048]{1,0:T(2,128)S(1)}, s32[]{:T(128)}, s32[]{:T(128)}, /*index=5*/s32[512]{0:T(512)S(1)}, s32...) while((s32[]{:T(128)}, f32[2,512]{1,0:T(2,128)S(1)}, ...), condition=%wide.region_10.10_spmd, body=%wide.region_4.9_spmd.sunk | while | flops 810552832 | bytes 2026211 | solution.py:55
  158.0 2.8 conditional.2
  162.7 12.5 %while.22 = (s32[]{:T(128)}, f32[2,512]{1,0:T(2,128)S(1)}, s32[2,2048]{1,0:T(2,128)S(1)}, s32[]{:T(128)}, s32[]{:T(128)}, /*index=5*/s32[512]{0:T(512)S(1)}, s32...) while((s32[]{:T(128)}, f32[2,512]{1,0:T(2,128)S(1)}, ...), condition=%wide.region_10.10_spmd, body=%wide.region_4.9_spmd.sunk | while | flops 810552832 | bytes 2026211 | solution.py:55
  166.1 2.8 conditional.2
  172.3 2.8 conditional.2
  177.1 12.5 %while.22 = (s32[]{:T(128)}, f32[2,512]{1,0:T(2,128)S(1)}, s32[2,2048]{1,0:T(2,128)S(1)}, s32[]{:T(128)}, s32[]{:T(128)}, /*index=5*/s32[512]{0:T(512)S(1)}, s32...) while((s32[]{:T(128)}, f32[2,512]{1,0:T(2,128)S(1)}, ...), condition=%wide.region_10.10_spmd, body=%wide.region_4.9_spmd.sunk | while | flops 810552832 | bytes 2026211 | solution.py:55
  180.4 2.8 conditional.2
  186.7 2.8 conditional.2
  191.4 12.5 %while.22 = (s32[]{:T(128)}, f32[2,512]{1,0:T(2,128)S(1)}, s32[2,2048]{1,0:T(2,128)S(1)}, s32[]{:T(128)}, s32[]{:T(128)}, /*index=5*/s32[512]{0:T(512)S(1)}, s32...) while((s32[]{:T(128)}, f32[2,512]{1,0:T(2,128)S(1)}, ...), condition=%wide.region_10.10_spmd, body=%wide.region_4.9_spmd.sunk | while | flops 810552832 | bytes 2026211 | solution.py:55
  194.8 2.8 conditional.2
  201.1 2.8 conditional.2
  205.8 12.5 %while.22 = (s32[]{:T(128)}, f32[2,512]{1,0:T(2,128)S(1)}, s32[2,2048]{1,0:T(2,128)S(1)}, s32[]{:T(128)}, s32[]{:T(128)}, /*index=5*/s32[512]{0:T(512)S(1)}, s32...) while((s32[]{:T(128)}, f32[2,512]{1,0:T(2,128)S(1)}, ...), condition=%wide.region_10.10_spmd, body=%wide.region_4.9_spmd.sunk | while | flops 810552832 | bytes 2026211 | solution.py:55
  209.2 2.8 conditional.2
  215.4 2.8 conditional.2
  220.2 12.5 %while.22 = (s32[]{:T(128)}, f32[2,512]{1,0:T(2,128)S(1)}, s32[2,2048]{1,0:T(2,128)S(1)}, s32[]{:T(128)}, s32[]{:T(128)}, /*index=5*/s32[512]{0:T(512)S(1)}, s32...) while((s32[]{:T(128)}, f32[2,512]{1,0:T(2,128)S(1)}, ...), condition=%wide.region_10.10_spmd, body=%wide.region_4.9_spmd.sunk | while | flops 810552832 | bytes 2026211 | solution.py:55
  229.8 2.8 conditional.2
  234.5 12.5 %while.22 = (s32[]{:T(128)}, f32[2,512]{1,0:T(2,128)S(1)}, s32[2,2048]{1,0:T(2,128)S(1)}, s32[]{:T(128)}, s32[]{:T(128)}, /*index=5*/s32[512]{0:T(512)S(1)}, s32...) while((s32[]{:T(128)}, f32[2,512]{1,0:T(2,128)S(1)}, ...), condition=%wide.region_10.10_spmd, body=%wide.region_4.9_spmd.sunk | while | flops 810552832 | bytes 2026211 | solution.py:55
  237.9 2.8 conditional.2
  244.2 2.8 conditional.2
  248.9 12.5 %while.22 = (s32[]{:T(128)}, f32[2,512]{1,0:T(2,128)S(1)}, s32[2,2048]{1,0:T(2,128)S(1)}, s32[]{:T(128)}, s32[]{:T(128)}, /*index=5*/s32[512]{0:T(512)S(1)}, s32...) while((s32[]{:T(128)}, f32[2,512]{1,0:T(2,128)S(1)}, ...), condition=%wide.region_10.10_spmd, body=%wide.region_4.9_spmd.sunk | while | flops 810552832 | bytes 2026211 | solution.py:55
  252.3 2.8 conditional.2
  258.5 2.8 conditional.2
  263.3 12.5 %while.22 = (s32[]{:T(128)}, f32[2,512]{1,0:T(2,128)S(1)}, s32[2,2048]{1,0:T(2,128)S(1)}, s32[]{:T(128)}, s32[]{:T(128)}, /*index=5*/s32[512]{0:T(512)S(1)}, s32...) while((s32[]{:T(128)}, f32[2,512]{1,0:T(2,128)S(1)}, ...), condition=%wide.region_10.10_spmd, body=%wide.region_4.9_spmd.sunk | while | flops 810552832 | bytes 2026211 | solution.py:55
  266.6 2.8 conditional.2
  272.9 2.8 conditional.2
  277.6 12.5 %while.22 = (s32[]{:T(128)}, f32[2,512]{1,0:T(2,128)S(1)}, s32[2,2048]{1,0:T(2,128)S(1)}, s32[]{:T(128)}, s32[]{:T(128)}, /*index=5*/s32[512]{0:T(512)S(1)}, s32...) while((s32[]{:T(128)}, f32[2,512]{1,0:T(2,128)S(1)}, ...), condition=%wide.region_10.10_spmd, body=%wide.region_4.9_spmd.sunk | while | flops 810552832 | bytes 2026211 | solution.py:55
  287.3 2.8 conditional.2
  292.0 12.5 %while.22 = (s32[]{:T(128)}, f32[2,512]{1,0:T(2,128)S(1)}, s32[2,2048]{1,0:T(2,128)S(1)}, s32[]{:T(128)}, s32[]{:T(128)}, /*index=5*/s32[512]{0:T(512)S(1)}, s32...) while((s32[]{:T(128)}, f32[2,512]{1,0:T(2,128)S(1)}, ...), condition=%wide.region_10.10_spmd, body=%wide.region_4.9_spmd.sunk | while | flops 810552832 | bytes 2026211 | solution.py:55
  295.4 2.8 conditional.2
  301.6 2.8 conditional.2
  306.4 12.5 %while.22 = (s32[]{:T(128)}, f32[2,512]{1,0:T(2,128)S(1)}, s32[2,2048]{1,0:T(2,128)S(1)}, s32[]{:T(128)}, s32[]{:T(128)}, /*index=5*/s32[512]{0:T(512)S(1)}, s32...) while((s32[]{:T(128)}, f32[2,512]{1,0:T(2,128)S(1)}, ...), condition=%wide.region_10.10_spmd, body=%wide.region_4.9_spmd.sunk | while | flops 810552832 | bytes 2026211 | solution.py:55
  309.7 2.8 conditional.2
  316.0 2.8 conditional.2
  320.7 12.5 %while.22 = (s32[]{:T(128)}, f32[2,512]{1,0:T(2,128)S(1)}, s32[2,2048]{1,0:T(2,128)S(1)}, s32[]{:T(128)}, s32[]{:T(128)}, /*index=5*/s32[512]{0:T(512)S(1)}, s32...) while((s32[]{:T(128)}, f32[2,512]{1,0:T(2,128)S(1)}, ...), condition=%wide.region_10.10_spmd, body=%wide.region_4.9_spmd.sunk | while | flops 810552832 | bytes 2026211 | solution.py:55
  330.4 2.8 conditional.2
  333.4 72.4 %pmax.7 = f32[8192]{0:T(1024)S(1)} all-reduce(f32[8192]{0:T(1024)S(1)} %bitcast.44), channel_id=1, replica_groups=mesh['row'=8,'col'=16] {'col'}, use_global_device_ids=true, to_apply=%region_13.14 | all-reduce | flops 8192 | bytes 65536 | tf_op jit(solution)/shard_map/pmax | solution.py:90
  (235 shorter events, 161.7 us)
Async XLA Ops:
  6.5 32.1 %all-gather.5.cloned.1.call-start = ((), (), s32[]{:S(2)}) async-start(), calls=%async_computation.1 | async-start | bytes 3538944 | tf_op jit(solution)/shard_map/all_gather | solution.py:88
  9.6 93.9 %all-gather.3.cloned.1.call-start = ((), (), s32[]{:S(2)}) async-start(), calls=%async_computation | async-start | bytes 6684672 | tf_op jit(solution)/shard_map/all_gather | solution.py:75
Sparse Core Ops, SparseCore 0:
  9.7 28.8 all-gather.4
  40.8 62.6 all-gather.2
where the time goes:
time: 416 us; the launch traced here: 413 us
  waiting for transfers between devices  91.7 us (22%)
  matrix products  89.2 us (21%)
  loops' own time  86 us (21%)
  blocking collectives  72.4 us (17%)
  other arithmetic  38.4 us (9%)
  local copies, waits for them, and re-layouts  22.1 us (5%)
  between operations  13.5 us (3%)
    dot_general x32, matrix products, scored(): lax.dot_general(rows_in, keys_in, (((1,), (1,)), ((), ())), preferred_ele...  89.2 us
    another operation x16, loops' own time, one_block(): lax.map(one_keys, (part_keys, part_label, part_index))  84.5 us
    pmax x1, blocking collectives, body(): whole = lax.pmax(partial_value, 'col')  72.4 us
    all_gather x1, waiting for transfers between devices, body(): group_rows = lax.all_gather(unit, 'col', axis=0, tiled=True)  64.9 us
    all_gather x1, waiting for transfers between devices, body(): lax.all_gather(unit, 'row', axis=0, tiled=True)  26.1 us
    reduce_min x32, other arithmetic, one_keys(): jnp.min(key_lab) <= query_high  23.5 us
    squeeze x16, local copies, waits for them, and re-layouts, accumulate(): best = lax.map(one_block, (query_blocks, label_blocks, index_blocks))  16.6 us
    reduce_max x16, other arithmetic, one_block(): query_high = jnp.max(block_label)  11.5 us
  transfers between devices with their start and end apart: 2, of which 2 were waited for; matrix products, arithmetic and copies ran while one was open for 1% of the time, Pallas kernels for 0%

commit v1 on v0

v1 whole, which is shorter than its diff:
```python
import functools

import jax
import jax.numpy as jnp
import numpy as np
from jax import lax
from jax.experimental import pallas as pl
from jax.experimental.pallas import tpu as pltpu
from jax.sharding import PartitionSpec as P

BLK = 256
SHARD = 512
D = 384
VMEM_LIMIT = 40 * 1024 * 1024

CORE = 16
X1, X3, Y1, Y3, Z1, Z3 = 32, 96, 4, 12, 1, 3
R_MASKS = (0, X1, X3, Y1, X1 ^ X3, X3 ^ Y1, Y1 ^ X1, X1 ^ X3 ^ Y1)
C_MASKS = (0, Y3, Z1, Z3, Y3 ^ Z1, Z1 ^ Z3, Z3 ^ Y3, Y3 ^ Z1 ^ Z3)
R_SENDS = ((0, X1), (0, X3), (0, Y1), (1, X3), (2, Y1), (3, X1), (5, X1))
C_SENDS = ((0, Y3), (0, Z1), (0, Z3), (1, Z1), (2, Z3), (3, Y3), (5, Y3))
STEP_OF = (0, 0, 0, 0, 1, 1, 1, 2)


def make_table():
    phases = [[], [], []]
    flips = {}
    for i, a in enumerate(R_MASKS):
        for j in range(16):
            b = C_MASKS[j % 8] ^ (CORE if j >= 8 else 0)
            w = a ^ b
            if w == 0:
                continue
            bit = CORE if j >= 8 else w & -w
            phase = max(STEP_OF[i], STEP_OF[j % 8])
            key = (bit, phase)
            flips[key] = flips.get(key, 0) ^ 1
            phases[phase].append((i | j << 4, a, b, bit, bit if flips[key] else 0))
    return [np.array(p, np.int32) for p in phases]


TABLES = make_table()
STARTS = np.cumsum([0] + [len(t) for t in TABLES])
TABLE = np.concatenate(TABLES).reshape(-1)
LIST = len(TABLE) // 5 + 8
VMEM = pltpu.VMEM
SMEM = pltpu.SMEM


def spec(space):
    return pl.BlockSpec(memory_space=space)


def unit_kernel(x_ref, unit_ref, flat_ref):
    values = x_ref[...].astype(jnp.float32)
    squares = jnp.sum(values * values, axis=1, keepdims=True)
    unit = values * lax.rsqrt(squares + 1e-06)
    unit_ref[...] = unit.astype(jnp.bfloat16)
    flat_ref[...] = unit.T.astype(jnp.bfloat16)


def unit_call(x):
    return pl.pallas_call(
        unit_kernel,
        out_shape=(
            jax.ShapeDtypeStruct((SHARD, D), jnp.bfloat16),
            jax.ShapeDtypeStruct((D, SHARD), jnp.bfloat16),
        ),
        in_specs=[spec(VMEM)],
        out_specs=(spec(VMEM), spec(VMEM)),
        compiler_params=pltpu.CompilerParams(vmem_limit_bytes=VMEM_LIMIT),
        cost_estimate=pl.CostEstimate(flops=1000000, bytes_accessed=1200000, transcendentals=512),
    )(x)


def self_kernel(here_ref, cluster_ref, table_ref, unit_ref, flat_ref, own_ref, list_ref, count_ref):
    here = here_ref[0]
    for phase in range(3):
        first = int(STARTS[phase])

        def candidate(n, count):
            code = table_ref[5 * n]
            a = 2 * (here ^ table_ref[5 * n + 1])
            b = 2 * (here ^ table_ref[5 * n + 2])
            mine = (here & table_ref[5 * n + 3]) == table_ref[5 * n + 4]
            a0, a1 = cluster_ref[a], cluster_ref[a + 1]
            b0, b1 = cluster_ref[b], cluster_ref[b + 1]
            quads = (
                jnp.where(a0 == b0, 1, 0)
                + jnp.where(a0 == b1, 2, 0)
                + jnp.where(a1 == b0, 4, 0)
                + jnp.where(a1 == b1, 8, 0)
            )
            list_ref[first + count] = code | (quads << 8)
            return count + jnp.where(mine & (quads != 0), 1, 0)

        count_ref[phase] = lax.fori_loop(first, int(STARTS[phase + 1]), candidate, jnp.int32(0))

    same = cluster_ref[2 * here] == cluster_ref[2 * here + 1]
    for half in range(2):
        rows = slice(half * BLK, half * BLK + BLK)
        scores = jnp.dot(unit_ref[rows, :], flat_ref[...], preferred_element_type=jnp.float32)
        row = lax.broadcasted_iota(jnp.int32, scores.shape, 0) + half * BLK
        col = lax.broadcasted_iota(jnp.int32, scores.shape, 1)
        keep = (row != col) & (same | ((row // BLK) == (col // BLK)))
        best = jnp.max(jnp.where(keep, scores, jnp.float32(-2.0)), axis=0, keepdims=True)
        if half == 0:
            own_ref[...] = best
        else:
            own_ref[...] = jnp.maximum(own_ref[...], best)


def self_call(here, cluster, table, unit, flat):
    return pl.pallas_call(
        self_kernel,
        out_shape=(
            jax.ShapeDtypeStruct((1, SHARD), jnp.float32),
            jax.ShapeDtypeStruct((LIST,), jnp.int32),
            jax.ShapeDtypeStruct((3,), jnp.int32),
        ),
        in_specs=[spec(SMEM), spec(SMEM), spec(SMEM), spec(VMEM), spec(VMEM)],
        out_specs=(spec(VMEM), spec(SMEM), spec(SMEM)),
        compiler_params=pltpu.CompilerParams(vmem_limit_bytes=VMEM_LIMIT),
        cost_estimate=pl.CostEstimate(flops=4000000000, bytes_accessed=1000000, transcendentals=0),
    )(here, cluster, table, unit, flat)


def score_kernel(phase, slots, list_ref, count_ref, *refs):
    a_in, refs = refs[:slots], refs[slots:]
    b_in, refs = refs[: 2 * slots], refs[2 * slots :]
    if phase:
        row_in, col_in, refs = refs[0], refs[1], refs[2:]
    if phase < 2:
        row_ref, col_ref, a_buf, b_buf = refs
    else:
        row_lo, row_hi, col_lo, col_hi, other, row_ref, col_ref, a_buf, b_buf = refs

    if phase:
        row_ref[...] = row_in[...]
        col_ref[...] = col_in[...]
    else:
        row_ref[...] = jnp.full(row_ref.shape, -2.0, jnp.float32)
        col_ref[...] = jnp.full(col_ref.shape, -2.0, jnp.float32)
    for n in range(slots):
        a_buf[n] = a_in[n][...]
        b_buf[n] = b_in[n][...]
        b_buf[8 + n] = b_in[slots + n][...]

    first = int(STARTS[phase])

    def fold(i, j, rows, cols, scores):
        best = scores[:, :128]
        for k in range(1, scores.shape[1] // 128):
            best = jnp.maximum(best, scores[:, 128 * k : 128 * k + 128])
        row_ref[i, rows, :] = jnp.maximum(row_ref[i, rows, :], best)
        down = jnp.max(scores.reshape(scores.shape[0] // 8, 8, scores.shape[1]), axis=0)
        col_ref[j, :, cols] = jnp.maximum(col_ref[j, :, cols], down)

    @pl.loop(0, count_ref[phase])
    def _(n):
        word = list_ref[first + n]
        i = word & 15
        j = (word >> 4) & 15
        quads = word >> 8

        @pl.when(quads == 15)
        def _():
            for half in range(2):
                rows = pl.ds(half * BLK, BLK)
                scores = jnp.dot(
                    a_buf[i, rows, :], b_buf[j], preferred_element_type=jnp.float32
                )
                fold(i, j, rows, slice(None), scores)

        @pl.when(quads != 15)
        def _():
            for quad in range(4):

                @pl.when(((quads >> quad) & 1) == 1)
                def _():
                    rows = pl.ds((quad // 2) * BLK, BLK)
                    cols = pl.ds((quad % 2) * BLK, BLK)
                    scores = jnp.dot(
                        a_buf[i, rows, :], b_buf[j, :, cols], preferred_element_type=jnp.float32
                    )
                    fold(i, j, rows, cols, scores)

    if phase == 2:
        for place, (low, high) in enumerate(((0, 3), (1, 6), (2, 5), (4, 7))):
            for out, slot in ((row_lo, low), (row_hi, high)):
                for k in range(4):
                    part = row_ref[slot, 128 * k : 128 * k + 128, :].T
                    out[place : place + 1, 128 * k : 128 * k + 128] = jnp.max(
                        part, axis=0, keepdims=True
                    )
        for place, (low, high) in enumerate(((0, 2), (1, 4), (3, 5), (6, 7))):
            for out, slot in ((col_lo, low), (col_hi, high)):
                out[place : place + 1, :] = jnp.max(col_ref[slot], axis=0, keepdims=True)
            other[place : place + 1, :] = jnp.max(col_ref[8 + low], axis=0, keepdims=True)
            other[4 + place : 5 + place, :] = jnp.max(col_ref[8 + high], axis=0, keepdims=True)


def score_call(phase, plan, count, a_list, b_list, state):
    slots = len(a_list)
    row_type = jax.ShapeDtypeStruct((8, SHARD, 128), jnp.float32)
    col_type = jax.ShapeDtypeStruct((16, 8, SHARD), jnp.float32)
    quarter = jax.ShapeDtypeStruct((4, SHARD), jnp.float32)
    scratch = [VMEM((8, SHARD, D), jnp.bfloat16), VMEM((16, D, SHARD), jnp.bfloat16)]
    if phase < 2:
        outs = (row_type, col_type)
    else:
        outs = (quarter,) * 4 + (jax.ShapeDtypeStruct((8, SHARD), jnp.float32),)
        scratch = [VMEM(row_type.shape, jnp.float32), VMEM(col_type.shape, jnp.float32)] + scratch
    operands = list(a_list) + list(b_list) + list(state)
    flops = (len(TABLES[phase]) // 4) * 2 * SHARD * SHARD * D
    return pl.pallas_call(
        functools.partial(score_kernel, phase, slots),
        out_shape=outs,
        in_specs=[spec(SMEM), spec(SMEM)] + [spec(VMEM)] * len(operands),
        out_specs=(spec(VMEM),) * len(outs),
        scratch_shapes=scratch,
        compiler_params=pltpu.CompilerParams(vmem_limit_bytes=VMEM_LIMIT),
        cost_estimate=pl.CostEstimate(flops=flops, bytes_accessed=8000000, transcendentals=0),
    )(plan, count, *operands)


def exchange(x, mask):
    return lax.ppermute(x, ("row", "col"), [(s, s ^ mask) for s in range(128)])


def body(embeddings, block_cluster):
    here = (lax.axis_index("row") * 16 + lax.axis_index("col")).astype(jnp.int32).reshape(1)
    unit, flat = unit_call(embeddings)
    own, plan, count = self_call(here, block_cluster, jnp.asarray(TABLE), unit, flat)
    rows, cols, others = [unit], [flat], [exchange(flat, CORE)]
    state = ()
    for phase, slots in enumerate(((1, 2, 3), (4, 5, 6), (7,))):
        for slot in slots:
            source, mask = R_SENDS[slot - 1]
            rows.append(exchange(rows[source], mask))
            source, mask = C_SENDS[slot - 1]
            cols.append(exchange(cols[source], mask))
        for slot in slots:
            others.append(exchange(cols[slot], CORE))
        state = score_call(phase, plan, count, rows, cols + others, state)
    row_lo, row_hi, col_lo, col_hi, other = state
    other = exchange(other, CORE)
    col_lo = jnp.maximum(col_lo, other[:4])
    col_hi = jnp.maximum(col_hi, other[4:])
    row_lo = jnp.maximum(row_lo, exchange(row_hi, Y1))
    col_lo = jnp.maximum(col_lo, exchange(col_hi, Z1))
    row_lo = jnp.maximum(row_lo[:2], exchange(row_lo[2:], X3))
    col_lo = jnp.maximum(col_lo[:2], exchange(col_lo[2:], Z3))
    row_lo = jnp.maximum(row_lo[:1], exchange(row_lo[1:], X1))
    col_lo = jnp.maximum(col_lo[:1], exchange(col_lo[1:], Y3))
    return jnp.maximum(own, jnp.maximum(row_lo, col_lo)).reshape(SHARD)


def solution(mesh):
    placed = (P(("row", "col"), None), P())
    return jax.shard_map(
        body, mesh=mesh, in_specs=placed, out_specs=P(("row", "col")), check_vma=False
    )
```

time: 416 us -> 94.7 us (0.23)
  the two profiles are of different devices: /device:TPU:4 before, /device:TPU:2 now
where the time goes in v1:
time: 94.7 us
  starting transfers between devices  41.9 us (44%)
  Pallas kernels  24 us (25%)
  waiting for transfers between devices  22.6 us (24%)
  local copies, waits for them, and re-layouts  5.42 us (6%)
    ppermute x29, starting transfers between devices, exchange(): return lax.ppermute(x, ('row', 'col'), [(s, s ^ mask) for s in range(128)])  41.9 us
    ppermute x29, waiting for transfers between devices, exchange(): return lax.ppermute(x, ('row', 'col'), [(s, s ^ mask) for s in range(128)])  22.6 us
    pallas_call x3, Pallas kernels, score_call(): pl.pallas_call(functools.partial(score_kernel, phase, slots), out_shape=o...  20.1 us
    unnamed x22, local copies, waits for them, and re-layouts  5.39 us
    pallas_call x1, Pallas kernels, self_call(): pl.pallas_call(self_kernel, out_shape=(jax.ShapeDtypeStruct((1, SHARD), j...  3.61 us
  transfers between devices with their start and end apart: 29, of which 12 were waited for; matrix products, arithmetic and copies ran while one was open for 0% of the time, Pallas kernels for 20%

profile of v1, /device:TPU:2, one launch (start us, length us, event | category | flops | bytes accessed | tf_op | source)
XLA Modules:
  0.0 94.7 jit_solution(16804031055750358512)
XLA Ops:
  0.0 1.0 %copy-done.8 = bf16[512,384]{1,0:T(8,128)(2,1)S(1)} copy-done((bf16[512,384]{1,0:T(8,128)(2,1)S(1)}, bf16[512,384]{1,0:T(8,128)(2,1)}, u32[]{:S(2)}) %copy-start.8) | copy-done | bytes 393240
  1.0 0.3 shard_map.37
  1.3 3.1 %collective-permute-start.7 = (bf16[384,512]{1,0:T(8,128)(2,1)S(1)}, bf16[384,512]{1,0:T(8,128)(2,1)S(1)}, u32[]{:S(2)}, u32[]{:S(2)}) collective-permute-start(bf16[384,512]{1,0:T(8,128)(2,1)S(1)} %get-tuple-element.20.flat_ref.refs_4_.refs_7_.refs_8_), channel_id=1, source_target_pairs={{0,12},{1,13},{2,14},{3,15},{4,8},{5,9},{6,10},{7,11},{8,4},{9,5},... | collective-permute-start | bytes 1179656 | tf_op jit(solution)/shard_map/ppermute | solution.py:228
  4.4 1.9 %collective-permute-start.8 = (bf16[384,512]{1,0:T(8,128)(2,1)S(1)}, bf16[384,512]{1,0:T(8,128)(2,1)S(1)}, u32[]{:S(2)}, u32[]{:S(2)}) collective-permute-start(bf16[384,512]{1,0:T(8,128)(2,1)S(1)} %get-tuple-element.20.flat_ref.refs_4_.refs_7_.refs_8_), channel_id=1, source_target_pairs={{0,1},{1,0},{2,3},{3,2},{4,5},{5,4},{6,7},{7,6},{8,9},{9,8},{10,11... | collective-permute-start | bytes 1179656 | tf_op jit(solution)/shard_map/ppermute | solution.py:228
  6.3 2.5 %collective-permute-start.9 = (bf16[384,512]{1,0:T(8,128)(2,1)S(1)}, bf16[384,512]{1,0:T(8,128)(2,1)S(1)}, u32[]{:S(2)}, u32[]{:S(2)}) collective-permute-start(bf16[384,512]{1,0:T(8,128)(2,1)S(1)} %get-tuple-element.20.flat_ref.refs_4_.refs_7_.refs_8_), channel_id=1, source_target_pairs={{0,3},{1,2},{2,1},{3,0},{4,7},{5,6},{6,5},{7,4},{8,11},{9,10},{10,... | collective-permute-start | bytes 1179656 | tf_op jit(solution)/shard_map/ppermute | solution.py:228
  8.8 0.5 collective-permute-start
  9.3 2.2 %collective-permute-start.1 = (bf16[512,384]{1,0:T(8,128)(2,1)S(1)}, bf16[512,384]{1,0:T(8,128)(2,1)S(1)}, u32[]{:S(2)}, u32[]{:S(2)}) collective-permute-start(bf16[512,384]{1,0:T(8,128)(2,1)S(1)} %get-tuple-element.19.unit_ref.refs_0_), channel_id=1, source_target_pairs={{0,96},{1,97},{2,98},{3,99},{4,100},{5,101},{6,102},{7,103},{8,104... | collective-permute-start | bytes 1179656 | tf_op jit(solution)/shard_map/ppermute | solution.py:228
  11.5 2.0 %collective-permute-done.7.refs_5_.refs_8_.refs_9_ = bf16[384,512]{1,0:T(8,128)(2,1)S(1)} collective-permute-done((bf16[384,512]{1,0:T(8,128)(2,1)S(1)}, bf16[384,512]{1,0:T(8,128)(2,1)S(1)}, u32[]{:S(2)}, u32[]{:S(2)}) %collective-permute-start.7) | collective-permute-done | bytes 393248 | tf_op jit(solution)/shard_map/ppermute | solution.py:228
  13.5 1.6 %collective-permute-done.8.refs_6_.refs_9_.refs_10_ = bf16[384,512]{1,0:T(8,128)(2,1)S(1)} collective-permute-done((bf16[384,512]{1,0:T(8,128)(2,1)S(1)}, bf16[384,512]{1,0:T(8,128)(2,1)S(1)}, u32[]{:S(2)}, u32[]{:S(2)}) %collective-permute-start.8) | collective-permute-done | bytes 393248 | tf_op jit(solution)/shard_map/ppermute | solution.py:228
  15.1 0.1 collective-permute-start.2
  15.3 2.5 %collective-permute-done.9.refs_7_.refs_10_.refs_11_ = bf16[384,512]{1,0:T(8,128)(2,1)S(1)} collective-permute-done((bf16[384,512]{1,0:T(8,128)(2,1)S(1)}, bf16[384,512]{1,0:T(8,128)(2,1)S(1)}, u32[]{:S(2)}, u32[]{:S(2)}) %collective-permute-start.9) | collective-permute-done | bytes 393248 | tf_op jit(solution)/shard_map/ppermute | solution.py:228
  17.8 0.0 collective-permute-start.15
  17.8 1.0 %collective-permute-done.refs_1_ = bf16[512,384]{1,0:T(8,128)(2,1)S(1)} collective-permute-done((bf16[512,384]{1,0:T(8,128)(2,1)S(1)}, bf16[512,384]{1,0:T(8,128)(2,1)S(1)}, u32[]{:S(2)}, u32[]{:S(2)}) %collective-permute-start) | collective-permute-done | bytes 393248 | tf_op jit(solution)/shard_map/ppermute | solution.py:228
  18.8 0.7 collective-permute-done.1.refs_2_
  19.5 0.0 collective-permute-start.17
  19.5 1.4 %collective-permute-start.11 = (bf16[384,512]{1,0:T(8,128)(2,1)S(1)}, bf16[384,512]{1,0:T(8,128)(2,1)}, u32[]{:S(2)}, u32[]{:S(2)}) collective-permute-start(bf16[384,512]{1,0:T(8,128)(2,1)S(1)} %collective-permute-done.8.refs_6_.refs_9_.refs_10_), channel_id=1, source_target_pairs={{0,3},{1,2},{2,1},{3,0},{4,7},{5,6},{6,5},{7,4},{8,11},{9,10},{10,... | collective-permute-start | bytes 1179656 | tf_op jit(solution)/shard_map/ppermute | solution.py:228
  20.9 4.1 %collective-permute-done.2.refs_3_ = bf16[512,384]{1,0:T(8,128)(2,1)S(1)} collective-permute-done((bf16[512,384]{1,0:T(8,128)(2,1)S(1)}, bf16[512,384]{1,0:T(8,128)(2,1)S(1)}, u32[]{:S(2)}, u32[]{:S(2)}) %collective-permute-start.2) | collective-permute-done | bytes 393248 | tf_op jit(solution)/shard_map/ppermute | solution.py:228
  25.0 1.9 %collective-permute-start.10 = (bf16[384,512]{1,0:T(8,128)(2,1)S(1)}, bf16[384,512]{1,0:T(8,128)(2,1)S(1)}, u32[]{:S(2)}, u32[]{:S(2)}) collective-permute-start(bf16[384,512]{1,0:T(8,128)(2,1)S(1)} %collective-permute-done.7.refs_5_.refs_8_.refs_9_), channel_id=1, source_target_pairs={{0,1},{1,0},{2,3},{3,2},{4,5},{5,4},{6,7},{7,6},{8,9},{9,8},{10,11... | collective-permute-start | bytes 1179656 | tf_op jit(solution)/shard_map/ppermute | solution.py:228
  26.9 0.8 copy-done
  27.7 3.0 %collective-permute-start.12 = (bf16[384,512]{1,0:T(8,128)(2,1)S(1)}, bf16[384,512]{1,0:T(8,128)(2,1)}, u32[]{:S(2)}, u32[]{:S(2)}) collective-permute-start(bf16[384,512]{1,0:T(8,128)(2,1)S(1)} %collective-permute-done.9.refs_7_.refs_10_.refs_11_), channel_id=1, source_target_pairs={{0,12},{1,13},{2,14},{3,15},{4,8},{5,9},{6,10},{7,11},{8,4},{9,5},... | collective-permute-start | bytes 1179656 | tf_op jit(solution)/shard_map/ppermute | solution.py:228
  30.7 0.8 copy-done.2
  31.4 0.7 copy-done.4
  32.2 1.5 %collective-permute-start.3 = (bf16[512,384]{1,0:T(8,128)(2,1)S(1)}, bf16[512,384]{1,0:T(8,128)(2,1)}, u32[]{:S(2)}, u32[]{:S(2)}) collective-permute-start(bf16[512,384]{1,0:T(8,128)(2,1)S(1)} %collective-permute-done.refs_1_), channel_id=1, source_target_pairs={{0,96},{1,97},{2,98},{3,99},{4,100},{5,101},{6,102},{7,103},{8,104... | collective-permute-start | bytes 1179656 | tf_op jit(solution)/shard_map/ppermute | solution.py:228
  33.7 1.8 %collective-permute-start.5 = (bf16[512,384]{1,0:T(8,128)(2,1)S(1)}, bf16[512,384]{1,0:T(8,128)(2,1)}, u32[]{:S(2)}, u32[]{:S(2)}) collective-permute-start(bf16[512,384]{1,0:T(8,128)(2,1)S(1)} %collective-permute-done.2.refs_3_), channel_id=1, source_target_pairs={{0,32},{1,33},{2,34},{3,35},{4,36},{5,37},{6,38},{7,39},{8,40},{9,... | collective-permute-start | bytes 1179656 | tf_op jit(solution)/shard_map/ppermute | solution.py:228
  35.5 0.7 copy-done.6
  36.2 3.5 %collective-permute-start.13 = (bf16[384,512]{1,0:T(8,128)(2,1)}, bf16[384,512]{1,0:T(8,128)(2,1)}, u32[]{:S(2)}, u32[]{:S(2)}) collective-permute-start(bf16[384,512]{1,0:T(8,128)(2,1)} %collective-permute-done.11.refs_12_.refs_13_), channel_id=1, source_target_pairs={{0,12},{1,13},{2,14},{3,15},{4,8},{5,9},{6,10},{7,11},{8,4},{9,5},... | collective-permute-start | bytes 1179656 | tf_op jit(solution)/shard_map/ppermute | solution.py:228
  39.8 2.1 %collective-permute-done.4.refs_5_ = bf16[512,384]{1,0:T(8,128)(2,1)} collective-permute-done((bf16[512,384]{1,0:T(8,128)(2,1)S(1)}, bf16[512,384]{1,0:T(8,128)(2,1)}, u32[]{:S(2)}, u32[]{:S(2)}) %collective-permute-start.4) | collective-permute-done | bytes 393248 | tf_op jit(solution)/shard_map/ppermute | solution.py:228
  41.8 0.7 collective-permute-done.3.refs_4_
  42.6 0.7 copy-done.9
  43.3 0.7 copy-done.10
  44.0 3.6 %shard_map.38 = (f32[1,512]{1,0:T(1,128)S(1)}, s32[135]{0:T(256)S(1)}, s32[3]{0:T(128)S(1)}) custom-call(s32[1]{0:T(128)} %bitcast.here_ref, s32[256]{0:T(256)S(1)} %copy-done.9, s32[635]{0:T(1024)S(1)} %copy-done.10, bf16[512,384]{1,0:T(8,128)(2,1)S(1)} %get-tuple-element.19.unit_ref.refs_0_, ...), custom_call_target="tpu_custom_call" | custom-call | flops 4000000000 | bytes 1000000 | tf_op jit(solution)/shard_map/pallas_call | solution.py:114
  47.6 1.8 %collective-permute-start.6 = (bf16[512,384]{1,0:T(8,128)(2,1)}, bf16[512,384]{1,0:T(8,128)(2,1)S(1)}, u32[]{:S(2)}, u32[]{:S(2)}) collective-permute-start(bf16[512,384]{1,0:T(8,128)(2,1)} %collective-permute-done.4.refs_5_), channel_id=1, source_target_pairs={{0,32},{1,33},{2,34},{3,35},{4,36},{5,37},{6,38},{7,39},{8,40},{9,... | collective-permute-start | bytes 1179656 | tf_op jit(solution)/shard_map/ppermute | solution.py:228
  49.4 0.2 collective-permute-start.21
  49.6 5.5 %shard_map.39 = (f32[8,512,128]{2,1,0:T(8,128)S(1)}, f32[16,8,512]{2,1,0:T(8,128)S(1)}) custom-call(s32[135]{0:T(256)S(1)} %get-tuple-element.22.list_ref, s32[3]{0:T(128)S(1)} %get-tuple-element.23.count_ref, bf16[512,384]{1,0:T(8,128)(2,1)S(1)} %get-tuple-element.19.unit_ref.refs_0_, bf16[512,384]{1,0:T(8,128)(2,1)S(1)} %collective-permute-done.refs_1_, ...), custom_call_target="tpu_custom_call" | custom-call | flops 1409286144 | bytes 8000000 | tf_op jit(solution)/shard_map/pallas_call | solution.py:216
  55.2 9.5 %shard_map.40 = (f32[8,512,128]{2,1,0:T(8,128)S(1)}, f32[16,8,512]{2,1,0:T(8,128)S(1)}) custom-call(s32[135]{0:T(256)S(1)} %get-tuple-element.22.list_ref, s32[3]{0:T(128)S(1)} %get-tuple-element.23.count_ref, bf16[512,384]{1,0:T(8,128)(2,1)S(1)} %get-tuple-element.19.unit_ref.refs_0_, bf16[512,384]{1,0:T(8,128)(2,1)S(1)} %collective-permute-done.refs_1_, ...), custom_call_target="tpu_custom_call" | custom-call | flops 3221225472 | bytes 8000000 | tf_op jit(solution)/shard_map/pallas_call | solution.py:216
  64.8 5.1 %shard_map.41 = (f32[4,512]{1,0:T(4,128)S(1)}, f32[4,512]{1,0:T(4,128)S(1)}, f32[4,512]{1,0:T(4,128)S(1)}, f32[4,512]{1,0:T(4,128)S(1)}, f32[8,512]{1,0:T(8,128)S(1)}) custom-call(s32[135]{0:T(256)S(1)} %get-tuple-element.22.list_ref, s32[3]{0:T(128)S(1)} %get-tuple-element.23.count_ref, bf16[512,384]{1,0:T(8,128)(2,1)S(1)} %get-tuple-element.19.unit_ref.refs_0_, ...), custom_call_target="tpu_custom_call" | custom-call | flops 1409286144 | bytes 8000000 | tf_op jit(solution)/shard_map/pallas_call | solution.py:216
  69.9 8.1 %collective-permute-start.25 = (f32[8,512]{1,0:T(8,128)S(1)}, f32[8,512]{1,0:T(8,128)S(1)}, u32[]{:S(2)}, u32[]{:S(2)}) collective-permute-start(f32[8,512]{1,0:T(8,128)S(1)} %get-tuple-element.31), channel_id=1, source_target_pairs={{0,16},{1,17},{2,18},{3,19},{4,20},{5,21},{6,22},{7,23},{8,24},{9,... | collective-permute-start | bytes 49160 | tf_op jit(solution)/shard_map/ppermute | solution.py:228
  77.9 1.7 %collective-permute-start.22 = (f32[4,512]{1,0:T(4,128)S(1)}, f32[4,512]{1,0:T(4,128)S(1)}, u32[]{:S(2)}, u32[]{:S(2)}) collective-permute-start(f32[4,512]{1,0:T(4,128)S(1)} %get-tuple-element.29), channel_id=1, source_target_pairs={{0,4},{1,5},{2,6},{3,7},{4,0},{5,1},{6,2},{7,3},{8,12},{9,13},{10,... | collective-permute-start | bytes 24584 | tf_op jit(solution)/shard_map/ppermute | solution.py:228
  79.7 0.4 collective-permute-start.26
  80.0 1.5 %collective-permute-done.22 = f32[4,512]{1,0:T(4,128)S(1)} collective-permute-done((f32[4,512]{1,0:T(4,128)S(1)}, f32[4,512]{1,0:T(4,128)S(1)}, u32[]{:S(2)}, u32[]{:S(2)}) %collective-permute-start.22) | collective-permute-done | bytes 8224 | tf_op jit(solution)/shard_map/ppermute | solution.py:228
  81.6 2.4 %collective-permute-start.23 = (f32[2,512]{1,0:T(2,128)S(1)}, f32[2,512]{1,0:T(2,128)S(1)}, u32[]{:S(2)}, u32[]{:S(2)}) collective-permute-start(f32[2,512]{1,0:T(2,128)S(1)} %slice.41), channel_id=1, source_target_pairs={{0,96},{1,97},{2,98},{3,99},{4,100},{5,101},{6,102},{7,103},{8,104... | collective-permute-start | bytes 12296 | tf_op jit(solution)/shard_map/ppermute | solution.py:228
  84.0 3.6 %collective-permute-start.27 = (f32[2,512]{1,0:T(2,128)S(1)}, f32[2,512]{1,0:T(2,128)S(1)}, u32[]{:S(2)}, u32[]{:S(2)}) collective-permute-start(f32[2,512]{1,0:T(2,128)S(1)} %slice.47), channel_id=1, source_target_pairs={{0,3},{1,2},{2,1},{3,0},{4,7},{5,6},{6,5},{7,4},{8,11},{9,10},{10,... | collective-permute-start | bytes 12296 | tf_op jit(solution)/shard_map/ppermute | solution.py:228
  87.7 0.1 collective-permute-start.24
  87.8 1.5 %collective-permute-done.27 = f32[2,512]{1,0:T(2,128)S(1)} collective-permute-done((f32[2,512]{1,0:T(2,128)S(1)}, f32[2,512]{1,0:T(2,128)S(1)}, u32[]{:S(2)}, u32[]{:S(2)}) %collective-permute-start.27) | collective-permute-done | bytes 4128 | tf_op jit(solution)/shard_map/ppermute | solution.py:228
  89.2 0.1 collective-permute-start.28
  89.3 2.0 %collective-permute-done.24 = f32[1,512]{1,0:T(1,128)S(1)} collective-permute-done((f32[1,512]{1,0:T(1,128)S(1)}, f32[1,512]{1,0:T(1,128)S(1)}, u32[]{:S(2)}, u32[]{:S(2)}) %collective-permute-start.24) | collective-permute-done | bytes 2080 | tf_op jit(solution)/shard_map/ppermute | solution.py:228
  91.3 2.8 %collective-permute-done.28 = f32[1,512]{1,0:T(1,128)S(1)} collective-permute-done((f32[1,512]{1,0:T(1,128)S(1)}, f32[1,512]{1,0:T(1,128)S(1)}, u32[]{:S(2)}, u32[]{:S(2)}) %collective-permute-start.28) | collective-permute-done | bytes 2080 | tf_op jit(solution)/shard_map/ppermute | solution.py:228
  94.1 0.6 fusion.2
  (47 shorter events, 0.1 us)
Async XLA Ops:
  0.0 1.0 %copy-start.8 = (bf16[512,384]{1,0:T(8,128)(2,1)S(1)}, bf16[512,384]{1,0:T(8,128)(2,1)}, u32[]{:S(2)}) copy-start(bf16[512,384]{1,0:T(8,128)(2,1)} %x_ref.1) | copy-start | bytes 1179652
  1.3 12.2 %collective-permute-start.7 = (bf16[384,512]{1,0:T(8,128)(2,1)S(1)}, bf16[384,512]{1,0:T(8,128)(2,1)S(1)}, u32[]{:S(2)}, u32[]{:S(2)}) collective-permute-start(bf16[384,512]{1,0:T(8,128)(2,1)S(1)} %get-tuple-element.20.flat_ref.refs_4_.refs_7_.refs_8_), channel_id=1, source_target_pairs={{0,12},{1,13},{2,14},{3,15},{4,8},{5,9},{6,10},{7,11},{8,4},{9,5},... | collective-permute-start | bytes 1179656 | tf_op jit(solution)/shard_map/ppermute | solution.py:228
  4.4 10.7 %collective-permute-start.8 = (bf16[384,512]{1,0:T(8,128)(2,1)S(1)}, bf16[384,512]{1,0:T(8,128)(2,1)S(1)}, u32[]{:S(2)}, u32[]{:S(2)}) collective-permute-start(bf16[384,512]{1,0:T(8,128)(2,1)S(1)} %get-tuple-element.20.flat_ref.refs_4_.refs_7_.refs_8_), channel_id=1, source_target_pairs={{0,1},{1,0},{2,3},{3,2},{4,5},{5,4},{6,7},{7,6},{8,9},{9,8},{10,11... | collective-permute-start | bytes 1179656 | tf_op jit(solution)/shard_map/ppermute | solution.py:228
  6.3 11.5 %collective-permute-start.9 = (bf16[384,512]{1,0:T(8,128)(2,1)S(1)}, bf16[384,512]{1,0:T(8,128)(2,1)S(1)}, u32[]{:S(2)}, u32[]{:S(2)}) collective-permute-start(bf16[384,512]{1,0:T(8,128)(2,1)S(1)} %get-tuple-element.20.flat_ref.refs_4_.refs_7_.refs_8_), channel_id=1, source_target_pairs={{0,3},{1,2},{2,1},{3,0},{4,7},{5,6},{6,5},{7,4},{8,11},{9,10},{10,... | collective-permute-start | bytes 1179656 | tf_op jit(solution)/shard_map/ppermute | solution.py:228
  8.8 10.0 %collective-permute-start = (bf16[512,384]{1,0:T(8,128)(2,1)S(1)}, bf16[512,384]{1,0:T(8,128)(2,1)S(1)}, u32[]{:S(2)}, u32[]{:S(2)}) collective-permute-start(bf16[512,384]{1,0:T(8,128)(2,1)S(1)} %get-tuple-element.19.unit_ref.refs_0_), channel_id=1, source_target_pairs={{0,32},{1,33},{2,34},{3,35},{4,36},{5,37},{6,38},{7,39},{8,40},{9,... | collective-permute-start | bytes 1179656 | tf_op jit(solution)/shard_map/ppermute | solution.py:228
  9.3 10.1 %collective-permute-start.1 = (bf16[512,384]{1,0:T(8,128)(2,1)S(1)}, bf16[512,384]{1,0:T(8,128)(2,1)S(1)}, u32[]{:S(2)}, u32[]{:S(2)}) collective-permute-start(bf16[512,384]{1,0:T(8,128)(2,1)S(1)} %get-tuple-element.19.unit_ref.refs_0_), channel_id=1, source_target_pairs={{0,96},{1,97},{2,98},{3,99},{4,100},{5,101},{6,102},{7,103},{8,104... | collective-permute-start | bytes 1179656 | tf_op jit(solution)/shard_map/ppermute | solution.py:228
  13.5 6.0 %collective-permute-start.14 = (bf16[384,512]{1,0:T(8,128)(2,1)S(1)}, bf16[384,512]{1,0:T(8,128)(2,1)S(1)}, u32[]{:S(2)}, u32[]{:S(2)}) collective-permute-start(bf16[384,512]{1,0:T(8,128)(2,1)S(1)} %get-tuple-element.20.flat_ref.refs_4_.refs_7_.refs_8_), channel_id=1, source_target_pairs={{0,16},{1,17},{2,18},{3,19},{4,20},{5,21},{6,22},{7,23},{8,24},{9,... | collective-permute-start | bytes 1179656 | tf_op jit(solution)/shard_map/ppermute | solution.py:228
  15.1 9.9 %collective-permute-start.2 = (bf16[512,384]{1,0:T(8,128)(2,1)S(1)}, bf16[512,384]{1,0:T(8,128)(2,1)S(1)}, u32[]{:S(2)}, u32[]{:S(2)}) collective-permute-start(bf16[512,384]{1,0:T(8,128)(2,1)S(1)} %get-tuple-element.19.unit_ref.refs_0_), channel_id=1, source_target_pairs={{0,4},{1,5},{2,6},{3,7},{4,0},{5,1},{6,2},{7,3},{8,12},{9,13},{10,... | collective-permute-start | bytes 1179656 | tf_op jit(solution)/shard_map/ppermute | solution.py:228
  17.8 9.1 %collective-permute-start.15 = (bf16[384,512]{1,0:T(8,128)(2,1)S(1)}, bf16[384,512]{1,0:T(8,128)(2,1)S(1)}, u32[]{:S(2)}, u32[]{:S(2)}) collective-permute-start(bf16[384,512]{1,0:T(8,128)(2,1)S(1)} %collective-permute-done.7.refs_5_.refs_8_.refs_9_), channel_id=1, source_target_pairs={{0,16},{1,17},{2,18},{3,19},{4,20},{5,21},{6,22},{7,23},{8,24},{9,... | collective-permute-start | bytes 1179656 | tf_op jit(solution)/shard_map/ppermute | solution.py:228
  18.8 11.8 %collective-permute-start.16 = (bf16[384,512]{1,0:T(8,128)(2,1)S(1)}, bf16[384,512]{1,0:T(8,128)(2,1)S(1)}, u32[]{:S(2)}, u32[]{:S(2)}) collective-permute-start(bf16[384,512]{1,0:T(8,128)(2,1)S(1)} %collective-permute-done.8.refs_6_.refs_9_.refs_10_), channel_id=1, source_target_pairs={{0,16},{1,17},{2,18},{3,19},{4,20},{5,21},{6,22},{7,23},{8,24},{9,... | collective-permute-start | bytes 1179656 | tf_op jit(solution)/shard_map/ppermute | solution.py:228
  19.5 11.9 %collective-permute-start.17 = (bf16[384,512]{1,0:T(8,128)(2,1)S(1)}, bf16[384,512]{1,0:T(8,128)(2,1)S(1)}, u32[]{:S(2)}, u32[]{:S(2)}) collective-permute-start(bf16[384,512]{1,0:T(8,128)(2,1)S(1)} %collective-permute-done.9.refs_7_.refs_10_.refs_11_), channel_id=1, source_target_pairs={{0,16},{1,17},{2,18},{3,19},{4,20},{5,21},{6,22},{7,23},{8,24},{9,... | collective-permute-start | bytes 1179656 | tf_op jit(solution)/shard_map/ppermute | solution.py:228
  19.5 14.2 %collective-permute-start.11 = (bf16[384,512]{1,0:T(8,128)(2,1)S(1)}, bf16[384,512]{1,0:T(8,128)(2,1)}, u32[]{:S(2)}, u32[]{:S(2)}) collective-permute-start(bf16[384,512]{1,0:T(8,128)(2,1)S(1)} %collective-permute-done.8.refs_6_.refs_9_.refs_10_), channel_id=1, source_target_pairs={{0,3},{1,2},{2,1},{3,0},{4,7},{5,6},{6,5},{7,4},{8,11},{9,10},{10,... | collective-permute-start | bytes 1179656 | tf_op jit(solution)/shard_map/ppermute | solution.py:228
  25.0 10.5 %collective-permute-start.10 = (bf16[384,512]{1,0:T(8,128)(2,1)S(1)}, bf16[384,512]{1,0:T(8,128)(2,1)S(1)}, u32[]{:S(2)}, u32[]{:S(2)}) collective-permute-start(bf16[384,512]{1,0:T(8,128)(2,1)S(1)} %collective-permute-done.7.refs_5_.refs_8_.refs_9_), channel_id=1, source_target_pairs={{0,1},{1,0},{2,3},{3,2},{4,5},{5,4},{6,7},{7,6},{8,9},{9,8},{10,11... | collective-permute-start | bytes 1179656 | tf_op jit(solution)/shard_map/ppermute | solution.py:228
  26.9 0.8 copy-start
  27.7 12.1 %collective-permute-start.12 = (bf16[384,512]{1,0:T(8,128)(2,1)S(1)}, bf16[384,512]{1,0:T(8,128)(2,1)}, u32[]{:S(2)}, u32[]{:S(2)}) collective-permute-start(bf16[384,512]{1,0:T(8,128)(2,1)S(1)} %collective-permute-done.9.refs_7_.refs_10_.refs_11_), channel_id=1, source_target_pairs={{0,12},{1,13},{2,14},{3,15},{4,8},{5,9},{6,10},{7,11},{8,4},{9,5},... | collective-permute-start | bytes 1179656 | tf_op jit(solution)/shard_map/ppermute | solution.py:228
  30.6 0.8 copy-start.2
  31.4 10.4 %collective-permute-start.4 = (bf16[512,384]{1,0:T(8,128)(2,1)S(1)}, bf16[512,384]{1,0:T(8,128)(2,1)}, u32[]{:S(2)}, u32[]{:S(2)}) collective-permute-start(bf16[512,384]{1,0:T(8,128)(2,1)S(1)} %collective-permute-done.1.refs_2_), channel_id=1, source_target_pairs={{0,4},{1,5},{2,6},{3,7},{4,0},{5,1},{6,2},{7,3},{8,12},{9,13},{10,... | collective-permute-start | bytes 1179656 | tf_op jit(solution)/shard_map/ppermute | solution.py:228
  31.4 0.7 copy-start.4
  32.2 10.4 %collective-permute-start.3 = (bf16[512,384]{1,0:T(8,128)(2,1)S(1)}, bf16[512,384]{1,0:T(8,128)(2,1)}, u32[]{:S(2)}, u32[]{:S(2)}) collective-permute-start(bf16[512,384]{1,0:T(8,128)(2,1)S(1)} %collective-permute-done.refs_1_), channel_id=1, source_target_pairs={{0,96},{1,97},{2,98},{3,99},{4,100},{5,101},{6,102},{7,103},{8,104... | collective-permute-start | bytes 1179656 | tf_op jit(solution)/shard_map/ppermute | solution.py:228
  33.7 13.9 %collective-permute-start.5 = (bf16[512,384]{1,0:T(8,128)(2,1)S(1)}, bf16[512,384]{1,0:T(8,128)(2,1)}, u32[]{:S(2)}, u32[]{:S(2)}) collective-permute-start(bf16[512,384]{1,0:T(8,128)(2,1)S(1)} %collective-permute-done.2.refs_3_), channel_id=1, source_target_pairs={{0,32},{1,33},{2,34},{3,35},{4,36},{5,37},{6,38},{7,39},{8,40},{9,... | collective-permute-start | bytes 1179656 | tf_op jit(solution)/shard_map/ppermute | solution.py:228
  35.5 0.7 copy-start.6
  36.2 13.2 %collective-permute-start.13 = (bf16[384,512]{1,0:T(8,128)(2,1)}, bf16[384,512]{1,0:T(8,128)(2,1)}, u32[]{:S(2)}, u32[]{:S(2)}) collective-permute-start(bf16[384,512]{1,0:T(8,128)(2,1)} %collective-permute-done.11.refs_12_.refs_13_), channel_id=1, source_target_pairs={{0,12},{1,13},{2,14},{3,15},{4,8},{5,9},{6,10},{7,11},{8,4},{9,5},... | collective-permute-start | bytes 1179656 | tf_op jit(solution)/shard_map/ppermute | solution.py:228
  39.7 15.4 %collective-permute-start.19 = (bf16[384,512]{1,0:T(8,128)(2,1)}, bf16[384,512]{1,0:T(8,128)(2,1)S(1)}, u32[]{:S(2)}, u32[]{:S(2)}) collective-permute-start(bf16[384,512]{1,0:T(8,128)(2,1)} %collective-permute-done.11.refs_12_.refs_13_), channel_id=1, source_target_pairs={{0,16},{1,17},{2,18},{3,19},{4,20},{5,21},{6,22},{7,23},{8,24},{9,... | collective-permute-start | bytes 1179656 | tf_op jit(solution)/shard_map/ppermute | solution.py:228
  41.8 13.4 %collective-permute-start.18 = (bf16[384,512]{1,0:T(8,128)(2,1)}, bf16[384,512]{1,0:T(8,128)(2,1)S(1)}, u32[]{:S(2)}, u32[]{:S(2)}) collective-permute-start(bf16[384,512]{1,0:T(8,128)(2,1)} %copy-done.6), channel_id=1, source_target_pairs={{0,16},{1,17},{2,18},{3,19},{4,20},{5,21},{6,22},{7,23},{8,24},{9,... | collective-permute-start | bytes 1179656 | tf_op jit(solution)/shard_map/ppermute | solution.py:228
  42.6 12.6 %collective-permute-start.20 = (bf16[384,512]{1,0:T(8,128)(2,1)}, bf16[384,512]{1,0:T(8,128)(2,1)S(1)}, u32[]{:S(2)}, u32[]{:S(2)}) collective-permute-start(bf16[384,512]{1,0:T(8,128)(2,1)} %collective-permute-done.12.refs_13_.refs_14_), channel_id=1, source_target_pairs={{0,16},{1,17},{2,18},{3,19},{4,20},{5,21},{6,22},{7,23},{8,24},{9,... | collective-permute-start | bytes 1179656 | tf_op jit(solution)/shard_map/ppermute | solution.py:228
  42.6 0.7 copy-start.9
  43.3 0.7 copy-start.10
  43.9 5.7 %copy-start.1 = (bf16[384,512]{1,0:T(8,128)(2,1)S(1)}, bf16[384,512]{1,0:T(8,128)(2,1)}, u32[]{:S(2)}) copy-start(bf16[384,512]{1,0:T(8,128)(2,1)} %copy-done) | copy-start | bytes 1179652
  43.9 5.7 %copy-start.3 = (bf16[384,512]{1,0:T(8,128)(2,1)S(1)}, bf16[384,512]{1,0:T(8,128)(2,1)}, u32[]{:S(2)}) copy-start(bf16[384,512]{1,0:T(8,128)(2,1)} %copy-done.2) | copy-start | bytes 1179652
  43.9 5.7 %copy-start.5 = (bf16[384,512]{1,0:T(8,128)(2,1)S(1)}, bf16[384,512]{1,0:T(8,128)(2,1)}, u32[]{:S(2)}) copy-start(bf16[384,512]{1,0:T(8,128)(2,1)} %copy-done.4) | copy-start | bytes 1179652
  47.6 17.2 %collective-permute-start.6 = (bf16[512,384]{1,0:T(8,128)(2,1)}, bf16[512,384]{1,0:T(8,128)(2,1)S(1)}, u32[]{:S(2)}, u32[]{:S(2)}) collective-permute-start(bf16[512,384]{1,0:T(8,128)(2,1)} %collective-permute-done.4.refs_5_), channel_id=1, source_target_pairs={{0,32},{1,33},{2,34},{3,35},{4,36},{5,37},{6,38},{7,39},{8,40},{9,... | collective-permute-start | bytes 1179656 | tf_op jit(solution)/shard_map/ppermute | solution.py:228
  49.4 15.4 %collective-permute-start.21 = (bf16[384,512]{1,0:T(8,128)(2,1)}, bf16[384,512]{1,0:T(8,128)(2,1)S(1)}, u32[]{:S(2)}, u32[]{:S(2)}) collective-permute-start(bf16[384,512]{1,0:T(8,128)(2,1)} %collective-permute-done.13.refs_15_), channel_id=1, source_target_pairs={{0,16},{1,17},{2,18},{3,19},{4,20},{5,21},{6,22},{7,23},{8,24},{9,... | collective-permute-start | bytes 1179656 | tf_op jit(solution)/shard_map/ppermute | solution.py:228
  49.6 5.6 %copy-start.7 = (bf16[384,512]{1,0:T(8,128)(2,1)S(1)}, bf16[384,512]{1,0:T(8,128)(2,1)}, u32[]{:S(2)}) copy-start(bf16[384,512]{1,0:T(8,128)(2,1)} %copy-done.6) | copy-start | bytes 1179652
  69.9 9.8 %collective-permute-start.25 = (f32[8,512]{1,0:T(8,128)S(1)}, f32[8,512]{1,0:T(8,128)S(1)}, u32[]{:S(2)}, u32[]{:S(2)}) collective-permute-start(f32[8,512]{1,0:T(8,128)S(1)} %get-tuple-element.31), channel_id=1, source_target_pairs={{0,16},{1,17},{2,18},{3,19},{4,20},{5,21},{6,22},{7,23},{8,24},{9,... | collective-permute-start | bytes 49160 | tf_op jit(solution)/shard_map/ppermute | solution.py:228
  77.9 3.7 %collective-permute-start.22 = (f32[4,512]{1,0:T(4,128)S(1)}, f32[4,512]{1,0:T(4,128)S(1)}, u32[]{:S(2)}, u32[]{:S(2)}) collective-permute-start(f32[4,512]{1,0:T(4,128)S(1)} %get-tuple-element.29), channel_id=1, source_target_pairs={{0,4},{1,5},{2,6},{3,7},{4,0},{5,1},{6,2},{7,3},{8,12},{9,13},{10,... | collective-permute-start | bytes 24584 | tf_op jit(solution)/shard_map/ppermute | solution.py:228
  79.7 4.3 %collective-permute-start.26 = (f32[4,512]{1,0:T(4,128)S(1)}, f32[4,512]{1,0:T(4,128)S(1)}, u32[]{:S(2)}, u32[]{:S(2)}) collective-permute-start(f32[4,512]{1,0:T(4,128)S(1)} %slice_maximum_fusion), channel_id=1, source_target_pairs={{0,1},{1,0},{2,3},{3,2},{4,5},{5,4},{6,7},{7,6},{8,9},{9,8},{10,11... | collective-permute-start | bytes 24584 | tf_op jit(solution)/shard_map/ppermute | solution.py:228
  81.6 6.1 %collective-permute-start.23 = (f32[2,512]{1,0:T(2,128)S(1)}, f32[2,512]{1,0:T(2,128)S(1)}, u32[]{:S(2)}, u32[]{:S(2)}) collective-permute-start(f32[2,512]{1,0:T(2,128)S(1)} %slice.41), channel_id=1, source_target_pairs={{0,96},{1,97},{2,98},{3,99},{4,100},{5,101},{6,102},{7,103},{8,104... | collective-permute-start | bytes 12296 | tf_op jit(solution)/shard_map/ppermute | solution.py:228
  84.0 5.2 %collective-permute-start.27 = (f32[2,512]{1,0:T(2,128)S(1)}, f32[2,512]{1,0:T(2,128)S(1)}, u32[]{:S(2)}, u32[]{:S(2)}) collective-permute-start(f32[2,512]{1,0:T(2,128)S(1)} %slice.47), channel_id=1, source_target_pairs={{0,3},{1,2},{2,1},{3,0},{4,7},{5,6},{6,5},{7,4},{8,11},{9,10},{10,... | collective-permute-start | bytes 12296 | tf_op jit(solution)/shard_map/ppermute | solution.py:228
  87.7 3.7 %collective-permute-start.24 = (f32[1,512]{1,0:T(1,128)S(1)}, f32[1,512]{1,0:T(1,128)S(1)}, u32[]{:S(2)}, u32[]{:S(2)}) collective-permute-start(f32[1,512]{1,0:T(1,128)S(1)} %slice.43), channel_id=1, source_target_pairs={{0,32},{1,33},{2,34},{3,35},{4,36},{5,37},{6,38},{7,39},{8,40},{9,... | collective-permute-start | bytes 6152 | tf_op jit(solution)/shard_map/ppermute | solution.py:228
  89.2 4.9 %collective-permute-start.28 = (f32[1,512]{1,0:T(1,128)S(1)}, f32[1,512]{1,0:T(1,128)S(1)}, u32[]{:S(2)}, u32[]{:S(2)}) collective-permute-start(f32[1,512]{1,0:T(1,128)S(1)} %slice.49), channel_id=1, source_target_pairs={{0,12},{1,13},{2,14},{3,15},{4,8},{5,9},{6,10},{7,11},{8,4},{9,5},... | collective-permute-start | bytes 6152 | tf_op jit(solution)/shard_map/ppermute | solution.py:228

commit v2 on v0

v2 whole, which is shorter than its diff:
```python
import functools

import jax
import jax.numpy as jnp
import numpy as np
from jax import lax
from jax.experimental import pallas as pl
from jax.experimental.pallas import tpu as pltpu
from jax.sharding import PartitionSpec as P

BLK = 256
SHARD = 512
D = 384
GROUP = 4
VMEM_LIMIT = 40 * 1024 * 1024

CORE = 16
X1, X3, Y1, Y3, Z1, Z3 = 32, 96, 4, 12, 1, 3
GENERATORS = ((X1, X3, Y1), (Y3, Z1, Z3))
SLOTS = ((), (0,), (1,), (2,), (0, 1), (1, 2), (2, 0), (0, 1, 2))
SENDS = ((0, 0), (0, 1), (0, 2), (1, 1), (2, 2), (3, 0), (5, 0))
PHASES = ((1, 2, 3), (4, 5, 6), (7,))


def mask_of(core, slot):
    mask = 0
    for generator in SLOTS[slot]:
        mask ^= GENERATORS[core][generator]
    return mask


def make_table():
    tables = []
    for core in range(2):
        for slots in PHASES:
            for i in slots:
                for j in range(i + 1):
                    a, b = mask_of(core, i), mask_of(1 - core, j)
                    code = 2 * (i - slots[0]) | (2 * j) << 4
                    bit = (a ^ b) & -(a ^ b)
                    if j < i or core == 0:
                        tables.append((code, a, b, 0, core, 1))
                    if j < i or core == 1:
                        tables.append((code, a, b, bit, (i + j) % 2, 0))
    return np.array(tables, np.int32).reshape(2, -1, 6)


TABLE = make_table()
COUNTS = [sum(2 * i + 1 for i in slots) for slots in PHASES]
STARTS = [0, COUNTS[0], COUNTS[0] + COUNTS[1], sum(COUNTS)]
ITEMS = STARTS[3]
STRIDE = ITEMS + GROUP
VMEM = pltpu.VMEM
SMEM = pltpu.SMEM


def spec(space):
    return pl.BlockSpec(memory_space=space)


def params():
    return pltpu.CompilerParams(vmem_limit_bytes=VMEM_LIMIT)


def unit_kernel(here_ref, own_ref, other_ref, out_ref):
    core = (here_ref[0] >> 4) & 1
    for ref, half in ((own_ref, core), (other_ref, 1 - core)):
        values = ref[...].astype(jnp.float32)
        squares = jnp.sum(values * values, axis=1, keepdims=True)
        out_ref[half] = (values * lax.rsqrt(squares + 1e-06)).astype(jnp.bfloat16)


def unit_call(here, own, other):
    return pl.pallas_call(
        unit_kernel,
        out_shape=jax.ShapeDtypeStruct((2, SHARD, D), jnp.bfloat16),
        in_specs=[spec(SMEM), spec(VMEM), spec(VMEM)],
        out_specs=spec(VMEM),
        compiler_params=params(),
        cost_estimate=pl.CostEstimate(flops=1000000, bytes_accessed=1600000, transcendentals=1024),
    )(here, own, other)


def dot(a, b):
    return lax.dot_general(a, b, (((1,), (1,)), ((), ())), preferred_element_type=jnp.float32)


def self_kernel(here_ref, cluster_ref, table_ref, unit_ref, own_ref, full_ref, part_ref, count_ref):
    here = here_ref[0]
    core = (here >> 4) & 1
    for phase in range(3):
        first = STARTS[phase] + GROUP * phase

        def candidate(n, counts):
            full, part = counts
            entry = 6 * (core * ITEMS + n)
            side = jnp.where((here & table_ref[entry + 3]) != 0, 1, 0) ^ table_ref[entry + 4]
            far = side ^ table_ref[entry + 5]
            a = 2 * (((here ^ table_ref[entry + 1]) & ~CORE) | (side << 4))
            b = 2 * (((here ^ table_ref[entry + 2]) & ~CORE) | (far << 4))
            code = table_ref[entry] + side + (far << 4)
            a0, a1 = cluster_ref[a], cluster_ref[a + 1]
            b0, b1 = cluster_ref[b], cluster_ref[b + 1]
            quads = (
                jnp.where(a0 == b0, 1, 0)
                + jnp.where(a0 == b1, 2, 0)
                + jnp.where(a1 == b0, 4, 0)
                + jnp.where(a1 == b1, 8, 0)
            )
            full_ref[first + full] = code
            part_ref[first + part] = code | (quads << 8)
            return (
                full + jnp.where(quads == 15, 1, 0),
                part + jnp.where((quads != 0) & (quads != 15), 1, 0),
            )

        end = STARTS[phase + 1] - (1 if phase == 2 else 0)
        full, part = lax.fori_loop(STARTS[phase], end, candidate, (jnp.int32(0), jnp.int32(0)))
        last = full_ref[first + jnp.maximum(full - 1, 0)]
        for n in range(GROUP - 1):
            full_ref[first + full + n] = last
        count_ref[2 * phase] = full
        count_ref[2 * phase + 1] = part
        if phase == 2:
            first = STARTS[3] + 3 * GROUP
            full, part = candidate(STARTS[3] - 1, (jnp.int32(0), jnp.int32(0)))
            count_ref[6] = full
            count_ref[7] = part

    first0 = cluster_ref[2 * here]
    first1 = cluster_ref[2 * here + 1]
    there = here ^ CORE
    second0 = cluster_ref[2 * there]
    second1 = cluster_ref[2 * there + 1]
    mine = unit_ref[core]
    best = jnp.full((8, SHARD), -2.0, jnp.float32)
    col = lax.broadcasted_iota(jnp.int32, (BLK, SHARD), 1)
    row = lax.broadcasted_iota(jnp.int32, (BLK, SHARD), 0)
    label = jnp.where(col[:1] < BLK, first0, first1)
    for half, name in ((0, first0), (1, first1)):
        scores = dot(unit_ref[core, half * BLK : half * BLK + BLK, :], mine)
        keep = (row + half * BLK != col) & (label == name)
        scores = jnp.where(keep, scores, jnp.float32(-2.0))
        best = jnp.maximum(best, jnp.max(scores.reshape(BLK // 8, 8, SHARD), axis=0))
    for half, name in ((0, second0), (1, second1)):
        scores = dot(unit_ref[1 - core, half * BLK : half * BLK + BLK, :], mine)
        scores = jnp.where(label == name, scores, jnp.float32(-2.0))
        best = jnp.maximum(best, jnp.max(scores.reshape(BLK // 8, 8, SHARD), axis=0))
    own_ref[...] = jnp.max(best, axis=0, keepdims=True)


def self_call(here, cluster, table, unit):
    lists = jax.ShapeDtypeStruct((ITEMS + 4 * GROUP,), jnp.int32)
    return pl.pallas_call(
        self_kernel,
        out_shape=(
            jax.ShapeDtypeStruct((1, SHARD), jnp.float32),
            lists,
            lists,
            jax.ShapeDtypeStruct((8,), jnp.int32),
        ),
        in_specs=[spec(SMEM), spec(SMEM), spec(SMEM), spec(VMEM)],
        out_specs=(spec(VMEM), spec(SMEM), spec(SMEM), spec(SMEM)),
        compiler_params=params(),
        cost_estimate=pl.CostEstimate(flops=4000000000, bytes_accessed=1000000, transcendentals=0),
    )(here, cluster, table, unit)


def fold(row_ref, col_ref, i, j, rows, cols, scores):
    best = scores[:, :128]
    for k in range(1, scores.shape[1] // 128):
        best = jnp.maximum(best, scores[:, 128 * k : 128 * k + 128])
    row_ref[i, rows, :] = jnp.maximum(row_ref[i, rows, :], best)
    down = jnp.max(scores.reshape(scores.shape[0] // 8, 8, scores.shape[1]), axis=0)
    col_ref[j, :, cols] = jnp.maximum(col_ref[j, :, cols], down)


def score_full(a_ref, b_ref, row_ref, col_ref, word):
    i = word & 15
    j = (word >> 4) & 15
    scores = dot(a_ref[i], b_ref[j])
    fold(row_ref, col_ref, i, j, slice(None), slice(None), scores)


def score_part(a_ref, b_ref, row_ref, col_ref, word):
    i = word & 15
    j = (word >> 4) & 15
    for quad in range(4):

        @pl.when(((word >> (8 + quad)) & 1) == 1)
        def _():
            rows = pl.ds((quad // 2) * BLK, BLK)
            cols = pl.ds((quad % 2) * BLK, BLK)
            scores = dot(a_ref[i, rows, :], b_ref[j, cols, :])
            fold(row_ref, col_ref, i, j, rows, cols, scores)


def score_lists(phase, full_ref, part_ref, count_ref, *refs):
    first = STARTS[phase] + GROUP * phase

    @pl.loop(0, count_ref[2 * phase], step=GROUP)
    def _(n):
        for k in range(GROUP):
            score_full(*refs, full_ref[first + n + k])

    @pl.loop(0, count_ref[2 * phase + 1])
    def _(n):
        score_part(*refs, part_ref[first + n])


def put_rows(out_ref, places, row_ref):
    for n, place in enumerate(places):
        for k in range(SHARD // 128):
            part = row_ref[n, 128 * k : 128 * k + 128, :].T
            out_ref[place : place + 1, 128 * k : 128 * k + 128] = jnp.max(
                part, axis=0, keepdims=True
            )


def score_kernel(phase, full_ref, part_ref, count_ref, *refs):
    slots = PHASES[phase]
    mine, refs = refs[: len(slots)], refs[len(slots) :]
    if phase == 0:
        theirs, refs = refs[:4], refs[4:]
        rows_out, col_ref, a_buf, b_buf, row_ref = refs
        col_ref[...] = jnp.full(col_ref.shape, -2.0, jnp.float32)
    else:
        theirs, refs = refs[:7], refs[7:]
        col_in, rows_out, col_ref, b_buf, a_buf, row_ref = refs
        col_ref[...] = col_in[...]
    row_ref[...] = jnp.full(row_ref.shape, -2.0, jnp.float32)
    for n, ref in enumerate(mine):
        a_buf[2 * n : 2 * n + 2] = ref[...]
    for n, ref in enumerate(theirs):
        b_buf[2 * n : 2 * n + 2] = ref[...]
    score_lists(phase, full_ref, part_ref, count_ref, a_buf, b_buf, row_ref, col_ref)
    put_rows(rows_out, range(2 * len(slots)), row_ref)


def score_call(phase, plan, mine, theirs, state):
    rows = 2 * len(PHASES[phase])
    col_type = jax.ShapeDtypeStruct((16, 8, SHARD), jnp.float32)
    row_type = jax.ShapeDtypeStruct((rows, SHARD), jnp.float32)
    b_type = jax.ShapeDtypeStruct((2 * len(theirs), SHARD, D), jnp.bfloat16)
    outs = (row_type, col_type)
    scratch = [VMEM((rows, SHARD, D), jnp.bfloat16)]
    if phase == 0:
        scratch = scratch + [VMEM(b_type.shape, jnp.bfloat16)]
    else:
        outs = outs + (b_type,)
    scratch = scratch + [VMEM((rows, SHARD, 128), jnp.float32)]
    operands = list(mine) + list(theirs) + list(state)
    flops = (COUNTS[phase] // 2) * 2 * SHARD * SHARD * D
    return pl.pallas_call(
        functools.partial(score_kernel, phase),
        out_shape=outs,
        in_specs=[spec(SMEM)] * 3 + [spec(VMEM)] * len(operands),
        out_specs=(spec(VMEM),) * len(outs),
        scratch_shapes=scratch,
        compiler_params=params(),
        cost_estimate=pl.CostEstimate(flops=flops, bytes_accessed=8000000, transcendentals=0),
    )(*plan, *operands)


def late_kernel(full_ref, part_ref, count_ref, mine, b_ref, col_in, row_ref, col_ref):
    row_ref[...] = jnp.full(row_ref.shape, -2.0, jnp.float32)
    col_ref[...] = col_in[...]
    score_lists(2, full_ref, part_ref, count_ref, mine, b_ref, row_ref, col_ref)


def late_call(plan, mine, b_buf, cols):
    outs = (
        jax.ShapeDtypeStruct((2, SHARD, 128), jnp.float32),
        jax.ShapeDtypeStruct((16, 8, SHARD), jnp.float32),
    )
    return pl.pallas_call(
        late_kernel,
        out_shape=outs,
        in_specs=[spec(SMEM)] * 3 + [spec(VMEM)] * 3,
        out_specs=(spec(VMEM),) * 2,
        compiler_params=params(),
        cost_estimate=pl.CostEstimate(
            flops=(COUNTS[2] // 2) * 2 * SHARD * SHARD * D, bytes_accessed=8000000, transcendentals=0
        ),
    )(*plan, mine, b_buf, cols)


KEPT = (0, 1, 2, 4)
SENT = (3, 6, 5, 7)


def last_kernel(
    full_ref, part_ref, count_ref, mine, theirs, row_in, col_in, rows0, rows1, keep_ref, send_ref, other_ref, row_ref, col_ref
):
    row_ref[...] = row_in[...]
    col_ref[...] = col_in[14:16]
    first = STARTS[3] + 3 * GROUP

    @pl.when(count_ref[6] != 0)
    def _():
        score_full(mine, theirs, row_ref, col_ref, full_ref[first] & 31)

    @pl.when(count_ref[7] != 0)
    def _():
        score_part(mine, theirs, row_ref, col_ref, part_ref[first] & ~224)

    keep_ref[0:2] = jnp.full((2, SHARD), -2.0, jnp.float32)
    for out_ref, slots in ((keep_ref, KEPT), (send_ref, SENT)):
        for place, slot in enumerate(slots):
            if slot in PHASES[0]:
                n = 2 * (slot - PHASES[0][0])
                out_ref[2 * place : 2 * place + 2] = rows0[n : n + 2]
            elif slot in PHASES[1]:
                n = 2 * (slot - PHASES[1][0])
                out_ref[2 * place : 2 * place + 2] = rows1[n : n + 2]
    put_rows(send_ref, (6, 7), row_ref)
    for place, slot in enumerate(KEPT + SENT):
        for half in range(2):
            ref, n = (col_ref, half) if slot == 7 else (col_in, 2 * slot + half)
            at = 2 * place + half
            other_ref[at : at + 1, :] = jnp.max(ref[n], axis=0, keepdims=True)


def last_call(plan, mine, theirs, rows2, cols, rows0, rows1):
    eight = jax.ShapeDtypeStruct((8, SHARD), jnp.float32)
    outs = (eight, eight, jax.ShapeDtypeStruct((16, SHARD), jnp.float32))
    return pl.pallas_call(
        last_kernel,
        out_shape=outs,
        in_specs=[spec(SMEM)] * 3 + [spec(VMEM)] * 6,
        out_specs=(spec(VMEM),) * 3,
        scratch_shapes=[VMEM((2, SHARD, 128), jnp.float32), VMEM((2, 8, SHARD), jnp.float32)],
        compiler_params=params(),
        cost_estimate=pl.CostEstimate(
            flops=2 * SHARD * SHARD * D, bytes_accessed=8000000, transcendentals=0
        ),
    )(*plan, mine, theirs, rows2, cols, rows0, rows1)


def swap(x):
    return lax.ppermute(x, ("row", "col"), [(s, s ^ CORE) for s in range(128)])


def exchange(x, generator):
    pairs = [(s, s ^ GENERATORS[(s >> 4) & 1][generator]) for s in range(128)]
    return lax.ppermute(x, ("row", "col"), pairs)


def body(embeddings, block_cluster):
    here = (lax.axis_index("row") * 16 + lax.axis_index("col")).astype(jnp.int32).reshape(1)
    unit = unit_call(here, embeddings, swap(embeddings))
    own, *plan = self_call(here, block_cluster, jnp.asarray(TABLE.reshape(-1)), unit)
    mine, theirs = [unit], [unit]
    for slot, (source, generator) in enumerate(SENDS, 1):
        mine.append(exchange(mine[source], generator))
        theirs.append(swap(mine[slot]))
    rows0, cols = score_call(0, plan, mine[1:4], theirs[:4], ())
    rows1, cols, b_buf = score_call(1, plan, mine[4:7], theirs[:7], (cols,))
    rows2, cols = late_call(plan, mine[7], b_buf, cols)
    keep, send, other = last_call(plan, mine[7], theirs[7], rows2, cols, rows0, rows1)
    other = swap(other)
    keep = jnp.maximum(keep, other[:8])
    send = jnp.maximum(send, other[8:])
    keep = jnp.maximum(keep, exchange(send, 2))
    keep = jnp.maximum(keep[:4], exchange(keep[4:], 1))
    keep = jnp.maximum(keep[:2], exchange(keep[2:], 0))
    second = (here & CORE) != 0
    ours = jnp.where(second, keep[1], keep[0])
    other = swap(jnp.where(second, keep[0], keep[1]))
    return jnp.maximum(own.reshape(SHARD), jnp.maximum(ours, other))


def solution(mesh):
    placed = (P(("row", "col"), None), P())
    return jax.shard_map(
        body, mesh=mesh, in_specs=placed, out_specs=P(("row", "col")), check_vma=False
    )
```

time: 416 us -> 83 us (0.20)
  the two profiles are of different devices: /device:TPU:4 before, /device:TPU:1 now
where the time goes in v2:
time: 83 us; the launch traced here: 82.6 us
  starting transfers between devices  34.7 us (42%)
  waiting for transfers between devices  28.1 us (34%)
  Pallas kernels  16.8 us (20%)
  local copies, waits for them, and re-layouts  2.37 us (3%)
    ppermute x10, waiting for transfers between devices, exchange(): return lax.ppermute(x, ('row', 'col'), pairs)  24.8 us
    ppermute x10, starting transfers between devices, exchange(): return lax.ppermute(x, ('row', 'col'), pairs)  22.5 us
    ppermute x10, starting transfers between devices, swap(): return lax.ppermute(x, ('row', 'col'), [(s, s ^ CORE) for s in range(128)])  12.2 us
    pallas_call x2, Pallas kernels, score_call(): pl.pallas_call(functools.partial(score_kernel, phase), out_shape=outs, in...  8.67 us
    pallas_call x1, Pallas kernels, self_call(): pl.pallas_call(self_kernel, out_shape=(jax.ShapeDtypeStruct((1, SHARD), j...  3.62 us
    pallas_call x1, Pallas kernels, late_call(): pl.pallas_call(late_kernel, out_shape=outs, in_specs=[spec(SMEM)] * 3 + [...  3.37 us
    ppermute x10, waiting for transfers between devices, swap(): return lax.ppermute(x, ('row', 'col'), [(s, s ^ CORE) for s in range(128)])  3.26 us
    unnamed x6, local copies, waits for them, and re-layouts  2.36 us
  transfers between devices with their start and end apart: 20, of which 11 were waited for; matrix products, arithmetic and copies ran while one was open for 0% of the time, Pallas kernels for 19%

profile of v2, /device:TPU:1, one launch (start us, length us, event | category | flops | bytes accessed | tf_op | source)
XLA Modules:
  0.0 82.6 jit_solution(2184681993881750028)
XLA Ops:
  0.0 1.4 %collective-permute-start = (bf16[512,384]{1,0:T(8,128)(2,1)}, bf16[512,384]{1,0:T(8,128)(2,1)S(1)}, u32[]{:S(2)}, u32[]{:S(2)}) collective-permute-start(bf16[512,384]{1,0:T(8,128)(2,1)} %own_ref.1), channel_id=1, source_target_pairs={{0,16},{1,17},{2,18},{3,19},{4,20},{5,21},{6,22},{7,23},{8,24},{9,... | collective-permute-start | bytes 1179656 | tf_op jit(solution)/shard_map/ppermute | solution.py:341
  1.4 1.6 %collective-permute-done.other_ref = bf16[512,384]{1,0:T(8,128)(2,1)S(1)} collective-permute-done((bf16[512,384]{1,0:T(8,128)(2,1)}, bf16[512,384]{1,0:T(8,128)(2,1)S(1)}, u32[]{:S(2)}, u32[]{:S(2)}) %collective-permute-start) | collective-permute-done | bytes 393248 | tf_op jit(solution)/shard_map/ppermute | solution.py:341
  3.0 1.0 %copy-done = bf16[512,384]{1,0:T(8,128)(2,1)S(1)} copy-done((bf16[512,384]{1,0:T(8,128)(2,1)S(1)}, bf16[512,384]{1,0:T(8,128)(2,1)}, u32[]{:S(2)}) %copy-start) | copy-done | bytes 393240
  4.0 0.3 shard_map.37.unit_ref.refs_3_
  4.3 1.8 %collective-permute-start.1 = (bf16[2,512,384]{2,1,0:T(8,128)(2,1)S(1)}, bf16[2,512,384]{2,1,0:T(8,128)(2,1)S(1)}, u32[]{:S(2)}, u32[]{:S(2)}) collective-permute-start(bf16[2,512,384]{2,1,0:T(8,128)(2,1)S(1)} %shard_map.37.unit_ref.refs_3_), channel_id=1, source_target_pairs={{0,96},{1,97},{2,98},{3,99},{4,100},{5,101},{6,102},{7,103},{8,104... | collective-permute-start | bytes 2359304 | tf_op jit(solution)/shard_map/ppermute | solution.py:346
  6.1 2.2 %collective-permute-start.7 = (bf16[2,512,384]{2,1,0:T(8,128)(2,1)S(1)}, bf16[2,512,384]{2,1,0:T(8,128)(2,1)S(1)}, u32[]{:S(2)}, u32[]{:S(2)}) collective-permute-start(bf16[2,512,384]{2,1,0:T(8,128)(2,1)S(1)} %shard_map.37.unit_ref.refs_3_), channel_id=1, source_target_pairs={{0,4},{1,5},{2,6},{3,7},{4,0},{5,1},{6,2},{7,3},{8,12},{9,13},{10,... | collective-permute-start | bytes 2359304 | tf_op jit(solution)/shard_map/ppermute | solution.py:346
  8.3 2.7 %collective-permute-start.5 = (bf16[2,512,384]{2,1,0:T(8,128)(2,1)S(1)}, bf16[2,512,384]{2,1,0:T(8,128)(2,1)S(1)}, u32[]{:S(2)}, u32[]{:S(2)}) collective-permute-start(bf16[2,512,384]{2,1,0:T(8,128)(2,1)S(1)} %shard_map.37.unit_ref.refs_3_), channel_id=1, source_target_pairs={{0,32},{1,33},{2,34},{3,35},{4,36},{5,37},{6,38},{7,39},{8,40},{9,... | collective-permute-start | bytes 2359304 | tf_op jit(solution)/shard_map/ppermute | solution.py:346
  11.0 4.7 %collective-permute-done.1.refs_1_ = bf16[2,512,384]{2,1,0:T(8,128)(2,1)S(1)} collective-permute-done((bf16[2,512,384]{2,1,0:T(8,128)(2,1)S(1)}, bf16[2,512,384]{2,1,0:T(8,128)(2,1)S(1)}, u32[]{:S(2)}, u32[]{:S(2)}) %collective-permute-start.1) | collective-permute-done | bytes 786464 | tf_op jit(solution)/shard_map/ppermute | solution.py:346
  15.7 3.6 %collective-permute-start.2 = (bf16[2,512,384]{2,1,0:T(8,128)(2,1)S(1)}, bf16[2,512,384]{2,1,0:T(8,128)(2,1)S(1)}, u32[]{:S(2)}, u32[]{:S(2)}) collective-permute-start(bf16[2,512,384]{2,1,0:T(8,128)(2,1)S(1)} %collective-permute-done.1.refs_1_), channel_id=1, source_target_pairs={{0,4},{1,5},{2,6},{3,7},{4,0},{5,1},{6,2},{7,3},{8,12},{9,13},{10,... | collective-permute-start | bytes 2359304 | tf_op jit(solution)/shard_map/ppermute | solution.py:346
  19.3 0.0 collective-permute-done.7.refs_2_
  19.3 0.3 collective-permute-start.11
  19.6 2.7 %collective-permute-start.8 = (bf16[2,512,384]{2,1,0:T(8,128)(2,1)S(1)}, bf16[2,512,384]{2,1,0:T(8,128)(2,1)S(1)}, u32[]{:S(2)}, u32[]{:S(2)}) collective-permute-start(bf16[2,512,384]{2,1,0:T(8,128)(2,1)S(1)} %collective-permute-done.7.refs_2_), channel_id=1, source_target_pairs={{0,32},{1,33},{2,34},{3,35},{4,36},{5,37},{6,38},{7,39},{8,40},{9,... | collective-permute-start | bytes 2359304 | tf_op jit(solution)/shard_map/ppermute | solution.py:346
  22.3 0.0 collective-permute-done.5.refs_0_
  22.3 1.6 %collective-permute-start.6 = (bf16[2,512,384]{2,1,0:T(8,128)(2,1)S(1)}, bf16[2,512,384]{2,1,0:T(8,128)(2,1)S(1)}, u32[]{:S(2)}, u32[]{:S(2)}) collective-permute-start(bf16[2,512,384]{2,1,0:T(8,128)(2,1)S(1)} %collective-permute-done.5.refs_0_), channel_id=1, source_target_pairs={{0,96},{1,97},{2,98},{3,99},{4,100},{5,101},{6,102},{7,103},{8,104... | collective-permute-start | bytes 2359304 | tf_op jit(solution)/shard_map/ppermute | solution.py:346
  23.9 0.0 collective-permute-start.9
  23.9 5.1 %collective-permute-done.2.refs_1_ = bf16[2,512,384]{2,1,0:T(8,128)(2,1)S(1)} collective-permute-done((bf16[2,512,384]{2,1,0:T(8,128)(2,1)S(1)}, bf16[2,512,384]{2,1,0:T(8,128)(2,1)S(1)}, u32[]{:S(2)}, u32[]{:S(2)}) %collective-permute-start.2) | collective-permute-done | bytes 786464 | tf_op jit(solution)/shard_map/ppermute | solution.py:346
  29.0 2.7 %collective-permute-start.3 = (bf16[2,512,384]{2,1,0:T(8,128)(2,1)S(1)}, bf16[2,512,384]{2,1,0:T(8,128)(2,1)S(1)}, u32[]{:S(2)}, u32[]{:S(2)}) collective-permute-start(bf16[2,512,384]{2,1,0:T(8,128)(2,1)S(1)} %collective-permute-done.2.refs_1_), channel_id=1, source_target_pairs={{0,32},{1,33},{2,34},{3,35},{4,36},{5,37},{6,38},{7,39},{8,40},{9,... | collective-permute-start | bytes 2359304 | tf_op jit(solution)/shard_map/ppermute | solution.py:346
  31.7 0.0 collective-permute-done.11.refs_6_
  31.7 0.0 collective-permute-start.10
  31.7 0.2 collective-permute-done.8.refs_2_
  31.9 0.3 collective-permute-start.14
  32.2 1.4 %collective-permute-done.6.refs_0_ = bf16[2,512,384]{2,1,0:T(8,128)(2,1)S(1)} collective-permute-done((bf16[2,512,384]{2,1,0:T(8,128)(2,1)S(1)}, bf16[2,512,384]{2,1,0:T(8,128)(2,1)S(1)}, u32[]{:S(2)}, u32[]{:S(2)}) %collective-permute-start.6) | collective-permute-done | bytes 786464 | tf_op jit(solution)/shard_map/ppermute | solution.py:346
  33.6 0.9 %collective-permute-start.12 = (bf16[2,512,384]{2,1,0:T(8,128)(2,1)S(1)}, bf16[2,512,384]{2,1,0:T(8,128)(2,1)S(1)}, u32[]{:S(2)}, u32[]{:S(2)}) collective-permute-start(bf16[2,512,384]{2,1,0:T(8,128)(2,1)S(1)} %collective-permute-done.6.refs_0_), channel_id=1, source_target_pairs={{0,16},{1,17},{2,18},{3,19},{4,20},{5,21},{6,22},{7,23},{8,24},{9,... | collective-permute-start | bytes 2359304 | tf_op jit(solution)/shard_map/ppermute | solution.py:341
  34.5 0.0 collective-permute-done.9.refs_4_
  34.5 0.0 collective-permute-start.13
  34.5 6.6 %collective-permute-done.3.mine = bf16[2,512,384]{2,1,0:T(8,128)(2,1)S(1)} collective-permute-done((bf16[2,512,384]{2,1,0:T(8,128)(2,1)S(1)}, bf16[2,512,384]{2,1,0:T(8,128)(2,1)S(1)}, u32[]{:S(2)}, u32[]{:S(2)}) %collective-permute-start.3) | collective-permute-done | bytes 786464 | tf_op jit(solution)/shard_map/ppermute | solution.py:346
  41.1 0.8 collective-permute-start.4
  41.9 0.7 copy-done.1
  42.6 0.7 copy-done.2
  43.3 3.6 %shard_map.38 = (f32[1,512]{1,0:T(1,128)S(1)}, s32[79]{0:T(128)S(1)}, s32[79]{0:T(128)S(1)}, s32[8]{0:T(128)S(1)}) custom-call(s32[1]{0:T(128)} %bitcast.here_ref, s32[256]{0:T(256)S(1)} %copy-done.1, s32[756]{0:T(1024)S(1)} %copy-done.2, bf16[2,512,384]{2,1,0:T(8,128)(2,1)S(1)} %shard_map.37.unit_ref.refs_3_), custom_call_target="tpu_custom_call" | custom-call | flops 4000000000 | bytes 1000000 | tf_op jit(solution)/shard_map/pallas_call | solution.py:154
  46.9 0.0 collective-permute-done.10.refs_5_
  46.9 2.9 %shard_map.39 = (f32[6,512]{1,0:T(8,128)S(1)}, f32[16,8,512]{2,1,0:T(8,128)S(1)}) custom-call(s32[79]{0:T(128)S(1)} %get-tuple-element.20.full_ref, s32[79]{0:T(128)S(1)} %get-tuple-element.21.part_ref, s32[8]{0:T(128)S(1)} %get-tuple-element.22.count_ref, bf16[2,512,384]{2,1,0:T(8,128)(2,1)S(1)} %collective-permute-done.5.refs_0_, ...), custom_call_target="tpu_custom_call" | custom-call | flops 1409286144 | bytes 8000000 | tf_op jit(solution)/shard_map/pallas_call | solution.py:254
  49.8 0.0 collective-permute-done.14.refs_9_
  49.8 0.0 collective-permute-done.13.refs_8_
  49.9 5.8 %shard_map.40 = (f32[6,512]{1,0:T(8,128)S(1)}, f32[16,8,512]{2,1,0:T(8,128)S(1)}, bf16[14,512,384]{2,1,0:T(8,128)(2,1)S(1)}) custom-call(s32[79]{0:T(128)S(1)} %get-tuple-element.20.full_ref, s32[79]{0:T(128)S(1)} %get-tuple-element.21.part_ref, s32[8]{0:T(128)S(1)} %get-tuple-element.22.count_ref, bf16[2,512,384]{2,1,0:T(8,128)(2,1)S(1)} %collective-permute-done.6.refs_0_, ...), custom_call_target="tpu_custom_call" | custom-call | flops 3221225472 | bytes 8000000 | tf_op jit(solution)/shard_map/pallas_call | solution.py:254
  55.6 3.4 %shard_map.41 = (f32[2,512,128]{2,1,0:T(8,128)S(1)}, f32[16,8,512]{2,1,0:T(8,128)S(1)}) custom-call(s32[79]{0:T(128)S(1)} %get-tuple-element.20.full_ref, s32[79]{0:T(128)S(1)} %get-tuple-element.21.part_ref, s32[8]{0:T(128)S(1)} %get-tuple-element.22.count_ref, bf16[2,512,384]{2,1,0:T(8,128)(2,1)S(1)} %collective-permute-done.3.mine, ...), custom_call_target="tpu_custom_call" | custom-call | flops 1409286144 | bytes 8000000 | tf_op jit(solution)/shard_map/pallas_call | solution.py:276
  59.0 0.8 shard_map.42
  59.8 1.8 %collective-permute-start.15 = (f32[16,512]{1,0:T(8,128)S(1)}, f32[16,512]{1,0:T(8,128)S(1)}, u32[]{:S(2)}, u32[]{:S(2)}) collective-permute-start(f32[16,512]{1,0:T(8,128)S(1)} %get-tuple-element.31), channel_id=1, source_target_pairs={{0,16},{1,17},{2,18},{3,19},{4,20},{5,21},{6,22},{7,23},{8,24},{9,... | collective-permute-start | bytes 98312 | tf_op jit(solution)/shard_map/ppermute | solution.py:341
  61.7 0.9 %collective-permute-done.15 = f32[16,512]{1,0:T(8,128)S(1)} collective-permute-done((f32[16,512]{1,0:T(8,128)S(1)}, f32[16,512]{1,0:T(8,128)S(1)}, u32[]{:S(2)}, u32[]{:S(2)}) %collective-permute-start.15) | collective-permute-done | bytes 32800 | tf_op jit(solution)/shard_map/ppermute | solution.py:341
  62.5 4.2 %collective-permute-start.16 = (f32[8,512]{1,0:T(8,128)S(1)}, f32[8,512]{1,0:T(8,128)S(1)}, u32[]{:S(2)}, u32[]{:S(2)}) collective-permute-start(f32[8,512]{1,0:T(8,128)S(1)} %slice_maximum_fusion), channel_id=1, source_target_pairs={{0,4},{1,5},{2,6},{3,7},{4,0},{5,1},{6,2},{7,3},{8,12},{9,13},{10,... | collective-permute-start | bytes 49160 | tf_op jit(solution)/shard_map/ppermute | solution.py:346
  66.7 1.1 %collective-permute-done.16 = f32[8,512]{1,0:T(8,128)S(1)} collective-permute-done((f32[8,512]{1,0:T(8,128)S(1)}, f32[8,512]{1,0:T(8,128)S(1)}, u32[]{:S(2)}, u32[]{:S(2)}) %collective-permute-start.16) | collective-permute-done | bytes 16416 | tf_op jit(solution)/shard_map/ppermute | solution.py:346
  67.9 0.1 collective-permute-start.17
  68.0 2.8 %collective-permute-done.17 = f32[4,512]{1,0:T(4,128)S(1)} collective-permute-done((f32[4,512]{1,0:T(4,128)S(1)}, f32[4,512]{1,0:T(4,128)S(1)}, u32[]{:S(2)}, u32[]{:S(2)}) %collective-permute-start.17) | collective-permute-done | bytes 8224 | tf_op jit(solution)/shard_map/ppermute | solution.py:346
  70.8 0.8 collective-permute-start.18
  71.5 3.0 %collective-permute-done.18 = f32[2,512]{1,0:T(2,128)S(1)} collective-permute-done((f32[2,512]{1,0:T(2,128)S(1)}, f32[2,512]{1,0:T(2,128)S(1)}, u32[]{:S(2)}, u32[]{:S(2)}) %collective-permute-start.18) | collective-permute-done | bytes 4128 | tf_op jit(solution)/shard_map/ppermute | solution.py:346
  74.5 6.6 %collective-permute-start.19 = (f32[512]{0:T(512)S(1)}, f32[512]{0:T(512)S(1)}, u32[]{:S(2)}, u32[]{:S(2)}) collective-permute-start(f32[512]{0:T(512)S(1)} %bitcast.7), channel_id=1, source_target_pairs={{0,16},{1,17},{2,18},{3,19},{4,20},{5,21},{6,22},{7,23},{8,24},{9,... | collective-permute-start | bytes 6152 | tf_op jit(solution)/shard_map/ppermute | solution.py:341
  81.2 0.8 collective-permute-done.19
  82.0 0.6 maximum_maximum_fusion
  (12 shorter events, 0.1 us)
Async XLA Ops:
  0.0 3.0 %collective-permute-start = (bf16[512,384]{1,0:T(8,128)(2,1)}, bf16[512,384]{1,0:T(8,128)(2,1)S(1)}, u32[]{:S(2)}, u32[]{:S(2)}) collective-permute-start(bf16[512,384]{1,0:T(8,128)(2,1)} %own_ref.1), channel_id=1, source_target_pairs={{0,16},{1,17},{2,18},{3,19},{4,20},{5,21},{6,22},{7,23},{8,24},{9,... | collective-permute-start | bytes 1179656 | tf_op jit(solution)/shard_map/ppermute | solution.py:341
  3.0 1.0 %copy-start = (bf16[512,384]{1,0:T(8,128)(2,1)S(1)}, bf16[512,384]{1,0:T(8,128)(2,1)}, u32[]{:S(2)}) copy-start(bf16[512,384]{1,0:T(8,128)(2,1)} %own_ref.1) | copy-start | bytes 1179652
  4.3 11.5 %collective-permute-start.1 = (bf16[2,512,384]{2,1,0:T(8,128)(2,1)S(1)}, bf16[2,512,384]{2,1,0:T(8,128)(2,1)S(1)}, u32[]{:S(2)}, u32[]{:S(2)}) collective-permute-start(bf16[2,512,384]{2,1,0:T(8,128)(2,1)S(1)} %shard_map.37.unit_ref.refs_3_), channel_id=1, source_target_pairs={{0,96},{1,97},{2,98},{3,99},{4,100},{5,101},{6,102},{7,103},{8,104... | collective-permute-start | bytes 2359304 | tf_op jit(solution)/shard_map/ppermute | solution.py:346
  6.1 13.3 %collective-permute-start.7 = (bf16[2,512,384]{2,1,0:T(8,128)(2,1)S(1)}, bf16[2,512,384]{2,1,0:T(8,128)(2,1)S(1)}, u32[]{:S(2)}, u32[]{:S(2)}) collective-permute-start(bf16[2,512,384]{2,1,0:T(8,128)(2,1)S(1)} %shard_map.37.unit_ref.refs_3_), channel_id=1, source_target_pairs={{0,4},{1,5},{2,6},{3,7},{4,0},{5,1},{6,2},{7,3},{8,12},{9,13},{10,... | collective-permute-start | bytes 2359304 | tf_op jit(solution)/shard_map/ppermute | solution.py:346
  8.3 14.0 %collective-permute-start.5 = (bf16[2,512,384]{2,1,0:T(8,128)(2,1)S(1)}, bf16[2,512,384]{2,1,0:T(8,128)(2,1)S(1)}, u32[]{:S(2)}, u32[]{:S(2)}) collective-permute-start(bf16[2,512,384]{2,1,0:T(8,128)(2,1)S(1)} %shard_map.37.unit_ref.refs_3_), channel_id=1, source_target_pairs={{0,32},{1,33},{2,34},{3,35},{4,36},{5,37},{6,38},{7,39},{8,40},{9,... | collective-permute-start | bytes 2359304 | tf_op jit(solution)/shard_map/ppermute | solution.py:346
  15.7 13.3 %collective-permute-start.2 = (bf16[2,512,384]{2,1,0:T(8,128)(2,1)S(1)}, bf16[2,512,384]{2,1,0:T(8,128)(2,1)S(1)}, u32[]{:S(2)}, u32[]{:S(2)}) collective-permute-start(bf16[2,512,384]{2,1,0:T(8,128)(2,1)S(1)} %collective-permute-done.1.refs_1_), channel_id=1, source_target_pairs={{0,4},{1,5},{2,6},{3,7},{4,0},{5,1},{6,2},{7,3},{8,12},{9,13},{10,... | collective-permute-start | bytes 2359304 | tf_op jit(solution)/shard_map/ppermute | solution.py:346
  19.3 12.4 %collective-permute-start.11 = (bf16[2,512,384]{2,1,0:T(8,128)(2,1)S(1)}, bf16[2,512,384]{2,1,0:T(8,128)(2,1)S(1)}, u32[]{:S(2)}, u32[]{:S(2)}) collective-permute-start(bf16[2,512,384]{2,1,0:T(8,128)(2,1)S(1)} %collective-permute-done.7.refs_2_), channel_id=1, source_target_pairs={{0,16},{1,17},{2,18},{3,19},{4,20},{5,21},{6,22},{7,23},{8,24},{9,... | collective-permute-start | bytes 2359304 | tf_op jit(solution)/shard_map/ppermute | solution.py:341
  19.6 12.4 %collective-permute-start.8 = (bf16[2,512,384]{2,1,0:T(8,128)(2,1)S(1)}, bf16[2,512,384]{2,1,0:T(8,128)(2,1)S(1)}, u32[]{:S(2)}, u32[]{:S(2)}) collective-permute-start(bf16[2,512,384]{2,1,0:T(8,128)(2,1)S(1)} %collective-permute-done.7.refs_2_), channel_id=1, source_target_pairs={{0,32},{1,33},{2,34},{3,35},{4,36},{5,37},{6,38},{7,39},{8,40},{9,... | collective-permute-start | bytes 2359304 | tf_op jit(solution)/shard_map/ppermute | solution.py:346
  22.3 11.3 %collective-permute-start.6 = (bf16[2,512,384]{2,1,0:T(8,128)(2,1)S(1)}, bf16[2,512,384]{2,1,0:T(8,128)(2,1)S(1)}, u32[]{:S(2)}, u32[]{:S(2)}) collective-permute-start(bf16[2,512,384]{2,1,0:T(8,128)(2,1)S(1)} %collective-permute-done.5.refs_0_), channel_id=1, source_target_pairs={{0,96},{1,97},{2,98},{3,99},{4,100},{5,101},{6,102},{7,103},{8,104... | collective-permute-start | bytes 2359304 | tf_op jit(solution)/shard_map/ppermute | solution.py:346
  23.9 10.6 %collective-permute-start.9 = (bf16[2,512,384]{2,1,0:T(8,128)(2,1)S(1)}, bf16[2,512,384]{2,1,0:T(8,128)(2,1)S(1)}, u32[]{:S(2)}, u32[]{:S(2)}) collective-permute-start(bf16[2,512,384]{2,1,0:T(8,128)(2,1)S(1)} %collective-permute-done.5.refs_0_), channel_id=1, source_target_pairs={{0,16},{1,17},{2,18},{3,19},{4,20},{5,21},{6,22},{7,23},{8,24},{9,... | collective-permute-start | bytes 2359304 | tf_op jit(solution)/shard_map/ppermute | solution.py:341
  29.0 12.1 %collective-permute-start.3 = (bf16[2,512,384]{2,1,0:T(8,128)(2,1)S(1)}, bf16[2,512,384]{2,1,0:T(8,128)(2,1)S(1)}, u32[]{:S(2)}, u32[]{:S(2)}) collective-permute-start(bf16[2,512,384]{2,1,0:T(8,128)(2,1)S(1)} %collective-permute-done.2.refs_1_), channel_id=1, source_target_pairs={{0,32},{1,33},{2,34},{3,35},{4,36},{5,37},{6,38},{7,39},{8,40},{9,... | collective-permute-start | bytes 2359304 | tf_op jit(solution)/shard_map/ppermute | solution.py:346
  31.7 15.2 %collective-permute-start.10 = (bf16[2,512,384]{2,1,0:T(8,128)(2,1)S(1)}, bf16[2,512,384]{2,1,0:T(8,128)(2,1)S(1)}, u32[]{:S(2)}, u32[]{:S(2)}) collective-permute-start(bf16[2,512,384]{2,1,0:T(8,128)(2,1)S(1)} %collective-permute-done.1.refs_1_), channel_id=1, source_target_pairs={{0,16},{1,17},{2,18},{3,19},{4,20},{5,21},{6,22},{7,23},{8,24},{9,... | collective-permute-start | bytes 2359304 | tf_op jit(solution)/shard_map/ppermute | solution.py:341
  31.9 17.9 %collective-permute-start.14 = (bf16[2,512,384]{2,1,0:T(8,128)(2,1)S(1)}, bf16[2,512,384]{2,1,0:T(8,128)(2,1)S(1)}, u32[]{:S(2)}, u32[]{:S(2)}) collective-permute-start(bf16[2,512,384]{2,1,0:T(8,128)(2,1)S(1)} %collective-permute-done.8.refs_2_), channel_id=1, source_target_pairs={{0,16},{1,17},{2,18},{3,19},{4,20},{5,21},{6,22},{7,23},{8,24},{9,... | collective-permute-start | bytes 2359304 | tf_op jit(solution)/shard_map/ppermute | solution.py:341
  33.6 16.2 %collective-permute-start.12 = (bf16[2,512,384]{2,1,0:T(8,128)(2,1)S(1)}, bf16[2,512,384]{2,1,0:T(8,128)(2,1)S(1)}, u32[]{:S(2)}, u32[]{:S(2)}) collective-permute-start(bf16[2,512,384]{2,1,0:T(8,128)(2,1)S(1)} %collective-permute-done.6.refs_0_), channel_id=1, source_target_pairs={{0,16},{1,17},{2,18},{3,19},{4,20},{5,21},{6,22},{7,23},{8,24},{9,... | collective-permute-start | bytes 2359304 | tf_op jit(solution)/shard_map/ppermute | solution.py:341
  34.5 15.3 %collective-permute-start.13 = (bf16[2,512,384]{2,1,0:T(8,128)(2,1)S(1)}, bf16[2,512,384]{2,1,0:T(8,128)(2,1)S(1)}, u32[]{:S(2)}, u32[]{:S(2)}) collective-permute-start(bf16[2,512,384]{2,1,0:T(8,128)(2,1)S(1)} %collective-permute-done.2.refs_1_), channel_id=1, source_target_pairs={{0,16},{1,17},{2,18},{3,19},{4,20},{5,21},{6,22},{7,23},{8,24},{9,... | collective-permute-start | bytes 2359304 | tf_op jit(solution)/shard_map/ppermute | solution.py:341
  41.1 17.9 %collective-permute-start.4 = (bf16[2,512,384]{2,1,0:T(8,128)(2,1)S(1)}, bf16[2,512,384]{2,1,0:T(8,128)(2,1)S(1)}, u32[]{:S(2)}, u32[]{:S(2)}) collective-permute-start(bf16[2,512,384]{2,1,0:T(8,128)(2,1)S(1)} %collective-permute-done.3.mine), channel_id=1, source_target_pairs={{0,16},{1,17},{2,18},{3,19},{4,20},{5,21},{6,22},{7,23},{8,24},{9,... | collective-permute-start | bytes 2359304 | tf_op jit(solution)/shard_map/ppermute | solution.py:341
  41.9 0.7 copy-start.1
  42.6 0.7 copy-start.2
  59.8 2.7 %collective-permute-start.15 = (f32[16,512]{1,0:T(8,128)S(1)}, f32[16,512]{1,0:T(8,128)S(1)}, u32[]{:S(2)}, u32[]{:S(2)}) collective-permute-start(f32[16,512]{1,0:T(8,128)S(1)} %get-tuple-element.31), channel_id=1, source_target_pairs={{0,16},{1,17},{2,18},{3,19},{4,20},{5,21},{6,22},{7,23},{8,24},{9,... | collective-permute-start | bytes 98312 | tf_op jit(solution)/shard_map/ppermute | solution.py:341
  62.5 5.3 %collective-permute-start.16 = (f32[8,512]{1,0:T(8,128)S(1)}, f32[8,512]{1,0:T(8,128)S(1)}, u32[]{:S(2)}, u32[]{:S(2)}) collective-permute-start(f32[8,512]{1,0:T(8,128)S(1)} %slice_maximum_fusion), channel_id=1, source_target_pairs={{0,4},{1,5},{2,6},{3,7},{4,0},{5,1},{6,2},{7,3},{8,12},{9,13},{10,... | collective-permute-start | bytes 49160 | tf_op jit(solution)/shard_map/ppermute | solution.py:346
  67.9 2.9 %collective-permute-start.17 = (f32[4,512]{1,0:T(4,128)S(1)}, f32[4,512]{1,0:T(4,128)S(1)}, u32[]{:S(2)}, u32[]{:S(2)}) collective-permute-start(f32[4,512]{1,0:T(4,128)S(1)} %slice.37), channel_id=1, source_target_pairs={{0,96},{1,97},{2,98},{3,99},{4,100},{5,101},{6,102},{7,103},{8,104... | collective-permute-start | bytes 24584 | tf_op jit(solution)/shard_map/ppermute | solution.py:346
  70.8 3.7 %collective-permute-start.18 = (f32[2,512]{1,0:T(2,128)S(1)}, f32[2,512]{1,0:T(2,128)S(1)}, u32[]{:S(2)}, u32[]{:S(2)}) collective-permute-start(f32[2,512]{1,0:T(2,128)S(1)} %slice.39), channel_id=1, source_target_pairs={{0,32},{1,33},{2,34},{3,35},{4,36},{5,37},{6,38},{7,39},{8,40},{9,... | collective-permute-start | bytes 12296 | tf_op jit(solution)/shard_map/ppermute | solution.py:346
  74.5 7.5 %collective-permute-start.19 = (f32[512]{0:T(512)S(1)}, f32[512]{0:T(512)S(1)}, u32[]{:S(2)}, u32[]{:S(2)}) collective-permute-start(f32[512]{0:T(512)S(1)} %bitcast.7), channel_id=1, source_target_pairs={{0,16},{1,17},{2,18},{3,19},{4,20},{5,21},{6,22},{7,23},{8,24},{9,... | collective-permute-start | bytes 6152 | tf_op jit(solution)/shard_map/ppermute | solution.py:341

commit v3 on v2

v3 whole, which is shorter than its diff:
```python
import functools

import jax
import jax.numpy as jnp
import numpy as np
from jax import lax
from jax.experimental import pallas as pl
from jax.experimental.pallas import tpu as pltpu
from jax.sharding import PartitionSpec as P

BLK = 256
SHARD = 512
D = 384
GROUP = 4
VMEM_LIMIT = 40 * 1024 * 1024

CORE = 16
X1, X3, Y1, Y3, Z1, Z3 = 32, 96, 4, 12, 1, 3
GENERATORS = ((X1, X3, Y1), (Y3, Z1, Z3))
SLOTS = ((), (0,), (1,), (2,), (0, 1), (1, 2), (2, 0), (0, 1, 2))
SENDS = ((0, 0), (0, 1), (0, 2), (1, 1), (2, 2), (3, 0))
HALVES = ((5, 0), (6, 1))
PHASES = (((1, 2, 3), 0, 4, 4), ((4, 5, 6), 0, 4, 4), ((4, 5, 6), 4, 7, 4), ((7,), 0, 7, 4), ((7,), 7, 8, 1))


def mask_of(core, slot):
    mask = 0
    for generator in SLOTS[slot]:
        mask ^= GENERATORS[core][generator]
    return mask


def make_table():
    tables = []
    for core in range(2):
        for slots, low, high, _ in PHASES:
            for i in slots:
                for j in range(low, min(i + 1, high)):
                    a, b = mask_of(core, i), mask_of(1 - core, j)
                    code = 2 * (i - slots[0]) | (2 * (j if low < 7 else 0)) << 4
                    bit = (a ^ b) & -(a ^ b)
                    if j < i or core == 0:
                        tables.append((code, a, b, 0, core, 1))
                    if j < i or core == 1:
                        tables.append((code, a, b, bit, (i + j) % 2, 0))
    return np.array(tables, np.int32).reshape(2, -1, 6)


TABLE = make_table()
COUNTS = [
    sum(2 if j < i else 1 for i in slots for j in range(low, min(i + 1, high)))
    for slots, low, high, _ in PHASES
]
STARTS = [sum(COUNTS[:n]) for n in range(len(PHASES) + 1)]
ITEMS = STARTS[-1]
LISTS = ITEMS + GROUP * len(PHASES)
VMEM = pltpu.VMEM
SMEM = pltpu.SMEM


def spec(space):
    return pl.BlockSpec(memory_space=space)


def params():
    return pltpu.CompilerParams(vmem_limit_bytes=VMEM_LIMIT)


def unit_of(x):
    values = x.astype(jnp.float32)
    squares = jnp.sum(values * values, axis=1, keepdims=True)
    return (values * lax.rsqrt(squares + 1e-06)).astype(jnp.bfloat16)


def own_kernel(x_ref, out_ref):
    out_ref[...] = unit_of(x_ref[...])


def pair_kernel(here_ref, own_ref, other_ref, out_ref):
    core = (here_ref[0] >> 4) & 1
    out_ref[core] = own_ref[...]
    out_ref[1 - core] = unit_of(other_ref[...])


def unit_call(here, x, other):
    cost = pl.CostEstimate(flops=1000000, bytes_accessed=1600000, transcendentals=512)
    own = pl.pallas_call(
        own_kernel,
        out_shape=jax.ShapeDtypeStruct((SHARD, D), jnp.bfloat16),
        in_specs=[spec(VMEM)],
        out_specs=spec(VMEM),
        compiler_params=params(),
        cost_estimate=cost,
    )(x)
    return pl.pallas_call(
        pair_kernel,
        out_shape=jax.ShapeDtypeStruct((2, SHARD, D), jnp.bfloat16),
        in_specs=[spec(SMEM), spec(VMEM), spec(VMEM)],
        out_specs=spec(VMEM),
        compiler_params=params(),
        cost_estimate=cost,
    )(here, own, other)


def dot(a, b):
    return lax.dot_general(a, b, (((1,), (1,)), ((), ())), preferred_element_type=jnp.float32)


def self_kernel(here_ref, cluster_ref, table_ref, unit_ref, own_ref, full_ref, part_ref, count_ref):
    here = here_ref[0]
    core = (here >> 4) & 1
    for phase in range(len(PHASES)):
        first = STARTS[phase] + GROUP * phase

        def candidate(n, counts):
            full, part = counts
            entry = 6 * (core * ITEMS + n)
            side = jnp.where((here & table_ref[entry + 3]) != 0, 1, 0) ^ table_ref[entry + 4]
            far = side ^ table_ref[entry + 5]
            a = 2 * (((here ^ table_ref[entry + 1]) & ~CORE) | (side << 4))
            b = 2 * (((here ^ table_ref[entry + 2]) & ~CORE) | (far << 4))
            code = table_ref[entry] + side + (far << 4)
            a0, a1 = cluster_ref[a], cluster_ref[a + 1]
            b0, b1 = cluster_ref[b], cluster_ref[b + 1]
            quads = (
                jnp.where(a0 == b0, 1, 0)
                + jnp.where(a0 == b1, 2, 0)
                + jnp.where(a1 == b0, 4, 0)
                + jnp.where(a1 == b1, 8, 0)
            )
            full_ref[first + full] = code
            part_ref[first + part] = code | (quads << 8)
            return (
                full + jnp.where(quads == 15, 1, 0),
                part + jnp.where((quads != 0) & (quads != 15), 1, 0),
            )

        full, part = lax.fori_loop(
            STARTS[phase], STARTS[phase + 1], candidate, (jnp.int32(0), jnp.int32(0))
        )
        last = full_ref[first + jnp.maximum(full - 1, 0)]
        for n in range(GROUP - 1):
            full_ref[first + full + n] = last
        count_ref[2 * phase] = full
        count_ref[2 * phase + 1] = part

    first0 = cluster_ref[2 * here]
    first1 = cluster_ref[2 * here + 1]
    there = here ^ CORE
    second0 = cluster_ref[2 * there]
    second1 = cluster_ref[2 * there + 1]
    mine = unit_ref[core]
    best = jnp.full((8, SHARD), -2.0, jnp.float32)
    col = lax.broadcasted_iota(jnp.int32, (BLK, SHARD), 1)
    row = lax.broadcasted_iota(jnp.int32, (BLK, SHARD), 0)
    label = jnp.where(col[:1] < BLK, first0, first1)
    for half, name in ((0, first0), (1, first1)):
        scores = dot(unit_ref[core, half * BLK : half * BLK + BLK, :], mine)
        keep = (row + half * BLK != col) & (label == name)
        scores = jnp.where(keep, scores, jnp.float32(-2.0))
        best = jnp.maximum(best, jnp.max(scores.reshape(BLK // 8, 8, SHARD), axis=0))
    for half, name in ((0, second0), (1, second1)):
        scores = dot(unit_ref[1 - core, half * BLK : half * BLK + BLK, :], mine)
        scores = jnp.where(label == name, scores, jnp.float32(-2.0))
        best = jnp.maximum(best, jnp.max(scores.reshape(BLK // 8, 8, SHARD), axis=0))
    own_ref[...] = jnp.max(best, axis=0, keepdims=True)


def self_call(here, cluster, table, unit):
    lists = jax.ShapeDtypeStruct((LISTS,), jnp.int32)
    return pl.pallas_call(
        self_kernel,
        out_shape=(
            jax.ShapeDtypeStruct((1, SHARD), jnp.float32),
            lists,
            lists,
            jax.ShapeDtypeStruct((2 * len(PHASES),), jnp.int32),
        ),
        in_specs=[spec(SMEM), spec(SMEM), spec(SMEM), spec(VMEM)],
        out_specs=(spec(VMEM), spec(SMEM), spec(SMEM), spec(SMEM)),
        compiler_params=params(),
        cost_estimate=pl.CostEstimate(flops=4000000000, bytes_accessed=1000000, transcendentals=0),
    )(here, cluster, table, unit)


def fold(row_ref, col_ref, i, j, rows, cols, scores):
    best = scores[:, :128]
    for k in range(1, scores.shape[1] // 128):
        best = jnp.maximum(best, scores[:, 128 * k : 128 * k + 128])
    row_ref[i, rows, :] = jnp.maximum(row_ref[i, rows, :], best)
    down = jnp.max(scores.reshape(scores.shape[0] // 8, 8, scores.shape[1]), axis=0)
    col_ref[j, :, cols] = jnp.maximum(col_ref[j, :, cols], down)


def score_full(a_ref, b_ref, row_ref, col_ref, word):
    i = word & 15
    j = (word >> 4) & 15
    scores = dot(a_ref[i], b_ref[j])
    fold(row_ref, col_ref, i, j, slice(None), slice(None), scores)


def score_part(a_ref, b_ref, row_ref, col_ref, word):
    i = word & 15
    j = (word >> 4) & 15
    for quad in range(4):

        @pl.when(((word >> (8 + quad)) & 1) == 1)
        def _():
            rows = pl.ds((quad // 2) * BLK, BLK)
            cols = pl.ds((quad % 2) * BLK, BLK)
            scores = dot(a_ref[i, rows, :], b_ref[j, cols, :])
            fold(row_ref, col_ref, i, j, rows, cols, scores)


def score_lists(phase, full_ref, part_ref, count_ref, *refs):
    first = STARTS[phase] + GROUP * phase
    group = PHASES[phase][3]

    @pl.loop(0, count_ref[2 * phase], step=group)
    def _(n):
        for k in range(group):
            score_full(*refs, full_ref[first + n + k])

    @pl.loop(0, count_ref[2 * phase + 1])
    def _(n):
        score_part(*refs, part_ref[first + n])


def put_rows(out_ref, place, row_ref, first):
    for half in range(2):
        at = place + half
        for k in range(SHARD // 128):
            part = row_ref[first + half, 128 * k : 128 * k + 128, :].T
            out_ref[at : at + 1, 128 * k : 128 * k + 128] = jnp.max(part, axis=0, keepdims=True)


def score_kernel(phase, full_ref, part_ref, count_ref, *refs):
    slots, low, high, _ = PHASES[phase]
    mine, refs = refs[: len(slots)], refs[len(slots) :]
    if phase == 0:
        theirs, refs = refs[:high], refs[high:]
        row_ref, col_ref, b_buf, a_buf = refs
        row_ref[...] = jnp.full(row_ref.shape, -2.0, jnp.float32)
        col_ref[...] = jnp.full(col_ref.shape, -2.0, jnp.float32)
    elif phase == 1:
        b_buf, col_in, row_ref, col_ref, a_buf = refs
        theirs = ()
        row_ref[...] = jnp.full(row_ref.shape, -2.0, jnp.float32)
        col_ref[...] = col_in[...]
    else:
        theirs, refs = refs[: high - low], refs[high - low :]
        b_in, col_in, row_in, row_ref, col_ref, b_buf, a_buf = refs
        b_buf[: 2 * low] = b_in[...]
        row_ref[...] = row_in[...]
        col_ref[...] = col_in[...]
    for n, ref in enumerate(mine):
        a_buf[2 * n : 2 * n + 2] = ref[...]
    for n, ref in enumerate(theirs, low):
        b_buf[2 * n : 2 * n + 2] = ref[...]
    score_lists(phase, full_ref, part_ref, count_ref, a_buf, b_buf, row_ref, col_ref)


ROWS = jax.ShapeDtypeStruct((6, SHARD, 128), jnp.float32)
COLS = jax.ShapeDtypeStruct((14, 8, SHARD), jnp.float32)


def score_call(phase, plan, mine, theirs, state):
    outs = (ROWS, COLS)
    if phase != 1:
        outs = outs + (jax.ShapeDtypeStruct((2 * PHASES[phase][2], SHARD, D), jnp.bfloat16),)
    operands = list(plan) + list(mine) + list(theirs) + list(state)
    return pl.pallas_call(
        functools.partial(score_kernel, phase),
        out_shape=outs,
        in_specs=[spec(SMEM)] * 3 + [spec(VMEM)] * (len(operands) - 3),
        out_specs=(spec(VMEM),) * len(outs),
        scratch_shapes=[VMEM((6, SHARD, D), jnp.bfloat16)],
        compiler_params=params(),
        cost_estimate=pl.CostEstimate(
            flops=COUNTS[phase] * SHARD * SHARD * D, bytes_accessed=8000000, transcendentals=0
        ),
    )(*operands)


KEPT = (0, 1, 2, 4)
SENT = (3, 6, 5, 7)


def last_kernel(full_ref, part_ref, count_ref, *refs):
    plan, mine, theirs, refs = (full_ref, part_ref, count_ref), refs[:2], refs[2:4], refs[4:]
    b_buf, col_in, rows0, rows1, keep_ref, send_ref, other_ref, refs = *refs[:7], refs[7:]
    a_buf, b_last, row_ref, col_ref, col_last = refs
    row_ref[...] = jnp.full(row_ref.shape, -2.0, jnp.float32)
    col_ref[...] = col_in[...]
    col_last[...] = jnp.full(col_last.shape, -2.0, jnp.float32)
    for half in range(2):
        a_buf[half] = mine[half][...]
        b_last[half] = theirs[half][...]
    score_lists(3, *plan, a_buf, b_buf, row_ref, col_ref)
    score_lists(4, *plan, a_buf, b_last, row_ref, col_last)
    keep_ref[0:2] = jnp.full((2, SHARD), -2.0, jnp.float32)
    for out_ref, slots in ((keep_ref, KEPT), (send_ref, SENT)):
        for place, slot in enumerate(slots):
            if slot == 7:
                put_rows(out_ref, 2 * place, row_ref, 0)
            elif slot > 3:
                put_rows(out_ref, 2 * place, rows1, 2 * slot - 8)
            elif slot > 0:
                put_rows(out_ref, 2 * place, rows0, 2 * slot - 2)
    for place, slot in enumerate(KEPT + SENT):
        for half in range(2):
            at = 2 * place + half
            down = col_last[half] if slot == 7 else col_ref[2 * slot + half]
            other_ref[at : at + 1, :] = jnp.max(down, axis=0, keepdims=True)


def last_call(plan, mine, theirs, state):
    eight = jax.ShapeDtypeStruct((8, SHARD), jnp.float32)
    outs = (eight, eight, jax.ShapeDtypeStruct((16, SHARD), jnp.float32))
    operands = list(plan) + list(mine) + list(theirs) + list(state)
    return pl.pallas_call(
        last_kernel,
        out_shape=outs,
        in_specs=[spec(SMEM)] * 3 + [spec(VMEM)] * (len(operands) - 3),
        out_specs=(spec(VMEM),) * 3,
        scratch_shapes=[
            VMEM((2, SHARD, D), jnp.bfloat16),
            VMEM((2, SHARD, D), jnp.bfloat16),
            VMEM((2, SHARD, 128), jnp.float32),
            VMEM(COLS.shape, jnp.float32),
            VMEM((2, 8, SHARD), jnp.float32),
        ],
        compiler_params=params(),
        cost_estimate=pl.CostEstimate(
            flops=COUNTS[3] * SHARD * SHARD * D, bytes_accessed=8000000, transcendentals=0
        ),
    )(*operands)


def swap(x):
    return lax.ppermute(x, ("row", "col"), [(s, s ^ CORE) for s in range(128)])


def exchange(x, generator):
    pairs = [(s, s ^ GENERATORS[(s >> 4) & 1][generator]) for s in range(128)]
    return lax.ppermute(x, ("row", "col"), pairs)


def after(x, *done):
    return lax.optimization_barrier((x, *done))[0]


def body(embeddings, block_cluster):
    here = (lax.axis_index("row") * 16 + lax.axis_index("col")).astype(jnp.int32).reshape(1)
    unit = unit_call(here, embeddings, swap(embeddings))
    own, *plan = self_call(here, block_cluster, jnp.asarray(TABLE.reshape(-1)), unit)
    mine, theirs = [unit], [unit]
    for slot in (1, 2, 3):
        source, generator = SENDS[slot - 1]
        mine.append(after(exchange(mine[source], generator), own))
        theirs.append(swap(mine[slot]))
    rows0, cols, b_buf = score_call(0, plan, mine[1:4], theirs[:4], ())
    for slot in (4, 5, 6):
        source, generator = SENDS[slot - 1]
        mine.append(after(exchange(mine[source], generator), cols))
        theirs.append(swap(mine[slot]))
    rows1, cols = score_call(1, plan, mine[4:7], (), (b_buf, cols))
    halves = [
        after(exchange(mine[source][half], generator), cols)
        for half, (source, generator) in enumerate(HALVES)
    ]
    swapped = [swap(x) for x in halves]
    rows1, cols, b_buf = score_call(2, plan, mine[4:7], theirs[4:7], (b_buf, cols, rows1))
    keep, send, other = last_call(plan, halves, swapped, (b_buf, cols, rows0, rows1))
    other = swap(other)
    keep = jnp.maximum(keep, other[:8])
    send = jnp.maximum(send, other[8:])
    keep = jnp.maximum(keep, exchange(send, 2))
    keep = jnp.maximum(keep[:4], exchange(keep[4:], 1))
    keep = jnp.maximum(keep[:2], exchange(keep[2:], 0))
    second = (here & CORE) != 0
    ours = jnp.where(second, keep[1], keep[0])
    other = swap(jnp.where(second, keep[0], keep[1]))
    return jnp.maximum(own.reshape(SHARD), jnp.maximum(ours, other))


def solution(mesh):
    placed = (P(("row", "col"), None), P())
    return jax.shard_map(
        body, mesh=mesh, in_specs=placed, out_specs=P(("row", "col")), check_vma=False
    )
```

time: 83 us -> 74.8 us (0.901)
  starting transfers between devices: 34.7 us -> 26.8 us
  waiting for transfers between devices: 28.1 us -> 23.4 us
  Pallas kernels: 16.8 us -> 20.1 us
  local copies, waits for them, and re-layouts: 2.37 us -> 3.66 us
    ppermute x10 -> x11, starting transfers between devices: 22.5 us -> 16 us  [exchange(): return lax.ppermute(x, ('row', 'col'), pairs)]
    pallas_call x1, Pallas kernels: 0.82 us -> 4.39 us  [last_call(): pl.pallas_call(last_kernel, out_shape=outs, in_specs=[spec(SMEM)] * 3 + [...]
    ppermute x10 -> x11, waiting for transfers between devices: 24.8 us -> 21.3 us  [exchange(): return lax.ppermute(x, ('row', 'col'), pairs)]
    pallas_call x2, Pallas kernels: 3.65 us -> 0.33 us  [the longest x1 0.17 us: unit_call(): pl.pallas_call(pair_kernel, out_shape=jax.ShapeDtypeStruct((2, SHARD, D),...]
    pallas_call x2 -> x3, Pallas kernels: 8.67 us -> 11.7 us  [score_call(): pl.pallas_call(functools.partial(score_kernel, phase), out_shape=outs, in...]
    ppermute x10 -> x11, starting transfers between devices: 12.2 us -> 10.7 us  [swap(): return lax.ppermute(x, ('row', 'col'), [(s, s ^ CORE) for s in range(128)])]
    unnamed x6 -> x8, local copies, waits for them, and re-layouts: 2.36 us -> 3.56 us
    ppermute x10 -> x11, waiting for transfers between devices: 3.26 us -> 2.11 us  [swap(): return lax.ppermute(x, ('row', 'col'), [(s, s ^ CORE) for s in range(128)])]
  transfers between devices with their start and end apart: 20 -> 22, of which waited for: 11 -> 12; matrix products, arithmetic and copies ran while one was open for 0% -> 0% of each run, Pallas kernels for 19% -> 21%
where the time goes in v3:
time: 74.8 us; the launch traced here: 74.6 us
  starting transfers between devices  26.8 us (36%)
  waiting for transfers between devices  23.4 us (31%)
  Pallas kernels  20.1 us (27%)
  local copies, waits for them, and re-layouts  3.66 us (5%)
    ppermute x11, waiting for transfers between devices, exchange(): return lax.ppermute(x, ('row', 'col'), pairs)  21.3 us
    ppermute x11, starting transfers between devices, exchange(): return lax.ppermute(x, ('row', 'col'), pairs)  16 us
    pallas_call x3, Pallas kernels, score_call(): pl.pallas_call(functools.partial(score_kernel, phase), out_shape=outs, in...  11.7 us
    ppermute x11, starting transfers between devices, swap(): return lax.ppermute(x, ('row', 'col'), [(s, s ^ CORE) for s in range(128)])  10.7 us
    pallas_call x1, Pallas kernels, last_call(): pl.pallas_call(last_kernel, out_shape=outs, in_specs=[spec(SMEM)] * 3 + [...  4.39 us
    pallas_call x1, Pallas kernels, self_call(): pl.pallas_call(self_kernel, out_shape=(jax.ShapeDtypeStruct((1, SHARD), j...  3.64 us
    unnamed x8, local copies, waits for them, and re-layouts  3.56 us
    ppermute x11, waiting for transfers between devices, swap(): return lax.ppermute(x, ('row', 'col'), [(s, s ^ CORE) for s in range(128)])  2.11 us
  transfers between devices with their start and end apart: 22, of which 12 were waited for; matrix products, arithmetic and copies ran while one was open for 0% of the time, Pallas kernels for 21%

profile of v3, /device:TPU:1, one launch (start us, length us, event | category | flops | bytes accessed | tf_op | source)
XLA Modules:
  0.0 74.6 jit_solution(16973020677125728798)
XLA Ops:
  0.0 1.4 %collective-permute-start = (bf16[512,384]{1,0:T(8,128)(2,1)}, bf16[512,384]{1,0:T(8,128)(2,1)S(1)}, u32[]{:S(2)}, u32[]{:S(2)}) collective-permute-start(bf16[512,384]{1,0:T(8,128)(2,1)} %x_ref.1), channel_id=1, source_target_pairs={{0,16},{1,17},{2,18},{3,19},{4,20},{5,21},{6,22},{7,23},{8,24},{9,... | collective-permute-start | bytes 1179656 | tf_op jit(solution)/shard_map/ppermute | solution.py:341
  1.4 1.0 %copy-done.1 = bf16[512,384]{1,0:T(8,128)(2,1)S(1)} copy-done((bf16[512,384]{1,0:T(8,128)(2,1)S(1)}, bf16[512,384]{1,0:T(8,128)(2,1)}, u32[]{:S(2)}) %copy-start.1) | copy-done | bytes 393240
  2.4 0.2 shard_map.37.own_ref
  2.6 0.4 collective-permute-done.other_ref
  3.0 0.2 shard_map.38.unit_ref.refs_3_
  3.2 2.9 %collective-permute-start.3 = (bf16[2,512,384]{2,1,0:T(8,128)(2,1)S(1)}, bf16[2,512,384]{2,1,0:T(8,128)(2,1)S(1)}, u32[]{:S(2)}, u32[]{:S(2)}) collective-permute-start(bf16[2,512,384]{2,1,0:T(8,128)(2,1)S(1)} %shard_map.38.unit_ref.refs_3_), channel_id=1, source_target_pairs={{0,32},{1,33},{2,34},{3,35},{4,36},{5,37},{6,38},{7,39},{8,40},{9,... | collective-permute-start | bytes 2359304 | tf_op jit(solution)/shard_map/ppermute | solution.py:346
  6.1 3.8 %collective-permute-start.4 = (bf16[2,512,384]{2,1,0:T(8,128)(2,1)S(1)}, bf16[2,512,384]{2,1,0:T(8,128)(2,1)S(1)}, u32[]{:S(2)}, u32[]{:S(2)}) collective-permute-start(bf16[2,512,384]{2,1,0:T(8,128)(2,1)S(1)} %shard_map.38.unit_ref.refs_3_), channel_id=1, source_target_pairs={{0,4},{1,5},{2,6},{3,7},{4,0},{5,1},{6,2},{7,3},{8,12},{9,13},{10,... | collective-permute-start | bytes 2359304 | tf_op jit(solution)/shard_map/ppermute | solution.py:346
  9.8 0.0 collective-permute-start.1
  9.8 3.6 %shard_map.39 = (f32[1,512]{1,0:T(1,128)S(1)}, s32[83]{0:T(128)S(1)}, s32[83]{0:T(128)S(1)}, s32[10]{0:T(128)S(1)}) custom-call(s32[1]{0:T(128)} %bitcast.here_ref, s32[256]{0:T(256)S(1)} %copy-done.2, s32[756]{0:T(1024)S(1)} %copy-done.3, bf16[2,512,384]{2,1,0:T(8,128)(2,1)S(1)} %shard_map.38.unit_ref.refs_3_), custom_call_target="tpu_custom_call" | custom-call | flops 4000000000 | bytes 1000000 | tf_op jit(solution)/shard_map/pallas_call | solution.py:171
  13.5 2.3 %collective-permute-done.3.refs_0_ = bf16[2,512,384]{2,1,0:T(8,128)(2,1)S(1)} collective-permute-done((bf16[2,512,384]{2,1,0:T(8,128)(2,1)S(1)}, bf16[2,512,384]{2,1,0:T(8,128)(2,1)S(1)}, u32[]{:S(2)}, u32[]{:S(2)}) %collective-permute-start.3) | collective-permute-done | bytes 786464 | tf_op jit(solution)/shard_map/ppermute | solution.py:346
  15.7 0.0 collective-permute-start.5
  15.7 3.8 %collective-permute-done.4.refs_2_ = bf16[2,512,384]{2,1,0:T(8,128)(2,1)S(1)} collective-permute-done((bf16[2,512,384]{2,1,0:T(8,128)(2,1)S(1)}, bf16[2,512,384]{2,1,0:T(8,128)(2,1)S(1)}, u32[]{:S(2)}, u32[]{:S(2)}) %collective-permute-start.4) | collective-permute-done | bytes 786464 | tf_op jit(solution)/shard_map/ppermute | solution.py:346
  19.5 1.2 %collective-permute-done.1.refs_1_ = bf16[2,512,384]{2,1,0:T(8,128)(2,1)S(1)} collective-permute-done((bf16[2,512,384]{2,1,0:T(8,128)(2,1)S(1)}, bf16[2,512,384]{2,1,0:T(8,128)(2,1)S(1)}, u32[]{:S(2)}, u32[]{:S(2)}) %collective-permute-start.1) | collective-permute-done | bytes 786464 | tf_op jit(solution)/shard_map/ppermute | solution.py:346
  20.7 0.0 collective-permute-start.6
  20.7 1.2 %collective-permute-start.10 = (bf16[2,512,384]{2,1,0:T(8,128)(2,1)S(1)}, bf16[2,512,384]{2,1,0:T(8,128)(2,1)S(1)}, u32[]{:S(2)}, u32[]{:S(2)}) collective-permute-start(bf16[2,512,384]{2,1,0:T(8,128)(2,1)S(1)} %collective-permute-done.4.refs_2_), channel_id=1, source_target_pairs={{0,32},{1,33},{2,34},{3,35},{4,36},{5,37},{6,38},{7,39},{8,40},{9,... | collective-permute-start | bytes 2359304 | tf_op jit(solution)/shard_map/ppermute | solution.py:346
  21.9 1.6 %collective-permute-start.9 = (bf16[2,512,384]{2,1,0:T(8,128)(2,1)S(1)}, bf16[2,512,384]{2,1,0:T(8,128)(2,1)S(1)}, u32[]{:S(2)}, u32[]{:S(2)}) collective-permute-start(bf16[2,512,384]{2,1,0:T(8,128)(2,1)S(1)} %collective-permute-done.3.refs_0_), channel_id=1, source_target_pairs={{0,96},{1,97},{2,98},{3,99},{4,100},{5,101},{6,102},{7,103},{8,104... | collective-permute-start | bytes 2359304 | tf_op jit(solution)/shard_map/ppermute | solution.py:346
  23.5 0.0 collective-permute-done.5.refs_4_
  23.5 2.2 %collective-permute-start.2 = (bf16[2,512,384]{2,1,0:T(8,128)(2,1)S(1)}, bf16[2,512,384]{2,1,0:T(8,128)(2,1)S(1)}, u32[]{:S(2)}, u32[]{:S(2)}) collective-permute-start(bf16[2,512,384]{2,1,0:T(8,128)(2,1)S(1)} %collective-permute-done.1.refs_1_), channel_id=1, source_target_pairs={{0,4},{1,5},{2,6},{3,7},{4,0},{5,1},{6,2},{7,3},{8,12},{9,13},{10,... | collective-permute-start | bytes 2359304 | tf_op jit(solution)/shard_map/ppermute | solution.py:346
  25.8 0.0 collective-permute-done.7.refs_6_
  25.8 0.0 collective-permute-done.6.refs_5_
  25.8 3.0 %shard_map.40 = (f32[6,512,128]{2,1,0:T(8,128)S(1)}, f32[14,8,512]{2,1,0:T(8,128)S(1)}, bf16[8,512,384]{2,1,0:T(8,128)(2,1)S(1)}) custom-call(s32[83]{0:T(128)S(1)} %get-tuple-element.29.full_ref, s32[83]{0:T(128)S(1)} %get-tuple-element.30.part_ref, s32[10]{0:T(128)S(1)} %get-tuple-element.31.count_ref, ...), custom_call_target="tpu_custom_call" | custom-call | flops 1509949440 | bytes 8000000 | tf_op jit(solution)/shard_map/pallas_call | solution.py:272
  28.8 4.2 %collective-permute-done.10.refs_2_ = bf16[2,512,384]{2,1,0:T(8,128)(2,1)S(1)} collective-permute-done((bf16[2,512,384]{2,1,0:T(8,128)(2,1)S(1)}, bf16[2,512,384]{2,1,0:T(8,128)(2,1)S(1)}, u32[]{:S(2)}, u32[]{:S(2)}) %collective-permute-start.10) | collective-permute-done | bytes 786464 | tf_op jit(solution)/shard_map/ppermute | solution.py:346
  33.0 0.2 collective-permute-done.9.refs_0_
  33.2 2.7 %collective-permute-start.16 = (bf16[2,512,384]{2,1,0:T(8,128)(2,1)S(1)}, bf16[2,512,384]{2,1,0:T(8,128)(2,1)S(1)}, u32[]{:S(2)}, u32[]{:S(2)}) collective-permute-start(bf16[2,512,384]{2,1,0:T(8,128)(2,1)S(1)} %collective-permute-done.10.refs_2_), channel_id=1, source_target_pairs={{0,16},{1,17},{2,18},{3,19},{4,20},{5,21},{6,22},{7,23},{8,24},{9,... | collective-permute-start | bytes 2359304 | tf_op jit(solution)/shard_map/ppermute | solution.py:341
  35.9 0.0 collective-permute-done.2.refs_1_
  35.9 0.8 %collective-permute-start.14 = (bf16[2,512,384]{2,1,0:T(8,128)(2,1)S(1)}, bf16[2,512,384]{2,1,0:T(8,128)(2,1)S(1)}, u32[]{:S(2)}, u32[]{:S(2)}) collective-permute-start(bf16[2,512,384]{2,1,0:T(8,128)(2,1)S(1)} %collective-permute-done.9.refs_0_), channel_id=1, source_target_pairs={{0,16},{1,17},{2,18},{3,19},{4,20},{5,21},{6,22},{7,23},{8,24},{9,... | collective-permute-start | bytes 2359304 | tf_op jit(solution)/shard_map/ppermute | solution.py:341
  36.8 0.0 collective-permute-start.15
  36.8 0.0 collective-permute-start.11
  36.8 0.9 %collective-permute-start.8 = (bf16[512,384]{1,0:T(8,128)(2,1)S(1)}, bf16[512,384]{1,0:T(8,128)(2,1)S(1)}, u32[]{:S(2)}, u32[]{:S(2)}) collective-permute-start(bf16[512,384]{1,0:T(8,128)(2,1)S(1)} %slice_bitcast_fusion.1), channel_id=1, source_target_pairs={{0,32},{1,33},{2,34},{3,35},{4,36},{5,37},{6,38},{7,39},{8,40},{9,... | collective-permute-start | bytes 1179656 | tf_op jit(solution)/shard_map/ppermute | solution.py:346
  37.7 3.5 %shard_map.41 = (f32[6,512,128]{2,1,0:T(8,128)S(1)}, f32[14,8,512]{2,1,0:T(8,128)S(1)}) custom-call(s32[83]{0:T(128)S(1)} %get-tuple-element.29.full_ref, s32[83]{0:T(128)S(1)} %get-tuple-element.30.part_ref, s32[10]{0:T(128)S(1)} %get-tuple-element.31.count_ref, bf16[2,512,384]{2,1,0:T(8,128)(2,1)S(1)} %collective-permute-done.9.refs_0_, ...), custom_call_target="tpu_custom_call" | custom-call | flops 2415919104 | bytes 8000000 | tf_op jit(solution)/shard_map/pallas_call | solution.py:272
  41.2 2.4 %collective-permute-done.11.refs_1_ = bf16[512,384]{1,0:T(8,128)(2,1)S(1)} collective-permute-done((bf16[512,384]{1,0:T(8,128)(2,1)S(1)}, bf16[512,384]{1,0:T(8,128)(2,1)S(1)}, u32[]{:S(2)}, u32[]{:S(2)}) %collective-permute-start.11) | collective-permute-done | bytes 393248 | tf_op jit(solution)/shard_map/ppermute | solution.py:346
  43.7 2.6 %collective-permute-start.13 = (bf16[512,384]{1,0:T(8,128)(2,1)S(1)}, bf16[512,384]{1,0:T(8,128)(2,1)S(1)}, u32[]{:S(2)}, u32[]{:S(2)}) collective-permute-start(bf16[512,384]{1,0:T(8,128)(2,1)S(1)} %collective-permute-done.11.refs_1_), channel_id=1, source_target_pairs={{0,16},{1,17},{2,18},{3,19},{4,20},{5,21},{6,22},{7,23},{8,24},{9,... | collective-permute-start | bytes 1179656 | tf_op jit(solution)/shard_map/ppermute | solution.py:341
  46.3 0.3 collective-permute-start.12
  46.6 0.0 collective-permute-done.15.refs_4_
  46.6 5.2 %shard_map.42 = (f32[6,512,128]{2,1,0:T(8,128)S(1)}, f32[14,8,512]{2,1,0:T(8,128)S(1)}, bf16[14,512,384]{2,1,0:T(8,128)(2,1)}) custom-call(s32[83]{0:T(128)S(1)} %get-tuple-element.29.full_ref, s32[83]{0:T(128)S(1)} %get-tuple-element.30.part_ref, s32[10]{0:T(128)S(1)} %get-tuple-element.31.count_ref, ...), custom_call_target="tpu_custom_call" | custom-call | flops 905969664 | bytes 8000000 | tf_op jit(solution)/shard_map/pallas_call | solution.py:272
  51.9 2.6 %copy-done = bf16[14,512,384]{2,1,0:T(8,128)(2,1)S(1)} copy-done((bf16[14,512,384]{2,1,0:T(8,128)(2,1)S(1)}, bf16[14,512,384]{2,1,0:T(8,128)(2,1)}, u32[]{:S(2)}) %copy-start) | copy-done | bytes 5505048
  54.4 4.4 %shard_map.43 = (f32[8,512]{1,0:T(8,128)S(1)}, f32[8,512]{1,0:T(8,128)S(1)}, f32[16,512]{1,0:T(8,128)S(1)}) custom-call(s32[83]{0:T(128)S(1)} %get-tuple-element.29.full_ref, s32[83]{0:T(128)S(1)} %get-tuple-element.30.part_ref, s32[10]{0:T(128)S(1)} %get-tuple-element.31.count_ref, bf16[512,384]{1,0:T(8,128)(2,1)S(1)} %collective-permute-done.8.refs_0_, ...), custom_call_target="tpu_custom_call" | custom-call | flops 1409286144 | bytes 8000000 | tf_op jit(solution)/shard_map/pallas_call | solution.py:321
  58.8 0.7 collective-permute-start.17
  59.5 0.9 %collective-permute-done.17 = f32[16,512]{1,0:T(8,128)S(1)} collective-permute-done((f32[16,512]{1,0:T(8,128)S(1)}, f32[16,512]{1,0:T(8,128)S(1)}, u32[]{:S(2)}, u32[]{:S(2)}) %collective-permute-start.17) | collective-permute-done | bytes 32800 | tf_op jit(solution)/shard_map/ppermute | solution.py:341
  60.4 3.2 %collective-permute-start.18 = (f32[8,512]{1,0:T(8,128)S(1)}, f32[8,512]{1,0:T(8,128)S(1)}, u32[]{:S(2)}, u32[]{:S(2)}) collective-permute-start(f32[8,512]{1,0:T(8,128)S(1)} %slice_maximum_fusion), channel_id=1, source_target_pairs={{0,4},{1,5},{2,6},{3,7},{4,0},{5,1},{6,2},{7,3},{8,12},{9,13},{10,... | collective-permute-start | bytes 49160 | tf_op jit(solution)/shard_map/ppermute | solution.py:346
  63.6 1.1 %collective-permute-done.18 = f32[8,512]{1,0:T(8,128)S(1)} collective-permute-done((f32[8,512]{1,0:T(8,128)S(1)}, f32[8,512]{1,0:T(8,128)S(1)}, u32[]{:S(2)}, u32[]{:S(2)}) %collective-permute-start.18) | collective-permute-done | bytes 16416 | tf_op jit(solution)/shard_map/ppermute | solution.py:346
  64.8 0.1 collective-permute-start.19
  64.8 2.5 %collective-permute-done.19 = f32[4,512]{1,0:T(4,128)S(1)} collective-permute-done((f32[4,512]{1,0:T(4,128)S(1)}, f32[4,512]{1,0:T(4,128)S(1)}, u32[]{:S(2)}, u32[]{:S(2)}) %collective-permute-start.19) | collective-permute-done | bytes 8224 | tf_op jit(solution)/shard_map/ppermute | solution.py:346
  67.3 0.1 collective-permute-start.20
  67.4 3.6 %collective-permute-done.20 = f32[2,512]{1,0:T(2,128)S(1)} collective-permute-done((f32[2,512]{1,0:T(2,128)S(1)}, f32[2,512]{1,0:T(2,128)S(1)}, u32[]{:S(2)}, u32[]{:S(2)}) %collective-permute-start.20) | collective-permute-done | bytes 4128 | tf_op jit(solution)/shard_map/ppermute | solution.py:346
  71.1 2.1 %collective-permute-start.21 = (f32[512]{0:T(512)S(1)}, f32[512]{0:T(512)S(1)}, u32[]{:S(2)}, u32[]{:S(2)}) collective-permute-start(f32[512]{0:T(512)S(1)} %bitcast.11), channel_id=1, source_target_pairs={{0,16},{1,17},{2,18},{3,19},{4,20},{5,21},{6,22},{7,23},{8,24},{9,... | collective-permute-start | bytes 6152 | tf_op jit(solution)/shard_map/ppermute | solution.py:341
  73.2 0.8 %collective-permute-done.21 = f32[512]{0:T(512)S(1)} collective-permute-done((f32[512]{0:T(512)S(1)}, f32[512]{0:T(512)S(1)}, u32[]{:S(2)}, u32[]{:S(2)}) %collective-permute-start.21) | collective-permute-done | bytes 2080 | tf_op jit(solution)/shard_map/ppermute | solution.py:341
  74.1 0.6 maximum_maximum_fusion
  (21 shorter events, 0.1 us)
Async XLA Ops:
  0.0 9.8 %copy-start.3 = (s32[756]{0:T(1024)S(1)}, s32[756]{0:T(1024)}, u32[]{:S(2)}) copy-start(s32[756]{0:T(1024)} %constant.17.clone.table_ref) | copy-start | bytes 9076
  0.0 9.8 %copy-start.2 = (s32[256]{0:T(256)S(1)}, s32[256]{0:T(256)}, u32[]{:S(2)}) copy-start(s32[256]{0:T(256)} %cluster_ref.1) | copy-start | bytes 3076
  0.0 3.0 %collective-permute-start = (bf16[512,384]{1,0:T(8,128)(2,1)}, bf16[512,384]{1,0:T(8,128)(2,1)S(1)}, u32[]{:S(2)}, u32[]{:S(2)}) collective-permute-start(bf16[512,384]{1,0:T(8,128)(2,1)} %x_ref.1), channel_id=1, source_target_pairs={{0,16},{1,17},{2,18},{3,19},{4,20},{5,21},{6,22},{7,23},{8,24},{9,... | collective-permute-start | bytes 1179656 | tf_op jit(solution)/shard_map/ppermute | solution.py:341
  1.4 1.0 %copy-start.1 = (bf16[512,384]{1,0:T(8,128)(2,1)S(1)}, bf16[512,384]{1,0:T(8,128)(2,1)}, u32[]{:S(2)}) copy-start(bf16[512,384]{1,0:T(8,128)(2,1)} %x_ref.1) | copy-start | bytes 1179652
  3.2 12.6 %collective-permute-start.3 = (bf16[2,512,384]{2,1,0:T(8,128)(2,1)S(1)}, bf16[2,512,384]{2,1,0:T(8,128)(2,1)S(1)}, u32[]{:S(2)}, u32[]{:S(2)}) collective-permute-start(bf16[2,512,384]{2,1,0:T(8,128)(2,1)S(1)} %shard_map.38.unit_ref.refs_3_), channel_id=1, source_target_pairs={{0,32},{1,33},{2,34},{3,35},{4,36},{5,37},{6,38},{7,39},{8,40},{9,... | collective-permute-start | bytes 2359304 | tf_op jit(solution)/shard_map/ppermute | solution.py:346
  6.1 13.4 %collective-permute-start.4 = (bf16[2,512,384]{2,1,0:T(8,128)(2,1)S(1)}, bf16[2,512,384]{2,1,0:T(8,128)(2,1)S(1)}, u32[]{:S(2)}, u32[]{:S(2)}) collective-permute-start(bf16[2,512,384]{2,1,0:T(8,128)(2,1)S(1)} %shard_map.38.unit_ref.refs_3_), channel_id=1, source_target_pairs={{0,4},{1,5},{2,6},{3,7},{4,0},{5,1},{6,2},{7,3},{8,12},{9,13},{10,... | collective-permute-start | bytes 2359304 | tf_op jit(solution)/shard_map/ppermute | solution.py:346
  9.8 10.8 %collective-permute-start.1 = (bf16[2,512,384]{2,1,0:T(8,128)(2,1)S(1)}, bf16[2,512,384]{2,1,0:T(8,128)(2,1)S(1)}, u32[]{:S(2)}, u32[]{:S(2)}) collective-permute-start(bf16[2,512,384]{2,1,0:T(8,128)(2,1)S(1)} %shard_map.38.unit_ref.refs_3_), channel_id=1, source_target_pairs={{0,96},{1,97},{2,98},{3,99},{4,100},{5,101},{6,102},{7,103},{8,104... | collective-permute-start | bytes 2359304 | tf_op jit(solution)/shard_map/ppermute | solution.py:346
  15.7 7.8 %collective-permute-start.5 = (bf16[2,512,384]{2,1,0:T(8,128)(2,1)S(1)}, bf16[2,512,384]{2,1,0:T(8,128)(2,1)S(1)}, u32[]{:S(2)}, u32[]{:S(2)}) collective-permute-start(bf16[2,512,384]{2,1,0:T(8,128)(2,1)S(1)} %collective-permute-done.3.refs_0_), channel_id=1, source_target_pairs={{0,16},{1,17},{2,18},{3,19},{4,20},{5,21},{6,22},{7,23},{8,24},{9,... | collective-permute-start | bytes 2359304 | tf_op jit(solution)/shard_map/ppermute | solution.py:341
  19.5 6.3 %collective-permute-start.7 = (bf16[2,512,384]{2,1,0:T(8,128)(2,1)S(1)}, bf16[2,512,384]{2,1,0:T(8,128)(2,1)S(1)}, u32[]{:S(2)}, u32[]{:S(2)}) collective-permute-start(bf16[2,512,384]{2,1,0:T(8,128)(2,1)S(1)} %collective-permute-done.4.refs_2_), channel_id=1, source_target_pairs={{0,16},{1,17},{2,18},{3,19},{4,20},{5,21},{6,22},{7,23},{8,24},{9,... | collective-permute-start | bytes 2359304 | tf_op jit(solution)/shard_map/ppermute | solution.py:341
  20.7 5.1 %collective-permute-start.6 = (bf16[2,512,384]{2,1,0:T(8,128)(2,1)S(1)}, bf16[2,512,384]{2,1,0:T(8,128)(2,1)S(1)}, u32[]{:S(2)}, u32[]{:S(2)}) collective-permute-start(bf16[2,512,384]{2,1,0:T(8,128)(2,1)S(1)} %collective-permute-done.1.refs_1_), channel_id=1, source_target_pairs={{0,16},{1,17},{2,18},{3,19},{4,20},{5,21},{6,22},{7,23},{8,24},{9,... | collective-permute-start | bytes 2359304 | tf_op jit(solution)/shard_map/ppermute | solution.py:341
  20.7 12.3 %collective-permute-start.10 = (bf16[2,512,384]{2,1,0:T(8,128)(2,1)S(1)}, bf16[2,512,384]{2,1,0:T(8,128)(2,1)S(1)}, u32[]{:S(2)}, u32[]{:S(2)}) collective-permute-start(bf16[2,512,384]{2,1,0:T(8,128)(2,1)S(1)} %collective-permute-done.4.refs_2_), channel_id=1, source_target_pairs={{0,32},{1,33},{2,34},{3,35},{4,36},{5,37},{6,38},{7,39},{8,40},{9,... | collective-permute-start | bytes 2359304 | tf_op jit(solution)/shard_map/ppermute | solution.py:346
  21.9 11.3 %collective-permute-start.9 = (bf16[2,512,384]{2,1,0:T(8,128)(2,1)S(1)}, bf16[2,512,384]{2,1,0:T(8,128)(2,1)S(1)}, u32[]{:S(2)}, u32[]{:S(2)}) collective-permute-start(bf16[2,512,384]{2,1,0:T(8,128)(2,1)S(1)} %collective-permute-done.3.refs_0_), channel_id=1, source_target_pairs={{0,96},{1,97},{2,98},{3,99},{4,100},{5,101},{6,102},{7,103},{8,104... | collective-permute-start | bytes 2359304 | tf_op jit(solution)/shard_map/ppermute | solution.py:346
  23.5 12.4 %collective-permute-start.2 = (bf16[2,512,384]{2,1,0:T(8,128)(2,1)S(1)}, bf16[2,512,384]{2,1,0:T(8,128)(2,1)S(1)}, u32[]{:S(2)}, u32[]{:S(2)}) collective-permute-start(bf16[2,512,384]{2,1,0:T(8,128)(2,1)S(1)} %collective-permute-done.1.refs_1_), channel_id=1, source_target_pairs={{0,4},{1,5},{2,6},{3,7},{4,0},{5,1},{6,2},{7,3},{8,12},{9,13},{10,... | collective-permute-start | bytes 2359304 | tf_op jit(solution)/shard_map/ppermute | solution.py:346
  33.2 13.4 %collective-permute-start.16 = (bf16[2,512,384]{2,1,0:T(8,128)(2,1)S(1)}, bf16[2,512,384]{2,1,0:T(8,128)(2,1)S(1)}, u32[]{:S(2)}, u32[]{:S(2)}) collective-permute-start(bf16[2,512,384]{2,1,0:T(8,128)(2,1)S(1)} %collective-permute-done.10.refs_2_), channel_id=1, source_target_pairs={{0,16},{1,17},{2,18},{3,19},{4,20},{5,21},{6,22},{7,23},{8,24},{9,... | collective-permute-start | bytes 2359304 | tf_op jit(solution)/shard_map/ppermute | solution.py:341
  35.9 10.7 %collective-permute-start.14 = (bf16[2,512,384]{2,1,0:T(8,128)(2,1)S(1)}, bf16[2,512,384]{2,1,0:T(8,128)(2,1)S(1)}, u32[]{:S(2)}, u32[]{:S(2)}) collective-permute-start(bf16[2,512,384]{2,1,0:T(8,128)(2,1)S(1)} %collective-permute-done.9.refs_0_), channel_id=1, source_target_pairs={{0,16},{1,17},{2,18},{3,19},{4,20},{5,21},{6,22},{7,23},{8,24},{9,... | collective-permute-start | bytes 2359304 | tf_op jit(solution)/shard_map/ppermute | solution.py:341
  36.8 9.9 %collective-permute-start.15 = (bf16[2,512,384]{2,1,0:T(8,128)(2,1)S(1)}, bf16[2,512,384]{2,1,0:T(8,128)(2,1)S(1)}, u32[]{:S(2)}, u32[]{:S(2)}) collective-permute-start(bf16[2,512,384]{2,1,0:T(8,128)(2,1)S(1)} %collective-permute-done.2.refs_1_), channel_id=1, source_target_pairs={{0,16},{1,17},{2,18},{3,19},{4,20},{5,21},{6,22},{7,23},{8,24},{9,... | collective-permute-start | bytes 2359304 | tf_op jit(solution)/shard_map/ppermute | solution.py:341
  36.8 6.9 %collective-permute-start.11 = (bf16[512,384]{1,0:T(8,128)(2,1)S(1)}, bf16[512,384]{1,0:T(8,128)(2,1)S(1)}, u32[]{:S(2)}, u32[]{:S(2)}) collective-permute-start(bf16[512,384]{1,0:T(8,128)(2,1)S(1)} %slice_bitcast_fusion), channel_id=1, source_target_pairs={{0,96},{1,97},{2,98},{3,99},{4,100},{5,101},{6,102},{7,103},{8,104... | collective-permute-start | bytes 1179656 | tf_op jit(solution)/shard_map/ppermute | solution.py:346
  36.8 9.5 %collective-permute-start.8 = (bf16[512,384]{1,0:T(8,128)(2,1)S(1)}, bf16[512,384]{1,0:T(8,128)(2,1)S(1)}, u32[]{:S(2)}, u32[]{:S(2)}) collective-permute-start(bf16[512,384]{1,0:T(8,128)(2,1)S(1)} %slice_bitcast_fusion.1), channel_id=1, source_target_pairs={{0,32},{1,33},{2,34},{3,35},{4,36},{5,37},{6,38},{7,39},{8,40},{9,... | collective-permute-start | bytes 1179656 | tf_op jit(solution)/shard_map/ppermute | solution.py:346
  43.7 8.2 %collective-permute-start.13 = (bf16[512,384]{1,0:T(8,128)(2,1)S(1)}, bf16[512,384]{1,0:T(8,128)(2,1)S(1)}, u32[]{:S(2)}, u32[]{:S(2)}) collective-permute-start(bf16[512,384]{1,0:T(8,128)(2,1)S(1)} %collective-permute-done.11.refs_1_), channel_id=1, source_target_pairs={{0,16},{1,17},{2,18},{3,19},{4,20},{5,21},{6,22},{7,23},{8,24},{9,... | collective-permute-start | bytes 1179656 | tf_op jit(solution)/shard_map/ppermute | solution.py:341
  46.3 5.6 %collective-permute-start.12 = (bf16[512,384]{1,0:T(8,128)(2,1)S(1)}, bf16[512,384]{1,0:T(8,128)(2,1)S(1)}, u32[]{:S(2)}, u32[]{:S(2)}) collective-permute-start(bf16[512,384]{1,0:T(8,128)(2,1)S(1)} %collective-permute-done.8.refs_0_), channel_id=1, source_target_pairs={{0,16},{1,17},{2,18},{3,19},{4,20},{5,21},{6,22},{7,23},{8,24},{9,... | collective-permute-start | bytes 1179656 | tf_op jit(solution)/shard_map/ppermute | solution.py:341
  51.9 2.6 %copy-start = (bf16[14,512,384]{2,1,0:T(8,128)(2,1)S(1)}, bf16[14,512,384]{2,1,0:T(8,128)(2,1)}, u32[]{:S(2)}) copy-start(bf16[14,512,384]{2,1,0:T(8,128)(2,1)} %get-tuple-element.44.refs_4_) | copy-start | bytes 16515076
  58.8 1.6 %collective-permute-start.17 = (f32[16,512]{1,0:T(8,128)S(1)}, f32[16,512]{1,0:T(8,128)S(1)}, u32[]{:S(2)}, u32[]{:S(2)}) collective-permute-start(f32[16,512]{1,0:T(8,128)S(1)} %get-tuple-element.49), channel_id=1, source_target_pairs={{0,16},{1,17},{2,18},{3,19},{4,20},{5,21},{6,22},{7,23},{8,24},{9,... | collective-permute-start | bytes 98312 | tf_op jit(solution)/shard_map/ppermute | solution.py:341
  60.4 4.3 %collective-permute-start.18 = (f32[8,512]{1,0:T(8,128)S(1)}, f32[8,512]{1,0:T(8,128)S(1)}, u32[]{:S(2)}, u32[]{:S(2)}) collective-permute-start(f32[8,512]{1,0:T(8,128)S(1)} %slice_maximum_fusion), channel_id=1, source_target_pairs={{0,4},{1,5},{2,6},{3,7},{4,0},{5,1},{6,2},{7,3},{8,12},{9,13},{10,... | collective-permute-start | bytes 49160 | tf_op jit(solution)/shard_map/ppermute | solution.py:346
  64.8 2.6 %collective-permute-start.19 = (f32[4,512]{1,0:T(4,128)S(1)}, f32[4,512]{1,0:T(4,128)S(1)}, u32[]{:S(2)}, u32[]{:S(2)}) collective-permute-start(f32[4,512]{1,0:T(4,128)S(1)} %slice.45), channel_id=1, source_target_pairs={{0,96},{1,97},{2,98},{3,99},{4,100},{5,101},{6,102},{7,103},{8,104... | collective-permute-start | bytes 24584 | tf_op jit(solution)/shard_map/ppermute | solution.py:346
  67.3 3.7 %collective-permute-start.20 = (f32[2,512]{1,0:T(2,128)S(1)}, f32[2,512]{1,0:T(2,128)S(1)}, u32[]{:S(2)}, u32[]{:S(2)}) collective-permute-start(f32[2,512]{1,0:T(2,128)S(1)} %slice.47), channel_id=1, source_target_pairs={{0,32},{1,33},{2,34},{3,35},{4,36},{5,37},{6,38},{7,39},{8,40},{9,... | collective-permute-start | bytes 12296 | tf_op jit(solution)/shard_map/ppermute | solution.py:346
  71.1 3.0 %collective-permute-start.21 = (f32[512]{0:T(512)S(1)}, f32[512]{0:T(512)S(1)}, u32[]{:S(2)}, u32[]{:S(2)}) collective-permute-start(f32[512]{0:T(512)S(1)} %bitcast.11), channel_id=1, source_target_pairs={{0,16},{1,17},{2,18},{3,19},{4,20},{5,21},{6,22},{7,23},{8,24},{9,... | collective-permute-start | bytes 6152 | tf_op jit(solution)/shard_map/ppermute | solution.py:341

commit v4 on v3

--- a/solution.py
+++ b/solution.py
@@ -12,7 +12,7 @@
 SHARD = 512
 D = 384
 GROUP = 4
-VMEM_LIMIT = 40 * 1024 * 1024
+VMEM_LIMIT = 20 * 1024 * 1024
 
 CORE = 16
 X1, X3, Y1, Y3, Z1, Z3 = 32, 96, 4, 12, 1, 3
@@ -20,7 +20,14 @@
 SLOTS = ((), (0,), (1,), (2,), (0, 1), (1, 2), (2, 0), (0, 1, 2))
 SENDS = ((0, 0), (0, 1), (0, 2), (1, 1), (2, 2), (3, 0))
 HALVES = ((5, 0), (6, 1))
-PHASES = (((1, 2, 3), 0, 4, 4), ((4, 5, 6), 0, 4, 4), ((4, 5, 6), 4, 7, 4), ((7,), 0, 7, 4), ((7,), 7, 8, 1))
+PHASES = (
+    ((1, 2, 3), 0, 4, 4),
+    ((4, 5, 6), 0, 4, 4),
+    ((4, 5, 6), 4, 7, 4),
+    ((7,), 0, 4, 4),
+    ((7,), 4, 7, 4),
+    ((7,), 7, 8, 1),
+)
 
 
 def mask_of(core, slot):
@@ -37,7 +44,7 @@
             for i in slots:
                 for j in range(low, min(i + 1, high)):
                     a, b = mask_of(core, i), mask_of(1 - core, j)
-                    code = 2 * (i - slots[0]) | (2 * (j if low < 7 else 0)) << 4
+                    code = 2 * (i - slots[0]) | (2 * (j - low)) << 4
                     bit = (a ^ b) & -(a ^ b)
                     if j < i or core == 0:
                         tables.append((code, a, b, 0, core, 1))
@@ -72,7 +79,7 @@
     return (values * lax.rsqrt(squares + 1e-06)).astype(jnp.bfloat16)
 
 
-def own_kernel(x_ref, out_ref):
+def first_kernel(x_ref, out_ref):
     out_ref[...] = unit_of(x_ref[...])
 
 
@@ -85,7 +92,7 @@
 def unit_call(here, x, other):
     cost = pl.CostEstimate(flops=1000000, bytes_accessed=1600000, transcendentals=512)
     own = pl.pallas_call(
-        own_kernel,
+        first_kernel,
         out_shape=jax.ShapeDtypeStruct((SHARD, D), jnp.bfloat16),
         in_specs=[spec(VMEM)],
         out_specs=spec(VMEM),
@@ -106,7 +113,7 @@
     return lax.dot_general(a, b, (((1,), (1,)), ((), ())), preferred_element_type=jnp.float32)
 
 
-def self_kernel(here_ref, cluster_ref, table_ref, unit_ref, own_ref, full_ref, part_ref, count_ref):
+def plan_kernel(here_ref, cluster_ref, table_ref, full_ref, part_ref, count_ref):
     here = here_ref[0]
     core = (here >> 4) & 1
     for phase in range(len(PHASES)):
@@ -144,6 +151,10 @@
         count_ref[2 * phase] = full
         count_ref[2 * phase + 1] = part
 
+
+def own_kernel(here_ref, cluster_ref, unit_ref, own_ref):
+    here = here_ref[0]
+    core = (here >> 4) & 1
     first0 = cluster_ref[2 * here]
     first1 = cluster_ref[2 * here + 1]
     there = here ^ CORE
@@ -166,21 +177,27 @@
     own_ref[...] = jnp.max(best, axis=0, keepdims=True)
 
 
-def self_call(here, cluster, table, unit):
+def plan_call(here, cluster, table):
     lists = jax.ShapeDtypeStruct((LISTS,), jnp.int32)
     return pl.pallas_call(
-        self_kernel,
-        out_shape=(
-            jax.ShapeDtypeStruct((1, SHARD), jnp.float32),
-            lists,
-            lists,
-            jax.ShapeDtypeStruct((2 * len(PHASES),), jnp.int32),
-        ),
-        in_specs=[spec(SMEM), spec(SMEM), spec(SMEM), spec(VMEM)],
-        out_specs=(spec(VMEM), spec(SMEM), spec(SMEM), spec(SMEM)),
+        plan_kernel,
+        out_shape=(lists, lists, jax.ShapeDtypeStruct((2 * len(PHASES),), jnp.int32)),
+        in_specs=[spec(SMEM)] * 3,
+        out_specs=(spec(SMEM),) * 3,
         compiler_params=params(),
-        cost_estimate=pl.CostEstimate(flops=4000000000, bytes_accessed=1000000, transcendentals=0),
-    )(here, cluster, table, unit)
+        cost_estimate=pl.CostEstimate(flops=3000000000, bytes_accessed=10000, transcendentals=0),
+    )(here, cluster, table)
+
+
+def own_call(here, cluster, unit):
+    return pl.pallas_call(
+        own_kernel,
+        out_shape=jax.ShapeDtypeStruct((1, SHARD), jnp.float32),
+        in_specs=[spec(SMEM), spec(SMEM), spec(VMEM)],
+        out_specs=spec(VMEM),
+        compiler_params=params(),
+        cost_estimate=pl.CostEstimate(flops=1000000000, bytes_accessed=1000000, transcendentals=0),
+    )(here, cluster, unit)
 
 
 def fold(row_ref, col_ref, i, j, rows, cols, scores):
@@ -234,52 +251,59 @@
             out_ref[at : at + 1, 128 * k : 128 * k + 128] = jnp.max(part, axis=0, keepdims=True)
 
 
-def score_kernel(phase, full_ref, part_ref, count_ref, *refs):
-    slots, low, high, _ = PHASES[phase]
-    mine, refs = refs[: len(slots)], refs[len(slots) :]
-    if phase == 0:
-        theirs, refs = refs[:high], refs[high:]
-        row_ref, col_ref, b_buf, a_buf = refs
-        row_ref[...] = jnp.full(row_ref.shape, -2.0, jnp.float32)
-        col_ref[...] = jnp.full(col_ref.shape, -2.0, jnp.float32)
-    elif phase == 1:
-        b_buf, col_in, row_ref, col_ref, a_buf = refs
-        theirs = ()
-        row_ref[...] = jnp.full(row_ref.shape, -2.0, jnp.float32)
-        col_ref[...] = col_in[...]
-    else:
-        theirs, refs = refs[: high - low], refs[high - low :]
-        b_in, col_in, row_in, row_ref, col_ref, b_buf, a_buf = refs
-        b_buf[: 2 * low] = b_in[...]
-        row_ref[...] = row_in[...]
-        col_ref[...] = col_in[...]
-    for n, ref in enumerate(mine):
-        a_buf[2 * n : 2 * n + 2] = ref[...]
-    for n, ref in enumerate(theirs, low):
-        b_buf[2 * n : 2 * n + 2] = ref[...]
-    score_lists(phase, full_ref, part_ref, count_ref, a_buf, b_buf, row_ref, col_ref)
+def clear(*refs):
+    for ref in refs:
+        ref[...] = jnp.full(ref.shape, -2.0, jnp.float32)
+
+
+def put(buf, refs):
+    for n, ref in enumerate(refs):
+        buf[2 * n : 2 * n + 2] = ref[...]
+
+
+def early_kernel(full_ref, part_ref, count_ref, *refs):
+    mine, theirs, (rows_out, col_ref, b_buf, a_buf, row_ref) = refs[:3], refs[3:7], refs[7:]
+    clear(row_ref, col_ref)
+    put(a_buf, mine)
+    put(b_buf, theirs)
+    score_lists(0, full_ref, part_ref, count_ref, a_buf, b_buf, row_ref, col_ref)
+    for slot in (1, 2, 3):
+        put_rows(rows_out, 2 * slot - 2, row_ref, 2 * slot - 2)
+
+
+def middle_kernel(full_ref, part_ref, count_ref, *refs):
+    mine, (b_buf, col_in, row_ref, col_ref, a_buf) = refs[:3], refs[3:]
+    clear(row_ref)
+    col_ref[...] = col_in[...]
+    put(a_buf, mine)
+    score_lists(1, full_ref, part_ref, count_ref, a_buf, b_buf, row_ref, col_ref)
 
 
 ROWS = jax.ShapeDtypeStruct((6, SHARD, 128), jnp.float32)
-COLS = jax.ShapeDtypeStruct((14, 8, SHARD), jnp.float32)
-
-
-def score_call(phase, plan, mine, theirs, state):
-    outs = (ROWS, COLS)
-    if phase != 1:
-        outs = outs + (jax.ShapeDtypeStruct((2 * PHASES[phase][2], SHARD, D), jnp.bfloat16),)
-    operands = list(plan) + list(mine) + list(theirs) + list(state)
+COLS = jax.ShapeDtypeStruct((8, 8, SHARD), jnp.float32)
+PACK = jax.ShapeDtypeStruct((6, SHARD, D), jnp.bfloat16)
+
+
+def kernel_call(kernel, operands, outs, scratch, flops, smem=3):
     return pl.pallas_call(
-        functools.partial(score_kernel, phase),
+        kernel,
         out_shape=outs,
-        in_specs=[spec(SMEM)] * 3 + [spec(VMEM)] * (len(operands) - 3),
-        out_specs=(spec(VMEM),) * len(outs),
-        scratch_shapes=[VMEM((6, SHARD, D), jnp.bfloat16)],
+        in_specs=[spec(SMEM)] * smem + [spec(VMEM)] * (len(operands) - smem),
+        out_specs=jax.tree.map(lambda _: spec(VMEM), outs),
+        scratch_shapes=[VMEM(x.shape, x.dtype) for x in scratch],
         compiler_params=params(),
-        cost_estimate=pl.CostEstimate(
-            flops=COUNTS[phase] * SHARD * SHARD * D, bytes_accessed=8000000, transcendentals=0
-        ),
+        cost_estimate=pl.CostEstimate(flops=flops, bytes_accessed=8000000, transcendentals=0),
     )(*operands)
+
+
+def early_call(plan, mine, theirs):
+    buf = jax.ShapeDtypeStruct((8, SHARD, D), jnp.bfloat16)
+    outs = (jax.ShapeDtypeStruct((6, SHARD), jnp.float32), COLS, buf)
+    return kernel_call(early_kernel, [*plan, *mine, *theirs], outs, [PACK, ROWS], 4000000000)
+
+
+def middle_call(plan, *operands):
+    return kernel_call(middle_kernel, [*plan, *operands], (ROWS, COLS, PACK), [], 5000000000)
 
 
 KEPT = (0, 1, 2, 4)
@@ -287,54 +311,50 @@
 
 
 def last_kernel(full_ref, part_ref, count_ref, *refs):
-    plan, mine, theirs, refs = (full_ref, part_ref, count_ref), refs[:2], refs[2:4], refs[4:]
-    b_buf, col_in, rows0, rows1, keep_ref, send_ref, other_ref, refs = *refs[:7], refs[7:]
-    a_buf, b_last, row_ref, col_ref, col_last = refs
-    row_ref[...] = jnp.full(row_ref.shape, -2.0, jnp.float32)
-    col_ref[...] = col_in[...]
-    col_last[...] = jnp.full(col_last.shape, -2.0, jnp.float32)
+    plan = (full_ref, part_ref, count_ref)
+    theirs, mine7, theirs7, refs = refs[:3], refs[3:5], refs[5:7], refs[7:]
+    a_mid, b_low, col_low_in, rows0, row_in, keep_ref, send_ref, other_ref, *refs = refs
+    b_mid, a_last, b_last, row_mid, row_last, col_low, col_mid, col_last = refs
+    clear(row_last, col_mid, col_last)
+    row_mid[...] = row_in[...]
+    col_low[...] = col_low_in[...]
+    put(b_mid, theirs)
     for half in range(2):
-        a_buf[half] = mine[half][...]
-        b_last[half] = theirs[half][...]
-    score_lists(3, *plan, a_buf, b_buf, row_ref, col_ref)
-    score_lists(4, *plan, a_buf, b_last, row_ref, col_last)
+        a_last[half] = mine7[half][...]
+        b_last[half] = theirs7[half][...]
+    score_lists(2, *plan, a_mid, b_mid, row_mid, col_mid)
+    score_lists(3, *plan, a_last, b_low, row_last, col_low)
+    score_lists(4, *plan, a_last, b_mid, row_last, col_mid)
+    score_lists(5, *plan, a_last, b_last, row_last, col_last)
     keep_ref[0:2] = jnp.full((2, SHARD), -2.0, jnp.float32)
     for out_ref, slots in ((keep_ref, KEPT), (send_ref, SENT)):
         for place, slot in enumerate(slots):
             if slot == 7:
-                put_rows(out_ref, 2 * place, row_ref, 0)
+                put_rows(out_ref, 2 * place, row_last, 0)
             elif slot > 3:
-                put_rows(out_ref, 2 * place, rows1, 2 * slot - 8)
+                put_rows(out_ref, 2 * place, row_mid, 2 * slot - 8)
             elif slot > 0:
-                put_rows(out_ref, 2 * place, rows0, 2 * slot - 2)
+                out_ref[2 * place : 2 * place + 2] = rows0[2 * slot - 2 : 2 * slot]
     for place, slot in enumerate(KEPT + SENT):
         for half in range(2):
             at = 2 * place + half
-            down = col_last[half] if slot == 7 else col_ref[2 * slot + half]
+            if slot == 7:
+                down = col_last[half]
+            elif slot > 3:
+                down = col_mid[2 * slot - 8 + half]
+            else:
+                down = col_low[2 * slot + half]
             other_ref[at : at + 1, :] = jnp.max(down, axis=0, keepdims=True)
 
 
-def last_call(plan, mine, theirs, state):
-    eight = jax.ShapeDtypeStruct((8, SHARD), jnp.float32)
-    outs = (eight, eight, jax.ShapeDtypeStruct((16, SHARD), jnp.float32))
-    operands = list(plan) + list(mine) + list(theirs) + list(state)
-    return pl.pallas_call(
-        last_kernel,
-        out_shape=outs,
-        in_specs=[spec(SMEM)] * 3 + [spec(VMEM)] * (len(operands) - 3),
-        out_specs=(spec(VMEM),) * 3,
-        scratch_shapes=[
-            VMEM((2, SHARD, D), jnp.bfloat16),
-            VMEM((2, SHARD, D), jnp.bfloat16),
-            VMEM((2, SHARD, 128), jnp.float32),
-            VMEM(COLS.shape, jnp.float32),
-            VMEM((2, 8, SHARD), jnp.float32),
-        ],
-        compiler_params=params(),
-        cost_estimate=pl.CostEstimate(
-            flops=COUNTS[3] * SHARD * SHARD * D, bytes_accessed=8000000, transcendentals=0
-        ),
-    )(*operands)
+def last_call(plan, *operands):
+    def f32(*shape):
+        return jax.ShapeDtypeStruct(shape, jnp.float32)
+
+    two = jax.ShapeDtypeStruct((2, SHARD, D), jnp.bfloat16)
+    outs = (f32(8, SHARD), f32(8, SHARD), f32(16, SHARD))
+    scratch = [PACK, two, two, ROWS, f32(2, SHARD, 128), COLS, f32(6, 8, SHARD), f32(2, 8, SHARD)]
+    return kernel_call(last_kernel, [*plan, *operands], outs, scratch, 5000000000)
 
 
 def swap(x):
@@ -353,25 +373,27 @@
 def body(embeddings, block_cluster):
     here = (lax.axis_index("row") * 16 + lax.axis_index("col")).astype(jnp.int32).reshape(1)
     unit = unit_call(here, embeddings, swap(embeddings))
-    own, *plan = self_call(here, block_cluster, jnp.asarray(TABLE.reshape(-1)), unit)
+    plan = plan_call(here, block_cluster, jnp.asarray(TABLE.reshape(-1)))
     mine, theirs = [unit], [unit]
-    for slot in (1, 2, 3):
-        source, generator = SENDS[slot - 1]
-        mine.append(after(exchange(mine[source], generator), own))
-        theirs.append(swap(mine[slot]))
-    rows0, cols, b_buf = score_call(0, plan, mine[1:4], theirs[:4], ())
-    for slot in (4, 5, 6):
-        source, generator = SENDS[slot - 1]
-        mine.append(after(exchange(mine[source], generator), cols))
-        theirs.append(swap(mine[slot]))
-    rows1, cols = score_call(1, plan, mine[4:7], (), (b_buf, cols))
+
+    def step(slots):
+        return [exchange(mine[SENDS[k - 1][0]], SENDS[k - 1][1]) for k in slots]
+
+    own = own_call(here, block_cluster, unit)
+    mine.extend(after(x, plan[2], own) for x in step((1, 2, 3)))
+    theirs.extend(swap(x) for x in mine[1:4])
+    rows0, cols, b_low = early_call(plan, mine[1:4], theirs)
+    mine.extend(after(x, cols) for x in step((4, 5, 6)))
     halves = [
-        after(exchange(mine[source][half], generator), cols)
-        for half, (source, generator) in enumerate(HALVES)
+        exchange(mine[source][half], generator) for half, (source, generator) in enumerate(HALVES)
     ]
+    theirs.extend(swap(x) for x in mine[4:7])
+    rows1, cols, a_mid = middle_call(plan, *mine[4:7], b_low, cols)
+    halves = [after(x, cols) for x in halves]
     swapped = [swap(x) for x in halves]
-    rows1, cols, b_buf = score_call(2, plan, mine[4:7], theirs[4:7], (b_buf, cols, rows1))
-    keep, send, other = last_call(plan, halves, swapped, (b_buf, cols, rows0, rows1))
+    keep, send, other = last_call(
+        plan, *theirs[4:7], *halves, *swapped, a_mid, b_low, cols, rows0, rows1
+    )
     other = swap(other)
     keep = jnp.maximum(keep, other[:8])
     send = jnp.maximum(send, other[8:])

time: 74.8 us -> 71.5 us (0.956); the launches traced: 74.6 us -> 70.4 us
  starting transfers between devices: 26.8 us -> 32 us
  waiting for transfers between devices: 23.4 us -> 19.6 us
  Pallas kernels: 20.1 us -> 16.9 us
  local copies, waits for them, and re-layouts: 3.66 us -> 1.1 us
    ppermute x11, waiting for transfers between devices: 21.3 us -> 16.1 us  [exchange(): return lax.ppermute(x, ('row', 'col'), pairs)]
    ppermute x11, starting transfers between devices: 10.7 us -> 14.9 us  [swap(): return lax.ppermute(x, ('row', 'col'), [(s, s ^ CORE) for s in range(128)])]
    pallas_call x6, Pallas kernels: 19.9 us -> 16.7 us  [the longest x3 12.2 us: kernel_call(): pl.pallas_call(kernel, out_shape=outs, in_specs=[spec(SMEM)] * smem + [sp...]
    unnamed x8 -> x6, local copies, waits for them, and re-layouts: 3.56 us -> 1 us
    ppermute x11, waiting for transfers between devices: 2.11 us -> 3.48 us  [swap(): return lax.ppermute(x, ('row', 'col'), [(s, s ^ CORE) for s in range(128)])]
    ppermute x11, starting transfers between devices: 16 us -> 17.1 us  [exchange(): return lax.ppermute(x, ('row', 'col'), pairs)]
  transfers between devices with their start and end apart: 22 -> 22, of which waited for: 12 -> 15; matrix products, arithmetic and copies ran while one was open for 0% -> 0% of each run, Pallas kernels for 21% -> 17%
where the time goes in v4:
time: 71.5 us; the launch traced here: 70.4 us
  starting transfers between devices  32 us (45%)
  waiting for transfers between devices  19.6 us (27%)
  Pallas kernels  16.9 us (24%)
  local copies, waits for them, and re-layouts  1.1 us (2%)
    ppermute x11, starting transfers between devices, exchange(): return lax.ppermute(x, ('row', 'col'), pairs)  17.1 us
    ppermute x11, waiting for transfers between devices, exchange(): return lax.ppermute(x, ('row', 'col'), pairs)  16.1 us
    ppermute x11, starting transfers between devices, swap(): return lax.ppermute(x, ('row', 'col'), [(s, s ^ CORE) for s in range(128)])  14.9 us
    pallas_call x3, Pallas kernels, kernel_call(): pl.pallas_call(kernel, out_shape=outs, in_specs=[spec(SMEM)] * smem + [sp...  12.2 us
    ppermute x11, waiting for transfers between devices, swap(): return lax.ppermute(x, ('row', 'col'), [(s, s ^ CORE) for s in range(128)])  3.48 us
    pallas_call x1, Pallas kernels, plan_call(): pl.pallas_call(plan_kernel, out_shape=(lists, lists, jax.ShapeDtypeStruct...  3.05 us
  transfers between devices with their start and end apart: 22, of which 15 were waited for; matrix products, arithmetic and copies ran while one was open for 0% of the time, Pallas kernels for 17%

profile of v4, /device:TPU:1, one launch (start us, length us, event | category | flops | bytes accessed | tf_op | source)
XLA Modules:
  0.0 70.4 jit_solution(13502702586599486252)
XLA Ops:
  0.0 1.4 %collective-permute-start = (bf16[512,384]{1,0:T(8,128)(2,1)}, bf16[512,384]{1,0:T(8,128)(2,1)S(1)}, u32[]{:S(2)}, u32[]{:S(2)}) collective-permute-start(bf16[512,384]{1,0:T(8,128)(2,1)} %x_ref.1), channel_id=1, source_target_pairs={{0,16},{1,17},{2,18},{3,19},{4,20},{5,21},{6,22},{7,23},{8,24},{9,... | collective-permute-start | bytes 1179656 | tf_op jit(solution)/shard_map/ppermute | solution.py:361
  1.4 1.0 %copy-done = bf16[512,384]{1,0:T(8,128)(2,1)S(1)} copy-done((bf16[512,384]{1,0:T(8,128)(2,1)S(1)}, bf16[512,384]{1,0:T(8,128)(2,1)}, u32[]{:S(2)}) %copy-start) | copy-done | bytes 393240
  2.4 0.2 shard_map.37.own_ref
  2.6 0.4 collective-permute-done.other_ref
  3.0 0.2 shard_map.38.unit_ref.refs_3_
  3.2 1.8 %collective-permute-start.3 = (bf16[2,512,384]{2,1,0:T(8,128)(2,1)S(1)}, bf16[2,512,384]{2,1,0:T(8,128)(2,1)S(1)}, u32[]{:S(2)}, u32[]{:S(2)}) collective-permute-start(bf16[2,512,384]{2,1,0:T(8,128)(2,1)S(1)} %shard_map.38.unit_ref.refs_3_), channel_id=1, source_target_pairs={{0,96},{1,97},{2,98},{3,99},{4,100},{5,101},{6,102},{7,103},{8,104... | collective-permute-start | bytes 2359304 | tf_op jit(solution)/shard_map/ppermute | solution.py:366
  5.0 2.2 %collective-permute-start.4 = (bf16[2,512,384]{2,1,0:T(8,128)(2,1)S(1)}, bf16[2,512,384]{2,1,0:T(8,128)(2,1)S(1)}, u32[]{:S(2)}, u32[]{:S(2)}) collective-permute-start(bf16[2,512,384]{2,1,0:T(8,128)(2,1)S(1)} %shard_map.38.unit_ref.refs_3_), channel_id=1, source_target_pairs={{0,4},{1,5},{2,6},{3,7},{4,0},{5,1},{6,2},{7,3},{8,12},{9,13},{10,... | collective-permute-start | bytes 2359304 | tf_op jit(solution)/shard_map/ppermute | solution.py:366
  7.2 2.7 %collective-permute-start.1 = (bf16[2,512,384]{2,1,0:T(8,128)(2,1)S(1)}, bf16[2,512,384]{2,1,0:T(8,128)(2,1)S(1)}, u32[]{:S(2)}, u32[]{:S(2)}) collective-permute-start(bf16[2,512,384]{2,1,0:T(8,128)(2,1)S(1)} %shard_map.38.unit_ref.refs_3_), channel_id=1, source_target_pairs={{0,32},{1,33},{2,34},{3,35},{4,36},{5,37},{6,38},{7,39},{8,40},{9,... | collective-permute-start | bytes 2359304 | tf_op jit(solution)/shard_map/ppermute | solution.py:366
  9.9 3.1 %shard_map.40 = (s32[87]{0:T(128)S(1)}, s32[87]{0:T(128)S(1)}, s32[12]{0:T(128)S(1)}) custom-call(s32[1]{0:T(128)} %bitcast.here_ref, s32[256]{0:T(256)S(1)} %copy-done.1, s32[756]{0:T(1024)S(1)} %copy-done.2), custom_call_target="tpu_custom_call" | custom-call | flops 3000000000 | bytes 10000 | tf_op jit(solution)/shard_map/pallas_call | solution.py:182
  13.0 1.3 %shard_map.39 = f32[1,512]{1,0:T(1,128)S(1)} custom-call(s32[1]{0:T(128)} %bitcast.here_ref, s32[256]{0:T(256)S(1)} %copy-done.1, bf16[2,512,384]{2,1,0:T(8,128)(2,1)S(1)} %shard_map.38.unit_ref.refs_3_), custom_call_target="tpu_custom_call" | custom-call | flops 1000000000 | bytes 1000000 | tf_op jit(solution)/shard_map/pallas_call | solution.py:193
  14.3 0.3 collective-permute-done.3.refs_1_
  14.6 2.2 %collective-permute-start.6 = (bf16[2,512,384]{2,1,0:T(8,128)(2,1)S(1)}, bf16[2,512,384]{2,1,0:T(8,128)(2,1)S(1)}, u32[]{:S(2)}, u32[]{:S(2)}) collective-permute-start(bf16[2,512,384]{2,1,0:T(8,128)(2,1)S(1)} %collective-permute-done.3.refs_1_), channel_id=1, source_target_pairs={{0,16},{1,17},{2,18},{3,19},{4,20},{5,21},{6,22},{7,23},{8,24},{9,... | collective-permute-start | bytes 2359304 | tf_op jit(solution)/shard_map/ppermute | solution.py:361
  16.8 0.2 collective-permute-done.4.refs_2_
  17.0 1.4 %collective-permute-start.7 = (bf16[2,512,384]{2,1,0:T(8,128)(2,1)S(1)}, bf16[2,512,384]{2,1,0:T(8,128)(2,1)S(1)}, u32[]{:S(2)}, u32[]{:S(2)}) collective-permute-start(bf16[2,512,384]{2,1,0:T(8,128)(2,1)S(1)} %collective-permute-done.4.refs_2_), channel_id=1, source_target_pairs={{0,16},{1,17},{2,18},{3,19},{4,20},{5,21},{6,22},{7,23},{8,24},{9,... | collective-permute-start | bytes 2359304 | tf_op jit(solution)/shard_map/ppermute | solution.py:361
  18.4 0.9 %collective-permute-done.1.refs_0_ = bf16[2,512,384]{2,1,0:T(8,128)(2,1)S(1)} collective-permute-done((bf16[2,512,384]{2,1,0:T(8,128)(2,1)S(1)}, bf16[2,512,384]{2,1,0:T(8,128)(2,1)S(1)}, u32[]{:S(2)}, u32[]{:S(2)}) %collective-permute-start.1) | collective-permute-done | bytes 786464 | tf_op jit(solution)/shard_map/ppermute | solution.py:366
  19.3 0.7 %collective-permute-start.5 = (bf16[2,512,384]{2,1,0:T(8,128)(2,1)S(1)}, bf16[2,512,384]{2,1,0:T(8,128)(2,1)S(1)}, u32[]{:S(2)}, u32[]{:S(2)}) collective-permute-start(bf16[2,512,384]{2,1,0:T(8,128)(2,1)S(1)} %collective-permute-done.1.refs_0_), channel_id=1, source_target_pairs={{0,16},{1,17},{2,18},{3,19},{4,20},{5,21},{6,22},{7,23},{8,24},{9,... | collective-permute-start | bytes 2359304 | tf_op jit(solution)/shard_map/ppermute | solution.py:361
  20.0 2.0 %collective-permute-start.11 = (bf16[2,512,384]{2,1,0:T(8,128)(2,1)S(1)}, bf16[2,512,384]{2,1,0:T(8,128)(2,1)S(1)}, u32[]{:S(2)}, u32[]{:S(2)}) collective-permute-start(bf16[2,512,384]{2,1,0:T(8,128)(2,1)S(1)} %collective-permute-done.4.refs_2_), channel_id=1, source_target_pairs={{0,32},{1,33},{2,34},{3,35},{4,36},{5,37},{6,38},{7,39},{8,40},{9,... | collective-permute-start | bytes 2359304 | tf_op jit(solution)/shard_map/ppermute | solution.py:366
  22.0 3.7 %collective-permute-start.9 = (bf16[2,512,384]{2,1,0:T(8,128)(2,1)S(1)}, bf16[2,512,384]{2,1,0:T(8,128)(2,1)S(1)}, u32[]{:S(2)}, u32[]{:S(2)}) collective-permute-start(bf16[2,512,384]{2,1,0:T(8,128)(2,1)S(1)} %collective-permute-done.3.refs_1_), channel_id=1, source_target_pairs={{0,4},{1,5},{2,6},{3,7},{4,0},{5,1},{6,2},{7,3},{8,12},{9,13},{10,... | collective-permute-start | bytes 2359304 | tf_op jit(solution)/shard_map/ppermute | solution.py:366
  25.7 0.0 collective-permute-done.6.refs_5_
  25.7 0.0 collective-permute-start.2
  25.7 0.0 collective-permute-done.7.refs_6_
  25.7 2.9 %shard_map.41 = (f32[6,512]{1,0:T(8,128)S(1)}, f32[8,8,512]{2,1,0:T(8,128)S(1)}, bf16[8,512,384]{2,1,0:T(8,128)(2,1)S(1)}) custom-call(s32[87]{0:T(128)S(1)} %get-tuple-element.25.full_ref, s32[87]{0:T(128)S(1)} %get-tuple-element.26.part_ref, s32[12]{0:T(128)S(1)} %get-tuple-element.27.count_ref, bf16[2,512,384]{2,1,0:T(8,128)(2,1)S(1)} %collective-permute-done.1.refs_0_, ...), custom_call_target="tpu_custom_call" | custom-call | flops 4000000000 | bytes 8000000 | tf_op jit(solution)/shard_map/pallas_call | solution.py:288
  28.6 3.7 %collective-permute-done.11.refs_2_ = bf16[2,512,384]{2,1,0:T(8,128)(2,1)S(1)} collective-permute-done((bf16[2,512,384]{2,1,0:T(8,128)(2,1)S(1)}, bf16[2,512,384]{2,1,0:T(8,128)(2,1)S(1)}, u32[]{:S(2)}, u32[]{:S(2)}) %collective-permute-start.11) | collective-permute-done | bytes 786464 | tf_op jit(solution)/shard_map/ppermute | solution.py:366
  32.4 2.7 %collective-permute-done.9.refs_1_ = bf16[2,512,384]{2,1,0:T(8,128)(2,1)S(1)} collective-permute-done((bf16[2,512,384]{2,1,0:T(8,128)(2,1)S(1)}, bf16[2,512,384]{2,1,0:T(8,128)(2,1)S(1)}, u32[]{:S(2)}, u32[]{:S(2)}) %collective-permute-start.9) | collective-permute-done | bytes 786464 | tf_op jit(solution)/shard_map/ppermute | solution.py:366
  35.1 0.5 collective-permute-start.10
  35.7 0.9 %collective-permute-done.2.refs_0_ = bf16[2,512,384]{2,1,0:T(8,128)(2,1)S(1)} collective-permute-done((bf16[2,512,384]{2,1,0:T(8,128)(2,1)S(1)}, bf16[2,512,384]{2,1,0:T(8,128)(2,1)S(1)}, u32[]{:S(2)}, u32[]{:S(2)}) %collective-permute-start.2) | collective-permute-done | bytes 786464 | tf_op jit(solution)/shard_map/ppermute | solution.py:366
  36.5 0.0 collective-permute-start.14
  36.5 1.1 %collective-permute-start.13 = (bf16[512,384]{1,0:T(8,128)(2,1)S(1)}, bf16[512,384]{1,0:T(8,128)(2,1)S(1)}, u32[]{:S(2)}, u32[]{:S(2)}) collective-permute-start(bf16[512,384]{1,0:T(8,128)(2,1)S(1)} %slice_bitcast_fusion.1), channel_id=1, source_target_pairs={{0,32},{1,33},{2,34},{3,35},{4,36},{5,37},{6,38},{7,39},{8,40},{9,... | collective-permute-start | bytes 1179656 | tf_op jit(solution)/shard_map/ppermute | solution.py:366
  37.6 0.1 collective-permute-start.8
  37.7 4.8 %shard_map.42 = (f32[6,512,128]{2,1,0:T(8,128)S(1)}, f32[8,8,512]{2,1,0:T(8,128)S(1)}, bf16[6,512,384]{2,1,0:T(8,128)(2,1)S(1)}) custom-call(s32[87]{0:T(128)S(1)} %get-tuple-element.25.full_ref, s32[87]{0:T(128)S(1)} %get-tuple-element.26.part_ref, s32[12]{0:T(128)S(1)} %get-tuple-element.27.count_ref, ...), custom_call_target="tpu_custom_call" | custom-call | flops 5000000000 | bytes 8000000 | tf_op jit(solution)/shard_map/pallas_call | solution.py:288
  42.5 0.9 %collective-permute-done.14.refs_4_ = bf16[512,384]{1,0:T(8,128)(2,1)S(1)} collective-permute-done((bf16[512,384]{1,0:T(8,128)(2,1)S(1)}, bf16[512,384]{1,0:T(8,128)(2,1)S(1)}, u32[]{:S(2)}, u32[]{:S(2)}) %collective-permute-start.14) | collective-permute-done | bytes 393248 | tf_op jit(solution)/shard_map/ppermute | solution.py:366
  43.5 1.3 %collective-permute-start.16 = (bf16[512,384]{1,0:T(8,128)(2,1)S(1)}, bf16[512,384]{1,0:T(8,128)(2,1)S(1)}, u32[]{:S(2)}, u32[]{:S(2)}) collective-permute-start(bf16[512,384]{1,0:T(8,128)(2,1)S(1)} %collective-permute-done.14.refs_4_), channel_id=1, source_target_pairs={{0,16},{1,17},{2,18},{3,19},{4,20},{5,21},{6,22},{7,23},{8,24},{9,... | collective-permute-start | bytes 1179656 | tf_op jit(solution)/shard_map/ppermute | solution.py:361
  44.7 0.5 collective-permute-start.15
  45.3 0.8 %collective-permute-done.16.refs_6_ = bf16[512,384]{1,0:T(8,128)(2,1)S(1)} collective-permute-done((bf16[512,384]{1,0:T(8,128)(2,1)S(1)}, bf16[512,384]{1,0:T(8,128)(2,1)S(1)}, u32[]{:S(2)}, u32[]{:S(2)}) %collective-permute-start.16) | collective-permute-done | bytes 393248 | tf_op jit(solution)/shard_map/ppermute | solution.py:361
  46.1 0.6 collective-permute-done.15.refs_5_
  46.7 0.0 collective-permute-done.12.refs_2_
  46.7 4.5 %shard_map.43 = (f32[8,512]{1,0:T(8,128)S(1)}, f32[8,512]{1,0:T(8,128)S(1)}, f32[16,512]{1,0:T(8,128)S(1)}) custom-call(s32[87]{0:T(128)S(1)} %get-tuple-element.25.full_ref, s32[87]{0:T(128)S(1)} %get-tuple-element.26.part_ref, s32[12]{0:T(128)S(1)} %get-tuple-element.27.count_ref, bf16[2,512,384]{2,1,0:T(8,128)(2,1)S(1)} %collective-permute-done.8.refs_0_, ...), custom_call_target="tpu_custom_call" | custom-call | flops 5000000000 | bytes 8000000 | tf_op jit(solution)/shard_map/pallas_call | solution.py:288
  51.2 0.5 collective-permute-start.17
  51.6 0.9 %collective-permute-done.17 = f32[16,512]{1,0:T(8,128)S(1)} collective-permute-done((f32[16,512]{1,0:T(8,128)S(1)}, f32[16,512]{1,0:T(8,128)S(1)}, u32[]{:S(2)}, u32[]{:S(2)}) %collective-permute-start.17) | collective-permute-done | bytes 32800 | tf_op jit(solution)/shard_map/ppermute | solution.py:361
  52.5 1.9 %collective-permute-start.18 = (f32[8,512]{1,0:T(8,128)S(1)}, f32[8,512]{1,0:T(8,128)S(1)}, u32[]{:S(2)}, u32[]{:S(2)}) collective-permute-start(f32[8,512]{1,0:T(8,128)S(1)} %slice_maximum_fusion), channel_id=1, source_target_pairs={{0,4},{1,5},{2,6},{3,7},{4,0},{5,1},{6,2},{7,3},{8,12},{9,13},{10,... | collective-permute-start | bytes 49160 | tf_op jit(solution)/shard_map/ppermute | solution.py:366
  54.4 1.9 %collective-permute-done.18 = f32[8,512]{1,0:T(8,128)S(1)} collective-permute-done((f32[8,512]{1,0:T(8,128)S(1)}, f32[8,512]{1,0:T(8,128)S(1)}, u32[]{:S(2)}, u32[]{:S(2)}) %collective-permute-start.18) | collective-permute-done | bytes 16416 | tf_op jit(solution)/shard_map/ppermute | solution.py:366
  56.3 1.0 %collective-permute-start.19 = (f32[4,512]{1,0:T(4,128)S(1)}, f32[4,512]{1,0:T(4,128)S(1)}, u32[]{:S(2)}, u32[]{:S(2)}) collective-permute-start(f32[4,512]{1,0:T(4,128)S(1)} %slice.45), channel_id=1, source_target_pairs={{0,96},{1,97},{2,98},{3,99},{4,100},{5,101},{6,102},{7,103},{8,104... | collective-permute-start | bytes 24584 | tf_op jit(solution)/shard_map/ppermute | solution.py:366
  57.3 1.6 %collective-permute-done.19 = f32[4,512]{1,0:T(4,128)S(1)} collective-permute-done((f32[4,512]{1,0:T(4,128)S(1)}, f32[4,512]{1,0:T(4,128)S(1)}, u32[]{:S(2)}, u32[]{:S(2)}) %collective-permute-start.19) | collective-permute-done | bytes 8224 | tf_op jit(solution)/shard_map/ppermute | solution.py:366
  58.9 0.7 %collective-permute-start.20 = (f32[2,512]{1,0:T(2,128)S(1)}, f32[2,512]{1,0:T(2,128)S(1)}, u32[]{:S(2)}, u32[]{:S(2)}) collective-permute-start(f32[2,512]{1,0:T(2,128)S(1)} %slice.47), channel_id=1, source_target_pairs={{0,32},{1,33},{2,34},{3,35},{4,36},{5,37},{6,38},{7,39},{8,40},{9,... | collective-permute-start | bytes 12296 | tf_op jit(solution)/shard_map/ppermute | solution.py:366
  59.7 3.0 %collective-permute-done.20 = f32[2,512]{1,0:T(2,128)S(1)} collective-permute-done((f32[2,512]{1,0:T(2,128)S(1)}, f32[2,512]{1,0:T(2,128)S(1)}, u32[]{:S(2)}, u32[]{:S(2)}) %collective-permute-start.20) | collective-permute-done | bytes 4128 | tf_op jit(solution)/shard_map/ppermute | solution.py:366
  62.7 6.3 %collective-permute-start.21 = (f32[512]{0:T(512)S(1)}, f32[512]{0:T(512)S(1)}, u32[]{:S(2)}, u32[]{:S(2)}) collective-permute-start(f32[512]{0:T(512)S(1)} %bitcast.11), channel_id=1, source_target_pairs={{0,16},{1,17},{2,18},{3,19},{4,20},{5,21},{6,22},{7,23},{8,24},{9,... | collective-permute-start | bytes 6152 | tf_op jit(solution)/shard_map/ppermute | solution.py:361
  69.0 0.8 %collective-permute-done.21 = f32[512]{0:T(512)S(1)} collective-permute-done((f32[512]{0:T(512)S(1)}, f32[512]{0:T(512)S(1)}, u32[]{:S(2)}, u32[]{:S(2)}) %collective-permute-start.21) | collective-permute-done | bytes 2080 | tf_op jit(solution)/shard_map/ppermute | solution.py:361
  69.8 0.6 maximum_maximum_fusion
  (19 shorter events, 0.1 us)
Async XLA Ops:
  0.0 9.9 %copy-start.2 = (s32[756]{0:T(1024)S(1)}, s32[756]{0:T(1024)}, u32[]{:S(2)}) copy-start(s32[756]{0:T(1024)} %constant.17.clone.table_ref) | copy-start | bytes 9076
  0.0 9.9 %copy-start.1 = (s32[256]{0:T(256)S(1)}, s32[256]{0:T(256)}, u32[]{:S(2)}) copy-start(s32[256]{0:T(256)} %cluster_ref.3) | copy-start | bytes 3076
  0.0 3.0 %collective-permute-start = (bf16[512,384]{1,0:T(8,128)(2,1)}, bf16[512,384]{1,0:T(8,128)(2,1)S(1)}, u32[]{:S(2)}, u32[]{:S(2)}) collective-permute-start(bf16[512,384]{1,0:T(8,128)(2,1)} %x_ref.1), channel_id=1, source_target_pairs={{0,16},{1,17},{2,18},{3,19},{4,20},{5,21},{6,22},{7,23},{8,24},{9,... | collective-permute-start | bytes 1179656 | tf_op jit(solution)/shard_map/ppermute | solution.py:361
  1.4 1.0 %copy-start = (bf16[512,384]{1,0:T(8,128)(2,1)S(1)}, bf16[512,384]{1,0:T(8,128)(2,1)}, u32[]{:S(2)}) copy-start(bf16[512,384]{1,0:T(8,128)(2,1)} %x_ref.1) | copy-start | bytes 1179652
  3.2 11.5 %collective-permute-start.3 = (bf16[2,512,384]{2,1,0:T(8,128)(2,1)S(1)}, bf16[2,512,384]{2,1,0:T(8,128)(2,1)S(1)}, u32[]{:S(2)}, u32[]{:S(2)}) collective-permute-start(bf16[2,512,384]{2,1,0:T(8,128)(2,1)S(1)} %shard_map.38.unit_ref.refs_3_), channel_id=1, source_target_pairs={{0,96},{1,97},{2,98},{3,99},{4,100},{5,101},{6,102},{7,103},{8,104... | collective-permute-start | bytes 2359304 | tf_op jit(solution)/shard_map/ppermute | solution.py:366
  5.0 12.1 %collective-permute-start.4 = (bf16[2,512,384]{2,1,0:T(8,128)(2,1)S(1)}, bf16[2,512,384]{2,1,0:T(8,128)(2,1)S(1)}, u32[]{:S(2)}, u32[]{:S(2)}) collective-permute-start(bf16[2,512,384]{2,1,0:T(8,128)(2,1)S(1)} %shard_map.38.unit_ref.refs_3_), channel_id=1, source_target_pairs={{0,4},{1,5},{2,6},{3,7},{4,0},{5,1},{6,2},{7,3},{8,12},{9,13},{10,... | collective-permute-start | bytes 2359304 | tf_op jit(solution)/shard_map/ppermute | solution.py:366
  7.2 12.1 %collective-permute-start.1 = (bf16[2,512,384]{2,1,0:T(8,128)(2,1)S(1)}, bf16[2,512,384]{2,1,0:T(8,128)(2,1)S(1)}, u32[]{:S(2)}, u32[]{:S(2)}) collective-permute-start(bf16[2,512,384]{2,1,0:T(8,128)(2,1)S(1)} %shard_map.38.unit_ref.refs_3_), channel_id=1, source_target_pairs={{0,32},{1,33},{2,34},{3,35},{4,36},{5,37},{6,38},{7,39},{8,40},{9,... | collective-permute-start | bytes 2359304 | tf_op jit(solution)/shard_map/ppermute | solution.py:366
  14.6 11.0 %collective-permute-start.6 = (bf16[2,512,384]{2,1,0:T(8,128)(2,1)S(1)}, bf16[2,512,384]{2,1,0:T(8,128)(2,1)S(1)}, u32[]{:S(2)}, u32[]{:S(2)}) collective-permute-start(bf16[2,512,384]{2,1,0:T(8,128)(2,1)S(1)} %collective-permute-done.3.refs_1_), channel_id=1, source_target_pairs={{0,16},{1,17},{2,18},{3,19},{4,20},{5,21},{6,22},{7,23},{8,24},{9,... | collective-permute-start | bytes 2359304 | tf_op jit(solution)/shard_map/ppermute | solution.py:361
  17.0 8.7 %collective-permute-start.7 = (bf16[2,512,384]{2,1,0:T(8,128)(2,1)S(1)}, bf16[2,512,384]{2,1,0:T(8,128)(2,1)S(1)}, u32[]{:S(2)}, u32[]{:S(2)}) collective-permute-start(bf16[2,512,384]{2,1,0:T(8,128)(2,1)S(1)} %collective-permute-done.4.refs_2_), channel_id=1, source_target_pairs={{0,16},{1,17},{2,18},{3,19},{4,20},{5,21},{6,22},{7,23},{8,24},{9,... | collective-permute-start | bytes 2359304 | tf_op jit(solution)/shard_map/ppermute | solution.py:361
  19.3 6.4 %collective-permute-start.5 = (bf16[2,512,384]{2,1,0:T(8,128)(2,1)S(1)}, bf16[2,512,384]{2,1,0:T(8,128)(2,1)S(1)}, u32[]{:S(2)}, u32[]{:S(2)}) collective-permute-start(bf16[2,512,384]{2,1,0:T(8,128)(2,1)S(1)} %collective-permute-done.1.refs_0_), channel_id=1, source_target_pairs={{0,16},{1,17},{2,18},{3,19},{4,20},{5,21},{6,22},{7,23},{8,24},{9,... | collective-permute-start | bytes 2359304 | tf_op jit(solution)/shard_map/ppermute | solution.py:361
  20.0 12.3 %collective-permute-start.11 = (bf16[2,512,384]{2,1,0:T(8,128)(2,1)S(1)}, bf16[2,512,384]{2,1,0:T(8,128)(2,1)S(1)}, u32[]{:S(2)}, u32[]{:S(2)}) collective-permute-start(bf16[2,512,384]{2,1,0:T(8,128)(2,1)S(1)} %collective-permute-done.4.refs_2_), channel_id=1, source_target_pairs={{0,32},{1,33},{2,34},{3,35},{4,36},{5,37},{6,38},{7,39},{8,40},{9,... | collective-permute-start | bytes 2359304 | tf_op jit(solution)/shard_map/ppermute | solution.py:366
  22.0 13.1 %collective-permute-start.9 = (bf16[2,512,384]{2,1,0:T(8,128)(2,1)S(1)}, bf16[2,512,384]{2,1,0:T(8,128)(2,1)S(1)}, u32[]{:S(2)}, u32[]{:S(2)}) collective-permute-start(bf16[2,512,384]{2,1,0:T(8,128)(2,1)S(1)} %collective-permute-done.3.refs_1_), channel_id=1, source_target_pairs={{0,4},{1,5},{2,6},{3,7},{4,0},{5,1},{6,2},{7,3},{8,12},{9,13},{10,... | collective-permute-start | bytes 2359304 | tf_op jit(solution)/shard_map/ppermute | solution.py:366
  25.7 10.8 %collective-permute-start.2 = (bf16[2,512,384]{2,1,0:T(8,128)(2,1)S(1)}, bf16[2,512,384]{2,1,0:T(8,128)(2,1)S(1)}, u32[]{:S(2)}, u32[]{:S(2)}) collective-permute-start(bf16[2,512,384]{2,1,0:T(8,128)(2,1)S(1)} %collective-permute-done.1.refs_0_), channel_id=1, source_target_pairs={{0,96},{1,97},{2,98},{3,99},{4,100},{5,101},{6,102},{7,103},{8,104... | collective-permute-start | bytes 2359304 | tf_op jit(solution)/shard_map/ppermute | solution.py:366
  35.1 11.6 %collective-permute-start.12 = (bf16[2,512,384]{2,1,0:T(8,128)(2,1)S(1)}, bf16[2,512,384]{2,1,0:T(8,128)(2,1)S(1)}, u32[]{:S(2)}, u32[]{:S(2)}) collective-permute-start(bf16[2,512,384]{2,1,0:T(8,128)(2,1)S(1)} %collective-permute-done.11.refs_2_), channel_id=1, source_target_pairs={{0,16},{1,17},{2,18},{3,19},{4,20},{5,21},{6,22},{7,23},{8,24},{9,... | collective-permute-start | bytes 2359304 | tf_op jit(solution)/shard_map/ppermute | solution.py:361
  35.1 11.6 %collective-permute-start.10 = (bf16[2,512,384]{2,1,0:T(8,128)(2,1)S(1)}, bf16[2,512,384]{2,1,0:T(8,128)(2,1)S(1)}, u32[]{:S(2)}, u32[]{:S(2)}) collective-permute-start(bf16[2,512,384]{2,1,0:T(8,128)(2,1)S(1)} %collective-permute-done.9.refs_1_), channel_id=1, source_target_pairs={{0,16},{1,17},{2,18},{3,19},{4,20},{5,21},{6,22},{7,23},{8,24},{9,... | collective-permute-start | bytes 2359304 | tf_op jit(solution)/shard_map/ppermute | solution.py:361
  36.5 6.9 %collective-permute-start.14 = (bf16[512,384]{1,0:T(8,128)(2,1)S(1)}, bf16[512,384]{1,0:T(8,128)(2,1)S(1)}, u32[]{:S(2)}, u32[]{:S(2)}) collective-permute-start(bf16[512,384]{1,0:T(8,128)(2,1)S(1)} %slice_bitcast_fusion), channel_id=1, source_target_pairs={{0,96},{1,97},{2,98},{3,99},{4,100},{5,101},{6,102},{7,103},{8,104... | collective-permute-start | bytes 1179656 | tf_op jit(solution)/shard_map/ppermute | solution.py:366
  36.5 8.2 %collective-permute-start.13 = (bf16[512,384]{1,0:T(8,128)(2,1)S(1)}, bf16[512,384]{1,0:T(8,128)(2,1)S(1)}, u32[]{:S(2)}, u32[]{:S(2)}) collective-permute-start(bf16[512,384]{1,0:T(8,128)(2,1)S(1)} %slice_bitcast_fusion.1), channel_id=1, source_target_pairs={{0,32},{1,33},{2,34},{3,35},{4,36},{5,37},{6,38},{7,39},{8,40},{9,... | collective-permute-start | bytes 1179656 | tf_op jit(solution)/shard_map/ppermute | solution.py:366
  37.6 9.1 %collective-permute-start.8 = (bf16[2,512,384]{2,1,0:T(8,128)(2,1)S(1)}, bf16[2,512,384]{2,1,0:T(8,128)(2,1)S(1)}, u32[]{:S(2)}, u32[]{:S(2)}) collective-permute-start(bf16[2,512,384]{2,1,0:T(8,128)(2,1)S(1)} %collective-permute-done.2.refs_0_), channel_id=1, source_target_pairs={{0,16},{1,17},{2,18},{3,19},{4,20},{5,21},{6,22},{7,23},{8,24},{9,... | collective-permute-start | bytes 2359304 | tf_op jit(solution)/shard_map/ppermute | solution.py:361
  43.5 2.6 %collective-permute-start.16 = (bf16[512,384]{1,0:T(8,128)(2,1)S(1)}, bf16[512,384]{1,0:T(8,128)(2,1)S(1)}, u32[]{:S(2)}, u32[]{:S(2)}) collective-permute-start(bf16[512,384]{1,0:T(8,128)(2,1)S(1)} %collective-permute-done.14.refs_4_), channel_id=1, source_target_pairs={{0,16},{1,17},{2,18},{3,19},{4,20},{5,21},{6,22},{7,23},{8,24},{9,... | collective-permute-start | bytes 1179656 | tf_op jit(solution)/shard_map/ppermute | solution.py:361
  44.7 1.9 %collective-permute-start.15 = (bf16[512,384]{1,0:T(8,128)(2,1)S(1)}, bf16[512,384]{1,0:T(8,128)(2,1)S(1)}, u32[]{:S(2)}, u32[]{:S(2)}) collective-permute-start(bf16[512,384]{1,0:T(8,128)(2,1)S(1)} %collective-permute-done.13.refs_3_), channel_id=1, source_target_pairs={{0,16},{1,17},{2,18},{3,19},{4,20},{5,21},{6,22},{7,23},{8,24},{9,... | collective-permute-start | bytes 1179656 | tf_op jit(solution)/shard_map/ppermute | solution.py:361
  51.2 1.3 %collective-permute-start.17 = (f32[16,512]{1,0:T(8,128)S(1)}, f32[16,512]{1,0:T(8,128)S(1)}, u32[]{:S(2)}, u32[]{:S(2)}) collective-permute-start(f32[16,512]{1,0:T(8,128)S(1)} %get-tuple-element.43), channel_id=1, source_target_pairs={{0,16},{1,17},{2,18},{3,19},{4,20},{5,21},{6,22},{7,23},{8,24},{9,... | collective-permute-start | bytes 98312 | tf_op jit(solution)/shard_map/ppermute | solution.py:361
  52.5 3.8 %collective-permute-start.18 = (f32[8,512]{1,0:T(8,128)S(1)}, f32[8,512]{1,0:T(8,128)S(1)}, u32[]{:S(2)}, u32[]{:S(2)}) collective-permute-start(f32[8,512]{1,0:T(8,128)S(1)} %slice_maximum_fusion), channel_id=1, source_target_pairs={{0,4},{1,5},{2,6},{3,7},{4,0},{5,1},{6,2},{7,3},{8,12},{9,13},{10,... | collective-permute-start | bytes 49160 | tf_op jit(solution)/shard_map/ppermute | solution.py:366
  56.3 2.6 %collective-permute-start.19 = (f32[4,512]{1,0:T(4,128)S(1)}, f32[4,512]{1,0:T(4,128)S(1)}, u32[]{:S(2)}, u32[]{:S(2)}) collective-permute-start(f32[4,512]{1,0:T(4,128)S(1)} %slice.45), channel_id=1, source_target_pairs={{0,96},{1,97},{2,98},{3,99},{4,100},{5,101},{6,102},{7,103},{8,104... | collective-permute-start | bytes 24584 | tf_op jit(solution)/shard_map/ppermute | solution.py:366
  58.9 3.7 %collective-permute-start.20 = (f32[2,512]{1,0:T(2,128)S(1)}, f32[2,512]{1,0:T(2,128)S(1)}, u32[]{:S(2)}, u32[]{:S(2)}) collective-permute-start(f32[2,512]{1,0:T(2,128)S(1)} %slice.47), channel_id=1, source_target_pairs={{0,32},{1,33},{2,34},{3,35},{4,36},{5,37},{6,38},{7,39},{8,40},{9,... | collective-permute-start | bytes 12296 | tf_op jit(solution)/shard_map/ppermute | solution.py:366
  62.7 7.1 %collective-permute-start.21 = (f32[512]{0:T(512)S(1)}, f32[512]{0:T(512)S(1)}, u32[]{:S(2)}, u32[]{:S(2)}) collective-permute-start(f32[512]{0:T(512)S(1)} %bitcast.11), channel_id=1, source_target_pairs={{0,16},{1,17},{2,18},{3,19},{4,20},{5,21},{6,22},{7,23},{8,24},{9,... | collective-permute-start | bytes 6152 | tf_op jit(solution)/shard_map/ppermute | solution.py:361

commit v5 on v4

--- a/solution.py
+++ b/solution.py
@@ -21,10 +21,13 @@
 SENDS = ((0, 0), (0, 1), (0, 2), (1, 1), (2, 2), (3, 0))
 HALVES = ((5, 0), (6, 1))
 PHASES = (
-    ((1, 2, 3), 0, 4, 4),
-    ((4, 5, 6), 0, 4, 4),
+    ((1, 2, 3), 0, 1, 4),
+    ((4, 5, 6), 0, 1, 4),
+    ((4, 5, 6), 1, 4, 4),
+    ((1, 2, 3), 1, 4, 4),
     ((4, 5, 6), 4, 7, 4),
-    ((7,), 0, 4, 4),
+    ((7,), 0, 1, 1),
+    ((7,), 1, 4, 4),
     ((7,), 4, 7, 4),
     ((7,), 7, 8, 1),
 )
@@ -261,26 +264,37 @@
         buf[2 * n : 2 * n + 2] = ref[...]
 
 
-def early_kernel(full_ref, part_ref, count_ref, *refs):
-    mine, theirs, (rows_out, col_ref, b_buf, a_buf, row_ref) = refs[:3], refs[3:7], refs[7:]
+def early_kernel(*refs):
+    plan, mine, (unit, pack_ref, row_ref, col_ref) = refs[:3], refs[3:6], refs[6:]
     clear(row_ref, col_ref)
-    put(a_buf, mine)
-    put(b_buf, theirs)
-    score_lists(0, full_ref, part_ref, count_ref, a_buf, b_buf, row_ref, col_ref)
-    for slot in (1, 2, 3):
-        put_rows(rows_out, 2 * slot - 2, row_ref, 2 * slot - 2)
-
-
-def middle_kernel(full_ref, part_ref, count_ref, *refs):
-    mine, (b_buf, col_in, row_ref, col_ref, a_buf) = refs[:3], refs[3:]
-    clear(row_ref)
-    col_ref[...] = col_in[...]
-    put(a_buf, mine)
-    score_lists(1, full_ref, part_ref, count_ref, a_buf, b_buf, row_ref, col_ref)
-
-
-ROWS = jax.ShapeDtypeStruct((6, SHARD, 128), jnp.float32)
-COLS = jax.ShapeDtypeStruct((8, 8, SHARD), jnp.float32)
+    put(pack_ref, mine)
+    score_lists(0, *plan, pack_ref, unit, row_ref, col_ref)
+
+
+def pack_kernel(a_ref, b_ref, c_ref, out_ref):
+    put(out_ref, (a_ref, b_ref, c_ref))
+
+
+def middle_kernel(*refs):
+    plan, (a_low, a_mid, b_own, b_low, row_in, col_in), outs = refs[:3], refs[3:9], refs[9:]
+    rows_out, row_mid, col_own, col_low, row_low = outs
+    clear(row_mid, col_low)
+    row_low[...] = row_in[...]
+    col_own[...] = col_in[...]
+    score_lists(1, *plan, a_mid, b_own, row_mid, col_own)
+    score_lists(2, *plan, a_mid, b_low, row_mid, col_low)
+    score_lists(3, *plan, a_low, b_low, row_low, col_low)
+    for n in range(0, 6, 2):
+        put_rows(rows_out, n, row_low, n)
+
+
+def f32(*shape):
+    return jax.ShapeDtypeStruct(shape, jnp.float32)
+
+
+ROWS = f32(6, SHARD, 128)
+COLS = f32(6, 8, SHARD)
+COLS2 = f32(2, 8, SHARD)
 PACK = jax.ShapeDtypeStruct((6, SHARD, D), jnp.bfloat16)
 
 
@@ -296,36 +310,36 @@
     )(*operands)
 
 
-def early_call(plan, mine, theirs):
-    buf = jax.ShapeDtypeStruct((8, SHARD, D), jnp.bfloat16)
-    outs = (jax.ShapeDtypeStruct((6, SHARD), jnp.float32), COLS, buf)
-    return kernel_call(early_kernel, [*plan, *mine, *theirs], outs, [PACK, ROWS], 4000000000)
+def early_call(plan, *operands):
+    return kernel_call(early_kernel, [*plan, *operands], (PACK, ROWS, COLS2), [], 3000000000)
 
 
 def middle_call(plan, *operands):
-    return kernel_call(middle_kernel, [*plan, *operands], (ROWS, COLS, PACK), [], 5000000000)
+    outs = (f32(6, SHARD), ROWS, COLS2, COLS)
+    return kernel_call(middle_kernel, [*plan, *operands], outs, [ROWS], 5000000000)
 
 
 KEPT = (0, 1, 2, 4)
 SENT = (3, 6, 5, 7)
 
 
-def last_kernel(full_ref, part_ref, count_ref, *refs):
-    plan = (full_ref, part_ref, count_ref)
-    theirs, mine7, theirs7, refs = refs[:3], refs[3:5], refs[5:7], refs[7:]
-    a_mid, b_low, col_low_in, rows0, row_in, keep_ref, send_ref, other_ref, *refs = refs
-    b_mid, a_last, b_last, row_mid, row_last, col_low, col_mid, col_last = refs
+def last_kernel(*refs):
+    plan, mine, theirs, refs = refs[:3], refs[3:5], refs[5:7], refs[7:]
+    (a_mid, b_own, b_low, b_mid, rows0, row_in, own_in, low_in), refs = refs[:8], refs[8:]
+    keep_ref, send_ref, other_ref, *refs = refs
+    a_last, b_last, row_mid, row_last, col_own, col_low, col_mid, col_last = refs
     clear(row_last, col_mid, col_last)
     row_mid[...] = row_in[...]
-    col_low[...] = col_low_in[...]
-    put(b_mid, theirs)
+    col_own[...] = own_in[...]
+    col_low[...] = low_in[...]
     for half in range(2):
-        a_last[half] = mine7[half][...]
-        b_last[half] = theirs7[half][...]
-    score_lists(2, *plan, a_mid, b_mid, row_mid, col_mid)
-    score_lists(3, *plan, a_last, b_low, row_last, col_low)
-    score_lists(4, *plan, a_last, b_mid, row_last, col_mid)
-    score_lists(5, *plan, a_last, b_last, row_last, col_last)
+        a_last[half] = mine[half][...]
+        b_last[half] = theirs[half][...]
+    score_lists(4, *plan, a_mid, b_mid, row_mid, col_mid)
+    score_lists(5, *plan, a_last, b_own, row_last, col_own)
+    score_lists(6, *plan, a_last, b_low, row_last, col_low)
+    score_lists(7, *plan, a_last, b_mid, row_last, col_mid)
+    score_lists(8, *plan, a_last, b_last, row_last, col_last)
     keep_ref[0:2] = jnp.full((2, SHARD), -2.0, jnp.float32)
     for out_ref, slots in ((keep_ref, KEPT), (send_ref, SENT)):
         for place, slot in enumerate(slots):
@@ -338,22 +352,15 @@
     for place, slot in enumerate(KEPT + SENT):
         for half in range(2):
             at = 2 * place + half
-            if slot == 7:
-                down = col_last[half]
-            elif slot > 3:
-                down = col_mid[2 * slot - 8 + half]
-            else:
-                down = col_low[2 * slot + half]
+            col_ref, n = ((col_own, 0), (col_low, 2), (col_mid, 8), (col_last, 14))[(slot + 2) // 3]
+            down = col_ref[2 * slot + half - n]
             other_ref[at : at + 1, :] = jnp.max(down, axis=0, keepdims=True)
 
 
 def last_call(plan, *operands):
-    def f32(*shape):
-        return jax.ShapeDtypeStruct(shape, jnp.float32)
-
     two = jax.ShapeDtypeStruct((2, SHARD, D), jnp.bfloat16)
     outs = (f32(8, SHARD), f32(8, SHARD), f32(16, SHARD))
-    scratch = [PACK, two, two, ROWS, f32(2, SHARD, 128), COLS, f32(6, 8, SHARD), f32(2, 8, SHARD)]
+    scratch = [two, two, ROWS, f32(2, SHARD, 128), COLS2, COLS, COLS, COLS2]
     return kernel_call(last_kernel, [*plan, *operands], outs, scratch, 5000000000)
 
 
@@ -374,25 +381,28 @@
     here = (lax.axis_index("row") * 16 + lax.axis_index("col")).astype(jnp.int32).reshape(1)
     unit = unit_call(here, embeddings, swap(embeddings))
     plan = plan_call(here, block_cluster, jnp.asarray(TABLE.reshape(-1)))
-    mine, theirs = [unit], [unit]
+    mine = [unit]
 
     def step(slots):
         return [exchange(mine[SENDS[k - 1][0]], SENDS[k - 1][1]) for k in slots]
 
     own = own_call(here, block_cluster, unit)
     mine.extend(after(x, plan[2], own) for x in step((1, 2, 3)))
-    theirs.extend(swap(x) for x in mine[1:4])
-    rows0, cols, b_low = early_call(plan, mine[1:4], theirs)
-    mine.extend(after(x, cols) for x in step((4, 5, 6)))
+    a_low, rows0, col_own = early_call(plan, *mine[1:4], unit)
+    b_low = swap(a_low)
+    mine.extend(after(x, a_low) for x in step((4, 5, 6)))
     halves = [
         exchange(mine[source][half], generator) for half, (source, generator) in enumerate(HALVES)
     ]
-    theirs.extend(swap(x) for x in mine[4:7])
-    rows1, cols, a_mid = middle_call(plan, *mine[4:7], b_low, cols)
-    halves = [after(x, cols) for x in halves]
+    a_mid = kernel_call(pack_kernel, mine[4:7], PACK, [], 1000000000, 0)
+    b_mid = swap(a_mid)
+    rows0, rows1, col_own, col_low = middle_call(
+        plan, a_low, a_mid, unit, b_low, rows0, col_own
+    )
+    halves = [after(x, col_low) for x in halves]
     swapped = [swap(x) for x in halves]
     keep, send, other = last_call(
-        plan, *theirs[4:7], *halves, *swapped, a_mid, b_low, cols, rows0, rows1
+        plan, *halves, *swapped, a_mid, unit, b_low, b_mid, rows0, rows1, col_own, col_low
     )
     other = swap(other)
     keep = jnp.maximum(keep, other[:8])

time: 71.5 us -> 74.7 us (1.045); the launches traced: 70.4 us -> 74.5 us
  Pallas kernels: 16.9 us -> 26.8 us
  starting transfers between devices: 32 us -> 25.7 us
    pallas_call x3 -> x4, Pallas kernels: 12.2 us -> 22.2 us  [kernel_call(): pl.pallas_call(kernel, out_shape=outs, in_specs=[spec(SMEM)] * smem + [sp...]
    ppermute x11 -> x7, starting transfers between devices: 14.9 us -> 6.31 us  [swap(): return lax.ppermute(x, ('row', 'col'), [(s, s ^ CORE) for s in range(128)])]
    ppermute x11, starting transfers between devices: 17.1 us -> 19.4 us  [exchange(): return lax.ppermute(x, ('row', 'col'), pairs)]
    ppermute x11 -> x7, waiting for transfers between devices: 3.48 us -> 3.87 us  [swap(): return lax.ppermute(x, ('row', 'col'), [(s, s ^ CORE) for s in range(128)])]
  transfers between devices with their start and end apart: 22 -> 18, of which waited for: 15 -> 13; matrix products, arithmetic and copies ran while one was open for 0% -> 0% of each run, Pallas kernels for 17% -> 25%
where the time goes in v5:
time: 74.7 us; the launch traced here: 74.5 us
  Pallas kernels  26.8 us (36%)
  starting transfers between devices  25.7 us (34%)
  waiting for transfers between devices  20.2 us (27%)
  local copies, waits for them, and re-layouts  1.1 us (1%)
    pallas_call x4, Pallas kernels, kernel_call(): pl.pallas_call(kernel, out_shape=outs, in_specs=[spec(SMEM)] * smem + [sp...  22.2 us
    ppermute x11, starting transfers between devices, exchange(): return lax.ppermute(x, ('row', 'col'), pairs)  19.4 us
    ppermute x11, waiting for transfers between devices, exchange(): return lax.ppermute(x, ('row', 'col'), pairs)  16.3 us
    ppermute x7, starting transfers between devices, swap(): return lax.ppermute(x, ('row', 'col'), [(s, s ^ CORE) for s in range(128)])  6.31 us
    ppermute x7, waiting for transfers between devices, swap(): return lax.ppermute(x, ('row', 'col'), [(s, s ^ CORE) for s in range(128)])  3.87 us
    pallas_call x1, Pallas kernels, plan_call(): pl.pallas_call(plan_kernel, out_shape=(lists, lists, jax.ShapeDtypeStruct...  3.07 us
  transfers between devices with their start and end apart: 18, of which 13 were waited for; matrix products, arithmetic and copies ran while one was open for 0% of the time, Pallas kernels for 25%

profile of v5, /device:TPU:1, one launch (start us, length us, event | category | flops | bytes accessed | tf_op | source)
XLA Modules:
  0.0 74.5 jit_solution(15727904251639231232)
XLA Ops:
  0.0 1.4 %collective-permute-start = (bf16[512,384]{1,0:T(8,128)(2,1)}, bf16[512,384]{1,0:T(8,128)(2,1)S(1)}, u32[]{:S(2)}, u32[]{:S(2)}) collective-permute-start(bf16[512,384]{1,0:T(8,128)(2,1)} %x_ref.1), channel_id=1, source_target_pairs={{0,16},{1,17},{2,18},{3,19},{4,20},{5,21},{6,22},{7,23},{8,24},{9,... | collective-permute-start | bytes 1179656 | tf_op jit(solution)/shard_map/ppermute | solution.py:368
  1.4 1.0 %copy-done = bf16[512,384]{1,0:T(8,128)(2,1)S(1)} copy-done((bf16[512,384]{1,0:T(8,128)(2,1)S(1)}, bf16[512,384]{1,0:T(8,128)(2,1)}, u32[]{:S(2)}) %copy-start) | copy-done | bytes 393240
  2.4 0.2 shard_map.37.own_ref
  2.6 0.4 collective-permute-done.other_ref
  3.0 0.2 shard_map.38.unit_ref.refs_6_.refs_5_.refs_8_
  3.2 1.8 %collective-permute-start.1 = (bf16[2,512,384]{2,1,0:T(8,128)(2,1)S(1)}, bf16[2,512,384]{2,1,0:T(8,128)(2,1)S(1)}, u32[]{:S(2)}, u32[]{:S(2)}) collective-permute-start(bf16[2,512,384]{2,1,0:T(8,128)(2,1)S(1)} %shard_map.38.unit_ref.refs_6_.refs_5_.refs_8_), channel_id=1, source_target_pairs={{0,96},{1,97},{2,98},{3,99},{4,100},{5,101},{6,102},{7,103},{8,104... | collective-permute-start | bytes 2359304 | tf_op jit(solution)/shard_map/ppermute | solution.py:373
  5.0 2.7 %collective-permute-start.3 = (bf16[2,512,384]{2,1,0:T(8,128)(2,1)S(1)}, bf16[2,512,384]{2,1,0:T(8,128)(2,1)S(1)}, u32[]{:S(2)}, u32[]{:S(2)}) collective-permute-start(bf16[2,512,384]{2,1,0:T(8,128)(2,1)S(1)} %shard_map.38.unit_ref.refs_6_.refs_5_.refs_8_), channel_id=1, source_target_pairs={{0,32},{1,33},{2,34},{3,35},{4,36},{5,37},{6,38},{7,39},{8,40},{9,... | collective-permute-start | bytes 2359304 | tf_op jit(solution)/shard_map/ppermute | solution.py:373
  7.7 2.2 %collective-permute-start.4 = (bf16[2,512,384]{2,1,0:T(8,128)(2,1)S(1)}, bf16[2,512,384]{2,1,0:T(8,128)(2,1)S(1)}, u32[]{:S(2)}, u32[]{:S(2)}) collective-permute-start(bf16[2,512,384]{2,1,0:T(8,128)(2,1)S(1)} %shard_map.38.unit_ref.refs_6_.refs_5_.refs_8_), channel_id=1, source_target_pairs={{0,4},{1,5},{2,6},{3,7},{4,0},{5,1},{6,2},{7,3},{8,12},{9,13},{10,... | collective-permute-start | bytes 2359304 | tf_op jit(solution)/shard_map/ppermute | solution.py:373
  9.9 0.0 copy-done.2
  9.9 0.0 copy-done.1
  9.9 3.1 %shard_map.40 = (s32[99]{0:T(128)S(1)}, s32[99]{0:T(128)S(1)}, s32[18]{0:T(128)S(1)}) custom-call(s32[1]{0:T(128)} %bitcast.here_ref, s32[256]{0:T(256)S(1)} %copy-done.1, s32[756]{0:T(1024)S(1)} %copy-done.2), custom_call_target="tpu_custom_call" | custom-call | flops 3000000000 | bytes 10000 | tf_op jit(solution)/shard_map/pallas_call | solution.py:185
  13.0 1.3 %shard_map.39 = f32[1,512]{1,0:T(1,128)S(1)} custom-call(s32[1]{0:T(128)} %bitcast.here_ref, s32[256]{0:T(256)S(1)} %copy-done.1, bf16[2,512,384]{2,1,0:T(8,128)(2,1)S(1)} %shard_map.38.unit_ref.refs_6_.refs_5_.refs_8_), custom_call_target="tpu_custom_call" | custom-call | flops 1000000000 | bytes 1000000 | tf_op jit(solution)/shard_map/pallas_call | solution.py:196
  14.3 0.3 collective-permute-done.1.refs_4_
  14.6 3.6 %collective-permute-start.2 = (bf16[2,512,384]{2,1,0:T(8,128)(2,1)S(1)}, bf16[2,512,384]{2,1,0:T(8,128)(2,1)S(1)}, u32[]{:S(2)}, u32[]{:S(2)}) collective-permute-start(bf16[2,512,384]{2,1,0:T(8,128)(2,1)S(1)} %collective-permute-done.1.refs_4_), channel_id=1, source_target_pairs={{0,4},{1,5},{2,6},{3,7},{4,0},{5,1},{6,2},{7,3},{8,12},{9,13},{10,... | collective-permute-start | bytes 2359304 | tf_op jit(solution)/shard_map/ppermute | solution.py:373
  18.2 0.0 collective-permute-done.3.refs_3_
  18.2 1.5 %collective-permute-done.4.refs_5_ = bf16[2,512,384]{2,1,0:T(8,128)(2,1)S(1)} collective-permute-done((bf16[2,512,384]{2,1,0:T(8,128)(2,1)S(1)}, bf16[2,512,384]{2,1,0:T(8,128)(2,1)S(1)}, u32[]{:S(2)}, u32[]{:S(2)}) %collective-permute-start.4) | collective-permute-done | bytes 786464 | tf_op jit(solution)/shard_map/ppermute | solution.py:373
  19.7 0.3 collective-permute-start.6
  20.1 1.0 %collective-permute-start.7 = (bf16[2,512,384]{2,1,0:T(8,128)(2,1)S(1)}, bf16[2,512,384]{2,1,0:T(8,128)(2,1)S(1)}, u32[]{:S(2)}, u32[]{:S(2)}) collective-permute-start(bf16[2,512,384]{2,1,0:T(8,128)(2,1)S(1)} %collective-permute-done.4.refs_5_), channel_id=1, source_target_pairs={{0,32},{1,33},{2,34},{3,35},{4,36},{5,37},{6,38},{7,39},{8,40},{9,... | collective-permute-start | bytes 2359304 | tf_op jit(solution)/shard_map/ppermute | solution.py:373
  21.0 3.4 %shard_map.41 = (bf16[6,512,384]{2,1,0:T(8,128)(2,1)S(1)}, f32[6,512,128]{2,1,0:T(8,128)S(1)}, f32[2,8,512]{2,1,0:T(8,128)S(1)}) custom-call(s32[99]{0:T(128)S(1)} %get-tuple-element.26.refs_0_, s32[99]{0:T(128)S(1)} %get-tuple-element.27.refs_1_, s32[18]{0:T(128)S(1)} %get-tuple-element.28.refs_2_, bf16[2,512,384]{2,1,0:T(8,128)(2,1)S(1)} %collective-permute-done.3.refs_3_, ...), custom_call_target="tpu_custom_call" | custom-call | flops 3000000000 | bytes 8000000 | tf_op jit(solution)/shard_map/pallas_call | solution.py:302
  24.5 0.1 collective-permute-start.8
  24.6 3.9 %collective-permute-done.2.b_ref = bf16[2,512,384]{2,1,0:T(8,128)(2,1)S(1)} collective-permute-done((bf16[2,512,384]{2,1,0:T(8,128)(2,1)S(1)}, bf16[2,512,384]{2,1,0:T(8,128)(2,1)S(1)}, u32[]{:S(2)}, u32[]{:S(2)}) %collective-permute-start.2) | collective-permute-done | bytes 786464 | tf_op jit(solution)/shard_map/ppermute | solution.py:373
  28.5 2.4 %collective-permute-done.6.a_ref = bf16[2,512,384]{2,1,0:T(8,128)(2,1)S(1)} collective-permute-done((bf16[2,512,384]{2,1,0:T(8,128)(2,1)S(1)}, bf16[2,512,384]{2,1,0:T(8,128)(2,1)S(1)}, u32[]{:S(2)}, u32[]{:S(2)}) %collective-permute-start.6) | collective-permute-done | bytes 786464 | tf_op jit(solution)/shard_map/ppermute | solution.py:373
  30.9 1.2 %collective-permute-done.7.c_ref = bf16[2,512,384]{2,1,0:T(8,128)(2,1)S(1)} collective-permute-done((bf16[2,512,384]{2,1,0:T(8,128)(2,1)S(1)}, bf16[2,512,384]{2,1,0:T(8,128)(2,1)S(1)}, u32[]{:S(2)}, u32[]{:S(2)}) %collective-permute-start.7) | collective-permute-done | bytes 786464 | tf_op jit(solution)/shard_map/ppermute | solution.py:373
  32.1 0.2 shard_map.42.refs_4_.refs_7_
  32.3 1.2 %collective-permute-start.12 = (bf16[6,512,384]{2,1,0:T(8,128)(2,1)S(1)}, bf16[6,512,384]{2,1,0:T(8,128)(2,1)S(1)}, u32[]{:S(2)}, u32[]{:S(2)}) collective-permute-start(bf16[6,512,384]{2,1,0:T(8,128)(2,1)S(1)} %shard_map.42.refs_4_.refs_7_), channel_id=1, source_target_pairs={{0,16},{1,17},{2,18},{3,19},{4,20},{5,21},{6,22},{7,23},{8,24},{9,... | collective-permute-start | bytes 7077896 | tf_op jit(solution)/shard_map/ppermute | solution.py:368
  33.6 2.0 %collective-permute-start.5 = (bf16[512,384]{1,0:T(8,128)(2,1)S(1)}, bf16[512,384]{1,0:T(8,128)(2,1)S(1)}, u32[]{:S(2)}, u32[]{:S(2)}) collective-permute-start(bf16[512,384]{1,0:T(8,128)(2,1)S(1)} %slice_bitcast_fusion.1), channel_id=1, source_target_pairs={{0,32},{1,33},{2,34},{3,35},{4,36},{5,37},{6,38},{7,39},{8,40},{9,... | collective-permute-start | bytes 1179656 | tf_op jit(solution)/shard_map/ppermute | solution.py:373
  35.6 1.7 %collective-permute-start.9 = (bf16[512,384]{1,0:T(8,128)(2,1)S(1)}, bf16[512,384]{1,0:T(8,128)(2,1)S(1)}, u32[]{:S(2)}, u32[]{:S(2)}) collective-permute-start(bf16[512,384]{1,0:T(8,128)(2,1)S(1)} %slice_bitcast_fusion), channel_id=1, source_target_pairs={{0,96},{1,97},{2,98},{3,99},{4,100},{5,101},{6,102},{7,103},{8,104... | collective-permute-start | bytes 1179656 | tf_op jit(solution)/shard_map/ppermute | solution.py:373
  37.3 0.0 collective-permute-done.8.refs_6_.refs_9_
  37.3 10.3 %shard_map.43 = (f32[6,512]{1,0:T(8,128)S(1)}, f32[6,512,128]{2,1,0:T(8,128)S(1)}, f32[2,8,512]{2,1,0:T(8,128)S(1)}, f32[6,8,512]{2,1,0:T(8,128)S(1)}) custom-call(s32[99]{0:T(128)S(1)} %get-tuple-element.26.refs_0_, s32[99]{0:T(128)S(1)} %get-tuple-element.27.refs_1_, s32[18]{0:T(128)S(1)} %get-tuple-element.28.refs_2_, ...), custom_call_target="tpu_custom_call" | custom-call | flops 5000000000 | bytes 8000000 | tf_op jit(solution)/shard_map/pallas_call | solution.py:302
  47.6 0.0 collective-permute-done.5.refs_3_
  47.7 0.0 collective-permute-done.9.refs_4_
  47.7 0.3 collective-permute-start.10
  47.9 0.5 collective-permute-start.11
  48.4 1.2 %collective-permute-done.10.refs_5_ = bf16[512,384]{1,0:T(8,128)(2,1)S(1)} collective-permute-done((bf16[512,384]{1,0:T(8,128)(2,1)S(1)}, bf16[512,384]{1,0:T(8,128)(2,1)S(1)}, u32[]{:S(2)}, u32[]{:S(2)}) %collective-permute-start.10) | collective-permute-done | bytes 393248 | tf_op jit(solution)/shard_map/ppermute | solution.py:368
  49.7 0.6 collective-permute-done.11.refs_6_
  50.2 0.0 collective-permute-done.12.refs_10_
  50.2 8.2 %shard_map.44 = (f32[8,512]{1,0:T(8,128)S(1)}, f32[8,512]{1,0:T(8,128)S(1)}, f32[16,512]{1,0:T(8,128)S(1)}) custom-call(s32[99]{0:T(128)S(1)} %get-tuple-element.26.refs_0_, s32[99]{0:T(128)S(1)} %get-tuple-element.27.refs_1_, s32[18]{0:T(128)S(1)} %get-tuple-element.28.refs_2_, bf16[512,384]{1,0:T(8,128)(2,1)S(1)} %collective-permute-done.5.refs_3_, ...), custom_call_target="tpu_custom_call" | custom-call | flops 5000000000 | bytes 8000000 | tf_op jit(solution)/shard_map/pallas_call | solution.py:302
  58.4 1.0 %collective-permute-start.13 = (f32[16,512]{1,0:T(8,128)S(1)}, f32[16,512]{1,0:T(8,128)S(1)}, u32[]{:S(2)}, u32[]{:S(2)}) collective-permute-start(f32[16,512]{1,0:T(8,128)S(1)} %get-tuple-element.45), channel_id=1, source_target_pairs={{0,16},{1,17},{2,18},{3,19},{4,20},{5,21},{6,22},{7,23},{8,24},{9,... | collective-permute-start | bytes 98312 | tf_op jit(solution)/shard_map/ppermute | solution.py:368
  59.4 0.9 %collective-permute-done.13 = f32[16,512]{1,0:T(8,128)S(1)} collective-permute-done((f32[16,512]{1,0:T(8,128)S(1)}, f32[16,512]{1,0:T(8,128)S(1)}, u32[]{:S(2)}, u32[]{:S(2)}) %collective-permute-start.13) | collective-permute-done | bytes 32800 | tf_op jit(solution)/shard_map/ppermute | solution.py:368
  60.3 3.5 %collective-permute-start.14 = (f32[8,512]{1,0:T(8,128)S(1)}, f32[8,512]{1,0:T(8,128)S(1)}, u32[]{:S(2)}, u32[]{:S(2)}) collective-permute-start(f32[8,512]{1,0:T(8,128)S(1)} %slice_maximum_fusion), channel_id=1, source_target_pairs={{0,4},{1,5},{2,6},{3,7},{4,0},{5,1},{6,2},{7,3},{8,12},{9,13},{10,... | collective-permute-start | bytes 49160 | tf_op jit(solution)/shard_map/ppermute | solution.py:373
  63.9 1.1 %collective-permute-done.14 = f32[8,512]{1,0:T(8,128)S(1)} collective-permute-done((f32[8,512]{1,0:T(8,128)S(1)}, f32[8,512]{1,0:T(8,128)S(1)}, u32[]{:S(2)}, u32[]{:S(2)}) %collective-permute-start.14) | collective-permute-done | bytes 16416 | tf_op jit(solution)/shard_map/ppermute | solution.py:373
  65.0 0.1 collective-permute-start.15
  65.1 2.5 %collective-permute-done.15 = f32[4,512]{1,0:T(4,128)S(1)} collective-permute-done((f32[4,512]{1,0:T(4,128)S(1)}, f32[4,512]{1,0:T(4,128)S(1)}, u32[]{:S(2)}, u32[]{:S(2)}) %collective-permute-start.15) | collective-permute-done | bytes 8224 | tf_op jit(solution)/shard_map/ppermute | solution.py:373
  67.6 0.4 collective-permute-start.16
  68.0 3.3 %collective-permute-done.16 = f32[2,512]{1,0:T(2,128)S(1)} collective-permute-done((f32[2,512]{1,0:T(2,128)S(1)}, f32[2,512]{1,0:T(2,128)S(1)}, u32[]{:S(2)}, u32[]{:S(2)}) %collective-permute-start.16) | collective-permute-done | bytes 4128 | tf_op jit(solution)/shard_map/ppermute | solution.py:373
  71.4 1.8 %collective-permute-start.17 = (f32[512]{0:T(512)S(1)}, f32[512]{0:T(512)S(1)}, u32[]{:S(2)}, u32[]{:S(2)}) collective-permute-start(f32[512]{0:T(512)S(1)} %bitcast.11), channel_id=1, source_target_pairs={{0,16},{1,17},{2,18},{3,19},{4,20},{5,21},{6,22},{7,23},{8,24},{9,... | collective-permute-start | bytes 6152 | tf_op jit(solution)/shard_map/ppermute | solution.py:368
  73.1 0.8 %collective-permute-done.17 = f32[512]{0:T(512)S(1)} collective-permute-done((f32[512]{0:T(512)S(1)}, f32[512]{0:T(512)S(1)}, u32[]{:S(2)}, u32[]{:S(2)}) %collective-permute-start.17) | collective-permute-done | bytes 2080 | tf_op jit(solution)/shard_map/ppermute | solution.py:368
  74.0 0.6 maximum_maximum_fusion
  (12 shorter events, 0.1 us)
Async XLA Ops:
  0.0 9.9 %copy-start.2 = (s32[756]{0:T(1024)S(1)}, s32[756]{0:T(1024)}, u32[]{:S(2)}) copy-start(s32[756]{0:T(1024)} %constant.17.clone.table_ref) | copy-start | bytes 9076
  0.0 9.9 %copy-start.1 = (s32[256]{0:T(256)S(1)}, s32[256]{0:T(256)}, u32[]{:S(2)}) copy-start(s32[256]{0:T(256)} %cluster_ref.3) | copy-start | bytes 3076
  0.0 3.0 %collective-permute-start = (bf16[512,384]{1,0:T(8,128)(2,1)}, bf16[512,384]{1,0:T(8,128)(2,1)S(1)}, u32[]{:S(2)}, u32[]{:S(2)}) collective-permute-start(bf16[512,384]{1,0:T(8,128)(2,1)} %x_ref.1), channel_id=1, source_target_pairs={{0,16},{1,17},{2,18},{3,19},{4,20},{5,21},{6,22},{7,23},{8,24},{9,... | collective-permute-start | bytes 1179656 | tf_op jit(solution)/shard_map/ppermute | solution.py:368
  1.4 1.0 %copy-start = (bf16[512,384]{1,0:T(8,128)(2,1)S(1)}, bf16[512,384]{1,0:T(8,128)(2,1)}, u32[]{:S(2)}) copy-start(bf16[512,384]{1,0:T(8,128)(2,1)} %x_ref.1) | copy-start | bytes 1179652
  3.2 11.5 %collective-permute-start.1 = (bf16[2,512,384]{2,1,0:T(8,128)(2,1)S(1)}, bf16[2,512,384]{2,1,0:T(8,128)(2,1)S(1)}, u32[]{:S(2)}, u32[]{:S(2)}) collective-permute-start(bf16[2,512,384]{2,1,0:T(8,128)(2,1)S(1)} %shard_map.38.unit_ref.refs_6_.refs_5_.refs_8_), channel_id=1, source_target_pairs={{0,96},{1,97},{2,98},{3,99},{4,100},{5,101},{6,102},{7,103},{8,104... | collective-permute-start | bytes 2359304 | tf_op jit(solution)/shard_map/ppermute | solution.py:373
  5.0 13.3 %collective-permute-start.3 = (bf16[2,512,384]{2,1,0:T(8,128)(2,1)S(1)}, bf16[2,512,384]{2,1,0:T(8,128)(2,1)S(1)}, u32[]{:S(2)}, u32[]{:S(2)}) collective-permute-start(bf16[2,512,384]{2,1,0:T(8,128)(2,1)S(1)} %shard_map.38.unit_ref.refs_6_.refs_5_.refs_8_), channel_id=1, source_target_pairs={{0,32},{1,33},{2,34},{3,35},{4,36},{5,37},{6,38},{7,39},{8,40},{9,... | collective-permute-start | bytes 2359304 | tf_op jit(solution)/shard_map/ppermute | solution.py:373
  7.7 12.1 %collective-permute-start.4 = (bf16[2,512,384]{2,1,0:T(8,128)(2,1)S(1)}, bf16[2,512,384]{2,1,0:T(8,128)(2,1)S(1)}, u32[]{:S(2)}, u32[]{:S(2)}) collective-permute-start(bf16[2,512,384]{2,1,0:T(8,128)(2,1)S(1)} %shard_map.38.unit_ref.refs_6_.refs_5_.refs_8_), channel_id=1, source_target_pairs={{0,4},{1,5},{2,6},{3,7},{4,0},{5,1},{6,2},{7,3},{8,12},{9,13},{10,... | collective-permute-start | bytes 2359304 | tf_op jit(solution)/shard_map/ppermute | solution.py:373
  14.6 13.8 %collective-permute-start.2 = (bf16[2,512,384]{2,1,0:T(8,128)(2,1)S(1)}, bf16[2,512,384]{2,1,0:T(8,128)(2,1)S(1)}, u32[]{:S(2)}, u32[]{:S(2)}) collective-permute-start(bf16[2,512,384]{2,1,0:T(8,128)(2,1)S(1)} %collective-permute-done.1.refs_4_), channel_id=1, source_target_pairs={{0,4},{1,5},{2,6},{3,7},{4,0},{5,1},{6,2},{7,3},{8,12},{9,13},{10,... | collective-permute-start | bytes 2359304 | tf_op jit(solution)/shard_map/ppermute | solution.py:373
  19.7 11.1 %collective-permute-start.6 = (bf16[2,512,384]{2,1,0:T(8,128)(2,1)S(1)}, bf16[2,512,384]{2,1,0:T(8,128)(2,1)S(1)}, u32[]{:S(2)}, u32[]{:S(2)}) collective-permute-start(bf16[2,512,384]{2,1,0:T(8,128)(2,1)S(1)} %collective-permute-done.3.refs_3_), channel_id=1, source_target_pairs={{0,96},{1,97},{2,98},{3,99},{4,100},{5,101},{6,102},{7,103},{8,104... | collective-permute-start | bytes 2359304 | tf_op jit(solution)/shard_map/ppermute | solution.py:373
  20.1 12.1 %collective-permute-start.7 = (bf16[2,512,384]{2,1,0:T(8,128)(2,1)S(1)}, bf16[2,512,384]{2,1,0:T(8,128)(2,1)S(1)}, u32[]{:S(2)}, u32[]{:S(2)}) collective-permute-start(bf16[2,512,384]{2,1,0:T(8,128)(2,1)S(1)} %collective-permute-done.4.refs_5_), channel_id=1, source_target_pairs={{0,32},{1,33},{2,34},{3,35},{4,36},{5,37},{6,38},{7,39},{8,40},{9,... | collective-permute-start | bytes 2359304 | tf_op jit(solution)/shard_map/ppermute | solution.py:373
  24.5 12.8 %collective-permute-start.8 = (bf16[6,512,384]{2,1,0:T(8,128)(2,1)S(1)}, bf16[6,512,384]{2,1,0:T(8,128)(2,1)S(1)}, u32[]{:S(2)}, u32[]{:S(2)}) collective-permute-start(bf16[6,512,384]{2,1,0:T(8,128)(2,1)S(1)} %get-tuple-element.32.refs_3_), channel_id=1, source_target_pairs={{0,16},{1,17},{2,18},{3,19},{4,20},{5,21},{6,22},{7,23},{8,24},{9,... | collective-permute-start | bytes 7077896 | tf_op jit(solution)/shard_map/ppermute | solution.py:368
  32.3 17.9 %collective-permute-start.12 = (bf16[6,512,384]{2,1,0:T(8,128)(2,1)S(1)}, bf16[6,512,384]{2,1,0:T(8,128)(2,1)S(1)}, u32[]{:S(2)}, u32[]{:S(2)}) collective-permute-start(bf16[6,512,384]{2,1,0:T(8,128)(2,1)S(1)} %shard_map.42.refs_4_.refs_7_), channel_id=1, source_target_pairs={{0,16},{1,17},{2,18},{3,19},{4,20},{5,21},{6,22},{7,23},{8,24},{9,... | collective-permute-start | bytes 7077896 | tf_op jit(solution)/shard_map/ppermute | solution.py:368
  33.6 14.1 %collective-permute-start.5 = (bf16[512,384]{1,0:T(8,128)(2,1)S(1)}, bf16[512,384]{1,0:T(8,128)(2,1)S(1)}, u32[]{:S(2)}, u32[]{:S(2)}) collective-permute-start(bf16[512,384]{1,0:T(8,128)(2,1)S(1)} %slice_bitcast_fusion.1), channel_id=1, source_target_pairs={{0,32},{1,33},{2,34},{3,35},{4,36},{5,37},{6,38},{7,39},{8,40},{9,... | collective-permute-start | bytes 1179656 | tf_op jit(solution)/shard_map/ppermute | solution.py:373
  35.6 12.1 %collective-permute-start.9 = (bf16[512,384]{1,0:T(8,128)(2,1)S(1)}, bf16[512,384]{1,0:T(8,128)(2,1)S(1)}, u32[]{:S(2)}, u32[]{:S(2)}) collective-permute-start(bf16[512,384]{1,0:T(8,128)(2,1)S(1)} %slice_bitcast_fusion), channel_id=1, source_target_pairs={{0,96},{1,97},{2,98},{3,99},{4,100},{5,101},{6,102},{7,103},{8,104... | collective-permute-start | bytes 1179656 | tf_op jit(solution)/shard_map/ppermute | solution.py:373
  47.7 2.0 %collective-permute-start.10 = (bf16[512,384]{1,0:T(8,128)(2,1)S(1)}, bf16[512,384]{1,0:T(8,128)(2,1)S(1)}, u32[]{:S(2)}, u32[]{:S(2)}) collective-permute-start(bf16[512,384]{1,0:T(8,128)(2,1)S(1)} %collective-permute-done.5.refs_3_), channel_id=1, source_target_pairs={{0,16},{1,17},{2,18},{3,19},{4,20},{5,21},{6,22},{7,23},{8,24},{9,... | collective-permute-start | bytes 1179656 | tf_op jit(solution)/shard_map/ppermute | solution.py:368
  47.9 2.3 %collective-permute-start.11 = (bf16[512,384]{1,0:T(8,128)(2,1)S(1)}, bf16[512,384]{1,0:T(8,128)(2,1)S(1)}, u32[]{:S(2)}, u32[]{:S(2)}) collective-permute-start(bf16[512,384]{1,0:T(8,128)(2,1)S(1)} %collective-permute-done.9.refs_4_), channel_id=1, source_target_pairs={{0,16},{1,17},{2,18},{3,19},{4,20},{5,21},{6,22},{7,23},{8,24},{9,... | collective-permute-start | bytes 1179656 | tf_op jit(solution)/shard_map/ppermute | solution.py:368
  58.4 1.9 %collective-permute-start.13 = (f32[16,512]{1,0:T(8,128)S(1)}, f32[16,512]{1,0:T(8,128)S(1)}, u32[]{:S(2)}, u32[]{:S(2)}) collective-permute-start(f32[16,512]{1,0:T(8,128)S(1)} %get-tuple-element.45), channel_id=1, source_target_pairs={{0,16},{1,17},{2,18},{3,19},{4,20},{5,21},{6,22},{7,23},{8,24},{9,... | collective-permute-start | bytes 98312 | tf_op jit(solution)/shard_map/ppermute | solution.py:368
  60.3 4.7 %collective-permute-start.14 = (f32[8,512]{1,0:T(8,128)S(1)}, f32[8,512]{1,0:T(8,128)S(1)}, u32[]{:S(2)}, u32[]{:S(2)}) collective-permute-start(f32[8,512]{1,0:T(8,128)S(1)} %slice_maximum_fusion), channel_id=1, source_target_pairs={{0,4},{1,5},{2,6},{3,7},{4,0},{5,1},{6,2},{7,3},{8,12},{9,13},{10,... | collective-permute-start | bytes 49160 | tf_op jit(solution)/shard_map/ppermute | solution.py:373
  65.0 2.6 %collective-permute-start.15 = (f32[4,512]{1,0:T(4,128)S(1)}, f32[4,512]{1,0:T(4,128)S(1)}, u32[]{:S(2)}, u32[]{:S(2)}) collective-permute-start(f32[4,512]{1,0:T(4,128)S(1)} %slice.45), channel_id=1, source_target_pairs={{0,96},{1,97},{2,98},{3,99},{4,100},{5,101},{6,102},{7,103},{8,104... | collective-permute-start | bytes 24584 | tf_op jit(solution)/shard_map/ppermute | solution.py:373
  67.6 3.7 %collective-permute-start.16 = (f32[2,512]{1,0:T(2,128)S(1)}, f32[2,512]{1,0:T(2,128)S(1)}, u32[]{:S(2)}, u32[]{:S(2)}) collective-permute-start(f32[2,512]{1,0:T(2,128)S(1)} %slice.47), channel_id=1, source_target_pairs={{0,32},{1,33},{2,34},{3,35},{4,36},{5,37},{6,38},{7,39},{8,40},{9,... | collective-permute-start | bytes 12296 | tf_op jit(solution)/shard_map/ppermute | solution.py:373
  71.4 2.6 %collective-permute-start.17 = (f32[512]{0:T(512)S(1)}, f32[512]{0:T(512)S(1)}, u32[]{:S(2)}, u32[]{:S(2)}) collective-permute-start(f32[512]{0:T(512)S(1)} %bitcast.11), channel_id=1, source_target_pairs={{0,16},{1,17},{2,18},{3,19},{4,20},{5,21},{6,22},{7,23},{8,24},{9,... | collective-permute-start | bytes 6152 | tf_op jit(solution)/shard_map/ppermute | solution.py:368

commit v6 on v5

v6 whole, which is shorter than its diff:
```python
import jax
import jax.numpy as jnp
from jax import lax
from jax.experimental import pallas as pl
from jax.experimental.pallas import tpu as pltpu
from jax.sharding import PartitionSpec as P

BLK = 256
SHARD = 512
D = 384
VMEM_LIMIT = 20 * 1024 * 1024

CORE = 16
X1, X3, Y1, Y3, Z1, Z3 = 32, 96, 4, 12, 1, 3
GENERATORS = ((X1, Y1, Y3), (X3, Z1, Z3))
SLOTS = ((), (0,), (1,), (2,), (0, 1), (1, 2), (2, 0), (0, 1, 2))
SENDS = ((0, 0), (0, 1), (0, 2), (1, 1), (2, 2), (3, 0))
HALVES = ((5, 0), (6, 1))


def mask_of(core, slot):
    mask = 0
    for generator in SLOTS[slot]:
        mask ^= GENERATORS[core][generator]
    return mask


EARLY = [(g, 0) for g in (1, 2, 3)]
MIDDLE = [(g, h) for g in (1, 2, 3) for h in range(1, g + 1)]
MIDDLE += [(g, h) for g in (4, 5, 6) for h in range(4)]
LAST = [(g, h) for g in (4, 5, 6, 7) for h in range(4, 8)] + [(7, h) for h in range(4)]
PHASES = ((EARLY, 1), (MIDDLE, 1), (LAST, 4))


def shared(g, h):
    return g == h or (g >= 4 and h >= 4)


COUNTS = [sum(2 if shared(g, h) else 4 for g, h in pairs) for pairs, _ in PHASES]
STARTS = [0, COUNTS[0] + 1, COUNTS[0] + COUNTS[1] + 2]
LISTS = sum(COUNTS) + 3
MARGIN = 24
MOST = 160
VMEM = pltpu.VMEM
SMEM = pltpu.SMEM


def spec(space):
    return pl.BlockSpec(memory_space=space)


def params():
    return pltpu.CompilerParams(vmem_limit_bytes=VMEM_LIMIT)


def unit_of(x):
    values = x.astype(jnp.float32)
    squares = jnp.sum(values * values, axis=1, keepdims=True)
    return (values * lax.rsqrt(squares + 1e-06)).astype(jnp.bfloat16)


def first_kernel(x_ref, out_ref):
    out_ref[...] = unit_of(x_ref[...])


def pair_kernel(here_ref, own_ref, other_ref, out_ref):
    core = (here_ref[0] >> 4) & 1
    out_ref[core] = own_ref[...]
    out_ref[1 - core] = unit_of(other_ref[...])


def unit_call(here, x, other):
    cost = pl.CostEstimate(flops=1000000, bytes_accessed=1600000, transcendentals=512)
    own = pl.pallas_call(
        first_kernel,
        out_shape=jax.ShapeDtypeStruct((SHARD, D), jnp.bfloat16),
        in_specs=[spec(VMEM)],
        out_specs=spec(VMEM),
        compiler_params=params(),
        cost_estimate=cost,
    )(x)
    return pl.pallas_call(
        pair_kernel,
        out_shape=jax.ShapeDtypeStruct((2, SHARD, D), jnp.bfloat16),
        in_specs=[spec(SMEM), spec(VMEM), spec(VMEM)],
        out_specs=spec(VMEM),
        compiler_params=params(),
        cost_estimate=cost,
    )(here, own, other)


def dot(a, b):
    return lax.dot_general(a, b, (((1,), (1,)), ((), ())), preferred_element_type=jnp.float32)


def plan_kernel(here_ref, cluster_ref, blocks_ref, full_ref, part_ref, count_ref, mine, theirs, share):
    here = here_ref[0]
    core = (here >> 4) & 1
    masks = [[mask_of(c, slot) for slot in range(8)] for c in range(2)]
    for slot in range(8):
        for ref, one, two in ((mine, 0, 1), (theirs, 1, 0)):
            chip = (here ^ jnp.where(core == 0, masks[one][slot], masks[two][slot])) & ~CORE
            for half in range(2):
                block = 2 * (chip | (half * CORE))
                ref[2 * slot + half] = cluster_ref[block] | (cluster_ref[block + 1] << 4)

    first = jnp.sum(jnp.where(blocks_ref[...] < cluster_ref[128], 1, 0))

    def held(slab):
        low, high = slab * 64, slab * 64 + 64
        return jnp.maximum(jnp.minimum(high, first + MOST) - jnp.maximum(low, first), 0)

    slab = here >> 5
    ours = held(slab)
    share[0] = 0
    for other in range(1, 4):
        there = held(slab ^ other)
        share[other] = jnp.where(
            ours + MARGIN <= there, 1, jnp.where(there + MARGIN <= ours, 2, 0)
        )

    for phase, (pairs, base) in enumerate(PHASES):
        full = jnp.int32(STARTS[phase])
        part = jnp.int32(STARTS[phase])

        def candidate(full, part, wanted, g, side, h, far):
            a, b = mine[2 * g + side], theirs[2 * h + far]
            same = a ^ b
            left, right = (a >> 4) ^ b, a ^ (b >> 4)
            quads = (
                jnp.where((same & 15) == 0, 1, 0)
                | jnp.where((right & 15) == 0, 2, 0)
                | jnp.where((left & 15) == 0, 4, 0)
                | jnp.where((same & 240) == 0, 8, 0)
            )
            code = (2 * (g - base) + side) | ((2 * h + far) << 4)
            full_ref[full] = code
            part_ref[part] = code | (quads << 8)
            whole = quads == 15
            full = full + jnp.where(wanted & whole, 1, 0)
            part = part + jnp.where(wanted & (quads != 0) & jnp.logical_not(whole), 1, 0)
            return full, part

        for g, h in pairs:
            w = jnp.where(
                core == 0, masks[0][g] ^ masks[1][h], masks[1][g] ^ masks[0][h]
            )
            kind = share[(w >> 5) & 3]
            bit = jnp.where((here & (w & -w)) != 0, 1, 0) ^ ((g + h) % 2)
            whole, half = kind == 1, kind == 0
            mixed = ((whole | half, core, 1 - core), (whole, 1 - core, core))
            plain = ((whole | (half & (bit == 0)), 0, 0), (whole | (half & (bit == 1)), 1, 1))
            if shared(g, h):
                for (one, side, far), (two, _, _), n in zip(mixed, plain, (0, 1)):
                    wanted = ((core == 0) & one) | ((core == 1) & two)
                    side = jnp.where(core == 0, side, n)
                    far = jnp.where(core == 0, far, n)
                    full, part = candidate(full, part, wanted, g, side, h, far)
            else:
                for wanted, side, far in mixed + plain:
                    full, part = candidate(full, part, wanted, g, side, h, far)
        count_ref[2 * phase] = full - STARTS[phase]
        count_ref[2 * phase + 1] = part - STARTS[phase]


def own_kernel(here_ref, cluster_ref, unit_ref, own_ref):
    here = here_ref[0]
    core = (here >> 4) & 1
    first0 = cluster_ref[2 * here]
    first1 = cluster_ref[2 * here + 1]
    there = here ^ CORE
    second0 = cluster_ref[2 * there]
    second1 = cluster_ref[2 * there + 1]
    mine = unit_ref[core]
    best = jnp.full((8, SHARD), -2.0, jnp.float32)
    col = lax.broadcasted_iota(jnp.int32, (BLK, SHARD), 1)
    row = lax.broadcasted_iota(jnp.int32, (BLK, SHARD), 0)
    label = jnp.where(col[:1] < BLK, first0, first1)
    for half, name in ((0, first0), (1, first1)):
        scores = dot(unit_ref[core, half * BLK : half * BLK + BLK, :], mine)
        keep = (row + half * BLK != col) & (label == name)
        scores = jnp.where(keep, scores, jnp.float32(-2.0))
        best = jnp.maximum(best, jnp.max(scores.reshape(BLK // 8, 8, SHARD), axis=0))
    for half, name in ((0, second0), (1, second1)):
        scores = dot(unit_ref[1 - core, half * BLK : half * BLK + BLK, :], mine)
        scores = jnp.where(label == name, scores, jnp.float32(-2.0))
        best = jnp.maximum(best, jnp.max(scores.reshape(BLK // 8, 8, SHARD), axis=0))
    own_ref[...] = jnp.max(best, axis=0, keepdims=True)


def plan_call(here, cluster):
    lists = jax.ShapeDtypeStruct((LISTS,), jnp.int32)
    return pl.pallas_call(
        plan_kernel,
        out_shape=(lists, lists, jax.ShapeDtypeStruct((2 * len(PHASES),), jnp.int32)),
        in_specs=[spec(SMEM), spec(SMEM), spec(VMEM)],
        out_specs=(spec(SMEM),) * 3,
        scratch_shapes=[SMEM((16,), jnp.int32), SMEM((16,), jnp.int32), SMEM((4,), jnp.int32)],
        compiler_params=params(),
        cost_estimate=pl.CostEstimate(flops=3000000000, bytes_accessed=10000, transcendentals=0),
    )(here, cluster, cluster.reshape(2, 128))


def own_call(here, cluster, unit):
    return pl.pallas_call(
        own_kernel,
        out_shape=jax.ShapeDtypeStruct((1, SHARD), jnp.float32),
        in_specs=[spec(SMEM), spec(SMEM), spec(VMEM)],
        out_specs=spec(VMEM),
        compiler_params=params(),
        cost_estimate=pl.CostEstimate(flops=1000000000, bytes_accessed=1000000, transcendentals=0),
    )(here, cluster, unit)


def fold(row_ref, col_ref, i, j, rows, cols, scores):
    best = scores[:, :128]
    for k in range(1, scores.shape[1] // 128):
        best = jnp.maximum(best, scores[:, 128 * k : 128 * k + 128])
    row_ref[i, rows, :] = jnp.maximum(row_ref[i, rows, :], best)
    down = jnp.max(scores.reshape(scores.shape[0] // 8, 8, scores.shape[1]), axis=0)
    col_ref[j, :, cols] = jnp.maximum(col_ref[j, :, cols], down)


def score_full(a_ref, b_ref, row_ref, col_ref, word):
    i = word & 15
    j = (word >> 4) & 15
    scores = dot(a_ref[i], b_ref[j])
    fold(row_ref, col_ref, i, j, slice(None), slice(None), scores)


def score_part(a_ref, b_ref, row_ref, col_ref, word):
    i = word & 15
    j = (word >> 4) & 15
    for quad in range(4):

        @pl.when(((word >> (8 + quad)) & 1) == 1)
        def _():
            rows = pl.ds((quad // 2) * BLK, BLK)
            cols = pl.ds((quad % 2) * BLK, BLK)
            scores = dot(a_ref[i, rows, :], b_ref[j, cols, :])
            fold(row_ref, col_ref, i, j, rows, cols, scores)


def score_lists(phase, full_ref, part_ref, count_ref, *refs):
    first = STARTS[phase]
    full = count_ref[2 * phase]
    fours = full & ~3

    def items(n, count):
        for k in range(count):
            score_full(*refs, full_ref[first + n + k])

    @pl.loop(0, fours, step=4)
    def _(n):
        items(n, 4)

    @pl.when((full & 2) != 0)
    def _():
        items(fours, 2)

    @pl.when((full & 1) != 0)
    def _():
        items(full - 1, 1)

    @pl.loop(0, count_ref[2 * phase + 1])
    def _(n):
        score_part(*refs, part_ref[first + n])


def put_rows(out_ref, place, row_ref, first):
    for half in range(2):
        at = place + half
        for k in range(SHARD // 128):
            part = row_ref[first + half, 128 * k : 128 * k + 128, :].T
            out_ref[at : at + 1, 128 * k : 128 * k + 128] = jnp.max(part, axis=0, keepdims=True)


def clear(*refs):
    for ref in refs:
        ref[...] = jnp.full(ref.shape, -2.0, jnp.float32)


def put(buf, refs):
    for n, ref in enumerate(refs):
        buf[2 * n : 2 * n + 2] = ref[...]


def early_kernel(*refs):
    plan, unit, mine, (pack_ref, row_ref, col_ref) = refs[:3], refs[3], refs[4:7], refs[7:]
    clear(row_ref, col_ref)
    put(pack_ref, mine)
    score_lists(0, *plan, pack_ref, unit, row_ref, col_ref)


def pack_kernel(a_ref, b_ref, c_ref, out_ref):
    put(out_ref, (a_ref, b_ref, c_ref))


def middle_kernel(*refs):
    plan, (unit, a_low, a_mid, b_low, row_in, col_in), outs = refs[:3], refs[3:9], refs[9:]
    rows_out, row_mid, col_ref, a_buf, b_buf, row_ref = outs
    row_ref[:6] = row_in[...]
    row_ref[6:] = jnp.full(row_mid.shape, -2.0, jnp.float32)
    col_ref[:2] = col_in[...]
    col_ref[2:] = jnp.full((6, 8, SHARD), -2.0, jnp.float32)
    a_buf[:6] = a_low[...]
    a_buf[6:] = a_mid[...]
    b_buf[:2] = unit[...]
    b_buf[2:] = b_low[...]
    score_lists(1, *plan, a_buf, b_buf, row_ref, col_ref)
    for n in range(0, 6, 2):
        put_rows(rows_out, n, row_ref, n)
    row_mid[...] = row_ref[6:]


def f32(*shape):
    return jax.ShapeDtypeStruct(shape, jnp.float32)


def shards(n):
    return jax.ShapeDtypeStruct((n, SHARD, D), jnp.bfloat16)


def rows_of(n):
    return f32(n, SHARD, 128)


def cols_of(n):
    return f32(n, 8, SHARD)


def kernel_call(kernel, operands, outs, scratch, flops, smem=3):
    return pl.pallas_call(
        kernel,
        out_shape=outs,
        in_specs=[spec(SMEM)] * smem + [spec(VMEM)] * (len(operands) - smem),
        out_specs=jax.tree.map(lambda _: spec(VMEM), outs),
        scratch_shapes=[VMEM(x.shape, x.dtype) for x in scratch],
        compiler_params=params(),
        cost_estimate=pl.CostEstimate(flops=flops, bytes_accessed=8000000, transcendentals=0),
    )(*operands)


def early_call(plan, *operands):
    outs = (shards(6), rows_of(6), cols_of(2))
    return kernel_call(early_kernel, [*plan, *operands], outs, [], 3000000000)


def middle_call(plan, *operands):
    outs = (f32(6, SHARD), rows_of(6), cols_of(8))
    scratch = [shards(12), shards(8), rows_of(12)]
    return kernel_call(middle_kernel, [*plan, *operands], outs, scratch, 5000000000)


KEPT = (0, 1, 2, 4)
SENT = (3, 6, 5, 7)


def last_kernel(*refs):
    plan, mine, theirs, refs = refs[:3], refs[3:5], refs[5:7], refs[7:]
    unit, a_mid, b_low, b_mid, rows0, row_in, col_in, keep_ref, send_ref, other_ref, *refs = refs
    a_buf, b_buf, row_ref, col_ref = refs
    a_buf[:6] = a_mid[...]
    b_buf[:2] = unit[...]
    b_buf[2:8] = b_low[...]
    b_buf[8:14] = b_mid[...]
    for half in range(2):
        a_buf[6 + half] = mine[half][...]
        b_buf[14 + half] = theirs[half][...]
    row_ref[:6] = row_in[...]
    row_ref[6:] = jnp.full((2, SHARD, 128), -2.0, jnp.float32)
    col_ref[:8] = col_in[...]
    col_ref[8:] = jnp.full(col_in.shape, -2.0, jnp.float32)
    score_lists(2, *plan, a_buf, b_buf, row_ref, col_ref)
    keep_ref[0:2] = jnp.full((2, SHARD), -2.0, jnp.float32)
    for out_ref, slots in ((keep_ref, KEPT), (send_ref, SENT)):
        for place, slot in enumerate(slots):
            if slot > 3:
                put_rows(out_ref, 2 * place, row_ref, 2 * slot - 8)
            elif slot > 0:
                out_ref[2 * place : 2 * place + 2] = rows0[2 * slot - 2 : 2 * slot]
    for place, slot in enumerate(KEPT + SENT):
        for half in range(2):
            at = 2 * place + half
            down = col_ref[2 * slot + half]
            other_ref[at : at + 1, :] = jnp.max(down, axis=0, keepdims=True)


def last_call(plan, *operands):
    outs = (f32(8, SHARD), f32(8, SHARD), f32(16, SHARD))
    scratch = [shards(8), shards(16), rows_of(8), cols_of(16)]
    return kernel_call(last_kernel, [*plan, *operands], outs, scratch, 5000000000)


def swap(x):
    return lax.ppermute(x, ("row", "col"), [(s, s ^ CORE) for s in range(128)])


def exchange(x, generator):
    pairs = [(s, s ^ GENERATORS[(s >> 4) & 1][generator]) for s in range(128)]
    return lax.ppermute(x, ("row", "col"), pairs)


def after(x, *done):
    return lax.optimization_barrier((x, *done))[0]


def body(embeddings, block_cluster):
    here = (lax.axis_index("row") * 16 + lax.axis_index("col")).astype(jnp.int32).reshape(1)
    unit = unit_call(here, embeddings, swap(embeddings))
    plan = plan_call(here, block_cluster)
    mine = [unit]

    def step(slots):
        return [exchange(mine[SENDS[k - 1][0]], SENDS[k - 1][1]) for k in slots]

    own = own_call(here, block_cluster, unit)
    mine.extend(after(x, plan[2], own) for x in step((1, 2, 3)))
    a_low, rows0, cols = early_call(plan, *mine)
    b_low = swap(a_low)
    mine.extend(after(x, a_low) for x in step((4, 5, 6)))
    halves = [
        exchange(mine[source][half], generator) for half, (source, generator) in enumerate(HALVES)
    ]
    a_mid = kernel_call(pack_kernel, mine[4:7], shards(6), [], 1000000000, 0)
    b_mid = swap(a_mid)
    rows0, rows1, cols = middle_call(plan, unit, a_low, a_mid, b_low, rows0, cols)
    halves = [after(x, cols) for x in halves]
    swapped = [swap(x) for x in halves]
    keep, send, other = last_call(
        plan, *halves, *swapped, unit, a_mid, b_low, b_mid, rows0, rows1, cols
    )
    other = swap(other)
    keep = jnp.maximum(keep, other[:8])
    send = jnp.maximum(send, other[8:])
    keep = jnp.maximum(keep, exchange(send, 2))
    keep = jnp.maximum(keep[:4], exchange(keep[4:], 1))
    keep = jnp.maximum(keep[:2], exchange(keep[2:], 0))
    second = (here & CORE) != 0
    ours = jnp.where(second, keep[1], keep[0])
    other = swap(jnp.where(second, keep[0], keep[1]))
    return jnp.maximum(own.reshape(SHARD), jnp.maximum(ours, other))


def solution(mesh):
    placed = (P(("row", "col"), None), P())
    return jax.shard_map(
        body, mesh=mesh, in_specs=placed, out_specs=P(("row", "col")), check_vma=False
    )
```

time: 74.7 us -> 68.1 us (0.912)
  Pallas kernels: 26.8 us -> 16 us
  starting transfers between devices: 25.7 us -> 30.4 us
    pallas_call x4, Pallas kernels: 22.2 us -> 10.8 us  [kernel_call(): pl.pallas_call(kernel, out_shape=outs, in_specs=[spec(SMEM)] * smem + [sp...]
    ppermute x7, starting transfers between devices: 6.31 us -> 9.59 us  [swap(): return lax.ppermute(x, ('row', 'col'), [(s, s ^ CORE) for s in range(128)])]
    ppermute x11, starting transfers between devices: 19.4 us -> 20.8 us  [exchange(): return lax.ppermute(x, ('row', 'col'), pairs)]
  transfers between devices with their start and end apart: 18 -> 18, of which waited for: 13 -> 12; matrix products, arithmetic and copies ran while one was open for 0% -> 0% of each run, Pallas kernels for 25% -> 18%
where the time goes in v6:
time: 68.1 us; the launch traced here: 68.3 us
  starting transfers between devices  30.4 us (45%)
  waiting for transfers between devices  20 us (29%)
  Pallas kernels  16 us (23%)
  local copies, waits for them, and re-layouts  1.09 us (2%)
    ppermute x11, starting transfers between devices, exchange(): return lax.ppermute(x, ('row', 'col'), pairs)  20.8 us
    ppermute x11, waiting for transfers between devices, exchange(): return lax.ppermute(x, ('row', 'col'), pairs)  16.1 us
    pallas_call x4, Pallas kernels, kernel_call(): pl.pallas_call(kernel, out_shape=outs, in_specs=[spec(SMEM)] * smem + [sp...  10.8 us
    ppermute x7, starting transfers between devices, swap(): return lax.ppermute(x, ('row', 'col'), [(s, s ^ CORE) for s in range(128)])  9.59 us
    ppermute x7, waiting for transfers between devices, swap(): return lax.ppermute(x, ('row', 'col'), [(s, s ^ CORE) for s in range(128)])  3.91 us
    pallas_call x1, Pallas kernels, plan_call(): pl.pallas_call(plan_kernel, out_shape=(lists, lists, jax.ShapeDtypeStruct...  3.62 us
  transfers between devices with their start and end apart: 18, of which 12 were waited for; matrix products, arithmetic and copies ran while one was open for 0% of the time, Pallas kernels for 18%

profile of v6, /device:TPU:1, one launch (start us, length us, event | category | flops | bytes accessed | tf_op | source)
XLA Modules:
  0.0 68.3 jit_solution(10896465929515998920)
XLA Ops:
  0.0 0.0 copy-start.1
  0.0 1.4 %collective-permute-start = (bf16[512,384]{1,0:T(8,128)(2,1)}, bf16[512,384]{1,0:T(8,128)(2,1)S(1)}, u32[]{:S(2)}, u32[]{:S(2)}) collective-permute-start(bf16[512,384]{1,0:T(8,128)(2,1)} %x_ref.1), channel_id=1, source_target_pairs={{0,16},{1,17},{2,18},{3,19},{4,20},{5,21},{6,22},{7,23},{8,24},{9,... | collective-permute-start | bytes 1179656 | tf_op jit(solution)/shard_map/ppermute | solution.py:396
  1.4 1.0 %copy-done = bf16[512,384]{1,0:T(8,128)(2,1)S(1)} copy-done((bf16[512,384]{1,0:T(8,128)(2,1)S(1)}, bf16[512,384]{1,0:T(8,128)(2,1)}, u32[]{:S(2)}) %copy-start) | copy-done | bytes 393240
  2.4 0.2 shard_map.28.own_ref
  2.6 0.4 collective-permute-done.other_ref
  3.0 0.2 shard_map.29.unit_ref.refs_3_.refs_7_
  3.2 1.8 %collective-permute-start.1 = (bf16[2,512,384]{2,1,0:T(8,128)(2,1)S(1)}, bf16[2,512,384]{2,1,0:T(8,128)(2,1)S(1)}, u32[]{:S(2)}, u32[]{:S(2)}) collective-permute-start(bf16[2,512,384]{2,1,0:T(8,128)(2,1)S(1)} %shard_map.29.unit_ref.refs_3_.refs_7_), channel_id=1, source_target_pairs={{0,4},{1,5},{2,6},{3,7},{4,0},{5,1},{6,2},{7,3},{8,12},{9,13},{10,... | collective-permute-start | bytes 2359304 | tf_op jit(solution)/shard_map/ppermute | solution.py:401
  5.0 2.5 %collective-permute-start.3 = (bf16[2,512,384]{2,1,0:T(8,128)(2,1)S(1)}, bf16[2,512,384]{2,1,0:T(8,128)(2,1)S(1)}, u32[]{:S(2)}, u32[]{:S(2)}) collective-permute-start(bf16[2,512,384]{2,1,0:T(8,128)(2,1)S(1)} %shard_map.29.unit_ref.refs_3_.refs_7_), channel_id=1, source_target_pairs={{0,32},{1,33},{2,34},{3,35},{4,36},{5,37},{6,38},{7,39},{8,40},{9,... | collective-permute-start | bytes 2359304 | tf_op jit(solution)/shard_map/ppermute | solution.py:401
  7.4 2.2 %collective-permute-start.4 = (bf16[2,512,384]{2,1,0:T(8,128)(2,1)S(1)}, bf16[2,512,384]{2,1,0:T(8,128)(2,1)S(1)}, u32[]{:S(2)}, u32[]{:S(2)}) collective-permute-start(bf16[2,512,384]{2,1,0:T(8,128)(2,1)S(1)} %shard_map.29.unit_ref.refs_3_.refs_7_), channel_id=1, source_target_pairs={{0,12},{1,13},{2,14},{3,15},{4,8},{5,9},{6,10},{7,11},{8,4},{9,5},... | collective-permute-start | bytes 2359304 | tf_op jit(solution)/shard_map/ppermute | solution.py:401
  9.7 0.0 copy-done.1
  9.7 3.6 %shard_map.31 = (s32[129]{0:T(256)S(1)}, s32[129]{0:T(256)S(1)}, s32[6]{0:T(128)S(1)}) custom-call(s32[1]{0:T(128)} %bitcast.here_ref, s32[256]{0:T(256)S(1)} %copy-done.1, s32[2,128]{1,0:T(2,128)S(1)} %bitcast.11), custom_call_target="tpu_custom_call" | custom-call | flops 3000000000 | bytes 10000 | tf_op jit(solution)/shard_map/pallas_call | solution.py:193
  13.3 1.3 %shard_map.30 = f32[1,512]{1,0:T(1,128)S(1)} custom-call(s32[1]{0:T(128)} %bitcast.here_ref, s32[256]{0:T(256)S(1)} %copy-done.1, bf16[2,512,384]{2,1,0:T(8,128)(2,1)S(1)} %shard_map.29.unit_ref.refs_3_.refs_7_), custom_call_target="tpu_custom_call" | custom-call | flops 1000000000 | bytes 1000000 | tf_op jit(solution)/shard_map/pallas_call | solution.py:205
  14.6 0.0 collective-permute-done.1.refs_5_
  14.6 3.6 %collective-permute-start.2 = (bf16[2,512,384]{2,1,0:T(8,128)(2,1)S(1)}, bf16[2,512,384]{2,1,0:T(8,128)(2,1)S(1)}, u32[]{:S(2)}, u32[]{:S(2)}) collective-permute-start(bf16[2,512,384]{2,1,0:T(8,128)(2,1)S(1)} %collective-permute-done.1.refs_5_), channel_id=1, source_target_pairs={{0,12},{1,13},{2,14},{3,15},{4,8},{5,9},{6,10},{7,11},{8,4},{9,5},... | collective-permute-start | bytes 2359304 | tf_op jit(solution)/shard_map/ppermute | solution.py:401
  18.2 0.0 collective-permute-done.3.refs_4_
  18.2 1.4 %collective-permute-done.4.refs_6_ = bf16[2,512,384]{2,1,0:T(8,128)(2,1)S(1)} collective-permute-done((bf16[2,512,384]{2,1,0:T(8,128)(2,1)S(1)}, bf16[2,512,384]{2,1,0:T(8,128)(2,1)S(1)}, u32[]{:S(2)}, u32[]{:S(2)}) %collective-permute-start.4) | collective-permute-done | bytes 786464 | tf_op jit(solution)/shard_map/ppermute | solution.py:401
  19.6 0.5 collective-permute-start.6
  20.1 0.7 %collective-permute-start.7 = (bf16[2,512,384]{2,1,0:T(8,128)(2,1)S(1)}, bf16[2,512,384]{2,1,0:T(8,128)(2,1)S(1)}, u32[]{:S(2)}, u32[]{:S(2)}) collective-permute-start(bf16[2,512,384]{2,1,0:T(8,128)(2,1)S(1)} %collective-permute-done.4.refs_6_), channel_id=1, source_target_pairs={{0,32},{1,33},{2,34},{3,35},{4,36},{5,37},{6,38},{7,39},{8,40},{9,... | collective-permute-start | bytes 2359304 | tf_op jit(solution)/shard_map/ppermute | solution.py:401
  20.8 1.6 %shard_map.32 = (bf16[6,512,384]{2,1,0:T(8,128)(2,1)S(1)}, f32[6,512,128]{2,1,0:T(8,128)S(1)}, f32[2,8,512]{2,1,0:T(8,128)S(1)}) custom-call(s32[129]{0:T(256)S(1)} %get-tuple-element.25.refs_0_, s32[129]{0:T(256)S(1)} %get-tuple-element.26.refs_1_, s32[6]{0:T(128)S(1)} %get-tuple-element.27.refs_2_, ...), custom_call_target="tpu_custom_call" | custom-call | flops 3000000000 | bytes 8000000 | tf_op jit(solution)/shard_map/pallas_call | solution.py:333
  22.4 0.3 collective-permute-start.8
  22.8 5.4 %collective-permute-done.2.b_ref = bf16[2,512,384]{2,1,0:T(8,128)(2,1)S(1)} collective-permute-done((bf16[2,512,384]{2,1,0:T(8,128)(2,1)S(1)}, bf16[2,512,384]{2,1,0:T(8,128)(2,1)S(1)}, u32[]{:S(2)}, u32[]{:S(2)}) %collective-permute-start.2) | collective-permute-done | bytes 786464 | tf_op jit(solution)/shard_map/ppermute | solution.py:401
  28.2 2.5 %collective-permute-done.6.a_ref = bf16[2,512,384]{2,1,0:T(8,128)(2,1)S(1)} collective-permute-done((bf16[2,512,384]{2,1,0:T(8,128)(2,1)S(1)}, bf16[2,512,384]{2,1,0:T(8,128)(2,1)S(1)}, u32[]{:S(2)}, u32[]{:S(2)}) %collective-permute-start.6) | collective-permute-done | bytes 786464 | tf_op jit(solution)/shard_map/ppermute | solution.py:401
  30.7 1.4 %collective-permute-done.7.c_ref = bf16[2,512,384]{2,1,0:T(8,128)(2,1)S(1)} collective-permute-done((bf16[2,512,384]{2,1,0:T(8,128)(2,1)S(1)}, bf16[2,512,384]{2,1,0:T(8,128)(2,1)S(1)}, u32[]{:S(2)}, u32[]{:S(2)}) %collective-permute-start.7) | collective-permute-done | bytes 786464 | tf_op jit(solution)/shard_map/ppermute | solution.py:401
  32.1 0.2 shard_map.33.refs_5_.refs_8_
  32.4 0.1 collective-permute-start.12
  32.5 1.7 %collective-permute-start.5 = (bf16[512,384]{1,0:T(8,128)(2,1)S(1)}, bf16[512,384]{1,0:T(8,128)(2,1)S(1)}, u32[]{:S(2)}, u32[]{:S(2)}) collective-permute-start(bf16[512,384]{1,0:T(8,128)(2,1)S(1)} %slice_bitcast_fusion.1), channel_id=1, source_target_pairs={{0,32},{1,33},{2,34},{3,35},{4,36},{5,37},{6,38},{7,39},{8,40},{9,... | collective-permute-start | bytes 1179656 | tf_op jit(solution)/shard_map/ppermute | solution.py:401
  34.2 1.7 %collective-permute-start.9 = (bf16[512,384]{1,0:T(8,128)(2,1)S(1)}, bf16[512,384]{1,0:T(8,128)(2,1)S(1)}, u32[]{:S(2)}, u32[]{:S(2)}) collective-permute-start(bf16[512,384]{1,0:T(8,128)(2,1)S(1)} %slice_bitcast_fusion), channel_id=1, source_target_pairs={{0,4},{1,5},{2,6},{3,7},{4,0},{5,1},{6,2},{7,3},{8,12},{9,13},{10,... | collective-permute-start | bytes 1179656 | tf_op jit(solution)/shard_map/ppermute | solution.py:401
  35.9 0.0 collective-permute-done.8.refs_6_.refs_9_
  35.9 5.5 %shard_map.34 = (f32[6,512]{1,0:T(8,128)S(1)}, f32[6,512,128]{2,1,0:T(8,128)S(1)}, f32[8,8,512]{2,1,0:T(8,128)S(1)}) custom-call(s32[129]{0:T(256)S(1)} %get-tuple-element.25.refs_0_, s32[129]{0:T(256)S(1)} %get-tuple-element.26.refs_1_, s32[6]{0:T(128)S(1)} %get-tuple-element.27.refs_2_, bf16[2,512,384]{2,1,0:T(8,128)(2,1)S(1)} %shard_map.29.unit_ref.refs_3_.refs_7_, ...), custom_call_target="tpu_custom_call" | custom-call | flops 5000000000 | bytes 8000000 | tf_op jit(solution)/shard_map/pallas_call | solution.py:333
  41.4 0.0 collective-permute-done.5.refs_3_
  41.4 0.0 collective-permute-done.9.refs_4_
  41.5 1.0 %collective-permute-start.10 = (bf16[512,384]{1,0:T(8,128)(2,1)S(1)}, bf16[512,384]{1,0:T(8,128)(2,1)S(1)}, u32[]{:S(2)}, u32[]{:S(2)}) collective-permute-start(bf16[512,384]{1,0:T(8,128)(2,1)S(1)} %collective-permute-done.5.refs_3_), channel_id=1, source_target_pairs={{0,16},{1,17},{2,18},{3,19},{4,20},{5,21},{6,22},{7,23},{8,24},{9,... | collective-permute-start | bytes 1179656 | tf_op jit(solution)/shard_map/ppermute | solution.py:396
  42.5 0.1 collective-permute-start.11
  42.6 1.3 %collective-permute-done.10.refs_5_ = bf16[512,384]{1,0:T(8,128)(2,1)S(1)} collective-permute-done((bf16[512,384]{1,0:T(8,128)(2,1)S(1)}, bf16[512,384]{1,0:T(8,128)(2,1)S(1)}, u32[]{:S(2)}, u32[]{:S(2)}) %collective-permute-start.10) | collective-permute-done | bytes 393248 | tf_op jit(solution)/shard_map/ppermute | solution.py:396
  43.8 0.6 collective-permute-done.11.refs_6_
  44.4 0.0 collective-permute-done.12.refs_10_
  44.4 3.5 %shard_map.35 = (f32[8,512]{1,0:T(8,128)S(1)}, f32[8,512]{1,0:T(8,128)S(1)}, f32[16,512]{1,0:T(8,128)S(1)}) custom-call(s32[129]{0:T(256)S(1)} %get-tuple-element.25.refs_0_, s32[129]{0:T(256)S(1)} %get-tuple-element.26.refs_1_, s32[6]{0:T(128)S(1)} %get-tuple-element.27.refs_2_, bf16[512,384]{1,0:T(8,128)(2,1)S(1)} %collective-permute-done.5.refs_3_, ...), custom_call_target="tpu_custom_call" | custom-call | flops 5000000000 | bytes 8000000 | tf_op jit(solution)/shard_map/pallas_call | solution.py:333
  47.9 2.2 %collective-permute-start.13 = (f32[16,512]{1,0:T(8,128)S(1)}, f32[16,512]{1,0:T(8,128)S(1)}, u32[]{:S(2)}, u32[]{:S(2)}) collective-permute-start(f32[16,512]{1,0:T(8,128)S(1)} %get-tuple-element.43), channel_id=1, source_target_pairs={{0,16},{1,17},{2,18},{3,19},{4,20},{5,21},{6,22},{7,23},{8,24},{9,... | collective-permute-start | bytes 98312 | tf_op jit(solution)/shard_map/ppermute | solution.py:396
  50.1 0.9 %collective-permute-done.13 = f32[16,512]{1,0:T(8,128)S(1)} collective-permute-done((f32[16,512]{1,0:T(8,128)S(1)}, f32[16,512]{1,0:T(8,128)S(1)}, u32[]{:S(2)}, u32[]{:S(2)}) %collective-permute-start.13) | collective-permute-done | bytes 32800 | tf_op jit(solution)/shard_map/ppermute | solution.py:396
  51.0 3.8 %collective-permute-start.14 = (f32[8,512]{1,0:T(8,128)S(1)}, f32[8,512]{1,0:T(8,128)S(1)}, u32[]{:S(2)}, u32[]{:S(2)}) collective-permute-start(f32[8,512]{1,0:T(8,128)S(1)} %slice_maximum_fusion), channel_id=1, source_target_pairs={{0,12},{1,13},{2,14},{3,15},{4,8},{5,9},{6,10},{7,11},{8,4},{9,5},... | collective-permute-start | bytes 49160 | tf_op jit(solution)/shard_map/ppermute | solution.py:401
  54.7 1.1 %collective-permute-done.14 = f32[8,512]{1,0:T(8,128)S(1)} collective-permute-done((f32[8,512]{1,0:T(8,128)S(1)}, f32[8,512]{1,0:T(8,128)S(1)}, u32[]{:S(2)}, u32[]{:S(2)}) %collective-permute-start.14) | collective-permute-done | bytes 16416 | tf_op jit(solution)/shard_map/ppermute | solution.py:401
  55.9 0.1 collective-permute-start.15
  55.9 2.8 %collective-permute-done.15 = f32[4,512]{1,0:T(4,128)S(1)} collective-permute-done((f32[4,512]{1,0:T(4,128)S(1)}, f32[4,512]{1,0:T(4,128)S(1)}, u32[]{:S(2)}, u32[]{:S(2)}) %collective-permute-start.15) | collective-permute-done | bytes 8224 | tf_op jit(solution)/shard_map/ppermute | solution.py:401
  58.7 2.3 %collective-permute-start.16 = (f32[2,512]{1,0:T(2,128)S(1)}, f32[2,512]{1,0:T(2,128)S(1)}, u32[]{:S(2)}, u32[]{:S(2)}) collective-permute-start(f32[2,512]{1,0:T(2,128)S(1)} %slice.47), channel_id=1, source_target_pairs={{0,32},{1,33},{2,34},{3,35},{4,36},{5,37},{6,38},{7,39},{8,40},{9,... | collective-permute-start | bytes 12296 | tf_op jit(solution)/shard_map/ppermute | solution.py:401
  61.0 1.5 %collective-permute-done.16 = f32[2,512]{1,0:T(2,128)S(1)} collective-permute-done((f32[2,512]{1,0:T(2,128)S(1)}, f32[2,512]{1,0:T(2,128)S(1)}, u32[]{:S(2)}, u32[]{:S(2)}) %collective-permute-start.16) | collective-permute-done | bytes 4128 | tf_op jit(solution)/shard_map/ppermute | solution.py:401
  62.5 4.4 %collective-permute-start.17 = (f32[512]{0:T(512)S(1)}, f32[512]{0:T(512)S(1)}, u32[]{:S(2)}, u32[]{:S(2)}) collective-permute-start(f32[512]{0:T(512)S(1)} %bitcast.13), channel_id=1, source_target_pairs={{0,16},{1,17},{2,18},{3,19},{4,20},{5,21},{6,22},{7,23},{8,24},{9,... | collective-permute-start | bytes 6152 | tf_op jit(solution)/shard_map/ppermute | solution.py:396
  66.9 0.8 %collective-permute-done.17 = f32[512]{0:T(512)S(1)} collective-permute-done((f32[512]{0:T(512)S(1)}, f32[512]{0:T(512)S(1)}, u32[]{:S(2)}, u32[]{:S(2)}) %collective-permute-start.17) | collective-permute-done | bytes 2080 | tf_op jit(solution)/shard_map/ppermute | solution.py:396
  67.7 0.6 maximum_maximum_fusion
  (10 shorter events, 0.1 us)
Async XLA Ops:
  0.0 9.7 %copy-start.1 = (s32[256]{0:T(256)S(1)}, s32[256]{0:T(256)}, u32[]{:S(2)}) copy-start(s32[256]{0:T(256)} %cluster_ref.3) | copy-start | bytes 3076
  0.0 3.0 %collective-permute-start = (bf16[512,384]{1,0:T(8,128)(2,1)}, bf16[512,384]{1,0:T(8,128)(2,1)S(1)}, u32[]{:S(2)}, u32[]{:S(2)}) collective-permute-start(bf16[512,384]{1,0:T(8,128)(2,1)} %x_ref.1), channel_id=1, source_target_pairs={{0,16},{1,17},{2,18},{3,19},{4,20},{5,21},{6,22},{7,23},{8,24},{9,... | collective-permute-start | bytes 1179656 | tf_op jit(solution)/shard_map/ppermute | solution.py:396
  1.4 1.0 %copy-start = (bf16[512,384]{1,0:T(8,128)(2,1)S(1)}, bf16[512,384]{1,0:T(8,128)(2,1)}, u32[]{:S(2)}) copy-start(bf16[512,384]{1,0:T(8,128)(2,1)} %x_ref.1) | copy-start | bytes 1179652
  3.2 11.5 %collective-permute-start.1 = (bf16[2,512,384]{2,1,0:T(8,128)(2,1)S(1)}, bf16[2,512,384]{2,1,0:T(8,128)(2,1)S(1)}, u32[]{:S(2)}, u32[]{:S(2)}) collective-permute-start(bf16[2,512,384]{2,1,0:T(8,128)(2,1)S(1)} %shard_map.29.unit_ref.refs_3_.refs_7_), channel_id=1, source_target_pairs={{0,4},{1,5},{2,6},{3,7},{4,0},{5,1},{6,2},{7,3},{8,12},{9,13},{10,... | collective-permute-start | bytes 2359304 | tf_op jit(solution)/shard_map/ppermute | solution.py:401
  5.0 13.3 %collective-permute-start.3 = (bf16[2,512,384]{2,1,0:T(8,128)(2,1)S(1)}, bf16[2,512,384]{2,1,0:T(8,128)(2,1)S(1)}, u32[]{:S(2)}, u32[]{:S(2)}) collective-permute-start(bf16[2,512,384]{2,1,0:T(8,128)(2,1)S(1)} %shard_map.29.unit_ref.refs_3_.refs_7_), channel_id=1, source_target_pairs={{0,32},{1,33},{2,34},{3,35},{4,36},{5,37},{6,38},{7,39},{8,40},{9,... | collective-permute-start | bytes 2359304 | tf_op jit(solution)/shard_map/ppermute | solution.py:401
  7.4 12.1 %collective-permute-start.4 = (bf16[2,512,384]{2,1,0:T(8,128)(2,1)S(1)}, bf16[2,512,384]{2,1,0:T(8,128)(2,1)S(1)}, u32[]{:S(2)}, u32[]{:S(2)}) collective-permute-start(bf16[2,512,384]{2,1,0:T(8,128)(2,1)S(1)} %shard_map.29.unit_ref.refs_3_.refs_7_), channel_id=1, source_target_pairs={{0,12},{1,13},{2,14},{3,15},{4,8},{5,9},{6,10},{7,11},{8,4},{9,5},... | collective-permute-start | bytes 2359304 | tf_op jit(solution)/shard_map/ppermute | solution.py:401
  14.6 13.6 %collective-permute-start.2 = (bf16[2,512,384]{2,1,0:T(8,128)(2,1)S(1)}, bf16[2,512,384]{2,1,0:T(8,128)(2,1)S(1)}, u32[]{:S(2)}, u32[]{:S(2)}) collective-permute-start(bf16[2,512,384]{2,1,0:T(8,128)(2,1)S(1)} %collective-permute-done.1.refs_5_), channel_id=1, source_target_pairs={{0,12},{1,13},{2,14},{3,15},{4,8},{5,9},{6,10},{7,11},{8,4},{9,5},... | collective-permute-start | bytes 2359304 | tf_op jit(solution)/shard_map/ppermute | solution.py:401
  19.6 11.1 %collective-permute-start.6 = (bf16[2,512,384]{2,1,0:T(8,128)(2,1)S(1)}, bf16[2,512,384]{2,1,0:T(8,128)(2,1)S(1)}, u32[]{:S(2)}, u32[]{:S(2)}) collective-permute-start(bf16[2,512,384]{2,1,0:T(8,128)(2,1)S(1)} %collective-permute-done.3.refs_4_), channel_id=1, source_target_pairs={{0,4},{1,5},{2,6},{3,7},{4,0},{5,1},{6,2},{7,3},{8,12},{9,13},{10,... | collective-permute-start | bytes 2359304 | tf_op jit(solution)/shard_map/ppermute | solution.py:401
  20.1 12.1 %collective-permute-start.7 = (bf16[2,512,384]{2,1,0:T(8,128)(2,1)S(1)}, bf16[2,512,384]{2,1,0:T(8,128)(2,1)S(1)}, u32[]{:S(2)}, u32[]{:S(2)}) collective-permute-start(bf16[2,512,384]{2,1,0:T(8,128)(2,1)S(1)} %collective-permute-done.4.refs_6_), channel_id=1, source_target_pairs={{0,32},{1,33},{2,34},{3,35},{4,36},{5,37},{6,38},{7,39},{8,40},{9,... | collective-permute-start | bytes 2359304 | tf_op jit(solution)/shard_map/ppermute | solution.py:401
  22.4 13.5 %collective-permute-start.8 = (bf16[6,512,384]{2,1,0:T(8,128)(2,1)S(1)}, bf16[6,512,384]{2,1,0:T(8,128)(2,1)S(1)}, u32[]{:S(2)}, u32[]{:S(2)}) collective-permute-start(bf16[6,512,384]{2,1,0:T(8,128)(2,1)S(1)} %get-tuple-element.31.refs_4_), channel_id=1, source_target_pairs={{0,16},{1,17},{2,18},{3,19},{4,20},{5,21},{6,22},{7,23},{8,24},{9,... | collective-permute-start | bytes 7077896 | tf_op jit(solution)/shard_map/ppermute | solution.py:396
  32.4 12.1 %collective-permute-start.12 = (bf16[6,512,384]{2,1,0:T(8,128)(2,1)S(1)}, bf16[6,512,384]{2,1,0:T(8,128)(2,1)S(1)}, u32[]{:S(2)}, u32[]{:S(2)}) collective-permute-start(bf16[6,512,384]{2,1,0:T(8,128)(2,1)S(1)} %shard_map.33.refs_5_.refs_8_), channel_id=1, source_target_pairs={{0,16},{1,17},{2,18},{3,19},{4,20},{5,21},{6,22},{7,23},{8,24},{9,... | collective-permute-start | bytes 7077896 | tf_op jit(solution)/shard_map/ppermute | solution.py:396
  32.5 8.9 %collective-permute-start.5 = (bf16[512,384]{1,0:T(8,128)(2,1)S(1)}, bf16[512,384]{1,0:T(8,128)(2,1)S(1)}, u32[]{:S(2)}, u32[]{:S(2)}) collective-permute-start(bf16[512,384]{1,0:T(8,128)(2,1)S(1)} %slice_bitcast_fusion.1), channel_id=1, source_target_pairs={{0,32},{1,33},{2,34},{3,35},{4,36},{5,37},{6,38},{7,39},{8,40},{9,... | collective-permute-start | bytes 1179656 | tf_op jit(solution)/shard_map/ppermute | solution.py:401
  34.2 7.2 %collective-permute-start.9 = (bf16[512,384]{1,0:T(8,128)(2,1)S(1)}, bf16[512,384]{1,0:T(8,128)(2,1)S(1)}, u32[]{:S(2)}, u32[]{:S(2)}) collective-permute-start(bf16[512,384]{1,0:T(8,128)(2,1)S(1)} %slice_bitcast_fusion), channel_id=1, source_target_pairs={{0,4},{1,5},{2,6},{3,7},{4,0},{5,1},{6,2},{7,3},{8,12},{9,13},{10,... | collective-permute-start | bytes 1179656 | tf_op jit(solution)/shard_map/ppermute | solution.py:401
  41.5 2.4 %collective-permute-start.10 = (bf16[512,384]{1,0:T(8,128)(2,1)S(1)}, bf16[512,384]{1,0:T(8,128)(2,1)S(1)}, u32[]{:S(2)}, u32[]{:S(2)}) collective-permute-start(bf16[512,384]{1,0:T(8,128)(2,1)S(1)} %collective-permute-done.5.refs_3_), channel_id=1, source_target_pairs={{0,16},{1,17},{2,18},{3,19},{4,20},{5,21},{6,22},{7,23},{8,24},{9,... | collective-permute-start | bytes 1179656 | tf_op jit(solution)/shard_map/ppermute | solution.py:396
  42.5 1.9 %collective-permute-start.11 = (bf16[512,384]{1,0:T(8,128)(2,1)S(1)}, bf16[512,384]{1,0:T(8,128)(2,1)S(1)}, u32[]{:S(2)}, u32[]{:S(2)}) collective-permute-start(bf16[512,384]{1,0:T(8,128)(2,1)S(1)} %collective-permute-done.9.refs_4_), channel_id=1, source_target_pairs={{0,16},{1,17},{2,18},{3,19},{4,20},{5,21},{6,22},{7,23},{8,24},{9,... | collective-permute-start | bytes 1179656 | tf_op jit(solution)/shard_map/ppermute | solution.py:396
  47.9 3.1 %collective-permute-start.13 = (f32[16,512]{1,0:T(8,128)S(1)}, f32[16,512]{1,0:T(8,128)S(1)}, u32[]{:S(2)}, u32[]{:S(2)}) collective-permute-start(f32[16,512]{1,0:T(8,128)S(1)} %get-tuple-element.43), channel_id=1, source_target_pairs={{0,16},{1,17},{2,18},{3,19},{4,20},{5,21},{6,22},{7,23},{8,24},{9,... | collective-permute-start | bytes 98312 | tf_op jit(solution)/shard_map/ppermute | solution.py:396
  51.0 4.9 %collective-permute-start.14 = (f32[8,512]{1,0:T(8,128)S(1)}, f32[8,512]{1,0:T(8,128)S(1)}, u32[]{:S(2)}, u32[]{:S(2)}) collective-permute-start(f32[8,512]{1,0:T(8,128)S(1)} %slice_maximum_fusion), channel_id=1, source_target_pairs={{0,12},{1,13},{2,14},{3,15},{4,8},{5,9},{6,10},{7,11},{8,4},{9,5},... | collective-permute-start | bytes 49160 | tf_op jit(solution)/shard_map/ppermute | solution.py:401
  55.9 2.9 %collective-permute-start.15 = (f32[4,512]{1,0:T(4,128)S(1)}, f32[4,512]{1,0:T(4,128)S(1)}, u32[]{:S(2)}, u32[]{:S(2)}) collective-permute-start(f32[4,512]{1,0:T(4,128)S(1)} %slice.45), channel_id=1, source_target_pairs={{0,4},{1,5},{2,6},{3,7},{4,0},{5,1},{6,2},{7,3},{8,12},{9,13},{10,... | collective-permute-start | bytes 24584 | tf_op jit(solution)/shard_map/ppermute | solution.py:401
  58.7 3.7 %collective-permute-start.16 = (f32[2,512]{1,0:T(2,128)S(1)}, f32[2,512]{1,0:T(2,128)S(1)}, u32[]{:S(2)}, u32[]{:S(2)}) collective-permute-start(f32[2,512]{1,0:T(2,128)S(1)} %slice.47), channel_id=1, source_target_pairs={{0,32},{1,33},{2,34},{3,35},{4,36},{5,37},{6,38},{7,39},{8,40},{9,... | collective-permute-start | bytes 12296 | tf_op jit(solution)/shard_map/ppermute | solution.py:401
  62.5 5.2 %collective-permute-start.17 = (f32[512]{0:T(512)S(1)}, f32[512]{0:T(512)S(1)}, u32[]{:S(2)}, u32[]{:S(2)}) collective-permute-start(f32[512]{0:T(512)S(1)} %bitcast.13), channel_id=1, source_target_pairs={{0,16},{1,17},{2,18},{3,19},{4,20},{5,21},{6,22},{7,23},{8,24},{9,... | collective-permute-start | bytes 6152 | tf_op jit(solution)/shard_map/ppermute | solution.py:396

commit v7 on v6

--- a/solution.py
+++ b/solution.py
@@ -26,19 +26,20 @@
 
 
 EARLY = [(g, 0) for g in (1, 2, 3)]
-MIDDLE = [(g, h) for g in (1, 2, 3) for h in range(1, g + 1)]
-MIDDLE += [(g, h) for g in (4, 5, 6) for h in range(4)]
-LAST = [(g, h) for g in (4, 5, 6, 7) for h in range(4, 8)] + [(7, h) for h in range(4)]
-PHASES = ((EARLY, 1), (MIDDLE, 1), (LAST, 4))
+SECOND = [(g, h) for g in (1, 2, 3) for h in range(1, g + 1)]
+MIDDLE = [(g, h) for g in (4, 5, 6) for h in range(4)]
+LAST = [(g, h) for g in (4, 5, 6) for h in (4, 5, 6)] + [(7, h) for h in range(7)]
+FINAL = [(7, 7)]
+PHASES = ((EARLY, 1, 0), (SECOND, 1, 1), (MIDDLE, 4, 0), (LAST, 4, 0), (FINAL, 7, 7))
 
 
 def shared(g, h):
-    return g == h or (g >= 4 and h >= 4)
-
-
-COUNTS = [sum(2 if shared(g, h) else 4 for g, h in pairs) for pairs, _ in PHASES]
-STARTS = [0, COUNTS[0] + 1, COUNTS[0] + COUNTS[1] + 2]
-LISTS = sum(COUNTS) + 3
+    return g == h or 4 <= min(g, h) <= max(g, h) <= 6
+
+
+COUNTS = [sum(2 if shared(g, h) else 4 for g, h in phase[0]) for phase in PHASES]
+STARTS = [sum(COUNTS[:n]) + n for n in range(len(PHASES))]
+LISTS = sum(COUNTS) + len(PHASES)
 MARGIN = 24
 MOST = 160
 VMEM = pltpu.VMEM
@@ -119,7 +120,7 @@
             ours + MARGIN <= there, 1, jnp.where(there + MARGIN <= ours, 2, 0)
         )
 
-    for phase, (pairs, base) in enumerate(PHASES):
+    for phase, (pairs, base_a, base_b) in enumerate(PHASES):
         full = jnp.int32(STARTS[phase])
         part = jnp.int32(STARTS[phase])
 
@@ -133,7 +134,7 @@
                 | jnp.where((left & 15) == 0, 4, 0)
                 | jnp.where((same & 240) == 0, 8, 0)
             )
-            code = (2 * (g - base) + side) | ((2 * h + far) << 4)
+            code = (2 * (g - base_a) + side) | ((2 * (h - base_b) + far) << 4)
             full_ref[full] = code
             part_ref[part] = code | (quads << 8)
             whole = quads == 15
@@ -285,32 +286,35 @@
         buf[2 * n : 2 * n + 2] = ref[...]
 
 
-def early_kernel(*refs):
-    plan, unit, mine, (pack_ref, row_ref, col_ref) = refs[:3], refs[3], refs[4:7], refs[7:]
-    clear(row_ref, col_ref)
-    put(pack_ref, mine)
-    score_lists(0, *plan, pack_ref, unit, row_ref, col_ref)
-
-
 def pack_kernel(a_ref, b_ref, c_ref, out_ref):
     put(out_ref, (a_ref, b_ref, c_ref))
 
 
-def middle_kernel(*refs):
-    plan, (unit, a_low, a_mid, b_low, row_in, col_in), outs = refs[:3], refs[3:9], refs[9:]
-    rows_out, row_mid, col_ref, a_buf, b_buf, row_ref = outs
-    row_ref[:6] = row_in[...]
-    row_ref[6:] = jnp.full(row_mid.shape, -2.0, jnp.float32)
+def early_kernel(*refs):
+    plan, (a_low, unit, row_ref, col_ref) = refs[:3], refs[3:]
+    clear(row_ref, col_ref)
+    score_lists(0, *plan, a_low, unit, row_ref, col_ref)
+
+
+def second_kernel(*refs):
+    plan, (a_low, unit, b_in, row_in, col_in), outs = refs[:3], refs[3:8], refs[8:]
+    rows_out, col_ref, b_low, row_ref, col_low = outs
+    b_low[:2] = unit[...]
+    b_low[2:] = b_in[...]
+    row_ref[...] = row_in[...]
+    clear(col_low)
+    score_lists(1, *plan, a_low, b_in, row_ref, col_low)
     col_ref[:2] = col_in[...]
-    col_ref[2:] = jnp.full((6, 8, SHARD), -2.0, jnp.float32)
-    a_buf[:6] = a_low[...]
-    a_buf[6:] = a_mid[...]
-    b_buf[:2] = unit[...]
-    b_buf[2:] = b_low[...]
-    score_lists(1, *plan, a_buf, b_buf, row_ref, col_ref)
+    col_ref[2:] = col_low[...]
     for n in range(0, 6, 2):
         put_rows(rows_out, n, row_ref, n)
-    row_mid[...] = row_ref[6:]
+
+
+def middle_kernel(*refs):
+    plan, (a_mid, b_low, col_in, row_ref, col_ref) = refs[:3], refs[3:]
+    clear(row_ref)
+    col_ref[...] = col_in[...]
+    score_lists(2, *plan, a_mid, b_low, row_ref, col_ref)
 
 
 def f32(*shape):
@@ -342,14 +346,19 @@
 
 
 def early_call(plan, *operands):
-    outs = (shards(6), rows_of(6), cols_of(2))
+    outs = (rows_of(6), cols_of(2))
     return kernel_call(early_kernel, [*plan, *operands], outs, [], 3000000000)
 
 
+def second_call(plan, *operands):
+    outs = (f32(6, SHARD), cols_of(8), shards(8))
+    scratch = [rows_of(6), cols_of(6)]
+    return kernel_call(second_kernel, [*plan, *operands], outs, scratch, 3000000000)
+
+
 def middle_call(plan, *operands):
-    outs = (f32(6, SHARD), rows_of(6), cols_of(8))
-    scratch = [shards(12), shards(8), rows_of(12)]
-    return kernel_call(middle_kernel, [*plan, *operands], outs, scratch, 5000000000)
+    outs = (rows_of(6), cols_of(8))
+    return kernel_call(middle_kernel, [*plan, *operands], outs, [], 5000000000)
 
 
 KEPT = (0, 1, 2, 4)
@@ -357,39 +366,54 @@
 
 
 def last_kernel(*refs):
-    plan, mine, theirs, refs = refs[:3], refs[3:5], refs[5:7], refs[7:]
-    unit, a_mid, b_low, b_mid, rows0, row_in, col_in, keep_ref, send_ref, other_ref, *refs = refs
-    a_buf, b_buf, row_ref, col_ref = refs
+    plan, mine, refs = refs[:3], refs[3:5], refs[5:]
+    a_mid, b_low, b_mid, row_in, col_in, row_ref, col_ref, a_buf, b_buf = refs
     a_buf[:6] = a_mid[...]
-    b_buf[:2] = unit[...]
-    b_buf[2:8] = b_low[...]
-    b_buf[8:14] = b_mid[...]
+    b_buf[:8] = b_low[...]
+    b_buf[8:] = b_mid[...]
     for half in range(2):
         a_buf[6 + half] = mine[half][...]
-        b_buf[14 + half] = theirs[half][...]
     row_ref[:6] = row_in[...]
     row_ref[6:] = jnp.full((2, SHARD, 128), -2.0, jnp.float32)
     col_ref[:8] = col_in[...]
-    col_ref[8:] = jnp.full(col_in.shape, -2.0, jnp.float32)
-    score_lists(2, *plan, a_buf, b_buf, row_ref, col_ref)
+    col_ref[8:] = jnp.full((6, 8, SHARD), -2.0, jnp.float32)
+    score_lists(3, *plan, a_buf, b_buf, row_ref, col_ref)
+
+
+def last_call(plan, *operands):
+    outs = (rows_of(8), cols_of(14))
+    return kernel_call(last_kernel, [*plan, *operands], outs, [shards(8), shards(14)], 5000000000)
+
+
+def final_kernel(*refs):
+    plan, mine, theirs, refs = refs[:3], refs[3:5], refs[5:7], refs[7:]
+    rows0, row_in, col_in, keep_ref, send_ref, other_ref, a_buf, b_buf, row_ref, col_ref = refs
+    for half in range(2):
+        a_buf[half] = mine[half][...]
+        b_buf[half] = theirs[half][...]
+    row_ref[...] = row_in[6:]
+    clear(col_ref)
+    score_lists(4, *plan, a_buf, b_buf, row_ref, col_ref)
     keep_ref[0:2] = jnp.full((2, SHARD), -2.0, jnp.float32)
     for out_ref, slots in ((keep_ref, KEPT), (send_ref, SENT)):
         for place, slot in enumerate(slots):
-            if slot > 3:
-                put_rows(out_ref, 2 * place, row_ref, 2 * slot - 8)
+            if slot == 7:
+                put_rows(out_ref, 2 * place, row_ref, 0)
+            elif slot > 3:
+                put_rows(out_ref, 2 * place, row_in, 2 * slot - 8)
             elif slot > 0:
                 out_ref[2 * place : 2 * place + 2] = rows0[2 * slot - 2 : 2 * slot]
     for place, slot in enumerate(KEPT + SENT):
         for half in range(2):
             at = 2 * place + half
-            down = col_ref[2 * slot + half]
+            down = col_ref[half] if slot == 7 else col_in[2 * slot + half]
             other_ref[at : at + 1, :] = jnp.max(down, axis=0, keepdims=True)
 
 
-def last_call(plan, *operands):
+def final_call(plan, *operands):
     outs = (f32(8, SHARD), f32(8, SHARD), f32(16, SHARD))
-    scratch = [shards(8), shards(16), rows_of(8), cols_of(16)]
-    return kernel_call(last_kernel, [*plan, *operands], outs, scratch, 5000000000)
+    scratch = [shards(2), shards(2), rows_of(2), cols_of(2)]
+    return kernel_call(final_kernel, [*plan, *operands], outs, scratch, 500000000)
 
 
 def swap(x):
@@ -416,20 +440,21 @@
 
     own = own_call(here, block_cluster, unit)
     mine.extend(after(x, plan[2], own) for x in step((1, 2, 3)))
-    a_low, rows0, cols = early_call(plan, *mine)
+    a_low = kernel_call(pack_kernel, mine[1:4], shards(6), [], 1000000000, 0)
     b_low = swap(a_low)
-    mine.extend(after(x, a_low) for x in step((4, 5, 6)))
+    rows0, cols = early_call(plan, a_low, unit)
+    rows0, cols, b_low = second_call(plan, a_low, unit, b_low, rows0, cols)
+    mine.extend(after(x, cols) for x in step((4, 5, 6)))
     halves = [
         exchange(mine[source][half], generator) for half, (source, generator) in enumerate(HALVES)
     ]
     a_mid = kernel_call(pack_kernel, mine[4:7], shards(6), [], 1000000000, 0)
     b_mid = swap(a_mid)
-    rows0, rows1, cols = middle_call(plan, unit, a_low, a_mid, b_low, rows0, cols)
+    rows1, cols = middle_call(plan, a_mid, b_low, cols)
     halves = [after(x, cols) for x in halves]
     swapped = [swap(x) for x in halves]
-    keep, send, other = last_call(
-        plan, *halves, *swapped, unit, a_mid, b_low, b_mid, rows0, rows1, cols
-    )
+    rows1, cols = last_call(plan, *halves, a_mid, b_low, b_mid, rows1, cols)
+    keep, send, other = final_call(plan, *halves, *swapped, rows0, rows1, cols)
     other = swap(other)
     keep = jnp.maximum(keep, other[:8])
     send = jnp.maximum(send, other[8:])

time: 68.1 us -> 67.9 us (level); the launches traced: 68.3 us -> 67.3 us
  starting transfers between devices: 30.4 us -> 28.3 us
  waiting for transfers between devices: 20 us -> 21.4 us
    ppermute x11, waiting for transfers between devices: 16.1 us -> 19.3 us  [exchange(): return lax.ppermute(x, ('row', 'col'), pairs)]
    ppermute x7, starting transfers between devices: 9.59 us -> 7.17 us  [swap(): return lax.ppermute(x, ('row', 'col'), [(s, s ^ CORE) for s in range(128)])]
    ppermute x7, waiting for transfers between devices: 3.91 us -> 2.1 us  [swap(): return lax.ppermute(x, ('row', 'col'), [(s, s ^ CORE) for s in range(128)])]
    pallas_call x4 -> x7, Pallas kernels: 10.8 us -> 10.6 us  [kernel_call(): pl.pallas_call(kernel, out_shape=outs, in_specs=[spec(SMEM)] * smem + [sp...]
  transfers between devices with their start and end apart: 18 -> 18, of which waited for: 12 -> 14; matrix products, arithmetic and copies ran while one was open for 0% -> 0% of each run, Pallas kernels for 18% -> 21%
where the time goes in v7:
time: 67.9 us; the launch traced here: 67.3 us
  starting transfers between devices  28.3 us (42%)
  waiting for transfers between devices  21.4 us (32%)
  Pallas kernels  15.9 us (23%)
  local copies, waits for them, and re-layouts  1.09 us (2%)
    ppermute x11, starting transfers between devices, exchange(): return lax.ppermute(x, ('row', 'col'), pairs)  21.1 us
    ppermute x11, waiting for transfers between devices, exchange(): return lax.ppermute(x, ('row', 'col'), pairs)  19.3 us
    pallas_call x7, Pallas kernels, kernel_call(): pl.pallas_call(kernel, out_shape=outs, in_specs=[spec(SMEM)] * smem + [sp...  10.6 us
    ppermute x7, starting transfers between devices, swap(): return lax.ppermute(x, ('row', 'col'), [(s, s ^ CORE) for s in range(128)])  7.17 us
    pallas_call x1, Pallas kernels, plan_call(): pl.pallas_call(plan_kernel, out_shape=(lists, lists, jax.ShapeDtypeStruct...  3.59 us
    ppermute x7, waiting for transfers between devices, swap(): return lax.ppermute(x, ('row', 'col'), [(s, s ^ CORE) for s in range(128)])  2.1 us
  transfers between devices with their start and end apart: 18, of which 14 were waited for; matrix products, arithmetic and copies ran while one was open for 0% of the time, Pallas kernels for 21%

profile of v7, /device:TPU:1, one launch (start us, length us, event | category | flops | bytes accessed | tf_op | source)
XLA Modules:
  0.0 67.3 jit_solution(4600991954588459569)
XLA Ops:
  0.0 1.4 %collective-permute-start = (bf16[512,384]{1,0:T(8,128)(2,1)}, bf16[512,384]{1,0:T(8,128)(2,1)S(1)}, u32[]{:S(2)}, u32[]{:S(2)}) collective-permute-start(bf16[512,384]{1,0:T(8,128)(2,1)} %x_ref.1), channel_id=1, source_target_pairs={{0,16},{1,17},{2,18},{3,19},{4,20},{5,21},{6,22},{7,23},{8,24},{9,... | collective-permute-start | bytes 1179656 | tf_op jit(solution)/shard_map/ppermute | solution.py:420
  1.4 1.0 %copy-done = bf16[512,384]{1,0:T(8,128)(2,1)S(1)} copy-done((bf16[512,384]{1,0:T(8,128)(2,1)S(1)}, bf16[512,384]{1,0:T(8,128)(2,1)}, u32[]{:S(2)}) %copy-start) | copy-done | bytes 393240
  2.4 0.2 shard_map.28.own_ref
  2.6 0.4 collective-permute-done.other_ref
  3.0 0.2 shard_map.29.unit_ref.refs_4_
  3.2 2.6 %collective-permute-start.3 = (bf16[2,512,384]{2,1,0:T(8,128)(2,1)S(1)}, bf16[2,512,384]{2,1,0:T(8,128)(2,1)S(1)}, u32[]{:S(2)}, u32[]{:S(2)}) collective-permute-start(bf16[2,512,384]{2,1,0:T(8,128)(2,1)S(1)} %shard_map.29.unit_ref.refs_4_), channel_id=1, source_target_pairs={{0,32},{1,33},{2,34},{3,35},{4,36},{5,37},{6,38},{7,39},{8,40},{9,... | collective-permute-start | bytes 2359304 | tf_op jit(solution)/shard_map/ppermute | solution.py:425
  5.8 3.8 %collective-permute-start.4 = (bf16[2,512,384]{2,1,0:T(8,128)(2,1)S(1)}, bf16[2,512,384]{2,1,0:T(8,128)(2,1)S(1)}, u32[]{:S(2)}, u32[]{:S(2)}) collective-permute-start(bf16[2,512,384]{2,1,0:T(8,128)(2,1)S(1)} %shard_map.29.unit_ref.refs_4_), channel_id=1, source_target_pairs={{0,12},{1,13},{2,14},{3,15},{4,8},{5,9},{6,10},{7,11},{8,4},{9,5},... | collective-permute-start | bytes 2359304 | tf_op jit(solution)/shard_map/ppermute | solution.py:425
  9.6 0.0 collective-permute-start.1
  9.6 3.6 %shard_map.31 = (s32[131]{0:T(256)S(1)}, s32[131]{0:T(256)S(1)}, s32[10]{0:T(128)S(1)}) custom-call(s32[1]{0:T(128)} %bitcast.here_ref, s32[256]{0:T(256)S(1)} %copy-done.1, s32[2,128]{1,0:T(2,128)S(1)} %bitcast.11), custom_call_target="tpu_custom_call" | custom-call | flops 3000000000 | bytes 10000 | tf_op jit(solution)/shard_map/pallas_call | solution.py:194
  13.2 1.3 %shard_map.30 = f32[1,512]{1,0:T(1,128)S(1)} custom-call(s32[1]{0:T(128)} %bitcast.here_ref, s32[256]{0:T(256)S(1)} %copy-done.1, bf16[2,512,384]{2,1,0:T(8,128)(2,1)S(1)} %shard_map.29.unit_ref.refs_4_), custom_call_target="tpu_custom_call" | custom-call | flops 1000000000 | bytes 1000000 | tf_op jit(solution)/shard_map/pallas_call | solution.py:206
  14.5 1.1 %collective-permute-done.3.a_ref = bf16[2,512,384]{2,1,0:T(8,128)(2,1)S(1)} collective-permute-done((bf16[2,512,384]{2,1,0:T(8,128)(2,1)S(1)}, bf16[2,512,384]{2,1,0:T(8,128)(2,1)S(1)}, u32[]{:S(2)}, u32[]{:S(2)}) %collective-permute-start.3) | collective-permute-done | bytes 786464 | tf_op jit(solution)/shard_map/ppermute | solution.py:425
  15.6 3.4 %collective-permute-done.4.c_ref = bf16[2,512,384]{2,1,0:T(8,128)(2,1)S(1)} collective-permute-done((bf16[2,512,384]{2,1,0:T(8,128)(2,1)S(1)}, bf16[2,512,384]{2,1,0:T(8,128)(2,1)S(1)}, u32[]{:S(2)}, u32[]{:S(2)}) %collective-permute-start.4) | collective-permute-done | bytes 786464 | tf_op jit(solution)/shard_map/ppermute | solution.py:425
  18.9 1.5 %collective-permute-done.1.b_ref = bf16[2,512,384]{2,1,0:T(8,128)(2,1)S(1)} collective-permute-done((bf16[2,512,384]{2,1,0:T(8,128)(2,1)S(1)}, bf16[2,512,384]{2,1,0:T(8,128)(2,1)S(1)}, u32[]{:S(2)}, u32[]{:S(2)}) %collective-permute-start.1) | collective-permute-done | bytes 786464 | tf_op jit(solution)/shard_map/ppermute | solution.py:425
  20.4 0.2 shard_map.32.refs_3_
  20.6 0.1 collective-permute-start.5
  20.7 1.6 %collective-permute-start.8 = (bf16[2,512,384]{2,1,0:T(8,128)(2,1)S(1)}, bf16[2,512,384]{2,1,0:T(8,128)(2,1)S(1)}, u32[]{:S(2)}, u32[]{:S(2)}) collective-permute-start(bf16[2,512,384]{2,1,0:T(8,128)(2,1)S(1)} %collective-permute-done.4.c_ref), channel_id=1, source_target_pairs={{0,32},{1,33},{2,34},{3,35},{4,36},{5,37},{6,38},{7,39},{8,40},{9,... | collective-permute-start | bytes 2359304 | tf_op jit(solution)/shard_map/ppermute | solution.py:425
  22.3 1.6 %collective-permute-start.7 = (bf16[2,512,384]{2,1,0:T(8,128)(2,1)S(1)}, bf16[2,512,384]{2,1,0:T(8,128)(2,1)S(1)}, u32[]{:S(2)}, u32[]{:S(2)}) collective-permute-start(bf16[2,512,384]{2,1,0:T(8,128)(2,1)S(1)} %collective-permute-done.3.a_ref), channel_id=1, source_target_pairs={{0,4},{1,5},{2,6},{3,7},{4,0},{5,1},{6,2},{7,3},{8,12},{9,13},{10,... | collective-permute-start | bytes 2359304 | tf_op jit(solution)/shard_map/ppermute | solution.py:425
  23.9 2.2 %collective-permute-start.2 = (bf16[2,512,384]{2,1,0:T(8,128)(2,1)S(1)}, bf16[2,512,384]{2,1,0:T(8,128)(2,1)S(1)}, u32[]{:S(2)}, u32[]{:S(2)}) collective-permute-start(bf16[2,512,384]{2,1,0:T(8,128)(2,1)S(1)} %collective-permute-done.1.b_ref), channel_id=1, source_target_pairs={{0,12},{1,13},{2,14},{3,15},{4,8},{5,9},{6,10},{7,11},{8,4},{9,5},... | collective-permute-start | bytes 2359304 | tf_op jit(solution)/shard_map/ppermute | solution.py:425
  26.2 1.4 %shard_map.33 = (f32[6,512,128]{2,1,0:T(8,128)S(1)}, f32[2,8,512]{2,1,0:T(8,128)S(1)}) custom-call(s32[131]{0:T(256)S(1)} %get-tuple-element.28.refs_0_, s32[131]{0:T(256)S(1)} %get-tuple-element.29.refs_1_, s32[10]{0:T(128)S(1)} %get-tuple-element.30.refs_2_, bf16[6,512,384]{2,1,0:T(8,128)(2,1)S(1)} %shard_map.32.refs_3_, ...), custom_call_target="tpu_custom_call" | custom-call | flops 3000000000 | bytes 8000000 | tf_op jit(solution)/shard_map/pallas_call | solution.py:337
  27.6 0.0 collective-permute-done.5.refs_5_
  27.6 3.2 %shard_map.34 = (f32[6,512]{1,0:T(8,128)S(1)}, f32[8,8,512]{2,1,0:T(8,128)S(1)}, bf16[8,512,384]{2,1,0:T(8,128)(2,1)S(1)}) custom-call(s32[131]{0:T(256)S(1)} %get-tuple-element.28.refs_0_, s32[131]{0:T(256)S(1)} %get-tuple-element.29.refs_1_, s32[10]{0:T(128)S(1)} %get-tuple-element.30.refs_2_, bf16[6,512,384]{2,1,0:T(8,128)(2,1)S(1)} %shard_map.32.refs_3_, ...), custom_call_target="tpu_custom_call" | custom-call | flops 3000000000 | bytes 8000000 | tf_op jit(solution)/shard_map/pallas_call | solution.py:337
  30.8 2.3 %collective-permute-done.8.c_ref = bf16[2,512,384]{2,1,0:T(8,128)(2,1)S(1)} collective-permute-done((bf16[2,512,384]{2,1,0:T(8,128)(2,1)S(1)}, bf16[2,512,384]{2,1,0:T(8,128)(2,1)S(1)}, u32[]{:S(2)}, u32[]{:S(2)}) %collective-permute-start.8) | collective-permute-done | bytes 786464 | tf_op jit(solution)/shard_map/ppermute | solution.py:425
  33.1 0.5 collective-permute-done.7.a_ref
  33.6 2.4 %collective-permute-done.2.b_ref = bf16[2,512,384]{2,1,0:T(8,128)(2,1)S(1)} collective-permute-done((bf16[2,512,384]{2,1,0:T(8,128)(2,1)S(1)}, bf16[2,512,384]{2,1,0:T(8,128)(2,1)S(1)}, u32[]{:S(2)}, u32[]{:S(2)}) %collective-permute-start.2) | collective-permute-done | bytes 786464 | tf_op jit(solution)/shard_map/ppermute | solution.py:425
  36.0 0.2 shard_map.35.refs_3_.refs_5_
  36.2 0.5 collective-permute-start.12
  36.7 0.2 collective-permute-start.9
  36.9 2.3 %collective-permute-start.6 = (bf16[512,384]{1,0:T(8,128)(2,1)S(1)}, bf16[512,384]{1,0:T(8,128)(2,1)S(1)}, u32[]{:S(2)}, u32[]{:S(2)}) collective-permute-start(bf16[512,384]{1,0:T(8,128)(2,1)S(1)} %slice_bitcast_fusion.1), channel_id=1, source_target_pairs={{0,32},{1,33},{2,34},{3,35},{4,36},{5,37},{6,38},{7,39},{8,40},{9,... | collective-permute-start | bytes 1179656 | tf_op jit(solution)/shard_map/ppermute | solution.py:425
  39.3 2.0 %shard_map.36 = (f32[6,512,128]{2,1,0:T(8,128)S(1)}, f32[8,8,512]{2,1,0:T(8,128)S(1)}) custom-call(s32[131]{0:T(256)S(1)} %get-tuple-element.28.refs_0_, s32[131]{0:T(256)S(1)} %get-tuple-element.29.refs_1_, s32[10]{0:T(128)S(1)} %get-tuple-element.30.refs_2_, bf16[6,512,384]{2,1,0:T(8,128)(2,1)S(1)} %shard_map.35.refs_3_.refs_5_, ...), custom_call_target="tpu_custom_call" | custom-call | flops 5000000000 | bytes 8000000 | tf_op jit(solution)/shard_map/pallas_call | solution.py:337
  41.3 2.4 %collective-permute-done.9.refs_4_ = bf16[512,384]{1,0:T(8,128)(2,1)S(1)} collective-permute-done((bf16[512,384]{1,0:T(8,128)(2,1)S(1)}, bf16[512,384]{1,0:T(8,128)(2,1)S(1)}, u32[]{:S(2)}, u32[]{:S(2)}) %collective-permute-start.9) | collective-permute-done | bytes 393248 | tf_op jit(solution)/shard_map/ppermute | solution.py:425
  43.7 1.2 %collective-permute-done.6.refs_3_ = bf16[512,384]{1,0:T(8,128)(2,1)S(1)} collective-permute-done((bf16[512,384]{1,0:T(8,128)(2,1)S(1)}, bf16[512,384]{1,0:T(8,128)(2,1)S(1)}, u32[]{:S(2)}, u32[]{:S(2)}) %collective-permute-start.6) | collective-permute-done | bytes 393248 | tf_op jit(solution)/shard_map/ppermute | solution.py:425
  44.9 0.3 collective-permute-start.11
  45.1 0.2 collective-permute-start.10
  45.4 0.0 collective-permute-done.12.refs_7_
  45.4 2.2 %shard_map.37 = (f32[8,512,128]{2,1,0:T(8,128)S(1)}, f32[14,8,512]{2,1,0:T(8,128)S(1)}) custom-call(s32[131]{0:T(256)S(1)} %get-tuple-element.28.refs_0_, s32[131]{0:T(256)S(1)} %get-tuple-element.29.refs_1_, s32[10]{0:T(128)S(1)} %get-tuple-element.30.refs_2_, bf16[512,384]{1,0:T(8,128)(2,1)S(1)} %collective-permute-done.6.refs_3_, ...), custom_call_target="tpu_custom_call" | custom-call | flops 5000000000 | bytes 8000000 | tf_op jit(solution)/shard_map/pallas_call | solution.py:337
  47.6 0.0 collective-permute-done.11.refs_6_
  47.6 1.4 %shard_map.38 = (f32[8,512]{1,0:T(8,128)S(1)}, f32[8,512]{1,0:T(8,128)S(1)}, f32[16,512]{1,0:T(8,128)S(1)}) custom-call(s32[131]{0:T(256)S(1)} %get-tuple-element.28.refs_0_, s32[131]{0:T(256)S(1)} %get-tuple-element.29.refs_1_, s32[10]{0:T(128)S(1)} %get-tuple-element.30.refs_2_, bf16[512,384]{1,0:T(8,128)(2,1)S(1)} %collective-permute-done.6.refs_3_, ...), custom_call_target="tpu_custom_call" | custom-call | flops 500000000 | bytes 8000000 | tf_op jit(solution)/shard_map/pallas_call | solution.py:337
  49.0 2.7 %collective-permute-start.13 = (f32[16,512]{1,0:T(8,128)S(1)}, f32[16,512]{1,0:T(8,128)S(1)}, u32[]{:S(2)}, u32[]{:S(2)}) collective-permute-start(f32[16,512]{1,0:T(8,128)S(1)} %get-tuple-element.49), channel_id=1, source_target_pairs={{0,16},{1,17},{2,18},{3,19},{4,20},{5,21},{6,22},{7,23},{8,24},{9,... | collective-permute-start | bytes 98312 | tf_op jit(solution)/shard_map/ppermute | solution.py:420
  51.7 0.9 %collective-permute-done.13 = f32[16,512]{1,0:T(8,128)S(1)} collective-permute-done((f32[16,512]{1,0:T(8,128)S(1)}, f32[16,512]{1,0:T(8,128)S(1)}, u32[]{:S(2)}, u32[]{:S(2)}) %collective-permute-start.13) | collective-permute-done | bytes 32800 | tf_op jit(solution)/shard_map/ppermute | solution.py:420
  52.5 2.5 %collective-permute-start.14 = (f32[8,512]{1,0:T(8,128)S(1)}, f32[8,512]{1,0:T(8,128)S(1)}, u32[]{:S(2)}, u32[]{:S(2)}) collective-permute-start(f32[8,512]{1,0:T(8,128)S(1)} %slice_maximum_fusion), channel_id=1, source_target_pairs={{0,12},{1,13},{2,14},{3,15},{4,8},{5,9},{6,10},{7,11},{8,4},{9,5},... | collective-permute-start | bytes 49160 | tf_op jit(solution)/shard_map/ppermute | solution.py:425
  55.1 1.3 %collective-permute-done.14 = f32[8,512]{1,0:T(8,128)S(1)} collective-permute-done((f32[8,512]{1,0:T(8,128)S(1)}, f32[8,512]{1,0:T(8,128)S(1)}, u32[]{:S(2)}, u32[]{:S(2)}) %collective-permute-start.14) | collective-permute-done | bytes 16416 | tf_op jit(solution)/shard_map/ppermute | solution.py:425
  56.4 0.2 collective-permute-start.15
  56.6 2.4 %collective-permute-done.15 = f32[4,512]{1,0:T(4,128)S(1)} collective-permute-done((f32[4,512]{1,0:T(4,128)S(1)}, f32[4,512]{1,0:T(4,128)S(1)}, u32[]{:S(2)}, u32[]{:S(2)}) %collective-permute-start.15) | collective-permute-done | bytes 8224 | tf_op jit(solution)/shard_map/ppermute | solution.py:425
  59.0 3.9 %collective-permute-start.16 = (f32[2,512]{1,0:T(2,128)S(1)}, f32[2,512]{1,0:T(2,128)S(1)}, u32[]{:S(2)}, u32[]{:S(2)}) collective-permute-start(f32[2,512]{1,0:T(2,128)S(1)} %slice.47), channel_id=1, source_target_pairs={{0,32},{1,33},{2,34},{3,35},{4,36},{5,37},{6,38},{7,39},{8,40},{9,... | collective-permute-start | bytes 12296 | tf_op jit(solution)/shard_map/ppermute | solution.py:425
  62.9 1.0 %collective-permute-done.16 = f32[2,512]{1,0:T(2,128)S(1)} collective-permute-done((f32[2,512]{1,0:T(2,128)S(1)}, f32[2,512]{1,0:T(2,128)S(1)}, u32[]{:S(2)}, u32[]{:S(2)}) %collective-permute-start.16) | collective-permute-done | bytes 4128 | tf_op jit(solution)/shard_map/ppermute | solution.py:425
  63.9 2.0 %collective-permute-start.17 = (f32[512]{0:T(512)S(1)}, f32[512]{0:T(512)S(1)}, u32[]{:S(2)}, u32[]{:S(2)}) collective-permute-start(f32[512]{0:T(512)S(1)} %bitcast.13), channel_id=1, source_target_pairs={{0,16},{1,17},{2,18},{3,19},{4,20},{5,21},{6,22},{7,23},{8,24},{9,... | collective-permute-start | bytes 6152 | tf_op jit(solution)/shard_map/ppermute | solution.py:420
  65.9 0.8 %collective-permute-done.17 = f32[512]{0:T(512)S(1)} collective-permute-done((f32[512]{0:T(512)S(1)}, f32[512]{0:T(512)S(1)}, u32[]{:S(2)}, u32[]{:S(2)}) %collective-permute-start.17) | collective-permute-done | bytes 2080 | tf_op jit(solution)/shard_map/ppermute | solution.py:420
  66.7 0.6 maximum_maximum_fusion
  (13 shorter events, 0.1 us)
Async XLA Ops:
  0.0 9.6 %copy-start.1 = (s32[256]{0:T(256)S(1)}, s32[256]{0:T(256)}, u32[]{:S(2)}) copy-start(s32[256]{0:T(256)} %cluster_ref.3) | copy-start | bytes 3076
  0.0 3.0 %collective-permute-start = (bf16[512,384]{1,0:T(8,128)(2,1)}, bf16[512,384]{1,0:T(8,128)(2,1)S(1)}, u32[]{:S(2)}, u32[]{:S(2)}) collective-permute-start(bf16[512,384]{1,0:T(8,128)(2,1)} %x_ref.1), channel_id=1, source_target_pairs={{0,16},{1,17},{2,18},{3,19},{4,20},{5,21},{6,22},{7,23},{8,24},{9,... | collective-permute-start | bytes 1179656 | tf_op jit(solution)/shard_map/ppermute | solution.py:420
  1.4 1.0 %copy-start = (bf16[512,384]{1,0:T(8,128)(2,1)S(1)}, bf16[512,384]{1,0:T(8,128)(2,1)}, u32[]{:S(2)}) copy-start(bf16[512,384]{1,0:T(8,128)(2,1)} %x_ref.1) | copy-start | bytes 1179652
  3.2 12.4 %collective-permute-start.3 = (bf16[2,512,384]{2,1,0:T(8,128)(2,1)S(1)}, bf16[2,512,384]{2,1,0:T(8,128)(2,1)S(1)}, u32[]{:S(2)}, u32[]{:S(2)}) collective-permute-start(bf16[2,512,384]{2,1,0:T(8,128)(2,1)S(1)} %shard_map.29.unit_ref.refs_4_), channel_id=1, source_target_pairs={{0,32},{1,33},{2,34},{3,35},{4,36},{5,37},{6,38},{7,39},{8,40},{9,... | collective-permute-start | bytes 2359304 | tf_op jit(solution)/shard_map/ppermute | solution.py:425
  5.8 13.1 %collective-permute-start.4 = (bf16[2,512,384]{2,1,0:T(8,128)(2,1)S(1)}, bf16[2,512,384]{2,1,0:T(8,128)(2,1)S(1)}, u32[]{:S(2)}, u32[]{:S(2)}) collective-permute-start(bf16[2,512,384]{2,1,0:T(8,128)(2,1)S(1)} %shard_map.29.unit_ref.refs_4_), channel_id=1, source_target_pairs={{0,12},{1,13},{2,14},{3,15},{4,8},{5,9},{6,10},{7,11},{8,4},{9,5},... | collective-permute-start | bytes 2359304 | tf_op jit(solution)/shard_map/ppermute | solution.py:425
  9.6 10.8 %collective-permute-start.1 = (bf16[2,512,384]{2,1,0:T(8,128)(2,1)S(1)}, bf16[2,512,384]{2,1,0:T(8,128)(2,1)S(1)}, u32[]{:S(2)}, u32[]{:S(2)}) collective-permute-start(bf16[2,512,384]{2,1,0:T(8,128)(2,1)S(1)} %shard_map.29.unit_ref.refs_4_), channel_id=1, source_target_pairs={{0,4},{1,5},{2,6},{3,7},{4,0},{5,1},{6,2},{7,3},{8,12},{9,13},{10,... | collective-permute-start | bytes 2359304 | tf_op jit(solution)/shard_map/ppermute | solution.py:425
  20.6 7.0 %collective-permute-start.5 = (bf16[6,512,384]{2,1,0:T(8,128)(2,1)S(1)}, bf16[6,512,384]{2,1,0:T(8,128)(2,1)S(1)}, u32[]{:S(2)}, u32[]{:S(2)}) collective-permute-start(bf16[6,512,384]{2,1,0:T(8,128)(2,1)S(1)} %shard_map.32.refs_3_), channel_id=1, source_target_pairs={{0,16},{1,17},{2,18},{3,19},{4,20},{5,21},{6,22},{7,23},{8,24},{9,... | collective-permute-start | bytes 7077896 | tf_op jit(solution)/shard_map/ppermute | solution.py:420
  20.7 12.4 %collective-permute-start.8 = (bf16[2,512,384]{2,1,0:T(8,128)(2,1)S(1)}, bf16[2,512,384]{2,1,0:T(8,128)(2,1)S(1)}, u32[]{:S(2)}, u32[]{:S(2)}) collective-permute-start(bf16[2,512,384]{2,1,0:T(8,128)(2,1)S(1)} %collective-permute-done.4.c_ref), channel_id=1, source_target_pairs={{0,32},{1,33},{2,34},{3,35},{4,36},{5,37},{6,38},{7,39},{8,40},{9,... | collective-permute-start | bytes 2359304 | tf_op jit(solution)/shard_map/ppermute | solution.py:425
  22.3 11.3 %collective-permute-start.7 = (bf16[2,512,384]{2,1,0:T(8,128)(2,1)S(1)}, bf16[2,512,384]{2,1,0:T(8,128)(2,1)S(1)}, u32[]{:S(2)}, u32[]{:S(2)}) collective-permute-start(bf16[2,512,384]{2,1,0:T(8,128)(2,1)S(1)} %collective-permute-done.3.a_ref), channel_id=1, source_target_pairs={{0,4},{1,5},{2,6},{3,7},{4,0},{5,1},{6,2},{7,3},{8,12},{9,13},{10,... | collective-permute-start | bytes 2359304 | tf_op jit(solution)/shard_map/ppermute | solution.py:425
  23.9 12.1 %collective-permute-start.2 = (bf16[2,512,384]{2,1,0:T(8,128)(2,1)S(1)}, bf16[2,512,384]{2,1,0:T(8,128)(2,1)S(1)}, u32[]{:S(2)}, u32[]{:S(2)}) collective-permute-start(bf16[2,512,384]{2,1,0:T(8,128)(2,1)S(1)} %collective-permute-done.1.b_ref), channel_id=1, source_target_pairs={{0,12},{1,13},{2,14},{3,15},{4,8},{5,9},{6,10},{7,11},{8,4},{9,5},... | collective-permute-start | bytes 2359304 | tf_op jit(solution)/shard_map/ppermute | solution.py:425
  36.2 9.2 %collective-permute-start.12 = (bf16[6,512,384]{2,1,0:T(8,128)(2,1)S(1)}, bf16[6,512,384]{2,1,0:T(8,128)(2,1)S(1)}, u32[]{:S(2)}, u32[]{:S(2)}) collective-permute-start(bf16[6,512,384]{2,1,0:T(8,128)(2,1)S(1)} %shard_map.35.refs_3_.refs_5_), channel_id=1, source_target_pairs={{0,16},{1,17},{2,18},{3,19},{4,20},{5,21},{6,22},{7,23},{8,24},{9,... | collective-permute-start | bytes 7077896 | tf_op jit(solution)/shard_map/ppermute | solution.py:420
  36.7 7.0 %collective-permute-start.9 = (bf16[512,384]{1,0:T(8,128)(2,1)S(1)}, bf16[512,384]{1,0:T(8,128)(2,1)S(1)}, u32[]{:S(2)}, u32[]{:S(2)}) collective-permute-start(bf16[512,384]{1,0:T(8,128)(2,1)S(1)} %slice_bitcast_fusion), channel_id=1, source_target_pairs={{0,4},{1,5},{2,6},{3,7},{4,0},{5,1},{6,2},{7,3},{8,12},{9,13},{10,... | collective-permute-start | bytes 1179656 | tf_op jit(solution)/shard_map/ppermute | solution.py:425
  36.9 7.9 %collective-permute-start.6 = (bf16[512,384]{1,0:T(8,128)(2,1)S(1)}, bf16[512,384]{1,0:T(8,128)(2,1)S(1)}, u32[]{:S(2)}, u32[]{:S(2)}) collective-permute-start(bf16[512,384]{1,0:T(8,128)(2,1)S(1)} %slice_bitcast_fusion.1), channel_id=1, source_target_pairs={{0,32},{1,33},{2,34},{3,35},{4,36},{5,37},{6,38},{7,39},{8,40},{9,... | collective-permute-start | bytes 1179656 | tf_op jit(solution)/shard_map/ppermute | solution.py:425
  44.9 2.8 %collective-permute-start.11 = (bf16[512,384]{1,0:T(8,128)(2,1)S(1)}, bf16[512,384]{1,0:T(8,128)(2,1)S(1)}, u32[]{:S(2)}, u32[]{:S(2)}) collective-permute-start(bf16[512,384]{1,0:T(8,128)(2,1)S(1)} %collective-permute-done.9.refs_4_), channel_id=1, source_target_pairs={{0,16},{1,17},{2,18},{3,19},{4,20},{5,21},{6,22},{7,23},{8,24},{9,... | collective-permute-start | bytes 1179656 | tf_op jit(solution)/shard_map/ppermute | solution.py:420
  45.1 2.5 %collective-permute-start.10 = (bf16[512,384]{1,0:T(8,128)(2,1)S(1)}, bf16[512,384]{1,0:T(8,128)(2,1)S(1)}, u32[]{:S(2)}, u32[]{:S(2)}) collective-permute-start(bf16[512,384]{1,0:T(8,128)(2,1)S(1)} %collective-permute-done.6.refs_3_), channel_id=1, source_target_pairs={{0,16},{1,17},{2,18},{3,19},{4,20},{5,21},{6,22},{7,23},{8,24},{9,... | collective-permute-start | bytes 1179656 | tf_op jit(solution)/shard_map/ppermute | solution.py:420
  49.0 3.5 %collective-permute-start.13 = (f32[16,512]{1,0:T(8,128)S(1)}, f32[16,512]{1,0:T(8,128)S(1)}, u32[]{:S(2)}, u32[]{:S(2)}) collective-permute-start(f32[16,512]{1,0:T(8,128)S(1)} %get-tuple-element.49), channel_id=1, source_target_pairs={{0,16},{1,17},{2,18},{3,19},{4,20},{5,21},{6,22},{7,23},{8,24},{9,... | collective-permute-start | bytes 98312 | tf_op jit(solution)/shard_map/ppermute | solution.py:420
  52.5 3.8 %collective-permute-start.14 = (f32[8,512]{1,0:T(8,128)S(1)}, f32[8,512]{1,0:T(8,128)S(1)}, u32[]{:S(2)}, u32[]{:S(2)}) collective-permute-start(f32[8,512]{1,0:T(8,128)S(1)} %slice_maximum_fusion), channel_id=1, source_target_pairs={{0,12},{1,13},{2,14},{3,15},{4,8},{5,9},{6,10},{7,11},{8,4},{9,5},... | collective-permute-start | bytes 49160 | tf_op jit(solution)/shard_map/ppermute | solution.py:425
  56.4 2.6 %collective-permute-start.15 = (f32[4,512]{1,0:T(4,128)S(1)}, f32[4,512]{1,0:T(4,128)S(1)}, u32[]{:S(2)}, u32[]{:S(2)}) collective-permute-start(f32[4,512]{1,0:T(4,128)S(1)} %slice.45), channel_id=1, source_target_pairs={{0,4},{1,5},{2,6},{3,7},{4,0},{5,1},{6,2},{7,3},{8,12},{9,13},{10,... | collective-permute-start | bytes 24584 | tf_op jit(solution)/shard_map/ppermute | solution.py:425
  59.0 4.9 %collective-permute-start.16 = (f32[2,512]{1,0:T(2,128)S(1)}, f32[2,512]{1,0:T(2,128)S(1)}, u32[]{:S(2)}, u32[]{:S(2)}) collective-permute-start(f32[2,512]{1,0:T(2,128)S(1)} %slice.47), channel_id=1, source_target_pairs={{0,32},{1,33},{2,34},{3,35},{4,36},{5,37},{6,38},{7,39},{8,40},{9,... | collective-permute-start | bytes 12296 | tf_op jit(solution)/shard_map/ppermute | solution.py:425
  63.9 2.8 %collective-permute-start.17 = (f32[512]{0:T(512)S(1)}, f32[512]{0:T(512)S(1)}, u32[]{:S(2)}, u32[]{:S(2)}) collective-permute-start(f32[512]{0:T(512)S(1)} %bitcast.13), channel_id=1, source_target_pairs={{0,16},{1,17},{2,18},{3,19},{4,20},{5,21},{6,22},{7,23},{8,24},{9,... | collective-permute-start | bytes 6152 | tf_op jit(solution)/shard_map/ppermute | solution.py:420

commit v8 on v7

--- a/solution.py
+++ b/solution.py
@@ -270,10 +270,16 @@
 
 def put_rows(out_ref, place, row_ref, first):
     for half in range(2):
-        at = place + half
         for k in range(SHARD // 128):
             part = row_ref[first + half, 128 * k : 128 * k + 128, :].T
-            out_ref[at : at + 1, 128 * k : 128 * k + 128] = jnp.max(part, axis=0, keepdims=True)
+            out_ref[place, pl.ds(4 * half + k, 1), :] = jnp.max(part, axis=0, keepdims=True)
+
+
+def put_cols(out_ref, place, col_ref, first):
+    for half in range(2):
+        down = jnp.max(col_ref[first + half], axis=0, keepdims=True)
+        for k in range(SHARD // 128):
+            out_ref[place, pl.ds(4 * half + k, 1), :] = down[:, 128 * k : 128 * k + 128]
 
 
 def clear(*refs):
@@ -306,8 +312,8 @@
     score_lists(1, *plan, a_low, b_in, row_ref, col_low)
     col_ref[:2] = col_in[...]
     col_ref[2:] = col_low[...]
-    for n in range(0, 6, 2):
-        put_rows(rows_out, n, row_ref, n)
+    for n in range(3):
+        put_rows(rows_out, n, row_ref, 2 * n)
 
 
 def middle_kernel(*refs):
@@ -347,22 +353,18 @@
 
 def early_call(plan, *operands):
     outs = (rows_of(6), cols_of(2))
-    return kernel_call(early_kernel, [*plan, *operands], outs, [], 3000000000)
+    return kernel_call(early_kernel, [*plan, *operands], outs, [], 30000000000)
 
 
 def second_call(plan, *operands):
-    outs = (f32(6, SHARD), cols_of(8), shards(8))
+    outs = (f32(3, 8, 128), cols_of(8), shards(8))
     scratch = [rows_of(6), cols_of(6)]
     return kernel_call(second_kernel, [*plan, *operands], outs, scratch, 3000000000)
 
 
 def middle_call(plan, *operands):
     outs = (rows_of(6), cols_of(8))
-    return kernel_call(middle_kernel, [*plan, *operands], outs, [], 5000000000)
-
-
-KEPT = (0, 1, 2, 4)
-SENT = (3, 6, 5, 7)
+    return kernel_call(middle_kernel, [*plan, *operands], outs, [], 30000000000)
 
 
 def last_kernel(*refs):
@@ -386,34 +388,63 @@
 
 
 def final_kernel(*refs):
-    plan, mine, theirs, refs = refs[:3], refs[3:5], refs[5:7], refs[7:]
-    rows0, row_in, col_in, keep_ref, send_ref, other_ref, a_buf, b_buf, row_ref, col_ref = refs
+    here_ref, plan, mine, theirs, refs = refs[0], refs[1:4], refs[4:6], refs[6:8], refs[8:]
+    rows0, row_in, col_in, part_ref, other_ref, a_buf, b_buf, row_ref, col_ref = refs
     for half in range(2):
         a_buf[half] = mine[half][...]
         b_buf[half] = theirs[half][...]
     row_ref[...] = row_in[6:]
     clear(col_ref)
     score_lists(4, *plan, a_buf, b_buf, row_ref, col_ref)
-    keep_ref[0:2] = jnp.full((2, SHARD), -2.0, jnp.float32)
-    for out_ref, slots in ((keep_ref, KEPT), (send_ref, SENT)):
-        for place, slot in enumerate(slots):
-            if slot == 7:
-                put_rows(out_ref, 2 * place, row_ref, 0)
-            elif slot > 3:
-                put_rows(out_ref, 2 * place, row_in, 2 * slot - 8)
-            elif slot > 0:
-                out_ref[2 * place : 2 * place + 2] = rows0[2 * slot - 2 : 2 * slot]
-    for place, slot in enumerate(KEPT + SENT):
-        for half in range(2):
-            at = 2 * place + half
-            down = col_ref[half] if slot == 7 else col_in[2 * slot + half]
-            other_ref[at : at + 1, :] = jnp.max(down, axis=0, keepdims=True)
-
-
-def final_call(plan, *operands):
-    outs = (f32(8, SHARD), f32(8, SHARD), f32(16, SHARD))
+    here = here_ref[0]
+    places = place_of(0, here), place_of(1, here)
+    core = (here >> 4) & 1
+    ours = jnp.where(core == 0, places[0], places[1])
+    others = jnp.where(core == 0, places[1], places[0])
+    part_ref[ours] = jnp.full((8, 128), -2.0, jnp.float32)
+    for slot in range(8):
+        place = ours ^ bits_of(slot)
+        if slot == 7:
+            put_rows(part_ref, place, row_ref, 0)
+            put_cols(other_ref, others ^ bits_of(slot), col_ref, 0)
+            continue
+        if slot > 3:
+            put_rows(part_ref, place, row_in, 2 * slot - 8)
+        elif slot > 0:
+            part_ref[place] = rows0[slot - 1]
+        put_cols(other_ref, others ^ bits_of(slot), col_in, 2 * slot)
+
+
+def final_call(*operands):
+    outs = (f32(8, 8, 128), f32(8, 8, 128))
     scratch = [shards(2), shards(2), rows_of(2), cols_of(2)]
-    return kernel_call(final_kernel, [*plan, *operands], outs, scratch, 500000000)
+    return kernel_call(final_kernel, operands, outs, scratch, 500000000, 4)
+
+
+def bits_of(slot):
+    return sum(1 << generator for generator in SLOTS[slot])
+
+
+def place_of(core, here):
+    if core == 0:
+        one, two, three = here >> 5, (here >> 2) ^ (here >> 3), here >> 3
+    else:
+        one, two, three = here >> 6, here ^ (here >> 1), here >> 1
+    return (one & 1) | ((two & 1) << 1) | ((three & 1) << 2)
+
+
+def groups():
+    found = [[0] * 8 for _ in range(16)]
+    firsts = {}
+    for here in range(128):
+        core = (here >> 4) & 1
+        first = here
+        place = place_of(core, here)
+        for generator in range(3):
+            if place >> generator & 1:
+                first ^= GENERATORS[core][generator]
+        found[firsts.setdefault(first, len(firsts))][place] = here
+    return found
 
 
 def swap(x):
@@ -454,17 +485,14 @@
     halves = [after(x, cols) for x in halves]
     swapped = [swap(x) for x in halves]
     rows1, cols = last_call(plan, *halves, a_mid, b_low, b_mid, rows1, cols)
-    keep, send, other = final_call(plan, *halves, *swapped, rows0, rows1, cols)
-    other = swap(other)
-    keep = jnp.maximum(keep, other[:8])
-    send = jnp.maximum(send, other[8:])
-    keep = jnp.maximum(keep, exchange(send, 2))
-    keep = jnp.maximum(keep[:4], exchange(keep[4:], 1))
-    keep = jnp.maximum(keep[:2], exchange(keep[2:], 0))
+    part, other = final_call(here, *plan, *halves, *swapped, rows0, rows1, cols)
+    part = jnp.maximum(part, swap(other))
+    part = lax.all_to_all(part, ("row", "col"), 0, 0, axis_index_groups=groups())
+    both = jnp.max(part, axis=0)
     second = (here & CORE) != 0
-    ours = jnp.where(second, keep[1], keep[0])
-    other = swap(jnp.where(second, keep[0], keep[1]))
-    return jnp.maximum(own.reshape(SHARD), jnp.maximum(ours, other))
+    ours = jnp.where(second, both[4:], both[:4])
+    other = swap(jnp.where(second, both[:4], both[4:]))
+    return jnp.maximum(own.reshape(SHARD), jnp.maximum(ours, other).reshape(SHARD))
 
 
 def solution(mesh):

time: 67.9 us -> 68 us (level)
  starting transfers between devices: 28.3 us -> 24.7 us
  waiting for transfers between devices: 21.4 us -> 23.3 us
  Pallas kernels: 15.9 us -> 17.6 us
    ppermute x11 -> x8, starting transfers between devices: 21.1 us -> 11.2 us  [exchange(): return lax.ppermute(x, ('row', 'col'), pairs)]
    all_to_all x0 -> x1, starting transfers between devices: none -> 8.04 us  [body(): lax.all_to_all(part, ('row', 'col'), 0, 0, axis_index_groups=groups())]
    ppermute x11 -> x8, waiting for transfers between devices: 19.3 us -> 11.4 us  [exchange(): return lax.ppermute(x, ('row', 'col'), pairs)]
    all_to_all x0 -> x1, waiting for transfers between devices: none -> 6.41 us  [body(): lax.all_to_all(part, ('row', 'col'), 0, 0, axis_index_groups=groups())]
    ppermute x7, waiting for transfers between devices: 2.1 us -> 5.5 us  [swap(): return lax.ppermute(x, ('row', 'col'), [(s, s ^ CORE) for s in range(128)])]
    pallas_call x7, Pallas kernels: 10.6 us -> 12.4 us  [kernel_call(): pl.pallas_call(kernel, out_shape=outs, in_specs=[spec(SMEM)] * smem + [sp...]
    ppermute x7, starting transfers between devices: 7.17 us -> 5.48 us  [swap(): return lax.ppermute(x, ('row', 'col'), [(s, s ^ CORE) for s in range(128)])]
  transfers between devices with their start and end apart: 18 -> 16, of which waited for: 14 -> 12; matrix products, arithmetic and copies ran while one was open for 0% -> 0% of each run, Pallas kernels for 21% -> 23%
where the time goes in v8:
time: 68 us
  starting transfers between devices  24.7 us (36%)
  waiting for transfers between devices  23.3 us (34%)
  Pallas kernels  17.6 us (26%)
  other arithmetic  1.21 us (2%)
  local copies, waits for them, and re-layouts  1.08 us (2%)
    pallas_call x7, Pallas kernels, kernel_call(): pl.pallas_call(kernel, out_shape=outs, in_specs=[spec(SMEM)] * smem + [sp...  12.4 us
    ppermute x8, waiting for transfers between devices, exchange(): return lax.ppermute(x, ('row', 'col'), pairs)  11.4 us
    ppermute x8, starting transfers between devices, exchange(): return lax.ppermute(x, ('row', 'col'), pairs)  11.2 us
    all_to_all x1, starting transfers between devices, body(): lax.all_to_all(part, ('row', 'col'), 0, 0, axis_index_groups=groups())  8.04 us
    all_to_all x1, waiting for transfers between devices, body(): lax.all_to_all(part, ('row', 'col'), 0, 0, axis_index_groups=groups())  6.41 us
    ppermute x7, waiting for transfers between devices, swap(): return lax.ppermute(x, ('row', 'col'), [(s, s ^ CORE) for s in range(128)])  5.5 us
    ppermute x7, starting transfers between devices, swap(): return lax.ppermute(x, ('row', 'col'), [(s, s ^ CORE) for s in range(128)])  5.48 us
    pallas_call x1, Pallas kernels, plan_call(): pl.pallas_call(plan_kernel, out_shape=(lists, lists, jax.ShapeDtypeStruct...  3.59 us
  transfers between devices with their start and end apart: 16, of which 12 were waited for; matrix products, arithmetic and copies ran while one was open for 0% of the time, Pallas kernels for 23%

profile of v8, /device:TPU:1, one launch (start us, length us, event | category | flops | bytes accessed | tf_op | source)
XLA Modules:
  0.0 68.0 jit_solution(17086842301994752473)
XLA Ops:
  0.0 0.0 copy-start.1
  0.0 1.4 %collective-permute-start = (bf16[512,384]{1,0:T(8,128)(2,1)}, bf16[512,384]{1,0:T(8,128)(2,1)S(1)}, u32[]{:S(2)}, u32[]{:S(2)}) collective-permute-start(bf16[512,384]{1,0:T(8,128)(2,1)} %x_ref.1), channel_id=1, source_target_pairs={{0,16},{1,17},{2,18},{3,19},{4,20},{5,21},{6,22},{7,23},{8,24},{9,... | collective-permute-start | bytes 1179656 | tf_op jit(solution)/shard_map/ppermute | solution.py:451
  1.4 1.0 %copy-done = bf16[512,384]{1,0:T(8,128)(2,1)S(1)} copy-done((bf16[512,384]{1,0:T(8,128)(2,1)S(1)}, bf16[512,384]{1,0:T(8,128)(2,1)}, u32[]{:S(2)}) %copy-start) | copy-done | bytes 393240
  2.4 0.2 shard_map.28.own_ref
  2.6 0.4 collective-permute-done.other_ref
  3.0 0.2 shard_map.29.unit_ref.refs_4_
  3.2 2.6 %collective-permute-start.3 = (bf16[2,512,384]{2,1,0:T(8,128)(2,1)S(1)}, bf16[2,512,384]{2,1,0:T(8,128)(2,1)S(1)}, u32[]{:S(2)}, u32[]{:S(2)}) collective-permute-start(bf16[2,512,384]{2,1,0:T(8,128)(2,1)S(1)} %shard_map.29.unit_ref.refs_4_), channel_id=1, source_target_pairs={{0,32},{1,33},{2,34},{3,35},{4,36},{5,37},{6,38},{7,39},{8,40},{9,... | collective-permute-start | bytes 2359304 | tf_op jit(solution)/shard_map/ppermute | solution.py:456
  5.8 3.8 %collective-permute-start.4 = (bf16[2,512,384]{2,1,0:T(8,128)(2,1)S(1)}, bf16[2,512,384]{2,1,0:T(8,128)(2,1)S(1)}, u32[]{:S(2)}, u32[]{:S(2)}) collective-permute-start(bf16[2,512,384]{2,1,0:T(8,128)(2,1)S(1)} %shard_map.29.unit_ref.refs_4_), channel_id=1, source_target_pairs={{0,12},{1,13},{2,14},{3,15},{4,8},{5,9},{6,10},{7,11},{8,4},{9,5},... | collective-permute-start | bytes 2359304 | tf_op jit(solution)/shard_map/ppermute | solution.py:456
  9.6 0.0 collective-permute-start.1
  9.6 0.0 copy-done.1
  9.6 3.6 %shard_map.31 = (s32[131]{0:T(256)S(1)}, s32[131]{0:T(256)S(1)}, s32[10]{0:T(128)S(1)}) custom-call(s32[1]{0:T(128)} %bitcast.here_ref.refs_0_, s32[256]{0:T(256)S(1)} %copy-done.1, s32[2,128]{1,0:T(2,128)S(1)} %bitcast.11), custom_call_target="tpu_custom_call" | custom-call | flops 3000000000 | bytes 10000 | tf_op jit(solution)/shard_map/pallas_call | solution.py:194
  13.2 1.3 %shard_map.30 = f32[1,512]{1,0:T(1,128)S(1)} custom-call(s32[1]{0:T(128)} %bitcast.here_ref.refs_0_, s32[256]{0:T(256)S(1)} %copy-done.1, bf16[2,512,384]{2,1,0:T(8,128)(2,1)S(1)} %shard_map.29.unit_ref.refs_4_), custom_call_target="tpu_custom_call" | custom-call | flops 1000000000 | bytes 1000000 | tf_op jit(solution)/shard_map/pallas_call | solution.py:206
  14.5 1.1 %collective-permute-done.3.a_ref = bf16[2,512,384]{2,1,0:T(8,128)(2,1)S(1)} collective-permute-done((bf16[2,512,384]{2,1,0:T(8,128)(2,1)S(1)}, bf16[2,512,384]{2,1,0:T(8,128)(2,1)S(1)}, u32[]{:S(2)}, u32[]{:S(2)}) %collective-permute-start.3) | collective-permute-done | bytes 786464 | tf_op jit(solution)/shard_map/ppermute | solution.py:456
  15.6 3.4 %collective-permute-done.4.c_ref = bf16[2,512,384]{2,1,0:T(8,128)(2,1)S(1)} collective-permute-done((bf16[2,512,384]{2,1,0:T(8,128)(2,1)S(1)}, bf16[2,512,384]{2,1,0:T(8,128)(2,1)S(1)}, u32[]{:S(2)}, u32[]{:S(2)}) %collective-permute-start.4) | collective-permute-done | bytes 786464 | tf_op jit(solution)/shard_map/ppermute | solution.py:456
  18.9 1.5 %collective-permute-done.1.b_ref = bf16[2,512,384]{2,1,0:T(8,128)(2,1)S(1)} collective-permute-done((bf16[2,512,384]{2,1,0:T(8,128)(2,1)S(1)}, bf16[2,512,384]{2,1,0:T(8,128)(2,1)S(1)}, u32[]{:S(2)}, u32[]{:S(2)}) %collective-permute-start.1) | collective-permute-done | bytes 786464 | tf_op jit(solution)/shard_map/ppermute | solution.py:456
  20.4 0.5 collective-permute-start.8
  20.9 0.0 collective-permute-start.7
  20.9 0.2 shard_map.32.refs_3_
  21.1 1.3 %collective-permute-start.2 = (bf16[2,512,384]{2,1,0:T(8,128)(2,1)S(1)}, bf16[2,512,384]{2,1,0:T(8,128)(2,1)S(1)}, u32[]{:S(2)}, u32[]{:S(2)}) collective-permute-start(bf16[2,512,384]{2,1,0:T(8,128)(2,1)S(1)} %collective-permute-done.1.b_ref), channel_id=1, source_target_pairs={{0,12},{1,13},{2,14},{3,15},{4,8},{5,9},{6,10},{7,11},{8,4},{9,5},... | collective-permute-start | bytes 2359304 | tf_op jit(solution)/shard_map/ppermute | solution.py:456
  22.4 0.0 collective-permute-start.5
  22.4 1.4 %shard_map.33 = (f32[6,512,128]{2,1,0:T(8,128)S(1)}, f32[2,8,512]{2,1,0:T(8,128)S(1)}) custom-call(s32[131]{0:T(256)S(1)} %get-tuple-element.27.refs_0_.refs_1_, s32[131]{0:T(256)S(1)} %get-tuple-element.28.refs_1_.refs_2_, s32[10]{0:T(128)S(1)} %get-tuple-element.29.refs_2_.refs_3_, bf16[6,512,384]{2,1,0:T(8,128)(2,1)S(1)} %shard_map.32.refs_3_, ...), custom_call_target="tpu_custom_call" | custom-call | flops 30000001024 | bytes 8000000 | tf_op jit(solution)/shard_map/pallas_call | solution.py:343
  23.8 3.1 %collective-permute-done.5.refs_5_ = bf16[6,512,384]{2,1,0:T(8,128)(2,1)S(1)} collective-permute-done((bf16[6,512,384]{2,1,0:T(8,128)(2,1)S(1)}, bf16[6,512,384]{2,1,0:T(8,128)(2,1)S(1)}, u32[]{:S(2)}, u32[]{:S(2)}) %collective-permute-start.5) | collective-permute-done | bytes 2359328 | tf_op jit(solution)/shard_map/ppermute | solution.py:451
  26.9 4.0 %shard_map.34 = (f32[3,8,128]{2,1,0:T(8,128)S(1)}, f32[8,8,512]{2,1,0:T(8,128)S(1)}, bf16[8,512,384]{2,1,0:T(8,128)(2,1)S(1)}) custom-call(s32[131]{0:T(256)S(1)} %get-tuple-element.27.refs_0_.refs_1_, s32[131]{0:T(256)S(1)} %get-tuple-element.28.refs_1_.refs_2_, s32[10]{0:T(128)S(1)} %get-tuple-element.29.refs_2_.refs_3_, ...), custom_call_target="tpu_custom_call" | custom-call | flops 3000000000 | bytes 8000000 | tf_op jit(solution)/shard_map/pallas_call | solution.py:343
  30.9 1.8 %collective-permute-done.8.c_ref = bf16[2,512,384]{2,1,0:T(8,128)(2,1)S(1)} collective-permute-done((bf16[2,512,384]{2,1,0:T(8,128)(2,1)S(1)}, bf16[2,512,384]{2,1,0:T(8,128)(2,1)S(1)}, u32[]{:S(2)}, u32[]{:S(2)}) %collective-permute-start.8) | collective-permute-done | bytes 786464 | tf_op jit(solution)/shard_map/ppermute | solution.py:456
  32.7 0.0 collective-permute-done.7.a_ref
  32.7 0.8 %collective-permute-done.2.b_ref = bf16[2,512,384]{2,1,0:T(8,128)(2,1)S(1)} collective-permute-done((bf16[2,512,384]{2,1,0:T(8,128)(2,1)S(1)}, bf16[2,512,384]{2,1,0:T(8,128)(2,1)S(1)}, u32[]{:S(2)}, u32[]{:S(2)}) %collective-permute-start.2) | collective-permute-done | bytes 786464 | tf_op jit(solution)/shard_map/ppermute | solution.py:456
  33.6 0.2 shard_map.35.refs_3_.refs_5_
  33.8 0.5 collective-permute-start.9
  34.3 1.2 %collective-permute-start.12 = (bf16[6,512,384]{2,1,0:T(8,128)(2,1)S(1)}, bf16[6,512,384]{2,1,0:T(8,128)(2,1)S(1)}, u32[]{:S(2)}, u32[]{:S(2)}) collective-permute-start(bf16[6,512,384]{2,1,0:T(8,128)(2,1)S(1)} %shard_map.35.refs_3_.refs_5_), channel_id=1, source_target_pairs={{0,16},{1,17},{2,18},{3,19},{4,20},{5,21},{6,22},{7,23},{8,24},{9,... | collective-permute-start | bytes 7077896 | tf_op jit(solution)/shard_map/ppermute | solution.py:451
  35.6 2.5 %collective-permute-start.6 = (bf16[512,384]{1,0:T(8,128)(2,1)S(1)}, bf16[512,384]{1,0:T(8,128)(2,1)S(1)}, u32[]{:S(2)}, u32[]{:S(2)}) collective-permute-start(bf16[512,384]{1,0:T(8,128)(2,1)S(1)} %slice_bitcast_fusion.1), channel_id=1, source_target_pairs={{0,32},{1,33},{2,34},{3,35},{4,36},{5,37},{6,38},{7,39},{8,40},{9,... | collective-permute-start | bytes 1179656 | tf_op jit(solution)/shard_map/ppermute | solution.py:456
  38.1 2.5 %shard_map.36 = (f32[6,512,128]{2,1,0:T(8,128)S(1)}, f32[8,8,512]{2,1,0:T(8,128)S(1)}) custom-call(s32[131]{0:T(256)S(1)} %get-tuple-element.27.refs_0_.refs_1_, s32[131]{0:T(256)S(1)} %get-tuple-element.28.refs_1_.refs_2_, s32[10]{0:T(128)S(1)} %get-tuple-element.29.refs_2_.refs_3_, bf16[6,512,384]{2,1,0:T(8,128)(2,1)S(1)} %shard_map.35.refs_3_.refs_5_, ...), custom_call_target="tpu_custom_call" | custom-call | flops 30000001024 | bytes 8000000 | tf_op jit(solution)/shard_map/pallas_call | solution.py:343
  40.6 0.4 collective-permute-done.9.refs_4_.refs_5_
  41.0 2.4 %collective-permute-done.6.refs_3_.refs_4_ = bf16[512,384]{1,0:T(8,128)(2,1)S(1)} collective-permute-done((bf16[512,384]{1,0:T(8,128)(2,1)S(1)}, bf16[512,384]{1,0:T(8,128)(2,1)S(1)}, u32[]{:S(2)}, u32[]{:S(2)}) %collective-permute-start.6) | collective-permute-done | bytes 393248 | tf_op jit(solution)/shard_map/ppermute | solution.py:456
  43.4 0.0 collective-permute-start.11
  43.4 0.5 collective-permute-start.10
  43.9 0.0 collective-permute-done.12.refs_7_
  43.9 2.7 %shard_map.37 = (f32[8,512,128]{2,1,0:T(8,128)S(1)}, f32[14,8,512]{2,1,0:T(8,128)S(1)}) custom-call(s32[131]{0:T(256)S(1)} %get-tuple-element.27.refs_0_.refs_1_, s32[131]{0:T(256)S(1)} %get-tuple-element.28.refs_1_.refs_2_, s32[10]{0:T(128)S(1)} %get-tuple-element.29.refs_2_.refs_3_, bf16[512,384]{1,0:T(8,128)(2,1)S(1)} %collective-permute-done.6.refs_3_.refs_4_, ...), custom_call_target="tpu_custom_call" | custom-call | flops 5000000000 | bytes 8000000 | tf_op jit(solution)/shard_map/pallas_call | solution.py:343
  46.6 0.0 collective-permute-done.11.refs_7_
  46.7 0.0 collective-permute-done.10.refs_6_
  46.7 1.4 %shard_map.38 = (f32[8,8,128]{2,1,0:T(8,128)S(1)}, f32[8,8,128]{2,1,0:T(8,128)S(1)}) custom-call(s32[1]{0:T(128)} %bitcast.here_ref.refs_0_, s32[131]{0:T(256)S(1)} %get-tuple-element.27.refs_0_.refs_1_, s32[131]{0:T(256)S(1)} %get-tuple-element.28.refs_1_.refs_2_, s32[10]{0:T(128)S(1)} %get-tuple-element.29.refs_2_.refs_3_, ...), custom_call_target="tpu_custom_call" | custom-call | flops 500000000 | bytes 8000000 | tf_op jit(solution)/shard_map/pallas_call | solution.py:343
  48.1 2.2 %collective-permute-start.13 = (f32[8,8,128]{2,1,0:T(8,128)S(1)}, f32[8,8,128]{2,1,0:T(8,128)S(1)}, u32[]{:S(2)}, u32[]{:S(2)}) collective-permute-start(f32[8,8,128]{2,1,0:T(8,128)S(1)} %get-tuple-element.48), channel_id=1, source_target_pairs={{0,16},{1,17},{2,18},{3,19},{4,20},{5,21},{6,22},{7,23},{8,24},{9,... | collective-permute-start | bytes 98312 | tf_op jit(solution)/shard_map/ppermute | solution.py:451
  50.3 0.9 %collective-permute-done.13 = f32[8,8,128]{2,1,0:T(8,128)S(1)} collective-permute-done((f32[8,8,128]{2,1,0:T(8,128)S(1)}, f32[8,8,128]{2,1,0:T(8,128)S(1)}, u32[]{:S(2)}, u32[]{:S(2)}) %collective-permute-start.13) | collective-permute-done | bytes 32800 | tf_op jit(solution)/shard_map/ppermute | solution.py:451
  51.1 0.6 max.9
  51.7 8.0 %all-to-all-start = ((f32[8,8,128]{2,1,0:T(8,128)}), f32[8,8,128]{2,1,0:T(8,128)S(1)}, u32[]{:S(2)}, u32[]{:S(2)}) async-start(f32[8,8,128]{2,1,0:T(8,128)} %max.9), calls=%async_computation | async-start | bytes 65536 | tf_op jit(solution)/shard_map/all_to_all | solution.py:490
  59.8 6.4 %all-to-all-done = f32[8,8,128]{2,1,0:T(8,128)S(1)} async-done(((f32[8,8,128]{2,1,0:T(8,128)}), f32[8,8,128]{2,1,0:T(8,128)S(1)}, u32[]{:S(2)}, u32[]{:S(2)}) %all-to-all-start) | async-done | bytes 32800 | tf_op jit(solution)/shard_map/all_to_all | solution.py:490
  66.2 0.1 collective-permute-start.14
  66.3 1.1 %collective-permute-done.14 = f32[4,128]{1,0:T(4,128)S(1)} collective-permute-done((f32[4,128]{1,0:T(4,128)S(1)}, f32[4,128]{1,0:T(4,128)S(1)}, u32[]{:S(2)}, u32[]{:S(2)}) %collective-permute-start.14) | collective-permute-done | bytes 2080 | tf_op jit(solution)/shard_map/ppermute | solution.py:451
  67.4 0.6 bitcast_maximum_fusion
  (5 shorter events, 0.1 us)
Async XLA Ops:
  0.0 9.6 %copy-start.1 = (s32[256]{0:T(256)S(1)}, s32[256]{0:T(256)}, u32[]{:S(2)}) copy-start(s32[256]{0:T(256)} %cluster_ref.3) | copy-start | bytes 3076
  0.0 3.0 %collective-permute-start = (bf16[512,384]{1,0:T(8,128)(2,1)}, bf16[512,384]{1,0:T(8,128)(2,1)S(1)}, u32[]{:S(2)}, u32[]{:S(2)}) collective-permute-start(bf16[512,384]{1,0:T(8,128)(2,1)} %x_ref.1), channel_id=1, source_target_pairs={{0,16},{1,17},{2,18},{3,19},{4,20},{5,21},{6,22},{7,23},{8,24},{9,... | collective-permute-start | bytes 1179656 | tf_op jit(solution)/shard_map/ppermute | solution.py:451
  1.4 1.0 %copy-start = (bf16[512,384]{1,0:T(8,128)(2,1)S(1)}, bf16[512,384]{1,0:T(8,128)(2,1)}, u32[]{:S(2)}) copy-start(bf16[512,384]{1,0:T(8,128)(2,1)} %x_ref.1) | copy-start | bytes 1179652
  3.2 12.4 %collective-permute-start.3 = (bf16[2,512,384]{2,1,0:T(8,128)(2,1)S(1)}, bf16[2,512,384]{2,1,0:T(8,128)(2,1)S(1)}, u32[]{:S(2)}, u32[]{:S(2)}) collective-permute-start(bf16[2,512,384]{2,1,0:T(8,128)(2,1)S(1)} %shard_map.29.unit_ref.refs_4_), channel_id=1, source_target_pairs={{0,32},{1,33},{2,34},{3,35},{4,36},{5,37},{6,38},{7,39},{8,40},{9,... | collective-permute-start | bytes 2359304 | tf_op jit(solution)/shard_map/ppermute | solution.py:456
  5.8 13.1 %collective-permute-start.4 = (bf16[2,512,384]{2,1,0:T(8,128)(2,1)S(1)}, bf16[2,512,384]{2,1,0:T(8,128)(2,1)S(1)}, u32[]{:S(2)}, u32[]{:S(2)}) collective-permute-start(bf16[2,512,384]{2,1,0:T(8,128)(2,1)S(1)} %shard_map.29.unit_ref.refs_4_), channel_id=1, source_target_pairs={{0,12},{1,13},{2,14},{3,15},{4,8},{5,9},{6,10},{7,11},{8,4},{9,5},... | collective-permute-start | bytes 2359304 | tf_op jit(solution)/shard_map/ppermute | solution.py:456
  9.6 10.8 %collective-permute-start.1 = (bf16[2,512,384]{2,1,0:T(8,128)(2,1)S(1)}, bf16[2,512,384]{2,1,0:T(8,128)(2,1)S(1)}, u32[]{:S(2)}, u32[]{:S(2)}) collective-permute-start(bf16[2,512,384]{2,1,0:T(8,128)(2,1)S(1)} %shard_map.29.unit_ref.refs_4_), channel_id=1, source_target_pairs={{0,4},{1,5},{2,6},{3,7},{4,0},{5,1},{6,2},{7,3},{8,12},{9,13},{10,... | collective-permute-start | bytes 2359304 | tf_op jit(solution)/shard_map/ppermute | solution.py:456
  20.4 12.3 %collective-permute-start.8 = (bf16[2,512,384]{2,1,0:T(8,128)(2,1)S(1)}, bf16[2,512,384]{2,1,0:T(8,128)(2,1)S(1)}, u32[]{:S(2)}, u32[]{:S(2)}) collective-permute-start(bf16[2,512,384]{2,1,0:T(8,128)(2,1)S(1)} %collective-permute-done.4.c_ref), channel_id=1, source_target_pairs={{0,32},{1,33},{2,34},{3,35},{4,36},{5,37},{6,38},{7,39},{8,40},{9,... | collective-permute-start | bytes 2359304 | tf_op jit(solution)/shard_map/ppermute | solution.py:456
  20.9 11.9 %collective-permute-start.7 = (bf16[2,512,384]{2,1,0:T(8,128)(2,1)S(1)}, bf16[2,512,384]{2,1,0:T(8,128)(2,1)S(1)}, u32[]{:S(2)}, u32[]{:S(2)}) collective-permute-start(bf16[2,512,384]{2,1,0:T(8,128)(2,1)S(1)} %collective-permute-done.3.a_ref), channel_id=1, source_target_pairs={{0,4},{1,5},{2,6},{3,7},{4,0},{5,1},{6,2},{7,3},{8,12},{9,13},{10,... | collective-permute-start | bytes 2359304 | tf_op jit(solution)/shard_map/ppermute | solution.py:456
  21.1 12.4 %collective-permute-start.2 = (bf16[2,512,384]{2,1,0:T(8,128)(2,1)S(1)}, bf16[2,512,384]{2,1,0:T(8,128)(2,1)S(1)}, u32[]{:S(2)}, u32[]{:S(2)}) collective-permute-start(bf16[2,512,384]{2,1,0:T(8,128)(2,1)S(1)} %collective-permute-done.1.b_ref), channel_id=1, source_target_pairs={{0,12},{1,13},{2,14},{3,15},{4,8},{5,9},{6,10},{7,11},{8,4},{9,5},... | collective-permute-start | bytes 2359304 | tf_op jit(solution)/shard_map/ppermute | solution.py:456
  22.4 4.5 %collective-permute-start.5 = (bf16[6,512,384]{2,1,0:T(8,128)(2,1)S(1)}, bf16[6,512,384]{2,1,0:T(8,128)(2,1)S(1)}, u32[]{:S(2)}, u32[]{:S(2)}) collective-permute-start(bf16[6,512,384]{2,1,0:T(8,128)(2,1)S(1)} %shard_map.32.refs_3_), channel_id=1, source_target_pairs={{0,16},{1,17},{2,18},{3,19},{4,20},{5,21},{6,22},{7,23},{8,24},{9,... | collective-permute-start | bytes 7077896 | tf_op jit(solution)/shard_map/ppermute | solution.py:451
  33.8 7.2 %collective-permute-start.9 = (bf16[512,384]{1,0:T(8,128)(2,1)S(1)}, bf16[512,384]{1,0:T(8,128)(2,1)S(1)}, u32[]{:S(2)}, u32[]{:S(2)}) collective-permute-start(bf16[512,384]{1,0:T(8,128)(2,1)S(1)} %slice_bitcast_fusion), channel_id=1, source_target_pairs={{0,4},{1,5},{2,6},{3,7},{4,0},{5,1},{6,2},{7,3},{8,12},{9,13},{10,... | collective-permute-start | bytes 1179656 | tf_op jit(solution)/shard_map/ppermute | solution.py:456
  34.3 9.6 %collective-permute-start.12 = (bf16[6,512,384]{2,1,0:T(8,128)(2,1)S(1)}, bf16[6,512,384]{2,1,0:T(8,128)(2,1)S(1)}, u32[]{:S(2)}, u32[]{:S(2)}) collective-permute-start(bf16[6,512,384]{2,1,0:T(8,128)(2,1)S(1)} %shard_map.35.refs_3_.refs_5_), channel_id=1, source_target_pairs={{0,16},{1,17},{2,18},{3,19},{4,20},{5,21},{6,22},{7,23},{8,24},{9,... | collective-permute-start | bytes 7077896 | tf_op jit(solution)/shard_map/ppermute | solution.py:451
  35.6 7.8 %collective-permute-start.6 = (bf16[512,384]{1,0:T(8,128)(2,1)S(1)}, bf16[512,384]{1,0:T(8,128)(2,1)S(1)}, u32[]{:S(2)}, u32[]{:S(2)}) collective-permute-start(bf16[512,384]{1,0:T(8,128)(2,1)S(1)} %slice_bitcast_fusion.1), channel_id=1, source_target_pairs={{0,32},{1,33},{2,34},{3,35},{4,36},{5,37},{6,38},{7,39},{8,40},{9,... | collective-permute-start | bytes 1179656 | tf_op jit(solution)/shard_map/ppermute | solution.py:456
  43.4 3.2 %collective-permute-start.11 = (bf16[512,384]{1,0:T(8,128)(2,1)S(1)}, bf16[512,384]{1,0:T(8,128)(2,1)S(1)}, u32[]{:S(2)}, u32[]{:S(2)}) collective-permute-start(bf16[512,384]{1,0:T(8,128)(2,1)S(1)} %collective-permute-done.9.refs_4_.refs_5_), channel_id=1, source_target_pairs={{0,16},{1,17},{2,18},{3,19},{4,20},{5,21},{6,22},{7,23},{8,24},{9,... | collective-permute-start | bytes 1179656 | tf_op jit(solution)/shard_map/ppermute | solution.py:451
  43.4 3.2 %collective-permute-start.10 = (bf16[512,384]{1,0:T(8,128)(2,1)S(1)}, bf16[512,384]{1,0:T(8,128)(2,1)S(1)}, u32[]{:S(2)}, u32[]{:S(2)}) collective-permute-start(bf16[512,384]{1,0:T(8,128)(2,1)S(1)} %collective-permute-done.6.refs_3_.refs_4_), channel_id=1, source_target_pairs={{0,16},{1,17},{2,18},{3,19},{4,20},{5,21},{6,22},{7,23},{8,24},{9,... | collective-permute-start | bytes 1179656 | tf_op jit(solution)/shard_map/ppermute | solution.py:451
  48.1 3.1 %collective-permute-start.13 = (f32[8,8,128]{2,1,0:T(8,128)S(1)}, f32[8,8,128]{2,1,0:T(8,128)S(1)}, u32[]{:S(2)}, u32[]{:S(2)}) collective-permute-start(f32[8,8,128]{2,1,0:T(8,128)S(1)} %get-tuple-element.48), channel_id=1, source_target_pairs={{0,16},{1,17},{2,18},{3,19},{4,20},{5,21},{6,22},{7,23},{8,24},{9,... | collective-permute-start | bytes 98312 | tf_op jit(solution)/shard_map/ppermute | solution.py:451
  51.7 14.4 %all-to-all-start = ((f32[8,8,128]{2,1,0:T(8,128)}), f32[8,8,128]{2,1,0:T(8,128)S(1)}, u32[]{:S(2)}, u32[]{:S(2)}) async-start(f32[8,8,128]{2,1,0:T(8,128)} %max.9), calls=%async_computation | async-start | bytes 65536 | tf_op jit(solution)/shard_map/all_to_all | solution.py:490
  66.2 1.2 %collective-permute-start.14 = (f32[4,128]{1,0:T(4,128)S(1)}, f32[4,128]{1,0:T(4,128)S(1)}, u32[]{:S(2)}, u32[]{:S(2)}) collective-permute-start(f32[4,128]{1,0:T(4,128)S(1)} %slice_select_fusion), channel_id=1, source_target_pairs={{0,16},{1,17},{2,18},{3,19},{4,20},{5,21},{6,22},{7,23},{8,24},{9,... | collective-permute-start | bytes 6152 | tf_op jit(solution)/shard_map/ppermute | solution.py:451

commit v9 on v7

--- a/solution.py
+++ b/solution.py
@@ -347,7 +347,7 @@
 
 def early_call(plan, *operands):
     outs = (rows_of(6), cols_of(2))
-    return kernel_call(early_kernel, [*plan, *operands], outs, [], 3000000000)
+    return kernel_call(early_kernel, [*plan, *operands], outs, [], 30000000000)
 
 
 def second_call(plan, *operands):
@@ -358,7 +358,7 @@
 
 def middle_call(plan, *operands):
     outs = (rows_of(6), cols_of(8))
-    return kernel_call(middle_kernel, [*plan, *operands], outs, [], 5000000000)
+    return kernel_call(middle_kernel, [*plan, *operands], outs, [], 30000000000)
 
 
 KEPT = (0, 1, 2, 4)

time: 67.9 us -> 68 us (level); the launches traced: 67.3 us -> 69.2 us
  starting transfers between devices: 28.3 us -> 29 us
    ppermute x7, starting transfers between devices: 7.17 us -> 10.4 us  [swap(): return lax.ppermute(x, ('row', 'col'), [(s, s ^ CORE) for s in range(128)])]
    ppermute x7, waiting for transfers between devices: 2.1 us -> 5.18 us  [swap(): return lax.ppermute(x, ('row', 'col'), [(s, s ^ CORE) for s in range(128)])]
    ppermute x11, starting transfers between devices: 21.1 us -> 18.6 us  [exchange(): return lax.ppermute(x, ('row', 'col'), pairs)]
    ppermute x11, waiting for transfers between devices: 19.3 us -> 16.8 us  [exchange(): return lax.ppermute(x, ('row', 'col'), pairs)]
where the time goes in v9:
time: 68 us; the launch traced here: 69.2 us
  starting transfers between devices  29 us (43%)
  waiting for transfers between devices  22 us (32%)
  Pallas kernels  16.3 us (24%)
  local copies, waits for them, and re-layouts  1.09 us (2%)
    ppermute x11, starting transfers between devices, exchange(): return lax.ppermute(x, ('row', 'col'), pairs)  18.6 us
    ppermute x11, waiting for transfers between devices, exchange(): return lax.ppermute(x, ('row', 'col'), pairs)  16.8 us
    pallas_call x7, Pallas kernels, kernel_call(): pl.pallas_call(kernel, out_shape=outs, in_specs=[spec(SMEM)] * smem + [sp...  11.1 us
    ppermute x7, starting transfers between devices, swap(): return lax.ppermute(x, ('row', 'col'), [(s, s ^ CORE) for s in range(128)])  10.4 us
    ppermute x7, waiting for transfers between devices, swap(): return lax.ppermute(x, ('row', 'col'), [(s, s ^ CORE) for s in range(128)])  5.18 us
    pallas_call x1, Pallas kernels, plan_call(): pl.pallas_call(plan_kernel, out_shape=(lists, lists, jax.ShapeDtypeStruct...  3.59 us
  transfers between devices with their start and end apart: 18, of which 14 were waited for; matrix products, arithmetic and copies ran while one was open for 0% of the time, Pallas kernels for 21%

profile of v9, /device:TPU:1, one launch (start us, length us, event | category | flops | bytes accessed | tf_op | source)
XLA Modules:
  0.0 69.2 jit_solution(11252888854072077853)
XLA Ops:
  0.0 1.4 %collective-permute-start = (bf16[512,384]{1,0:T(8,128)(2,1)}, bf16[512,384]{1,0:T(8,128)(2,1)S(1)}, u32[]{:S(2)}, u32[]{:S(2)}) collective-permute-start(bf16[512,384]{1,0:T(8,128)(2,1)} %x_ref.1), channel_id=1, source_target_pairs={{0,16},{1,17},{2,18},{3,19},{4,20},{5,21},{6,22},{7,23},{8,24},{9,... | collective-permute-start | bytes 1179656 | tf_op jit(solution)/shard_map/ppermute | solution.py:420
  1.4 1.0 %copy-done = bf16[512,384]{1,0:T(8,128)(2,1)S(1)} copy-done((bf16[512,384]{1,0:T(8,128)(2,1)S(1)}, bf16[512,384]{1,0:T(8,128)(2,1)}, u32[]{:S(2)}) %copy-start) | copy-done | bytes 393240
  2.4 0.2 shard_map.28.own_ref
  2.6 0.4 collective-permute-done.other_ref
  3.0 0.2 shard_map.29.unit_ref.refs_4_
  3.2 2.6 %collective-permute-start.3 = (bf16[2,512,384]{2,1,0:T(8,128)(2,1)S(1)}, bf16[2,512,384]{2,1,0:T(8,128)(2,1)S(1)}, u32[]{:S(2)}, u32[]{:S(2)}) collective-permute-start(bf16[2,512,384]{2,1,0:T(8,128)(2,1)S(1)} %shard_map.29.unit_ref.refs_4_), channel_id=1, source_target_pairs={{0,32},{1,33},{2,34},{3,35},{4,36},{5,37},{6,38},{7,39},{8,40},{9,... | collective-permute-start | bytes 2359304 | tf_op jit(solution)/shard_map/ppermute | solution.py:425
  5.8 3.8 %collective-permute-start.4 = (bf16[2,512,384]{2,1,0:T(8,128)(2,1)S(1)}, bf16[2,512,384]{2,1,0:T(8,128)(2,1)S(1)}, u32[]{:S(2)}, u32[]{:S(2)}) collective-permute-start(bf16[2,512,384]{2,1,0:T(8,128)(2,1)S(1)} %shard_map.29.unit_ref.refs_4_), channel_id=1, source_target_pairs={{0,12},{1,13},{2,14},{3,15},{4,8},{5,9},{6,10},{7,11},{8,4},{9,5},... | collective-permute-start | bytes 2359304 | tf_op jit(solution)/shard_map/ppermute | solution.py:425
  9.6 0.0 collective-permute-start.1
  9.6 3.6 %shard_map.31 = (s32[131]{0:T(256)S(1)}, s32[131]{0:T(256)S(1)}, s32[10]{0:T(128)S(1)}) custom-call(s32[1]{0:T(128)} %bitcast.here_ref, s32[256]{0:T(256)S(1)} %copy-done.1, s32[2,128]{1,0:T(2,128)S(1)} %bitcast.11), custom_call_target="tpu_custom_call" | custom-call | flops 3000000000 | bytes 10000 | tf_op jit(solution)/shard_map/pallas_call | solution.py:194
  13.2 1.3 %shard_map.30 = f32[1,512]{1,0:T(1,128)S(1)} custom-call(s32[1]{0:T(128)} %bitcast.here_ref, s32[256]{0:T(256)S(1)} %copy-done.1, bf16[2,512,384]{2,1,0:T(8,128)(2,1)S(1)} %shard_map.29.unit_ref.refs_4_), custom_call_target="tpu_custom_call" | custom-call | flops 1000000000 | bytes 1000000 | tf_op jit(solution)/shard_map/pallas_call | solution.py:206
  14.5 1.1 %collective-permute-done.3.a_ref = bf16[2,512,384]{2,1,0:T(8,128)(2,1)S(1)} collective-permute-done((bf16[2,512,384]{2,1,0:T(8,128)(2,1)S(1)}, bf16[2,512,384]{2,1,0:T(8,128)(2,1)S(1)}, u32[]{:S(2)}, u32[]{:S(2)}) %collective-permute-start.3) | collective-permute-done | bytes 786464 | tf_op jit(solution)/shard_map/ppermute | solution.py:425
  15.6 3.4 %collective-permute-done.4.c_ref = bf16[2,512,384]{2,1,0:T(8,128)(2,1)S(1)} collective-permute-done((bf16[2,512,384]{2,1,0:T(8,128)(2,1)S(1)}, bf16[2,512,384]{2,1,0:T(8,128)(2,1)S(1)}, u32[]{:S(2)}, u32[]{:S(2)}) %collective-permute-start.4) | collective-permute-done | bytes 786464 | tf_op jit(solution)/shard_map/ppermute | solution.py:425
  18.9 1.5 %collective-permute-done.1.b_ref = bf16[2,512,384]{2,1,0:T(8,128)(2,1)S(1)} collective-permute-done((bf16[2,512,384]{2,1,0:T(8,128)(2,1)S(1)}, bf16[2,512,384]{2,1,0:T(8,128)(2,1)S(1)}, u32[]{:S(2)}, u32[]{:S(2)}) %collective-permute-start.1) | collective-permute-done | bytes 786464 | tf_op jit(solution)/shard_map/ppermute | solution.py:425
  20.4 0.5 collective-permute-start.8
  20.9 0.0 collective-permute-start.7
  20.9 0.2 shard_map.32.refs_3_
  21.1 1.3 %collective-permute-start.2 = (bf16[2,512,384]{2,1,0:T(8,128)(2,1)S(1)}, bf16[2,512,384]{2,1,0:T(8,128)(2,1)S(1)}, u32[]{:S(2)}, u32[]{:S(2)}) collective-permute-start(bf16[2,512,384]{2,1,0:T(8,128)(2,1)S(1)} %collective-permute-done.1.b_ref), channel_id=1, source_target_pairs={{0,12},{1,13},{2,14},{3,15},{4,8},{5,9},{6,10},{7,11},{8,4},{9,5},... | collective-permute-start | bytes 2359304 | tf_op jit(solution)/shard_map/ppermute | solution.py:425
  22.4 0.0 collective-permute-start.5
  22.4 1.4 %shard_map.33 = (f32[6,512,128]{2,1,0:T(8,128)S(1)}, f32[2,8,512]{2,1,0:T(8,128)S(1)}) custom-call(s32[131]{0:T(256)S(1)} %get-tuple-element.28.refs_0_, s32[131]{0:T(256)S(1)} %get-tuple-element.29.refs_1_, s32[10]{0:T(128)S(1)} %get-tuple-element.30.refs_2_, bf16[6,512,384]{2,1,0:T(8,128)(2,1)S(1)} %shard_map.32.refs_3_, ...), custom_call_target="tpu_custom_call" | custom-call | flops 30000001024 | bytes 8000000 | tf_op jit(solution)/shard_map/pallas_call | solution.py:337
  23.8 3.1 %collective-permute-done.5.refs_5_ = bf16[6,512,384]{2,1,0:T(8,128)(2,1)S(1)} collective-permute-done((bf16[6,512,384]{2,1,0:T(8,128)(2,1)S(1)}, bf16[6,512,384]{2,1,0:T(8,128)(2,1)S(1)}, u32[]{:S(2)}, u32[]{:S(2)}) %collective-permute-start.5) | collective-permute-done | bytes 2359328 | tf_op jit(solution)/shard_map/ppermute | solution.py:420
  26.9 3.2 %shard_map.34 = (f32[6,512]{1,0:T(8,128)S(1)}, f32[8,8,512]{2,1,0:T(8,128)S(1)}, bf16[8,512,384]{2,1,0:T(8,128)(2,1)S(1)}) custom-call(s32[131]{0:T(256)S(1)} %get-tuple-element.28.refs_0_, s32[131]{0:T(256)S(1)} %get-tuple-element.29.refs_1_, s32[10]{0:T(128)S(1)} %get-tuple-element.30.refs_2_, bf16[6,512,384]{2,1,0:T(8,128)(2,1)S(1)} %shard_map.32.refs_3_, ...), custom_call_target="tpu_custom_call" | custom-call | flops 3000000000 | bytes 8000000 | tf_op jit(solution)/shard_map/pallas_call | solution.py:337
  30.1 2.6 %collective-permute-done.8.c_ref = bf16[2,512,384]{2,1,0:T(8,128)(2,1)S(1)} collective-permute-done((bf16[2,512,384]{2,1,0:T(8,128)(2,1)S(1)}, bf16[2,512,384]{2,1,0:T(8,128)(2,1)S(1)}, u32[]{:S(2)}, u32[]{:S(2)}) %collective-permute-start.8) | collective-permute-done | bytes 786464 | tf_op jit(solution)/shard_map/ppermute | solution.py:425
  32.7 0.0 collective-permute-done.7.a_ref
  32.7 0.8 %collective-permute-done.2.b_ref = bf16[2,512,384]{2,1,0:T(8,128)(2,1)S(1)} collective-permute-done((bf16[2,512,384]{2,1,0:T(8,128)(2,1)S(1)}, bf16[2,512,384]{2,1,0:T(8,128)(2,1)S(1)}, u32[]{:S(2)}, u32[]{:S(2)}) %collective-permute-start.2) | collective-permute-done | bytes 786464 | tf_op jit(solution)/shard_map/ppermute | solution.py:425
  33.6 0.2 shard_map.35.refs_3_.refs_5_
  33.8 0.5 collective-permute-start.9
  34.3 1.2 %collective-permute-start.12 = (bf16[6,512,384]{2,1,0:T(8,128)(2,1)S(1)}, bf16[6,512,384]{2,1,0:T(8,128)(2,1)S(1)}, u32[]{:S(2)}, u32[]{:S(2)}) collective-permute-start(bf16[6,512,384]{2,1,0:T(8,128)(2,1)S(1)} %shard_map.35.refs_3_.refs_5_), channel_id=1, source_target_pairs={{0,16},{1,17},{2,18},{3,19},{4,20},{5,21},{6,22},{7,23},{8,24},{9,... | collective-permute-start | bytes 7077896 | tf_op jit(solution)/shard_map/ppermute | solution.py:420
  35.6 2.5 %collective-permute-start.6 = (bf16[512,384]{1,0:T(8,128)(2,1)S(1)}, bf16[512,384]{1,0:T(8,128)(2,1)S(1)}, u32[]{:S(2)}, u32[]{:S(2)}) collective-permute-start(bf16[512,384]{1,0:T(8,128)(2,1)S(1)} %slice_bitcast_fusion.1), channel_id=1, source_target_pairs={{0,32},{1,33},{2,34},{3,35},{4,36},{5,37},{6,38},{7,39},{8,40},{9,... | collective-permute-start | bytes 1179656 | tf_op jit(solution)/shard_map/ppermute | solution.py:425
  38.1 2.5 %shard_map.36 = (f32[6,512,128]{2,1,0:T(8,128)S(1)}, f32[8,8,512]{2,1,0:T(8,128)S(1)}) custom-call(s32[131]{0:T(256)S(1)} %get-tuple-element.28.refs_0_, s32[131]{0:T(256)S(1)} %get-tuple-element.29.refs_1_, s32[10]{0:T(128)S(1)} %get-tuple-element.30.refs_2_, bf16[6,512,384]{2,1,0:T(8,128)(2,1)S(1)} %shard_map.35.refs_3_.refs_5_, ...), custom_call_target="tpu_custom_call" | custom-call | flops 30000001024 | bytes 8000000 | tf_op jit(solution)/shard_map/pallas_call | solution.py:337
  40.5 0.5 collective-permute-done.9.refs_4_
  41.0 2.4 %collective-permute-done.6.refs_3_ = bf16[512,384]{1,0:T(8,128)(2,1)S(1)} collective-permute-done((bf16[512,384]{1,0:T(8,128)(2,1)S(1)}, bf16[512,384]{1,0:T(8,128)(2,1)S(1)}, u32[]{:S(2)}, u32[]{:S(2)}) %collective-permute-start.6) | collective-permute-done | bytes 393248 | tf_op jit(solution)/shard_map/ppermute | solution.py:425
  43.4 0.0 collective-permute-start.11
  43.4 0.5 collective-permute-start.10
  43.9 0.0 collective-permute-done.12.refs_7_
  43.9 2.2 %shard_map.37 = (f32[8,512,128]{2,1,0:T(8,128)S(1)}, f32[14,8,512]{2,1,0:T(8,128)S(1)}) custom-call(s32[131]{0:T(256)S(1)} %get-tuple-element.28.refs_0_, s32[131]{0:T(256)S(1)} %get-tuple-element.29.refs_1_, s32[10]{0:T(128)S(1)} %get-tuple-element.30.refs_2_, bf16[512,384]{1,0:T(8,128)(2,1)S(1)} %collective-permute-done.6.refs_3_, ...), custom_call_target="tpu_custom_call" | custom-call | flops 5000000000 | bytes 8000000 | tf_op jit(solution)/shard_map/pallas_call | solution.py:337
  46.2 0.0 collective-permute-done.11.refs_6_
  46.2 1.4 %shard_map.38 = (f32[8,512]{1,0:T(8,128)S(1)}, f32[8,512]{1,0:T(8,128)S(1)}, f32[16,512]{1,0:T(8,128)S(1)}) custom-call(s32[131]{0:T(256)S(1)} %get-tuple-element.28.refs_0_, s32[131]{0:T(256)S(1)} %get-tuple-element.29.refs_1_, s32[10]{0:T(128)S(1)} %get-tuple-element.30.refs_2_, bf16[512,384]{1,0:T(8,128)(2,1)S(1)} %collective-permute-done.6.refs_3_, ...), custom_call_target="tpu_custom_call" | custom-call | flops 500000000 | bytes 8000000 | tf_op jit(solution)/shard_map/pallas_call | solution.py:337
  47.6 2.7 %collective-permute-start.13 = (f32[16,512]{1,0:T(8,128)S(1)}, f32[16,512]{1,0:T(8,128)S(1)}, u32[]{:S(2)}, u32[]{:S(2)}) collective-permute-start(f32[16,512]{1,0:T(8,128)S(1)} %get-tuple-element.49), channel_id=1, source_target_pairs={{0,16},{1,17},{2,18},{3,19},{4,20},{5,21},{6,22},{7,23},{8,24},{9,... | collective-permute-start | bytes 98312 | tf_op jit(solution)/shard_map/ppermute | solution.py:420
  50.3 0.9 %collective-permute-done.13 = f32[16,512]{1,0:T(8,128)S(1)} collective-permute-done((f32[16,512]{1,0:T(8,128)S(1)}, f32[16,512]{1,0:T(8,128)S(1)}, u32[]{:S(2)}, u32[]{:S(2)}) %collective-permute-start.13) | collective-permute-done | bytes 32800 | tf_op jit(solution)/shard_map/ppermute | solution.py:420
  51.1 3.8 %collective-permute-start.14 = (f32[8,512]{1,0:T(8,128)S(1)}, f32[8,512]{1,0:T(8,128)S(1)}, u32[]{:S(2)}, u32[]{:S(2)}) collective-permute-start(f32[8,512]{1,0:T(8,128)S(1)} %slice_maximum_fusion), channel_id=1, source_target_pairs={{0,12},{1,13},{2,14},{3,15},{4,8},{5,9},{6,10},{7,11},{8,4},{9,5},... | collective-permute-start | bytes 49160 | tf_op jit(solution)/shard_map/ppermute | solution.py:425
  54.9 1.1 %collective-permute-done.14 = f32[8,512]{1,0:T(8,128)S(1)} collective-permute-done((f32[8,512]{1,0:T(8,128)S(1)}, f32[8,512]{1,0:T(8,128)S(1)}, u32[]{:S(2)}, u32[]{:S(2)}) %collective-permute-start.14) | collective-permute-done | bytes 16416 | tf_op jit(solution)/shard_map/ppermute | solution.py:425
  56.0 0.1 collective-permute-start.15
  56.1 2.5 %collective-permute-done.15 = f32[4,512]{1,0:T(4,128)S(1)} collective-permute-done((f32[4,512]{1,0:T(4,128)S(1)}, f32[4,512]{1,0:T(4,128)S(1)}, u32[]{:S(2)}, u32[]{:S(2)}) %collective-permute-start.15) | collective-permute-done | bytes 8224 | tf_op jit(solution)/shard_map/ppermute | solution.py:425
  58.6 3.6 %collective-permute-start.16 = (f32[2,512]{1,0:T(2,128)S(1)}, f32[2,512]{1,0:T(2,128)S(1)}, u32[]{:S(2)}, u32[]{:S(2)}) collective-permute-start(f32[2,512]{1,0:T(2,128)S(1)} %slice.47), channel_id=1, source_target_pairs={{0,32},{1,33},{2,34},{3,35},{4,36},{5,37},{6,38},{7,39},{8,40},{9,... | collective-permute-start | bytes 12296 | tf_op jit(solution)/shard_map/ppermute | solution.py:425
  62.2 1.0 %collective-permute-done.16 = f32[2,512]{1,0:T(2,128)S(1)} collective-permute-done((f32[2,512]{1,0:T(2,128)S(1)}, f32[2,512]{1,0:T(2,128)S(1)}, u32[]{:S(2)}, u32[]{:S(2)}) %collective-permute-start.16) | collective-permute-done | bytes 4128 | tf_op jit(solution)/shard_map/ppermute | solution.py:425
  63.2 4.6 %collective-permute-start.17 = (f32[512]{0:T(512)S(1)}, f32[512]{0:T(512)S(1)}, u32[]{:S(2)}, u32[]{:S(2)}) collective-permute-start(f32[512]{0:T(512)S(1)} %bitcast.13), channel_id=1, source_target_pairs={{0,16},{1,17},{2,18},{3,19},{4,20},{5,21},{6,22},{7,23},{8,24},{9,... | collective-permute-start | bytes 6152 | tf_op jit(solution)/shard_map/ppermute | solution.py:420
  67.8 0.8 %collective-permute-done.17 = f32[512]{0:T(512)S(1)} collective-permute-done((f32[512]{0:T(512)S(1)}, f32[512]{0:T(512)S(1)}, u32[]{:S(2)}, u32[]{:S(2)}) %collective-permute-start.17) | collective-permute-done | bytes 2080 | tf_op jit(solution)/shard_map/ppermute | solution.py:420
  68.6 0.6 maximum_maximum_fusion
  (13 shorter events, 0.1 us)
Async XLA Ops:
  0.0 9.6 %copy-start.1 = (s32[256]{0:T(256)S(1)}, s32[256]{0:T(256)}, u32[]{:S(2)}) copy-start(s32[256]{0:T(256)} %cluster_ref.3) | copy-start | bytes 3076
  0.0 3.0 %collective-permute-start = (bf16[512,384]{1,0:T(8,128)(2,1)}, bf16[512,384]{1,0:T(8,128)(2,1)S(1)}, u32[]{:S(2)}, u32[]{:S(2)}) collective-permute-start(bf16[512,384]{1,0:T(8,128)(2,1)} %x_ref.1), channel_id=1, source_target_pairs={{0,16},{1,17},{2,18},{3,19},{4,20},{5,21},{6,22},{7,23},{8,24},{9,... | collective-permute-start | bytes 1179656 | tf_op jit(solution)/shard_map/ppermute | solution.py:420
  1.4 1.0 %copy-start = (bf16[512,384]{1,0:T(8,128)(2,1)S(1)}, bf16[512,384]{1,0:T(8,128)(2,1)}, u32[]{:S(2)}) copy-start(bf16[512,384]{1,0:T(8,128)(2,1)} %x_ref.1) | copy-start | bytes 1179652
  3.2 12.4 %collective-permute-start.3 = (bf16[2,512,384]{2,1,0:T(8,128)(2,1)S(1)}, bf16[2,512,384]{2,1,0:T(8,128)(2,1)S(1)}, u32[]{:S(2)}, u32[]{:S(2)}) collective-permute-start(bf16[2,512,384]{2,1,0:T(8,128)(2,1)S(1)} %shard_map.29.unit_ref.refs_4_), channel_id=1, source_target_pairs={{0,32},{1,33},{2,34},{3,35},{4,36},{5,37},{6,38},{7,39},{8,40},{9,... | collective-permute-start | bytes 2359304 | tf_op jit(solution)/shard_map/ppermute | solution.py:425
  5.8 13.1 %collective-permute-start.4 = (bf16[2,512,384]{2,1,0:T(8,128)(2,1)S(1)}, bf16[2,512,384]{2,1,0:T(8,128)(2,1)S(1)}, u32[]{:S(2)}, u32[]{:S(2)}) collective-permute-start(bf16[2,512,384]{2,1,0:T(8,128)(2,1)S(1)} %shard_map.29.unit_ref.refs_4_), channel_id=1, source_target_pairs={{0,12},{1,13},{2,14},{3,15},{4,8},{5,9},{6,10},{7,11},{8,4},{9,5},... | collective-permute-start | bytes 2359304 | tf_op jit(solution)/shard_map/ppermute | solution.py:425
  9.6 10.8 %collective-permute-start.1 = (bf16[2,512,384]{2,1,0:T(8,128)(2,1)S(1)}, bf16[2,512,384]{2,1,0:T(8,128)(2,1)S(1)}, u32[]{:S(2)}, u32[]{:S(2)}) collective-permute-start(bf16[2,512,384]{2,1,0:T(8,128)(2,1)S(1)} %shard_map.29.unit_ref.refs_4_), channel_id=1, source_target_pairs={{0,4},{1,5},{2,6},{3,7},{4,0},{5,1},{6,2},{7,3},{8,12},{9,13},{10,... | collective-permute-start | bytes 2359304 | tf_op jit(solution)/shard_map/ppermute | solution.py:425
  20.4 12.3 %collective-permute-start.8 = (bf16[2,512,384]{2,1,0:T(8,128)(2,1)S(1)}, bf16[2,512,384]{2,1,0:T(8,128)(2,1)S(1)}, u32[]{:S(2)}, u32[]{:S(2)}) collective-permute-start(bf16[2,512,384]{2,1,0:T(8,128)(2,1)S(1)} %collective-permute-done.4.c_ref), channel_id=1, source_target_pairs={{0,32},{1,33},{2,34},{3,35},{4,36},{5,37},{6,38},{7,39},{8,40},{9,... | collective-permute-start | bytes 2359304 | tf_op jit(solution)/shard_map/ppermute | solution.py:425
  20.9 11.9 %collective-permute-start.7 = (bf16[2,512,384]{2,1,0:T(8,128)(2,1)S(1)}, bf16[2,512,384]{2,1,0:T(8,128)(2,1)S(1)}, u32[]{:S(2)}, u32[]{:S(2)}) collective-permute-start(bf16[2,512,384]{2,1,0:T(8,128)(2,1)S(1)} %collective-permute-done.3.a_ref), channel_id=1, source_target_pairs={{0,4},{1,5},{2,6},{3,7},{4,0},{5,1},{6,2},{7,3},{8,12},{9,13},{10,... | collective-permute-start | bytes 2359304 | tf_op jit(solution)/shard_map/ppermute | solution.py:425
  21.1 12.4 %collective-permute-start.2 = (bf16[2,512,384]{2,1,0:T(8,128)(2,1)S(1)}, bf16[2,512,384]{2,1,0:T(8,128)(2,1)S(1)}, u32[]{:S(2)}, u32[]{:S(2)}) collective-permute-start(bf16[2,512,384]{2,1,0:T(8,128)(2,1)S(1)} %collective-permute-done.1.b_ref), channel_id=1, source_target_pairs={{0,12},{1,13},{2,14},{3,15},{4,8},{5,9},{6,10},{7,11},{8,4},{9,5},... | collective-permute-start | bytes 2359304 | tf_op jit(solution)/shard_map/ppermute | solution.py:425
  22.4 4.5 %collective-permute-start.5 = (bf16[6,512,384]{2,1,0:T(8,128)(2,1)S(1)}, bf16[6,512,384]{2,1,0:T(8,128)(2,1)S(1)}, u32[]{:S(2)}, u32[]{:S(2)}) collective-permute-start(bf16[6,512,384]{2,1,0:T(8,128)(2,1)S(1)} %shard_map.32.refs_3_), channel_id=1, source_target_pairs={{0,16},{1,17},{2,18},{3,19},{4,20},{5,21},{6,22},{7,23},{8,24},{9,... | collective-permute-start | bytes 7077896 | tf_op jit(solution)/shard_map/ppermute | solution.py:420
  33.8 7.2 %collective-permute-start.9 = (bf16[512,384]{1,0:T(8,128)(2,1)S(1)}, bf16[512,384]{1,0:T(8,128)(2,1)S(1)}, u32[]{:S(2)}, u32[]{:S(2)}) collective-permute-start(bf16[512,384]{1,0:T(8,128)(2,1)S(1)} %slice_bitcast_fusion), channel_id=1, source_target_pairs={{0,4},{1,5},{2,6},{3,7},{4,0},{5,1},{6,2},{7,3},{8,12},{9,13},{10,... | collective-permute-start | bytes 1179656 | tf_op jit(solution)/shard_map/ppermute | solution.py:425
  34.3 9.6 %collective-permute-start.12 = (bf16[6,512,384]{2,1,0:T(8,128)(2,1)S(1)}, bf16[6,512,384]{2,1,0:T(8,128)(2,1)S(1)}, u32[]{:S(2)}, u32[]{:S(2)}) collective-permute-start(bf16[6,512,384]{2,1,0:T(8,128)(2,1)S(1)} %shard_map.35.refs_3_.refs_5_), channel_id=1, source_target_pairs={{0,16},{1,17},{2,18},{3,19},{4,20},{5,21},{6,22},{7,23},{8,24},{9,... | collective-permute-start | bytes 7077896 | tf_op jit(solution)/shard_map/ppermute | solution.py:420
  35.6 7.8 %collective-permute-start.6 = (bf16[512,384]{1,0:T(8,128)(2,1)S(1)}, bf16[512,384]{1,0:T(8,128)(2,1)S(1)}, u32[]{:S(2)}, u32[]{:S(2)}) collective-permute-start(bf16[512,384]{1,0:T(8,128)(2,1)S(1)} %slice_bitcast_fusion.1), channel_id=1, source_target_pairs={{0,32},{1,33},{2,34},{3,35},{4,36},{5,37},{6,38},{7,39},{8,40},{9,... | collective-permute-start | bytes 1179656 | tf_op jit(solution)/shard_map/ppermute | solution.py:425
  43.4 2.7 %collective-permute-start.11 = (bf16[512,384]{1,0:T(8,128)(2,1)S(1)}, bf16[512,384]{1,0:T(8,128)(2,1)S(1)}, u32[]{:S(2)}, u32[]{:S(2)}) collective-permute-start(bf16[512,384]{1,0:T(8,128)(2,1)S(1)} %collective-permute-done.9.refs_4_), channel_id=1, source_target_pairs={{0,16},{1,17},{2,18},{3,19},{4,20},{5,21},{6,22},{7,23},{8,24},{9,... | collective-permute-start | bytes 1179656 | tf_op jit(solution)/shard_map/ppermute | solution.py:420
  43.4 2.8 %collective-permute-start.10 = (bf16[512,384]{1,0:T(8,128)(2,1)S(1)}, bf16[512,384]{1,0:T(8,128)(2,1)S(1)}, u32[]{:S(2)}, u32[]{:S(2)}) collective-permute-start(bf16[512,384]{1,0:T(8,128)(2,1)S(1)} %collective-permute-done.6.refs_3_), channel_id=1, source_target_pairs={{0,16},{1,17},{2,18},{3,19},{4,20},{5,21},{6,22},{7,23},{8,24},{9,... | collective-permute-start | bytes 1179656 | tf_op jit(solution)/shard_map/ppermute | solution.py:420
  47.6 3.5 %collective-permute-start.13 = (f32[16,512]{1,0:T(8,128)S(1)}, f32[16,512]{1,0:T(8,128)S(1)}, u32[]{:S(2)}, u32[]{:S(2)}) collective-permute-start(f32[16,512]{1,0:T(8,128)S(1)} %get-tuple-element.49), channel_id=1, source_target_pairs={{0,16},{1,17},{2,18},{3,19},{4,20},{5,21},{6,22},{7,23},{8,24},{9,... | collective-permute-start | bytes 98312 | tf_op jit(solution)/shard_map/ppermute | solution.py:420
  51.1 4.9 %collective-permute-start.14 = (f32[8,512]{1,0:T(8,128)S(1)}, f32[8,512]{1,0:T(8,128)S(1)}, u32[]{:S(2)}, u32[]{:S(2)}) collective-permute-start(f32[8,512]{1,0:T(8,128)S(1)} %slice_maximum_fusion), channel_id=1, source_target_pairs={{0,12},{1,13},{2,14},{3,15},{4,8},{5,9},{6,10},{7,11},{8,4},{9,5},... | collective-permute-start | bytes 49160 | tf_op jit(solution)/shard_map/ppermute | solution.py:425
  56.0 2.6 %collective-permute-start.15 = (f32[4,512]{1,0:T(4,128)S(1)}, f32[4,512]{1,0:T(4,128)S(1)}, u32[]{:S(2)}, u32[]{:S(2)}) collective-permute-start(f32[4,512]{1,0:T(4,128)S(1)} %slice.45), channel_id=1, source_target_pairs={{0,4},{1,5},{2,6},{3,7},{4,0},{5,1},{6,2},{7,3},{8,12},{9,13},{10,... | collective-permute-start | bytes 24584 | tf_op jit(solution)/shard_map/ppermute | solution.py:425
  58.6 4.6 %collective-permute-start.16 = (f32[2,512]{1,0:T(2,128)S(1)}, f32[2,512]{1,0:T(2,128)S(1)}, u32[]{:S(2)}, u32[]{:S(2)}) collective-permute-start(f32[2,512]{1,0:T(2,128)S(1)} %slice.47), channel_id=1, source_target_pairs={{0,32},{1,33},{2,34},{3,35},{4,36},{5,37},{6,38},{7,39},{8,40},{9,... | collective-permute-start | bytes 12296 | tf_op jit(solution)/shard_map/ppermute | solution.py:425
  63.2 5.4 %collective-permute-start.17 = (f32[512]{0:T(512)S(1)}, f32[512]{0:T(512)S(1)}, u32[]{:S(2)}, u32[]{:S(2)}) collective-permute-start(f32[512]{0:T(512)S(1)} %bitcast.13), channel_id=1, source_target_pairs={{0,16},{1,17},{2,18},{3,19},{4,20},{5,21},{6,22},{7,23},{8,24},{9,... | collective-permute-start | bytes 6152 | tf_op jit(solution)/shard_map/ppermute | solution.py:420

commit v10 on v9

--- a/solution.py
+++ b/solution.py
@@ -28,9 +28,19 @@
 EARLY = [(g, 0) for g in (1, 2, 3)]
 SECOND = [(g, h) for g in (1, 2, 3) for h in range(1, g + 1)]
 MIDDLE = [(g, h) for g in (4, 5, 6) for h in range(4)]
-LAST = [(g, h) for g in (4, 5, 6) for h in (4, 5, 6)] + [(7, h) for h in range(7)]
+LATE = [(g, h) for g in (4, 5, 6) for h in (4, 5, 6)]
+LAST = [(7, h) for h in range(4)]
+LAST2 = [(7, h) for h in (4, 5, 6)]
 FINAL = [(7, 7)]
-PHASES = ((EARLY, 1, 0), (SECOND, 1, 1), (MIDDLE, 4, 0), (LAST, 4, 0), (FINAL, 7, 7))
+PHASES = (
+    (EARLY, 1, 0),
+    (SECOND, 1, 1),
+    (MIDDLE, 4, 0),
+    (LATE, 4, 4),
+    (LAST, 7, 0),
+    (LAST2, 7, 4),
+    (FINAL, 7, 7),
+)
 
 
 def shared(g, h):
@@ -268,12 +278,15 @@
         score_part(*refs, part_ref[first + n])
 
 
-def put_rows(out_ref, place, row_ref, first):
+def put_rows(out_ref, place, first, *row_refs):
     for half in range(2):
         at = place + half
         for k in range(SHARD // 128):
-            part = row_ref[first + half, 128 * k : 128 * k + 128, :].T
-            out_ref[at : at + 1, 128 * k : 128 * k + 128] = jnp.max(part, axis=0, keepdims=True)
+            lines = slice(128 * k, 128 * k + 128)
+            part = row_refs[0][first + half, lines, :]
+            for ref in row_refs[1:]:
+                part = jnp.maximum(part, ref[first + half, lines, :])
+            out_ref[at : at + 1, lines] = jnp.max(part.T, axis=0, keepdims=True)
 
 
 def clear(*refs):
@@ -307,7 +320,7 @@
     col_ref[:2] = col_in[...]
     col_ref[2:] = col_low[...]
     for n in range(0, 6, 2):
-        put_rows(rows_out, n, row_ref, n)
+        put_rows(rows_out, n, n, row_ref)
 
 
 def middle_kernel(*refs):
@@ -367,46 +380,49 @@
 
 def last_kernel(*refs):
     plan, mine, refs = refs[:3], refs[3:5], refs[5:]
-    a_mid, b_low, b_mid, row_in, col_in, row_ref, col_ref, a_buf, b_buf = refs
-    a_buf[:6] = a_mid[...]
-    b_buf[:8] = b_low[...]
-    b_buf[8:] = b_mid[...]
+    a_mid, b_low, b_mid, col_in, row_mid, row_last, col_low, col_mid, a_last = refs
+    clear(row_mid, row_last, col_mid)
     for half in range(2):
-        a_buf[6 + half] = mine[half][...]
-    row_ref[:6] = row_in[...]
-    row_ref[6:] = jnp.full((2, SHARD, 128), -2.0, jnp.float32)
-    col_ref[:8] = col_in[...]
-    col_ref[8:] = jnp.full((6, 8, SHARD), -2.0, jnp.float32)
-    score_lists(3, *plan, a_buf, b_buf, row_ref, col_ref)
+        a_last[half] = mine[half][...]
+    col_low[...] = col_in[...]
+    score_lists(3, *plan, a_mid, b_mid, row_mid, col_mid)
+    score_lists(4, *plan, a_last, b_low, row_last, col_low)
+    score_lists(5, *plan, a_last, b_mid, row_last, col_mid)
 
 
 def last_call(plan, *operands):
-    outs = (rows_of(8), cols_of(14))
-    return kernel_call(last_kernel, [*plan, *operands], outs, [shards(8), shards(14)], 5000000000)
+    outs = (rows_of(6), rows_of(2), cols_of(8), cols_of(6))
+    return kernel_call(last_kernel, [*plan, *operands], outs, [shards(2)], 5000000000)
 
 
 def final_kernel(*refs):
     plan, mine, theirs, refs = refs[:3], refs[3:5], refs[5:7], refs[7:]
-    rows0, row_in, col_in, keep_ref, send_ref, other_ref, a_buf, b_buf, row_ref, col_ref = refs
+    rows0, row_one, row_two, row_in, low_in, mid_in, refs = *refs[:6], refs[6:]
+    keep_ref, send_ref, other_ref, a_buf, b_buf, row_ref, col_ref = refs
     for half in range(2):
         a_buf[half] = mine[half][...]
         b_buf[half] = theirs[half][...]
-    row_ref[...] = row_in[6:]
+    row_ref[...] = row_in[...]
     clear(col_ref)
-    score_lists(4, *plan, a_buf, b_buf, row_ref, col_ref)
+    score_lists(6, *plan, a_buf, b_buf, row_ref, col_ref)
     keep_ref[0:2] = jnp.full((2, SHARD), -2.0, jnp.float32)
     for out_ref, slots in ((keep_ref, KEPT), (send_ref, SENT)):
         for place, slot in enumerate(slots):
             if slot == 7:
-                put_rows(out_ref, 2 * place, row_ref, 0)
+                put_rows(out_ref, 2 * place, 0, row_ref)
             elif slot > 3:
-                put_rows(out_ref, 2 * place, row_in, 2 * slot - 8)
+                put_rows(out_ref, 2 * place, 2 * slot - 8, row_one, row_two)
             elif slot > 0:
                 out_ref[2 * place : 2 * place + 2] = rows0[2 * slot - 2 : 2 * slot]
     for place, slot in enumerate(KEPT + SENT):
         for half in range(2):
             at = 2 * place + half
-            down = col_ref[half] if slot == 7 else col_in[2 * slot + half]
+            if slot == 7:
+                down = col_ref[half]
+            elif slot > 3:
+                down = mid_in[2 * slot - 8 + half]
+            else:
+                down = low_in[2 * slot + half]
             other_ref[at : at + 1, :] = jnp.max(down, axis=0, keepdims=True)
 
 
@@ -453,8 +469,10 @@
     rows1, cols = middle_call(plan, a_mid, b_low, cols)
     halves = [after(x, cols) for x in halves]
     swapped = [swap(x) for x in halves]
-    rows1, cols = last_call(plan, *halves, a_mid, b_low, b_mid, rows1, cols)
-    keep, send, other = final_call(plan, *halves, *swapped, rows0, rows1, cols)
+    rows2, rows3, cols, cols2 = last_call(plan, *halves, a_mid, b_low, b_mid, cols)
+    keep, send, other = final_call(
+        plan, *halves, *swapped, rows0, rows1, rows2, rows3, cols, cols2
+    )
     other = swap(other)
     keep = jnp.maximum(keep, other[:8])
     send = jnp.maximum(send, other[8:])

time: 68 us -> 68.5 us (level)
  starting transfers between devices: 29 us -> 22.8 us
  Pallas kernels: 16.3 us -> 19.5 us
  waiting for transfers between devices: 22 us -> 25 us
    ppermute x7, starting transfers between devices: 10.4 us -> 4.73 us  [swap(): return lax.ppermute(x, ('row', 'col'), [(s, s ^ CORE) for s in range(128)])]
    pallas_call x7, Pallas kernels: 11.1 us -> 14.3 us  [kernel_call(): pl.pallas_call(kernel, out_shape=outs, in_specs=[spec(SMEM)] * smem + [sp...]
    ppermute x11, waiting for transfers between devices: 16.8 us -> 19.3 us  [exchange(): return lax.ppermute(x, ('row', 'col'), pairs)]
  transfers between devices with their start and end apart: 18 -> 18, of which waited for: 14 -> 14; matrix products, arithmetic and copies ran while one was open for 0% -> 0% of each run, Pallas kernels for 21% -> 25%
where the time goes in v10:
time: 68.5 us; the launch traced here: 69.2 us
  waiting for transfers between devices  25 us (36%)
  starting transfers between devices  22.8 us (33%)
  Pallas kernels  19.5 us (28%)
  local copies, waits for them, and re-layouts  1.09 us (2%)
    ppermute x11, waiting for transfers between devices, exchange(): return lax.ppermute(x, ('row', 'col'), pairs)  19.3 us
    ppermute x11, starting transfers between devices, exchange(): return lax.ppermute(x, ('row', 'col'), pairs)  18.1 us
    pallas_call x7, Pallas kernels, kernel_call(): pl.pallas_call(kernel, out_shape=outs, in_specs=[spec(SMEM)] * smem + [sp...  14.3 us
    ppermute x7, waiting for transfers between devices, swap(): return lax.ppermute(x, ('row', 'col'), [(s, s ^ CORE) for s in range(128)])  5.78 us
    ppermute x7, starting transfers between devices, swap(): return lax.ppermute(x, ('row', 'col'), [(s, s ^ CORE) for s in range(128)])  4.73 us
    pallas_call x1, Pallas kernels, plan_call(): pl.pallas_call(plan_kernel, out_shape=(lists, lists, jax.ShapeDtypeStruct...  3.57 us
  transfers between devices with their start and end apart: 18, of which 14 were waited for; matrix products, arithmetic and copies ran while one was open for 0% of the time, Pallas kernels for 25%

profile of v10, /device:TPU:1, one launch (start us, length us, event | category | flops | bytes accessed | tf_op | source)
XLA Modules:
  0.0 69.2 jit_solution(9878907490523048838)
XLA Ops:
  0.0 1.4 %collective-permute-start = (bf16[512,384]{1,0:T(8,128)(2,1)}, bf16[512,384]{1,0:T(8,128)(2,1)S(1)}, u32[]{:S(2)}, u32[]{:S(2)}) collective-permute-start(bf16[512,384]{1,0:T(8,128)(2,1)} %x_ref.1), channel_id=1, source_target_pairs={{0,16},{1,17},{2,18},{3,19},{4,20},{5,21},{6,22},{7,23},{8,24},{9,... | collective-permute-start | bytes 1179656 | tf_op jit(solution)/shard_map/ppermute | solution.py:436
  1.4 1.0 %copy-done = bf16[512,384]{1,0:T(8,128)(2,1)S(1)} copy-done((bf16[512,384]{1,0:T(8,128)(2,1)S(1)}, bf16[512,384]{1,0:T(8,128)(2,1)}, u32[]{:S(2)}) %copy-start) | copy-done | bytes 393240
  2.4 0.2 shard_map.28.own_ref
  2.6 0.4 collective-permute-done.other_ref
  3.0 0.2 shard_map.29.unit_ref.refs_4_
  3.2 2.6 %collective-permute-start.3 = (bf16[2,512,384]{2,1,0:T(8,128)(2,1)S(1)}, bf16[2,512,384]{2,1,0:T(8,128)(2,1)S(1)}, u32[]{:S(2)}, u32[]{:S(2)}) collective-permute-start(bf16[2,512,384]{2,1,0:T(8,128)(2,1)S(1)} %shard_map.29.unit_ref.refs_4_), channel_id=1, source_target_pairs={{0,32},{1,33},{2,34},{3,35},{4,36},{5,37},{6,38},{7,39},{8,40},{9,... | collective-permute-start | bytes 2359304 | tf_op jit(solution)/shard_map/ppermute | solution.py:441
  5.8 3.8 %collective-permute-start.4 = (bf16[2,512,384]{2,1,0:T(8,128)(2,1)S(1)}, bf16[2,512,384]{2,1,0:T(8,128)(2,1)S(1)}, u32[]{:S(2)}, u32[]{:S(2)}) collective-permute-start(bf16[2,512,384]{2,1,0:T(8,128)(2,1)S(1)} %shard_map.29.unit_ref.refs_4_), channel_id=1, source_target_pairs={{0,12},{1,13},{2,14},{3,15},{4,8},{5,9},{6,10},{7,11},{8,4},{9,5},... | collective-permute-start | bytes 2359304 | tf_op jit(solution)/shard_map/ppermute | solution.py:441
  9.6 0.0 collective-permute-start.1
  9.6 3.6 %shard_map.31 = (s32[133]{0:T(256)S(1)}, s32[133]{0:T(256)S(1)}, s32[14]{0:T(128)S(1)}) custom-call(s32[1]{0:T(128)} %bitcast.here_ref, s32[256]{0:T(256)S(1)} %copy-done.1, s32[2,128]{1,0:T(2,128)S(1)} %bitcast.11), custom_call_target="tpu_custom_call" | custom-call | flops 3000000000 | bytes 10000 | tf_op jit(solution)/shard_map/pallas_call | solution.py:204
  13.1 1.3 %shard_map.30 = f32[1,512]{1,0:T(1,128)S(1)} custom-call(s32[1]{0:T(128)} %bitcast.here_ref, s32[256]{0:T(256)S(1)} %copy-done.1, bf16[2,512,384]{2,1,0:T(8,128)(2,1)S(1)} %shard_map.29.unit_ref.refs_4_), custom_call_target="tpu_custom_call" | custom-call | flops 1000000000 | bytes 1000000 | tf_op jit(solution)/shard_map/pallas_call | solution.py:216
  14.5 1.1 %collective-permute-done.3.a_ref = bf16[2,512,384]{2,1,0:T(8,128)(2,1)S(1)} collective-permute-done((bf16[2,512,384]{2,1,0:T(8,128)(2,1)S(1)}, bf16[2,512,384]{2,1,0:T(8,128)(2,1)S(1)}, u32[]{:S(2)}, u32[]{:S(2)}) %collective-permute-start.3) | collective-permute-done | bytes 786464 | tf_op jit(solution)/shard_map/ppermute | solution.py:441
  15.6 3.4 %collective-permute-done.4.c_ref = bf16[2,512,384]{2,1,0:T(8,128)(2,1)S(1)} collective-permute-done((bf16[2,512,384]{2,1,0:T(8,128)(2,1)S(1)}, bf16[2,512,384]{2,1,0:T(8,128)(2,1)S(1)}, u32[]{:S(2)}, u32[]{:S(2)}) %collective-permute-start.4) | collective-permute-done | bytes 786464 | tf_op jit(solution)/shard_map/ppermute | solution.py:441
  18.9 1.5 %collective-permute-done.1.b_ref = bf16[2,512,384]{2,1,0:T(8,128)(2,1)S(1)} collective-permute-done((bf16[2,512,384]{2,1,0:T(8,128)(2,1)S(1)}, bf16[2,512,384]{2,1,0:T(8,128)(2,1)S(1)}, u32[]{:S(2)}, u32[]{:S(2)}) %collective-permute-start.1) | collective-permute-done | bytes 786464 | tf_op jit(solution)/shard_map/ppermute | solution.py:441
  20.4 0.5 collective-permute-start.8
  20.9 0.0 collective-permute-start.7
  20.9 0.2 shard_map.32.refs_3_
  21.1 1.3 %collective-permute-start.2 = (bf16[2,512,384]{2,1,0:T(8,128)(2,1)S(1)}, bf16[2,512,384]{2,1,0:T(8,128)(2,1)S(1)}, u32[]{:S(2)}, u32[]{:S(2)}) collective-permute-start(bf16[2,512,384]{2,1,0:T(8,128)(2,1)S(1)} %collective-permute-done.1.b_ref), channel_id=1, source_target_pairs={{0,12},{1,13},{2,14},{3,15},{4,8},{5,9},{6,10},{7,11},{8,4},{9,5},... | collective-permute-start | bytes 2359304 | tf_op jit(solution)/shard_map/ppermute | solution.py:441
  22.4 0.0 collective-permute-start.5
  22.4 1.2 %shard_map.33 = (f32[6,512,128]{2,1,0:T(8,128)S(1)}, f32[2,8,512]{2,1,0:T(8,128)S(1)}) custom-call(s32[133]{0:T(256)S(1)} %get-tuple-element.30.refs_0_, s32[133]{0:T(256)S(1)} %get-tuple-element.31.refs_1_, s32[14]{0:T(128)S(1)} %get-tuple-element.32.refs_2_, bf16[6,512,384]{2,1,0:T(8,128)(2,1)S(1)} %shard_map.32.refs_3_, ...), custom_call_target="tpu_custom_call" | custom-call | flops 30000001024 | bytes 8000000 | tf_op jit(solution)/shard_map/pallas_call | solution.py:350
  23.6 3.4 %collective-permute-done.5.refs_5_ = bf16[6,512,384]{2,1,0:T(8,128)(2,1)S(1)} collective-permute-done((bf16[6,512,384]{2,1,0:T(8,128)(2,1)S(1)}, bf16[6,512,384]{2,1,0:T(8,128)(2,1)S(1)}, u32[]{:S(2)}, u32[]{:S(2)}) %collective-permute-start.5) | collective-permute-done | bytes 2359328 | tf_op jit(solution)/shard_map/ppermute | solution.py:436
  26.9 2.7 %shard_map.34 = (f32[6,512]{1,0:T(8,128)S(1)}, f32[8,8,512]{2,1,0:T(8,128)S(1)}, bf16[8,512,384]{2,1,0:T(8,128)(2,1)S(1)}) custom-call(s32[133]{0:T(256)S(1)} %get-tuple-element.30.refs_0_, s32[133]{0:T(256)S(1)} %get-tuple-element.31.refs_1_, s32[14]{0:T(128)S(1)} %get-tuple-element.32.refs_2_, bf16[6,512,384]{2,1,0:T(8,128)(2,1)S(1)} %shard_map.32.refs_3_, ...), custom_call_target="tpu_custom_call" | custom-call | flops 3000000000 | bytes 8000000 | tf_op jit(solution)/shard_map/pallas_call | solution.py:350
  29.6 3.2 %collective-permute-done.8.c_ref = bf16[2,512,384]{2,1,0:T(8,128)(2,1)S(1)} collective-permute-done((bf16[2,512,384]{2,1,0:T(8,128)(2,1)S(1)}, bf16[2,512,384]{2,1,0:T(8,128)(2,1)S(1)}, u32[]{:S(2)}, u32[]{:S(2)}) %collective-permute-start.8) | collective-permute-done | bytes 786464 | tf_op jit(solution)/shard_map/ppermute | solution.py:441
  32.7 0.0 collective-permute-done.7.a_ref
  32.7 0.8 %collective-permute-done.2.b_ref = bf16[2,512,384]{2,1,0:T(8,128)(2,1)S(1)} collective-permute-done((bf16[2,512,384]{2,1,0:T(8,128)(2,1)S(1)}, bf16[2,512,384]{2,1,0:T(8,128)(2,1)S(1)}, u32[]{:S(2)}, u32[]{:S(2)}) %collective-permute-start.2) | collective-permute-done | bytes 786464 | tf_op jit(solution)/shard_map/ppermute | solution.py:441
  33.6 0.2 shard_map.35.refs_3_.refs_5_
  33.8 0.5 collective-permute-start.9
  34.3 1.2 %collective-permute-start.12 = (bf16[6,512,384]{2,1,0:T(8,128)(2,1)S(1)}, bf16[6,512,384]{2,1,0:T(8,128)(2,1)S(1)}, u32[]{:S(2)}, u32[]{:S(2)}) collective-permute-start(bf16[6,512,384]{2,1,0:T(8,128)(2,1)S(1)} %shard_map.35.refs_3_.refs_5_), channel_id=1, source_target_pairs={{0,16},{1,17},{2,18},{3,19},{4,20},{5,21},{6,22},{7,23},{8,24},{9,... | collective-permute-start | bytes 7077896 | tf_op jit(solution)/shard_map/ppermute | solution.py:436
  35.6 2.5 %collective-permute-start.6 = (bf16[512,384]{1,0:T(8,128)(2,1)S(1)}, bf16[512,384]{1,0:T(8,128)(2,1)S(1)}, u32[]{:S(2)}, u32[]{:S(2)}) collective-permute-start(bf16[512,384]{1,0:T(8,128)(2,1)S(1)} %slice_bitcast_fusion.1), channel_id=1, source_target_pairs={{0,32},{1,33},{2,34},{3,35},{4,36},{5,37},{6,38},{7,39},{8,40},{9,... | collective-permute-start | bytes 1179656 | tf_op jit(solution)/shard_map/ppermute | solution.py:441
  38.1 2.4 %shard_map.36 = (f32[6,512,128]{2,1,0:T(8,128)S(1)}, f32[8,8,512]{2,1,0:T(8,128)S(1)}) custom-call(s32[133]{0:T(256)S(1)} %get-tuple-element.30.refs_0_, s32[133]{0:T(256)S(1)} %get-tuple-element.31.refs_1_, s32[14]{0:T(128)S(1)} %get-tuple-element.32.refs_2_, bf16[6,512,384]{2,1,0:T(8,128)(2,1)S(1)} %shard_map.35.refs_3_.refs_5_, ...), custom_call_target="tpu_custom_call" | custom-call | flops 30000001024 | bytes 8000000 | tf_op jit(solution)/shard_map/pallas_call | solution.py:350
  40.5 0.5 collective-permute-done.9.refs_4_
  41.0 2.4 %collective-permute-done.6.refs_3_ = bf16[512,384]{1,0:T(8,128)(2,1)S(1)} collective-permute-done((bf16[512,384]{1,0:T(8,128)(2,1)S(1)}, bf16[512,384]{1,0:T(8,128)(2,1)S(1)}, u32[]{:S(2)}, u32[]{:S(2)}) %collective-permute-start.6) | collective-permute-done | bytes 393248 | tf_op jit(solution)/shard_map/ppermute | solution.py:441
  43.4 0.0 collective-permute-start.11
  43.4 0.5 collective-permute-start.10
  43.9 0.0 collective-permute-done.12.refs_7_
  43.9 5.5 %shard_map.37 = (f32[6,512,128]{2,1,0:T(8,128)S(1)}, f32[2,512,128]{2,1,0:T(8,128)S(1)}, f32[8,8,512]{2,1,0:T(8,128)S(1)}, f32[6,8,512]{2,1,0:T(8,128)S(1)}) custom-call(s32[133]{0:T(256)S(1)} %get-tuple-element.30.refs_0_, s32[133]{0:T(256)S(1)} %get-tuple-element.31.refs_1_, s32[14]{0:T(128)S(1)} %get-tuple-element.32.refs_2_, ...), custom_call_target="tpu_custom_call" | custom-call | flops 5000000000 | bytes 8000000 | tf_op jit(solution)/shard_map/pallas_call | solution.py:350
  49.5 0.0 collective-permute-done.11.refs_6_
  49.5 2.1 %shard_map.38 = (f32[8,512]{1,0:T(8,128)S(1)}, f32[8,512]{1,0:T(8,128)S(1)}, f32[16,512]{1,0:T(8,128)S(1)}) custom-call(s32[133]{0:T(256)S(1)} %get-tuple-element.30.refs_0_, s32[133]{0:T(256)S(1)} %get-tuple-element.31.refs_1_, s32[14]{0:T(128)S(1)} %get-tuple-element.32.refs_2_, bf16[512,384]{1,0:T(8,128)(2,1)S(1)} %collective-permute-done.6.refs_3_, ...), custom_call_target="tpu_custom_call" | custom-call | flops 500000000 | bytes 8000000 | tf_op jit(solution)/shard_map/pallas_call | solution.py:350
  51.6 1.5 %collective-permute-start.13 = (f32[16,512]{1,0:T(8,128)S(1)}, f32[16,512]{1,0:T(8,128)S(1)}, u32[]{:S(2)}, u32[]{:S(2)}) collective-permute-start(f32[16,512]{1,0:T(8,128)S(1)} %get-tuple-element.53), channel_id=1, source_target_pairs={{0,16},{1,17},{2,18},{3,19},{4,20},{5,21},{6,22},{7,23},{8,24},{9,... | collective-permute-start | bytes 98312 | tf_op jit(solution)/shard_map/ppermute | solution.py:436
  53.1 0.9 %collective-permute-done.13 = f32[16,512]{1,0:T(8,128)S(1)} collective-permute-done((f32[16,512]{1,0:T(8,128)S(1)}, f32[16,512]{1,0:T(8,128)S(1)}, u32[]{:S(2)}, u32[]{:S(2)}) %collective-permute-start.13) | collective-permute-done | bytes 32800 | tf_op jit(solution)/shard_map/ppermute | solution.py:436
  53.9 5.9 %collective-permute-start.14 = (f32[8,512]{1,0:T(8,128)S(1)}, f32[8,512]{1,0:T(8,128)S(1)}, u32[]{:S(2)}, u32[]{:S(2)}) collective-permute-start(f32[8,512]{1,0:T(8,128)S(1)} %slice_maximum_fusion), channel_id=1, source_target_pairs={{0,12},{1,13},{2,14},{3,15},{4,8},{5,9},{6,10},{7,11},{8,4},{9,5},... | collective-permute-start | bytes 49160 | tf_op jit(solution)/shard_map/ppermute | solution.py:441
  59.9 1.1 %collective-permute-done.14 = f32[8,512]{1,0:T(8,128)S(1)} collective-permute-done((f32[8,512]{1,0:T(8,128)S(1)}, f32[8,512]{1,0:T(8,128)S(1)}, u32[]{:S(2)}, u32[]{:S(2)}) %collective-permute-start.14) | collective-permute-done | bytes 16416 | tf_op jit(solution)/shard_map/ppermute | solution.py:441
  61.0 0.1 collective-permute-start.15
  61.1 2.5 %collective-permute-done.15 = f32[4,512]{1,0:T(4,128)S(1)} collective-permute-done((f32[4,512]{1,0:T(4,128)S(1)}, f32[4,512]{1,0:T(4,128)S(1)}, u32[]{:S(2)}, u32[]{:S(2)}) %collective-permute-start.15) | collective-permute-done | bytes 8224 | tf_op jit(solution)/shard_map/ppermute | solution.py:441
  63.6 0.9 %collective-permute-start.16 = (f32[2,512]{1,0:T(2,128)S(1)}, f32[2,512]{1,0:T(2,128)S(1)}, u32[]{:S(2)}, u32[]{:S(2)}) collective-permute-start(f32[2,512]{1,0:T(2,128)S(1)} %slice.47), channel_id=1, source_target_pairs={{0,32},{1,33},{2,34},{3,35},{4,36},{5,37},{6,38},{7,39},{8,40},{9,... | collective-permute-start | bytes 12296 | tf_op jit(solution)/shard_map/ppermute | solution.py:441
  64.5 2.9 %collective-permute-done.16 = f32[2,512]{1,0:T(2,128)S(1)} collective-permute-done((f32[2,512]{1,0:T(2,128)S(1)}, f32[2,512]{1,0:T(2,128)S(1)}, u32[]{:S(2)}, u32[]{:S(2)}) %collective-permute-start.16) | collective-permute-done | bytes 4128 | tf_op jit(solution)/shard_map/ppermute | solution.py:441
  67.4 0.1 collective-permute-start.17
  67.4 1.1 %collective-permute-done.17 = f32[512]{0:T(512)S(1)} collective-permute-done((f32[512]{0:T(512)S(1)}, f32[512]{0:T(512)S(1)}, u32[]{:S(2)}, u32[]{:S(2)}) %collective-permute-start.17) | collective-permute-done | bytes 2080 | tf_op jit(solution)/shard_map/ppermute | solution.py:436
  68.6 0.6 maximum_maximum_fusion
  (13 shorter events, 0.1 us)
Async XLA Ops:
  0.0 9.6 %copy-start.1 = (s32[256]{0:T(256)S(1)}, s32[256]{0:T(256)}, u32[]{:S(2)}) copy-start(s32[256]{0:T(256)} %cluster_ref.3) | copy-start | bytes 3076
  0.0 3.0 %collective-permute-start = (bf16[512,384]{1,0:T(8,128)(2,1)}, bf16[512,384]{1,0:T(8,128)(2,1)S(1)}, u32[]{:S(2)}, u32[]{:S(2)}) collective-permute-start(bf16[512,384]{1,0:T(8,128)(2,1)} %x_ref.1), channel_id=1, source_target_pairs={{0,16},{1,17},{2,18},{3,19},{4,20},{5,21},{6,22},{7,23},{8,24},{9,... | collective-permute-start | bytes 1179656 | tf_op jit(solution)/shard_map/ppermute | solution.py:436
  1.4 1.0 %copy-start = (bf16[512,384]{1,0:T(8,128)(2,1)S(1)}, bf16[512,384]{1,0:T(8,128)(2,1)}, u32[]{:S(2)}) copy-start(bf16[512,384]{1,0:T(8,128)(2,1)} %x_ref.1) | copy-start | bytes 1179652
  3.2 12.4 %collective-permute-start.3 = (bf16[2,512,384]{2,1,0:T(8,128)(2,1)S(1)}, bf16[2,512,384]{2,1,0:T(8,128)(2,1)S(1)}, u32[]{:S(2)}, u32[]{:S(2)}) collective-permute-start(bf16[2,512,384]{2,1,0:T(8,128)(2,1)S(1)} %shard_map.29.unit_ref.refs_4_), channel_id=1, source_target_pairs={{0,32},{1,33},{2,34},{3,35},{4,36},{5,37},{6,38},{7,39},{8,40},{9,... | collective-permute-start | bytes 2359304 | tf_op jit(solution)/shard_map/ppermute | solution.py:441
  5.8 13.1 %collective-permute-start.4 = (bf16[2,512,384]{2,1,0:T(8,128)(2,1)S(1)}, bf16[2,512,384]{2,1,0:T(8,128)(2,1)S(1)}, u32[]{:S(2)}, u32[]{:S(2)}) collective-permute-start(bf16[2,512,384]{2,1,0:T(8,128)(2,1)S(1)} %shard_map.29.unit_ref.refs_4_), channel_id=1, source_target_pairs={{0,12},{1,13},{2,14},{3,15},{4,8},{5,9},{6,10},{7,11},{8,4},{9,5},... | collective-permute-start | bytes 2359304 | tf_op jit(solution)/shard_map/ppermute | solution.py:441
  9.6 10.8 %collective-permute-start.1 = (bf16[2,512,384]{2,1,0:T(8,128)(2,1)S(1)}, bf16[2,512,384]{2,1,0:T(8,128)(2,1)S(1)}, u32[]{:S(2)}, u32[]{:S(2)}) collective-permute-start(bf16[2,512,384]{2,1,0:T(8,128)(2,1)S(1)} %shard_map.29.unit_ref.refs_4_), channel_id=1, source_target_pairs={{0,4},{1,5},{2,6},{3,7},{4,0},{5,1},{6,2},{7,3},{8,12},{9,13},{10,... | collective-permute-start | bytes 2359304 | tf_op jit(solution)/shard_map/ppermute | solution.py:441
  20.4 12.3 %collective-permute-start.8 = (bf16[2,512,384]{2,1,0:T(8,128)(2,1)S(1)}, bf16[2,512,384]{2,1,0:T(8,128)(2,1)S(1)}, u32[]{:S(2)}, u32[]{:S(2)}) collective-permute-start(bf16[2,512,384]{2,1,0:T(8,128)(2,1)S(1)} %collective-permute-done.4.c_ref), channel_id=1, source_target_pairs={{0,32},{1,33},{2,34},{3,35},{4,36},{5,37},{6,38},{7,39},{8,40},{9,... | collective-permute-start | bytes 2359304 | tf_op jit(solution)/shard_map/ppermute | solution.py:441
  20.9 11.9 %collective-permute-start.7 = (bf16[2,512,384]{2,1,0:T(8,128)(2,1)S(1)}, bf16[2,512,384]{2,1,0:T(8,128)(2,1)S(1)}, u32[]{:S(2)}, u32[]{:S(2)}) collective-permute-start(bf16[2,512,384]{2,1,0:T(8,128)(2,1)S(1)} %collective-permute-done.3.a_ref), channel_id=1, source_target_pairs={{0,4},{1,5},{2,6},{3,7},{4,0},{5,1},{6,2},{7,3},{8,12},{9,13},{10,... | collective-permute-start | bytes 2359304 | tf_op jit(solution)/shard_map/ppermute | solution.py:441
  21.1 12.4 %collective-permute-start.2 = (bf16[2,512,384]{2,1,0:T(8,128)(2,1)S(1)}, bf16[2,512,384]{2,1,0:T(8,128)(2,1)S(1)}, u32[]{:S(2)}, u32[]{:S(2)}) collective-permute-start(bf16[2,512,384]{2,1,0:T(8,128)(2,1)S(1)} %collective-permute-done.1.b_ref), channel_id=1, source_target_pairs={{0,12},{1,13},{2,14},{3,15},{4,8},{5,9},{6,10},{7,11},{8,4},{9,5},... | collective-permute-start | bytes 2359304 | tf_op jit(solution)/shard_map/ppermute | solution.py:441
  22.4 4.5 %collective-permute-start.5 = (bf16[6,512,384]{2,1,0:T(8,128)(2,1)S(1)}, bf16[6,512,384]{2,1,0:T(8,128)(2,1)S(1)}, u32[]{:S(2)}, u32[]{:S(2)}) collective-permute-start(bf16[6,512,384]{2,1,0:T(8,128)(2,1)S(1)} %shard_map.32.refs_3_), channel_id=1, source_target_pairs={{0,16},{1,17},{2,18},{3,19},{4,20},{5,21},{6,22},{7,23},{8,24},{9,... | collective-permute-start | bytes 7077896 | tf_op jit(solution)/shard_map/ppermute | solution.py:436
  33.8 7.2 %collective-permute-start.9 = (bf16[512,384]{1,0:T(8,128)(2,1)S(1)}, bf16[512,384]{1,0:T(8,128)(2,1)S(1)}, u32[]{:S(2)}, u32[]{:S(2)}) collective-permute-start(bf16[512,384]{1,0:T(8,128)(2,1)S(1)} %slice_bitcast_fusion), channel_id=1, source_target_pairs={{0,4},{1,5},{2,6},{3,7},{4,0},{5,1},{6,2},{7,3},{8,12},{9,13},{10,... | collective-permute-start | bytes 1179656 | tf_op jit(solution)/shard_map/ppermute | solution.py:441
  34.3 9.6 %collective-permute-start.12 = (bf16[6,512,384]{2,1,0:T(8,128)(2,1)S(1)}, bf16[6,512,384]{2,1,0:T(8,128)(2,1)S(1)}, u32[]{:S(2)}, u32[]{:S(2)}) collective-permute-start(bf16[6,512,384]{2,1,0:T(8,128)(2,1)S(1)} %shard_map.35.refs_3_.refs_5_), channel_id=1, source_target_pairs={{0,16},{1,17},{2,18},{3,19},{4,20},{5,21},{6,22},{7,23},{8,24},{9,... | collective-permute-start | bytes 7077896 | tf_op jit(solution)/shard_map/ppermute | solution.py:436
  35.6 7.8 %collective-permute-start.6 = (bf16[512,384]{1,0:T(8,128)(2,1)S(1)}, bf16[512,384]{1,0:T(8,128)(2,1)S(1)}, u32[]{:S(2)}, u32[]{:S(2)}) collective-permute-start(bf16[512,384]{1,0:T(8,128)(2,1)S(1)} %slice_bitcast_fusion.1), channel_id=1, source_target_pairs={{0,32},{1,33},{2,34},{3,35},{4,36},{5,37},{6,38},{7,39},{8,40},{9,... | collective-permute-start | bytes 1179656 | tf_op jit(solution)/shard_map/ppermute | solution.py:441
  43.4 6.1 %collective-permute-start.11 = (bf16[512,384]{1,0:T(8,128)(2,1)S(1)}, bf16[512,384]{1,0:T(8,128)(2,1)S(1)}, u32[]{:S(2)}, u32[]{:S(2)}) collective-permute-start(bf16[512,384]{1,0:T(8,128)(2,1)S(1)} %collective-permute-done.9.refs_4_), channel_id=1, source_target_pairs={{0,16},{1,17},{2,18},{3,19},{4,20},{5,21},{6,22},{7,23},{8,24},{9,... | collective-permute-start | bytes 1179656 | tf_op jit(solution)/shard_map/ppermute | solution.py:436
  43.4 6.1 %collective-permute-start.10 = (bf16[512,384]{1,0:T(8,128)(2,1)S(1)}, bf16[512,384]{1,0:T(8,128)(2,1)S(1)}, u32[]{:S(2)}, u32[]{:S(2)}) collective-permute-start(bf16[512,384]{1,0:T(8,128)(2,1)S(1)} %collective-permute-done.6.refs_3_), channel_id=1, source_target_pairs={{0,16},{1,17},{2,18},{3,19},{4,20},{5,21},{6,22},{7,23},{8,24},{9,... | collective-permute-start | bytes 1179656 | tf_op jit(solution)/shard_map/ppermute | solution.py:436
  51.6 2.3 %collective-permute-start.13 = (f32[16,512]{1,0:T(8,128)S(1)}, f32[16,512]{1,0:T(8,128)S(1)}, u32[]{:S(2)}, u32[]{:S(2)}) collective-permute-start(f32[16,512]{1,0:T(8,128)S(1)} %get-tuple-element.53), channel_id=1, source_target_pairs={{0,16},{1,17},{2,18},{3,19},{4,20},{5,21},{6,22},{7,23},{8,24},{9,... | collective-permute-start | bytes 98312 | tf_op jit(solution)/shard_map/ppermute | solution.py:436
  53.9 7.1 %collective-permute-start.14 = (f32[8,512]{1,0:T(8,128)S(1)}, f32[8,512]{1,0:T(8,128)S(1)}, u32[]{:S(2)}, u32[]{:S(2)}) collective-permute-start(f32[8,512]{1,0:T(8,128)S(1)} %slice_maximum_fusion), channel_id=1, source_target_pairs={{0,12},{1,13},{2,14},{3,15},{4,8},{5,9},{6,10},{7,11},{8,4},{9,5},... | collective-permute-start | bytes 49160 | tf_op jit(solution)/shard_map/ppermute | solution.py:441
  61.0 2.6 %collective-permute-start.15 = (f32[4,512]{1,0:T(4,128)S(1)}, f32[4,512]{1,0:T(4,128)S(1)}, u32[]{:S(2)}, u32[]{:S(2)}) collective-permute-start(f32[4,512]{1,0:T(4,128)S(1)} %slice.45), channel_id=1, source_target_pairs={{0,4},{1,5},{2,6},{3,7},{4,0},{5,1},{6,2},{7,3},{8,12},{9,13},{10,... | collective-permute-start | bytes 24584 | tf_op jit(solution)/shard_map/ppermute | solution.py:441
  63.6 3.7 %collective-permute-start.16 = (f32[2,512]{1,0:T(2,128)S(1)}, f32[2,512]{1,0:T(2,128)S(1)}, u32[]{:S(2)}, u32[]{:S(2)}) collective-permute-start(f32[2,512]{1,0:T(2,128)S(1)} %slice.47), channel_id=1, source_target_pairs={{0,32},{1,33},{2,34},{3,35},{4,36},{5,37},{6,38},{7,39},{8,40},{9,... | collective-permute-start | bytes 12296 | tf_op jit(solution)/shard_map/ppermute | solution.py:441
  67.4 1.2 %collective-permute-start.17 = (f32[512]{0:T(512)S(1)}, f32[512]{0:T(512)S(1)}, u32[]{:S(2)}, u32[]{:S(2)}) collective-permute-start(f32[512]{0:T(512)S(1)} %bitcast.13), channel_id=1, source_target_pairs={{0,16},{1,17},{2,18},{3,19},{4,20},{5,21},{6,22},{7,23},{8,24},{9,... | collective-permute-start | bytes 6152 | tf_op jit(solution)/shard_map/ppermute | solution.py:436

commit v11 on v10

--- a/solution.py
+++ b/solution.py
@@ -397,23 +397,13 @@
 
 def final_kernel(*refs):
     plan, mine, theirs, refs = refs[:3], refs[3:5], refs[5:7], refs[7:]
-    rows0, row_one, row_two, row_in, low_in, mid_in, refs = *refs[:6], refs[6:]
-    keep_ref, send_ref, other_ref, a_buf, b_buf, row_ref, col_ref = refs
+    row_in, low_in, mid_in, other_ref, row_ref, a_buf, b_buf, col_ref = refs
     for half in range(2):
         a_buf[half] = mine[half][...]
         b_buf[half] = theirs[half][...]
     row_ref[...] = row_in[...]
     clear(col_ref)
     score_lists(6, *plan, a_buf, b_buf, row_ref, col_ref)
-    keep_ref[0:2] = jnp.full((2, SHARD), -2.0, jnp.float32)
-    for out_ref, slots in ((keep_ref, KEPT), (send_ref, SENT)):
-        for place, slot in enumerate(slots):
-            if slot == 7:
-                put_rows(out_ref, 2 * place, 0, row_ref)
-            elif slot > 3:
-                put_rows(out_ref, 2 * place, 2 * slot - 8, row_one, row_two)
-            elif slot > 0:
-                out_ref[2 * place : 2 * place + 2] = rows0[2 * slot - 2 : 2 * slot]
     for place, slot in enumerate(KEPT + SENT):
         for half in range(2):
             at = 2 * place + half
@@ -427,9 +417,26 @@
 
 
 def final_call(plan, *operands):
-    outs = (f32(8, SHARD), f32(8, SHARD), f32(16, SHARD))
-    scratch = [shards(2), shards(2), rows_of(2), cols_of(2)]
+    outs = (f32(16, SHARD), rows_of(2))
+    scratch = [shards(2), shards(2), cols_of(2)]
     return kernel_call(final_kernel, [*plan, *operands], outs, scratch, 500000000)
+
+
+def rows_kernel(rows0, row_one, row_two, row_last, keep_ref, send_ref):
+    keep_ref[0:2] = jnp.full((2, SHARD), -2.0, jnp.float32)
+    for out_ref, slots in ((keep_ref, KEPT), (send_ref, SENT)):
+        for place, slot in enumerate(slots):
+            if slot == 7:
+                put_rows(out_ref, 2 * place, 0, row_last)
+            elif slot > 3:
+                put_rows(out_ref, 2 * place, 2 * slot - 8, row_one, row_two)
+            elif slot > 0:
+                out_ref[2 * place : 2 * place + 2] = rows0[2 * slot - 2 : 2 * slot]
+
+
+def rows_call(*operands):
+    outs = (f32(8, SHARD), f32(8, SHARD))
+    return kernel_call(rows_kernel, operands, outs, [], 500000000, 0)
 
 
 def swap(x):
@@ -470,9 +477,8 @@
     halves = [after(x, cols) for x in halves]
     swapped = [swap(x) for x in halves]
     rows2, rows3, cols, cols2 = last_call(plan, *halves, a_mid, b_low, b_mid, cols)
-    keep, send, other = final_call(
-        plan, *halves, *swapped, rows0, rows1, rows2, rows3, cols, cols2
-    )
+    other, row7 = final_call(plan, *halves, *swapped, rows3, cols, cols2)
+    keep, send = rows_call(rows0, rows1, rows2, row7)
     other = swap(other)
     keep = jnp.maximum(keep, other[:8])
     send = jnp.maximum(send, other[8:])

time: 68.5 us -> 66.9 us (0.977); the launches traced: 69.2 us -> 65.8 us
  waiting for transfers between devices: 25 us -> 21.7 us
    ppermute x11, waiting for transfers between devices: 19.3 us -> 16.5 us  [exchange(): return lax.ppermute(x, ('row', 'col'), pairs)]
    pallas_call x7 -> x8, Pallas kernels: 14.3 us -> 13.7 us  [kernel_call(): pl.pallas_call(kernel, out_shape=outs, in_specs=[spec(SMEM)] * smem + [sp...]
  transfers between devices with their start and end apart: 18 -> 18, of which waited for: 14 -> 14; matrix products, arithmetic and copies ran while one was open for 0% -> 0% of each run, Pallas kernels for 25% -> 26%
where the time goes in v11:
time: 66.9 us; the launch traced here: 65.8 us
  starting transfers between devices  23.4 us (35%)
  waiting for transfers between devices  21.7 us (32%)
  Pallas kernels  18.9 us (28%)
  local copies, waits for them, and re-layouts  1.09 us (2%)
    ppermute x11, starting transfers between devices, exchange(): return lax.ppermute(x, ('row', 'col'), pairs)  18.3 us
    ppermute x11, waiting for transfers between devices, exchange(): return lax.ppermute(x, ('row', 'col'), pairs)  16.5 us
    pallas_call x8, Pallas kernels, kernel_call(): pl.pallas_call(kernel, out_shape=outs, in_specs=[spec(SMEM)] * smem + [sp...  13.7 us
    ppermute x7, waiting for transfers between devices, swap(): return lax.ppermute(x, ('row', 'col'), [(s, s ^ CORE) for s in range(128)])  5.15 us
    ppermute x7, starting transfers between devices, swap(): return lax.ppermute(x, ('row', 'col'), [(s, s ^ CORE) for s in range(128)])  5.12 us
    pallas_call x1, Pallas kernels, plan_call(): pl.pallas_call(plan_kernel, out_shape=(lists, lists, jax.ShapeDtypeStruct...  3.57 us
  transfers between devices with their start and end apart: 18, of which 14 were waited for; matrix products, arithmetic and copies ran while one was open for 0% of the time, Pallas kernels for 26%

profile of v11, /device:TPU:1, one launch (start us, length us, event | category | flops | bytes accessed | tf_op | source)
XLA Modules:
  0.0 65.8 jit_solution(16693113224611327066)
XLA Ops:
  0.0 1.4 %collective-permute-start = (bf16[512,384]{1,0:T(8,128)(2,1)}, bf16[512,384]{1,0:T(8,128)(2,1)S(1)}, u32[]{:S(2)}, u32[]{:S(2)}) collective-permute-start(bf16[512,384]{1,0:T(8,128)(2,1)} %x_ref.1), channel_id=1, source_target_pairs={{0,16},{1,17},{2,18},{3,19},{4,20},{5,21},{6,22},{7,23},{8,24},{9,... | collective-permute-start | bytes 1179656 | tf_op jit(solution)/shard_map/ppermute | solution.py:443
  1.4 1.0 %copy-done = bf16[512,384]{1,0:T(8,128)(2,1)S(1)} copy-done((bf16[512,384]{1,0:T(8,128)(2,1)S(1)}, bf16[512,384]{1,0:T(8,128)(2,1)}, u32[]{:S(2)}) %copy-start) | copy-done | bytes 393240
  2.4 0.2 shard_map.28.own_ref
  2.6 0.4 collective-permute-done.other_ref
  3.0 0.2 shard_map.29.unit_ref.refs_4_
  3.2 3.9 %collective-permute-start.3 = (bf16[2,512,384]{2,1,0:T(8,128)(2,1)S(1)}, bf16[2,512,384]{2,1,0:T(8,128)(2,1)S(1)}, u32[]{:S(2)}, u32[]{:S(2)}) collective-permute-start(bf16[2,512,384]{2,1,0:T(8,128)(2,1)S(1)} %shard_map.29.unit_ref.refs_4_), channel_id=1, source_target_pairs={{0,12},{1,13},{2,14},{3,15},{4,8},{5,9},{6,10},{7,11},{8,4},{9,5},... | collective-permute-start | bytes 2359304 | tf_op jit(solution)/shard_map/ppermute | solution.py:448
  7.1 0.0 collective-permute-start.2
  7.1 2.5 %collective-permute-start.1 = (bf16[2,512,384]{2,1,0:T(8,128)(2,1)S(1)}, bf16[2,512,384]{2,1,0:T(8,128)(2,1)S(1)}, u32[]{:S(2)}, u32[]{:S(2)}) collective-permute-start(bf16[2,512,384]{2,1,0:T(8,128)(2,1)S(1)} %shard_map.29.unit_ref.refs_4_), channel_id=1, source_target_pairs={{0,32},{1,33},{2,34},{3,35},{4,36},{5,37},{6,38},{7,39},{8,40},{9,... | collective-permute-start | bytes 2359304 | tf_op jit(solution)/shard_map/ppermute | solution.py:448
  9.6 3.6 %shard_map.31 = (s32[133]{0:T(256)S(1)}, s32[133]{0:T(256)S(1)}, s32[14]{0:T(128)S(1)}) custom-call(s32[1]{0:T(128)} %bitcast.here_ref, s32[256]{0:T(256)S(1)} %copy-done.1, s32[2,128]{1,0:T(2,128)S(1)} %bitcast.11), custom_call_target="tpu_custom_call" | custom-call | flops 3000000000 | bytes 10000 | tf_op jit(solution)/shard_map/pallas_call | solution.py:204
  13.1 1.3 %shard_map.30 = f32[1,512]{1,0:T(1,128)S(1)} custom-call(s32[1]{0:T(128)} %bitcast.here_ref, s32[256]{0:T(256)S(1)} %copy-done.1, bf16[2,512,384]{2,1,0:T(8,128)(2,1)S(1)} %shard_map.29.unit_ref.refs_4_), custom_call_target="tpu_custom_call" | custom-call | flops 1000000000 | bytes 1000000 | tf_op jit(solution)/shard_map/pallas_call | solution.py:216
  14.5 2.0 %collective-permute-done.3.c_ref = bf16[2,512,384]{2,1,0:T(8,128)(2,1)S(1)} collective-permute-done((bf16[2,512,384]{2,1,0:T(8,128)(2,1)S(1)}, bf16[2,512,384]{2,1,0:T(8,128)(2,1)S(1)}, u32[]{:S(2)}, u32[]{:S(2)}) %collective-permute-start.3) | collective-permute-done | bytes 786464 | tf_op jit(solution)/shard_map/ppermute | solution.py:448
  16.5 1.8 %collective-permute-done.2.b_ref = bf16[2,512,384]{2,1,0:T(8,128)(2,1)S(1)} collective-permute-done((bf16[2,512,384]{2,1,0:T(8,128)(2,1)S(1)}, bf16[2,512,384]{2,1,0:T(8,128)(2,1)S(1)}, u32[]{:S(2)}, u32[]{:S(2)}) %collective-permute-start.2) | collective-permute-done | bytes 786464 | tf_op jit(solution)/shard_map/ppermute | solution.py:448
  18.2 0.9 %collective-permute-done.1.a_ref = bf16[2,512,384]{2,1,0:T(8,128)(2,1)S(1)} collective-permute-done((bf16[2,512,384]{2,1,0:T(8,128)(2,1)S(1)}, bf16[2,512,384]{2,1,0:T(8,128)(2,1)S(1)}, u32[]{:S(2)}, u32[]{:S(2)}) %collective-permute-start.1) | collective-permute-done | bytes 786464 | tf_op jit(solution)/shard_map/ppermute | solution.py:448
  19.1 2.5 %collective-permute-start.7 = (bf16[2,512,384]{2,1,0:T(8,128)(2,1)S(1)}, bf16[2,512,384]{2,1,0:T(8,128)(2,1)S(1)}, u32[]{:S(2)}, u32[]{:S(2)}) collective-permute-start(bf16[2,512,384]{2,1,0:T(8,128)(2,1)S(1)} %collective-permute-done.3.c_ref), channel_id=1, source_target_pairs={{0,32},{1,33},{2,34},{3,35},{4,36},{5,37},{6,38},{7,39},{8,40},{9,... | collective-permute-start | bytes 2359304 | tf_op jit(solution)/shard_map/ppermute | solution.py:448
  21.6 0.5 collective-permute-start.6
  22.1 0.2 shard_map.32.refs_3_
  22.3 1.0 %collective-permute-start.5 = (bf16[2,512,384]{2,1,0:T(8,128)(2,1)S(1)}, bf16[2,512,384]{2,1,0:T(8,128)(2,1)S(1)}, u32[]{:S(2)}, u32[]{:S(2)}) collective-permute-start(bf16[2,512,384]{2,1,0:T(8,128)(2,1)S(1)} %collective-permute-done.1.a_ref), channel_id=1, source_target_pairs={{0,4},{1,5},{2,6},{3,7},{4,0},{5,1},{6,2},{7,3},{8,12},{9,13},{10,... | collective-permute-start | bytes 2359304 | tf_op jit(solution)/shard_map/ppermute | solution.py:448
  23.4 0.0 collective-permute-start.4
  23.4 1.2 %shard_map.33 = (f32[6,512,128]{2,1,0:T(8,128)S(1)}, f32[2,8,512]{2,1,0:T(8,128)S(1)}) custom-call(s32[133]{0:T(256)S(1)} %get-tuple-element.31.refs_0_, s32[133]{0:T(256)S(1)} %get-tuple-element.32.refs_1_, s32[14]{0:T(128)S(1)} %get-tuple-element.33.refs_2_, bf16[6,512,384]{2,1,0:T(8,128)(2,1)S(1)} %shard_map.32.refs_3_, ...), custom_call_target="tpu_custom_call" | custom-call | flops 30000001024 | bytes 8000000 | tf_op jit(solution)/shard_map/pallas_call | solution.py:350
  24.5 3.4 %collective-permute-done.4.refs_5_ = bf16[6,512,384]{2,1,0:T(8,128)(2,1)S(1)} collective-permute-done((bf16[6,512,384]{2,1,0:T(8,128)(2,1)S(1)}, bf16[6,512,384]{2,1,0:T(8,128)(2,1)S(1)}, u32[]{:S(2)}, u32[]{:S(2)}) %collective-permute-start.4) | collective-permute-done | bytes 2359328 | tf_op jit(solution)/shard_map/ppermute | solution.py:443
  27.9 2.7 %shard_map.34 = (f32[6,512]{1,0:T(8,128)S(1)}, f32[8,8,512]{2,1,0:T(8,128)S(1)}, bf16[8,512,384]{2,1,0:T(8,128)(2,1)S(1)}) custom-call(s32[133]{0:T(256)S(1)} %get-tuple-element.31.refs_0_, s32[133]{0:T(256)S(1)} %get-tuple-element.32.refs_1_, s32[14]{0:T(128)S(1)} %get-tuple-element.33.refs_2_, bf16[6,512,384]{2,1,0:T(8,128)(2,1)S(1)} %shard_map.32.refs_3_, ...), custom_call_target="tpu_custom_call" | custom-call | flops 3000000000 | bytes 8000000 | tf_op jit(solution)/shard_map/pallas_call | solution.py:350
  30.6 0.9 %collective-permute-done.7.c_ref = bf16[2,512,384]{2,1,0:T(8,128)(2,1)S(1)} collective-permute-done((bf16[2,512,384]{2,1,0:T(8,128)(2,1)S(1)}, bf16[2,512,384]{2,1,0:T(8,128)(2,1)S(1)}, u32[]{:S(2)}, u32[]{:S(2)}) %collective-permute-start.7) | collective-permute-done | bytes 786464 | tf_op jit(solution)/shard_map/ppermute | solution.py:448
  31.5 2.2 %collective-permute-done.6.b_ref = bf16[2,512,384]{2,1,0:T(8,128)(2,1)S(1)} collective-permute-done((bf16[2,512,384]{2,1,0:T(8,128)(2,1)S(1)}, bf16[2,512,384]{2,1,0:T(8,128)(2,1)S(1)}, u32[]{:S(2)}, u32[]{:S(2)}) %collective-permute-start.6) | collective-permute-done | bytes 786464 | tf_op jit(solution)/shard_map/ppermute | solution.py:448
  33.7 0.0 collective-permute-done.5.a_ref
  33.8 0.2 shard_map.35.refs_3_.refs_5_
  34.0 1.1 %collective-permute-start.9 = (bf16[512,384]{1,0:T(8,128)(2,1)S(1)}, bf16[512,384]{1,0:T(8,128)(2,1)S(1)}, u32[]{:S(2)}, u32[]{:S(2)}) collective-permute-start(bf16[512,384]{1,0:T(8,128)(2,1)S(1)} %slice_bitcast_fusion), channel_id=1, source_target_pairs={{0,4},{1,5},{2,6},{3,7},{4,0},{5,1},{6,2},{7,3},{8,12},{9,13},{10,... | collective-permute-start | bytes 1179656 | tf_op jit(solution)/shard_map/ppermute | solution.py:448
  35.1 0.9 %collective-permute-start.8 = (bf16[512,384]{1,0:T(8,128)(2,1)S(1)}, bf16[512,384]{1,0:T(8,128)(2,1)S(1)}, u32[]{:S(2)}, u32[]{:S(2)}) collective-permute-start(bf16[512,384]{1,0:T(8,128)(2,1)S(1)} %slice_bitcast_fusion.1), channel_id=1, source_target_pairs={{0,32},{1,33},{2,34},{3,35},{4,36},{5,37},{6,38},{7,39},{8,40},{9,... | collective-permute-start | bytes 1179656 | tf_op jit(solution)/shard_map/ppermute | solution.py:448
  36.0 0.0 collective-permute-start.10
  36.0 3.1 %shard_map.36 = (f32[6,512,128]{2,1,0:T(8,128)S(1)}, f32[8,8,512]{2,1,0:T(8,128)S(1)}) custom-call(s32[133]{0:T(256)S(1)} %get-tuple-element.31.refs_0_, s32[133]{0:T(256)S(1)} %get-tuple-element.32.refs_1_, s32[14]{0:T(128)S(1)} %get-tuple-element.33.refs_2_, bf16[6,512,384]{2,1,0:T(8,128)(2,1)S(1)} %shard_map.35.refs_3_.refs_5_, ...), custom_call_target="tpu_custom_call" | custom-call | flops 30000001024 | bytes 8000000 | tf_op jit(solution)/shard_map/pallas_call | solution.py:350
  39.1 2.1 %collective-permute-done.9.refs_4_ = bf16[512,384]{1,0:T(8,128)(2,1)S(1)} collective-permute-done((bf16[512,384]{1,0:T(8,128)(2,1)S(1)}, bf16[512,384]{1,0:T(8,128)(2,1)S(1)}, u32[]{:S(2)}, u32[]{:S(2)}) %collective-permute-start.9) | collective-permute-done | bytes 393248 | tf_op jit(solution)/shard_map/ppermute | solution.py:448
  41.2 1.7 %collective-permute-done.8.refs_3_ = bf16[512,384]{1,0:T(8,128)(2,1)S(1)} collective-permute-done((bf16[512,384]{1,0:T(8,128)(2,1)S(1)}, bf16[512,384]{1,0:T(8,128)(2,1)S(1)}, u32[]{:S(2)}, u32[]{:S(2)}) %collective-permute-start.8) | collective-permute-done | bytes 393248 | tf_op jit(solution)/shard_map/ppermute | solution.py:448
  42.9 0.5 collective-permute-start.11
  43.4 0.0 collective-permute-done.10.refs_7_
  43.4 4.2 %shard_map.37 = (f32[6,512,128]{2,1,0:T(8,128)S(1)}, f32[2,512,128]{2,1,0:T(8,128)S(1)}, f32[8,8,512]{2,1,0:T(8,128)S(1)}, f32[6,8,512]{2,1,0:T(8,128)S(1)}) custom-call(s32[133]{0:T(256)S(1)} %get-tuple-element.31.refs_0_, s32[133]{0:T(256)S(1)} %get-tuple-element.32.refs_1_, s32[14]{0:T(128)S(1)} %get-tuple-element.33.refs_2_, ...), custom_call_target="tpu_custom_call" | custom-call | flops 5000000000 | bytes 8000000 | tf_op jit(solution)/shard_map/pallas_call | solution.py:350
  47.6 0.0 collective-permute-done.12.refs_6_
  47.7 1.5 %shard_map.38 = (f32[16,512]{1,0:T(8,128)S(1)}, f32[2,512,128]{2,1,0:T(8,128)S(1)}) custom-call(s32[133]{0:T(256)S(1)} %get-tuple-element.31.refs_0_, s32[133]{0:T(256)S(1)} %get-tuple-element.32.refs_1_, s32[14]{0:T(128)S(1)} %get-tuple-element.33.refs_2_, bf16[512,384]{1,0:T(8,128)(2,1)S(1)} %collective-permute-done.8.refs_3_, ...), custom_call_target="tpu_custom_call" | custom-call | flops 500000000 | bytes 8000000 | tf_op jit(solution)/shard_map/pallas_call | solution.py:350
  49.2 0.1 collective-permute-start.13
  49.3 0.6 shard_map.39
  49.9 0.6 collective-permute-done.13
  50.5 3.3 %collective-permute-start.14 = (f32[8,512]{1,0:T(8,128)S(1)}, f32[8,512]{1,0:T(8,128)S(1)}, u32[]{:S(2)}, u32[]{:S(2)}) collective-permute-start(f32[8,512]{1,0:T(8,128)S(1)} %slice_maximum_fusion), channel_id=1, source_target_pairs={{0,12},{1,13},{2,14},{3,15},{4,8},{5,9},{6,10},{7,11},{8,4},{9,5},... | collective-permute-start | bytes 49160 | tf_op jit(solution)/shard_map/ppermute | solution.py:448
  53.8 1.1 %collective-permute-done.14 = f32[8,512]{1,0:T(8,128)S(1)} collective-permute-done((f32[8,512]{1,0:T(8,128)S(1)}, f32[8,512]{1,0:T(8,128)S(1)}, u32[]{:S(2)}, u32[]{:S(2)}) %collective-permute-start.14) | collective-permute-done | bytes 16416 | tf_op jit(solution)/shard_map/ppermute | solution.py:448
  55.0 0.1 collective-permute-start.15
  55.1 2.5 %collective-permute-done.15 = f32[4,512]{1,0:T(4,128)S(1)} collective-permute-done((f32[4,512]{1,0:T(4,128)S(1)}, f32[4,512]{1,0:T(4,128)S(1)}, u32[]{:S(2)}, u32[]{:S(2)}) %collective-permute-start.15) | collective-permute-done | bytes 8224 | tf_op jit(solution)/shard_map/ppermute | solution.py:448
  57.6 2.4 %collective-permute-start.16 = (f32[2,512]{1,0:T(2,128)S(1)}, f32[2,512]{1,0:T(2,128)S(1)}, u32[]{:S(2)}, u32[]{:S(2)}) collective-permute-start(f32[2,512]{1,0:T(2,128)S(1)} %slice.47), channel_id=1, source_target_pairs={{0,32},{1,33},{2,34},{3,35},{4,36},{5,37},{6,38},{7,39},{8,40},{9,... | collective-permute-start | bytes 12296 | tf_op jit(solution)/shard_map/ppermute | solution.py:448
  60.0 1.3 %collective-permute-done.16 = f32[2,512]{1,0:T(2,128)S(1)} collective-permute-done((f32[2,512]{1,0:T(2,128)S(1)}, f32[2,512]{1,0:T(2,128)S(1)}, u32[]{:S(2)}, u32[]{:S(2)}) %collective-permute-start.16) | collective-permute-done | bytes 4128 | tf_op jit(solution)/shard_map/ppermute | solution.py:448
  61.3 3.1 %collective-permute-start.17 = (f32[512]{0:T(512)S(1)}, f32[512]{0:T(512)S(1)}, u32[]{:S(2)}, u32[]{:S(2)}) collective-permute-start(f32[512]{0:T(512)S(1)} %bitcast.13), channel_id=1, source_target_pairs={{0,16},{1,17},{2,18},{3,19},{4,20},{5,21},{6,22},{7,23},{8,24},{9,... | collective-permute-start | bytes 6152 | tf_op jit(solution)/shard_map/ppermute | solution.py:443
  64.4 0.8 %collective-permute-done.17 = f32[512]{0:T(512)S(1)} collective-permute-done((f32[512]{0:T(512)S(1)}, f32[512]{0:T(512)S(1)}, u32[]{:S(2)}, u32[]{:S(2)}) %collective-permute-start.17) | collective-permute-done | bytes 2080 | tf_op jit(solution)/shard_map/ppermute | solution.py:443
  65.2 0.6 maximum_maximum_fusion
  (14 shorter events, 0.1 us)
Async XLA Ops:
  0.0 9.6 %copy-start.1 = (s32[256]{0:T(256)S(1)}, s32[256]{0:T(256)}, u32[]{:S(2)}) copy-start(s32[256]{0:T(256)} %cluster_ref.3) | copy-start | bytes 3076
  0.0 3.0 %collective-permute-start = (bf16[512,384]{1,0:T(8,128)(2,1)}, bf16[512,384]{1,0:T(8,128)(2,1)S(1)}, u32[]{:S(2)}, u32[]{:S(2)}) collective-permute-start(bf16[512,384]{1,0:T(8,128)(2,1)} %x_ref.1), channel_id=1, source_target_pairs={{0,16},{1,17},{2,18},{3,19},{4,20},{5,21},{6,22},{7,23},{8,24},{9,... | collective-permute-start | bytes 1179656 | tf_op jit(solution)/shard_map/ppermute | solution.py:443
  1.4 1.0 %copy-start = (bf16[512,384]{1,0:T(8,128)(2,1)S(1)}, bf16[512,384]{1,0:T(8,128)(2,1)}, u32[]{:S(2)}) copy-start(bf16[512,384]{1,0:T(8,128)(2,1)} %x_ref.1) | copy-start | bytes 1179652
  3.2 13.3 %collective-permute-start.3 = (bf16[2,512,384]{2,1,0:T(8,128)(2,1)S(1)}, bf16[2,512,384]{2,1,0:T(8,128)(2,1)S(1)}, u32[]{:S(2)}, u32[]{:S(2)}) collective-permute-start(bf16[2,512,384]{2,1,0:T(8,128)(2,1)S(1)} %shard_map.29.unit_ref.refs_4_), channel_id=1, source_target_pairs={{0,12},{1,13},{2,14},{3,15},{4,8},{5,9},{6,10},{7,11},{8,4},{9,5},... | collective-permute-start | bytes 2359304 | tf_op jit(solution)/shard_map/ppermute | solution.py:448
  7.1 11.1 %collective-permute-start.2 = (bf16[2,512,384]{2,1,0:T(8,128)(2,1)S(1)}, bf16[2,512,384]{2,1,0:T(8,128)(2,1)S(1)}, u32[]{:S(2)}, u32[]{:S(2)}) collective-permute-start(bf16[2,512,384]{2,1,0:T(8,128)(2,1)S(1)} %shard_map.29.unit_ref.refs_4_), channel_id=1, source_target_pairs={{0,4},{1,5},{2,6},{3,7},{4,0},{5,1},{6,2},{7,3},{8,12},{9,13},{10,... | collective-permute-start | bytes 2359304 | tf_op jit(solution)/shard_map/ppermute | solution.py:448
  7.1 12.1 %collective-permute-start.1 = (bf16[2,512,384]{2,1,0:T(8,128)(2,1)S(1)}, bf16[2,512,384]{2,1,0:T(8,128)(2,1)S(1)}, u32[]{:S(2)}, u32[]{:S(2)}) collective-permute-start(bf16[2,512,384]{2,1,0:T(8,128)(2,1)S(1)} %shard_map.29.unit_ref.refs_4_), channel_id=1, source_target_pairs={{0,32},{1,33},{2,34},{3,35},{4,36},{5,37},{6,38},{7,39},{8,40},{9,... | collective-permute-start | bytes 2359304 | tf_op jit(solution)/shard_map/ppermute | solution.py:448
  19.1 12.3 %collective-permute-start.7 = (bf16[2,512,384]{2,1,0:T(8,128)(2,1)S(1)}, bf16[2,512,384]{2,1,0:T(8,128)(2,1)S(1)}, u32[]{:S(2)}, u32[]{:S(2)}) collective-permute-start(bf16[2,512,384]{2,1,0:T(8,128)(2,1)S(1)} %collective-permute-done.3.c_ref), channel_id=1, source_target_pairs={{0,32},{1,33},{2,34},{3,35},{4,36},{5,37},{6,38},{7,39},{8,40},{9,... | collective-permute-start | bytes 2359304 | tf_op jit(solution)/shard_map/ppermute | solution.py:448
  21.6 12.1 %collective-permute-start.6 = (bf16[2,512,384]{2,1,0:T(8,128)(2,1)S(1)}, bf16[2,512,384]{2,1,0:T(8,128)(2,1)S(1)}, u32[]{:S(2)}, u32[]{:S(2)}) collective-permute-start(bf16[2,512,384]{2,1,0:T(8,128)(2,1)S(1)} %collective-permute-done.2.b_ref), channel_id=1, source_target_pairs={{0,12},{1,13},{2,14},{3,15},{4,8},{5,9},{6,10},{7,11},{8,4},{9,5},... | collective-permute-start | bytes 2359304 | tf_op jit(solution)/shard_map/ppermute | solution.py:448
  22.3 11.3 %collective-permute-start.5 = (bf16[2,512,384]{2,1,0:T(8,128)(2,1)S(1)}, bf16[2,512,384]{2,1,0:T(8,128)(2,1)S(1)}, u32[]{:S(2)}, u32[]{:S(2)}) collective-permute-start(bf16[2,512,384]{2,1,0:T(8,128)(2,1)S(1)} %collective-permute-done.1.a_ref), channel_id=1, source_target_pairs={{0,4},{1,5},{2,6},{3,7},{4,0},{5,1},{6,2},{7,3},{8,12},{9,13},{10,... | collective-permute-start | bytes 2359304 | tf_op jit(solution)/shard_map/ppermute | solution.py:448
  23.4 4.5 %collective-permute-start.4 = (bf16[6,512,384]{2,1,0:T(8,128)(2,1)S(1)}, bf16[6,512,384]{2,1,0:T(8,128)(2,1)S(1)}, u32[]{:S(2)}, u32[]{:S(2)}) collective-permute-start(bf16[6,512,384]{2,1,0:T(8,128)(2,1)S(1)} %shard_map.32.refs_3_), channel_id=1, source_target_pairs={{0,16},{1,17},{2,18},{3,19},{4,20},{5,21},{6,22},{7,23},{8,24},{9,... | collective-permute-start | bytes 7077896 | tf_op jit(solution)/shard_map/ppermute | solution.py:443
  34.0 7.2 %collective-permute-start.9 = (bf16[512,384]{1,0:T(8,128)(2,1)S(1)}, bf16[512,384]{1,0:T(8,128)(2,1)S(1)}, u32[]{:S(2)}, u32[]{:S(2)}) collective-permute-start(bf16[512,384]{1,0:T(8,128)(2,1)S(1)} %slice_bitcast_fusion), channel_id=1, source_target_pairs={{0,4},{1,5},{2,6},{3,7},{4,0},{5,1},{6,2},{7,3},{8,12},{9,13},{10,... | collective-permute-start | bytes 1179656 | tf_op jit(solution)/shard_map/ppermute | solution.py:448
  35.1 7.8 %collective-permute-start.8 = (bf16[512,384]{1,0:T(8,128)(2,1)S(1)}, bf16[512,384]{1,0:T(8,128)(2,1)S(1)}, u32[]{:S(2)}, u32[]{:S(2)}) collective-permute-start(bf16[512,384]{1,0:T(8,128)(2,1)S(1)} %slice_bitcast_fusion.1), channel_id=1, source_target_pairs={{0,32},{1,33},{2,34},{3,35},{4,36},{5,37},{6,38},{7,39},{8,40},{9,... | collective-permute-start | bytes 1179656 | tf_op jit(solution)/shard_map/ppermute | solution.py:448
  36.0 7.4 %collective-permute-start.10 = (bf16[6,512,384]{2,1,0:T(8,128)(2,1)S(1)}, bf16[6,512,384]{2,1,0:T(8,128)(2,1)S(1)}, u32[]{:S(2)}, u32[]{:S(2)}) collective-permute-start(bf16[6,512,384]{2,1,0:T(8,128)(2,1)S(1)} %shard_map.35.refs_3_.refs_5_), channel_id=1, source_target_pairs={{0,16},{1,17},{2,18},{3,19},{4,20},{5,21},{6,22},{7,23},{8,24},{9,... | collective-permute-start | bytes 7077896 | tf_op jit(solution)/shard_map/ppermute | solution.py:443
  42.9 4.7 %collective-permute-start.12 = (bf16[512,384]{1,0:T(8,128)(2,1)S(1)}, bf16[512,384]{1,0:T(8,128)(2,1)S(1)}, u32[]{:S(2)}, u32[]{:S(2)}) collective-permute-start(bf16[512,384]{1,0:T(8,128)(2,1)S(1)} %collective-permute-done.9.refs_4_), channel_id=1, source_target_pairs={{0,16},{1,17},{2,18},{3,19},{4,20},{5,21},{6,22},{7,23},{8,24},{9,... | collective-permute-start | bytes 1179656 | tf_op jit(solution)/shard_map/ppermute | solution.py:443
  42.9 4.7 %collective-permute-start.11 = (bf16[512,384]{1,0:T(8,128)(2,1)S(1)}, bf16[512,384]{1,0:T(8,128)(2,1)S(1)}, u32[]{:S(2)}, u32[]{:S(2)}) collective-permute-start(bf16[512,384]{1,0:T(8,128)(2,1)S(1)} %collective-permute-done.8.refs_3_), channel_id=1, source_target_pairs={{0,16},{1,17},{2,18},{3,19},{4,20},{5,21},{6,22},{7,23},{8,24},{9,... | collective-permute-start | bytes 1179656 | tf_op jit(solution)/shard_map/ppermute | solution.py:443
  49.2 1.3 %collective-permute-start.13 = (f32[16,512]{1,0:T(8,128)S(1)}, f32[16,512]{1,0:T(8,128)S(1)}, u32[]{:S(2)}, u32[]{:S(2)}) collective-permute-start(f32[16,512]{1,0:T(8,128)S(1)} %get-tuple-element.55), channel_id=1, source_target_pairs={{0,16},{1,17},{2,18},{3,19},{4,20},{5,21},{6,22},{7,23},{8,24},{9,... | collective-permute-start | bytes 98312 | tf_op jit(solution)/shard_map/ppermute | solution.py:443
  50.5 4.5 %collective-permute-start.14 = (f32[8,512]{1,0:T(8,128)S(1)}, f32[8,512]{1,0:T(8,128)S(1)}, u32[]{:S(2)}, u32[]{:S(2)}) collective-permute-start(f32[8,512]{1,0:T(8,128)S(1)} %slice_maximum_fusion), channel_id=1, source_target_pairs={{0,12},{1,13},{2,14},{3,15},{4,8},{5,9},{6,10},{7,11},{8,4},{9,5},... | collective-permute-start | bytes 49160 | tf_op jit(solution)/shard_map/ppermute | solution.py:448
  55.0 2.6 %collective-permute-start.15 = (f32[4,512]{1,0:T(4,128)S(1)}, f32[4,512]{1,0:T(4,128)S(1)}, u32[]{:S(2)}, u32[]{:S(2)}) collective-permute-start(f32[4,512]{1,0:T(4,128)S(1)} %slice.45), channel_id=1, source_target_pairs={{0,4},{1,5},{2,6},{3,7},{4,0},{5,1},{6,2},{7,3},{8,12},{9,13},{10,... | collective-permute-start | bytes 24584 | tf_op jit(solution)/shard_map/ppermute | solution.py:448
  57.6 3.7 %collective-permute-start.16 = (f32[2,512]{1,0:T(2,128)S(1)}, f32[2,512]{1,0:T(2,128)S(1)}, u32[]{:S(2)}, u32[]{:S(2)}) collective-permute-start(f32[2,512]{1,0:T(2,128)S(1)} %slice.47), channel_id=1, source_target_pairs={{0,32},{1,33},{2,34},{3,35},{4,36},{5,37},{6,38},{7,39},{8,40},{9,... | collective-permute-start | bytes 12296 | tf_op jit(solution)/shard_map/ppermute | solution.py:448
  61.3 3.9 %collective-permute-start.17 = (f32[512]{0:T(512)S(1)}, f32[512]{0:T(512)S(1)}, u32[]{:S(2)}, u32[]{:S(2)}) collective-permute-start(f32[512]{0:T(512)S(1)} %bitcast.13), channel_id=1, source_target_pairs={{0,16},{1,17},{2,18},{3,19},{4,20},{5,21},{6,22},{7,23},{8,24},{9,... | collective-permute-start | bytes 6152 | tf_op jit(solution)/shard_map/ppermute | solution.py:443

commit v12 on v11

--- a/solution.py
+++ b/solution.py
@@ -311,7 +311,7 @@
 
 def second_kernel(*refs):
     plan, (a_low, unit, b_in, row_in, col_in), outs = refs[:3], refs[3:8], refs[8:]
-    rows_out, col_ref, b_low, row_ref, col_low = outs
+    row_ref, col_ref, b_low, col_low = outs
     b_low[:2] = unit[...]
     b_low[2:] = b_in[...]
     row_ref[...] = row_in[...]
@@ -319,8 +319,6 @@
     score_lists(1, *plan, a_low, b_in, row_ref, col_low)
     col_ref[:2] = col_in[...]
     col_ref[2:] = col_low[...]
-    for n in range(0, 6, 2):
-        put_rows(rows_out, n, n, row_ref)
 
 
 def middle_kernel(*refs):
@@ -364,8 +362,8 @@
 
 
 def second_call(plan, *operands):
-    outs = (f32(6, SHARD), cols_of(8), shards(8))
-    scratch = [rows_of(6), cols_of(6)]
+    outs = (rows_of(6), cols_of(8), shards(8))
+    scratch = [cols_of(6)]
     return kernel_call(second_kernel, [*plan, *operands], outs, scratch, 3000000000)
 
 
@@ -431,7 +429,7 @@
             elif slot > 3:
                 put_rows(out_ref, 2 * place, 2 * slot - 8, row_one, row_two)
             elif slot > 0:
-                out_ref[2 * place : 2 * place + 2] = rows0[2 * slot - 2 : 2 * slot]
+                put_rows(out_ref, 2 * place, 2 * slot - 2, rows0)
 
 
 def rows_call(*operands):

time: 66.9 us -> 65.9 us (0.985)
  waiting for transfers between devices: 21.7 us -> 19.7 us
  starting transfers between devices: 23.4 us -> 24.5 us
    ppermute x7, starting transfers between devices: 5.12 us -> 6.68 us  [swap(): return lax.ppermute(x, ('row', 'col'), [(s, s ^ CORE) for s in range(128)])]
    ppermute x7, waiting for transfers between devices: 5.15 us -> 3.77 us  [swap(): return lax.ppermute(x, ('row', 'col'), [(s, s ^ CORE) for s in range(128)])]
  transfers between devices with their start and end apart: 18 -> 18, of which waited for: 14 -> 12; matrix products, arithmetic and copies ran while one was open for 0% -> 0% of each run, Pallas kernels for 26% -> 27%
where the time goes in v12:
time: 65.9 us; the launch traced here: 64.7 us
  starting transfers between devices  24.5 us (37%)
  waiting for transfers between devices  19.7 us (30%)
  Pallas kernels  18.6 us (28%)
  local copies, waits for them, and re-layouts  1.09 us (2%)
    ppermute x11, starting transfers between devices, exchange(): return lax.ppermute(x, ('row', 'col'), pairs)  17.9 us
    ppermute x11, waiting for transfers between devices, exchange(): return lax.ppermute(x, ('row', 'col'), pairs)  15.9 us
    pallas_call x8, Pallas kernels, kernel_call(): pl.pallas_call(kernel, out_shape=outs, in_specs=[spec(SMEM)] * smem + [sp...  13.4 us
    ppermute x7, starting transfers between devices, swap(): return lax.ppermute(x, ('row', 'col'), [(s, s ^ CORE) for s in range(128)])  6.68 us
    ppermute x7, waiting for transfers between devices, swap(): return lax.ppermute(x, ('row', 'col'), [(s, s ^ CORE) for s in range(128)])  3.77 us
    pallas_call x1, Pallas kernels, plan_call(): pl.pallas_call(plan_kernel, out_shape=(lists, lists, jax.ShapeDtypeStruct...  3.57 us
  transfers between devices with their start and end apart: 18, of which 12 were waited for; matrix products, arithmetic and copies ran while one was open for 0% of the time, Pallas kernels for 27%

profile of v12, /device:TPU:1, one launch (start us, length us, event | category | flops | bytes accessed | tf_op | source)
XLA Modules:
  0.0 64.7 jit_solution(11183374195099453146)
XLA Ops:
  0.0 1.4 %collective-permute-start = (bf16[512,384]{1,0:T(8,128)(2,1)}, bf16[512,384]{1,0:T(8,128)(2,1)S(1)}, u32[]{:S(2)}, u32[]{:S(2)}) collective-permute-start(bf16[512,384]{1,0:T(8,128)(2,1)} %x_ref.1), channel_id=1, source_target_pairs={{0,16},{1,17},{2,18},{3,19},{4,20},{5,21},{6,22},{7,23},{8,24},{9,... | collective-permute-start | bytes 1179656 | tf_op jit(solution)/shard_map/ppermute | solution.py:441
  1.4 1.0 %copy-done = bf16[512,384]{1,0:T(8,128)(2,1)S(1)} copy-done((bf16[512,384]{1,0:T(8,128)(2,1)S(1)}, bf16[512,384]{1,0:T(8,128)(2,1)}, u32[]{:S(2)}) %copy-start) | copy-done | bytes 393240
  2.4 0.2 shard_map.28.own_ref
  2.6 0.4 collective-permute-done.other_ref
  3.0 0.2 shard_map.29.unit_ref.refs_4_
  3.2 3.9 %collective-permute-start.3 = (bf16[2,512,384]{2,1,0:T(8,128)(2,1)S(1)}, bf16[2,512,384]{2,1,0:T(8,128)(2,1)S(1)}, u32[]{:S(2)}, u32[]{:S(2)}) collective-permute-start(bf16[2,512,384]{2,1,0:T(8,128)(2,1)S(1)} %shard_map.29.unit_ref.refs_4_), channel_id=1, source_target_pairs={{0,12},{1,13},{2,14},{3,15},{4,8},{5,9},{6,10},{7,11},{8,4},{9,5},... | collective-permute-start | bytes 2359304 | tf_op jit(solution)/shard_map/ppermute | solution.py:446
  7.1 0.0 collective-permute-start.2
  7.1 2.5 %collective-permute-start.1 = (bf16[2,512,384]{2,1,0:T(8,128)(2,1)S(1)}, bf16[2,512,384]{2,1,0:T(8,128)(2,1)S(1)}, u32[]{:S(2)}, u32[]{:S(2)}) collective-permute-start(bf16[2,512,384]{2,1,0:T(8,128)(2,1)S(1)} %shard_map.29.unit_ref.refs_4_), channel_id=1, source_target_pairs={{0,32},{1,33},{2,34},{3,35},{4,36},{5,37},{6,38},{7,39},{8,40},{9,... | collective-permute-start | bytes 2359304 | tf_op jit(solution)/shard_map/ppermute | solution.py:446
  9.6 3.6 %shard_map.31 = (s32[133]{0:T(256)S(1)}, s32[133]{0:T(256)S(1)}, s32[14]{0:T(128)S(1)}) custom-call(s32[1]{0:T(128)} %bitcast.here_ref, s32[256]{0:T(256)S(1)} %copy-done.1, s32[2,128]{1,0:T(2,128)S(1)} %bitcast.11), custom_call_target="tpu_custom_call" | custom-call | flops 3000000000 | bytes 10000 | tf_op jit(solution)/shard_map/pallas_call | solution.py:204
  13.1 1.3 %shard_map.30 = f32[1,512]{1,0:T(1,128)S(1)} custom-call(s32[1]{0:T(128)} %bitcast.here_ref, s32[256]{0:T(256)S(1)} %copy-done.1, bf16[2,512,384]{2,1,0:T(8,128)(2,1)S(1)} %shard_map.29.unit_ref.refs_4_), custom_call_target="tpu_custom_call" | custom-call | flops 1000000000 | bytes 1000000 | tf_op jit(solution)/shard_map/pallas_call | solution.py:216
  14.5 2.0 %collective-permute-done.3.c_ref = bf16[2,512,384]{2,1,0:T(8,128)(2,1)S(1)} collective-permute-done((bf16[2,512,384]{2,1,0:T(8,128)(2,1)S(1)}, bf16[2,512,384]{2,1,0:T(8,128)(2,1)S(1)}, u32[]{:S(2)}, u32[]{:S(2)}) %collective-permute-start.3) | collective-permute-done | bytes 786464 | tf_op jit(solution)/shard_map/ppermute | solution.py:446
  16.5 1.8 %collective-permute-done.2.b_ref = bf16[2,512,384]{2,1,0:T(8,128)(2,1)S(1)} collective-permute-done((bf16[2,512,384]{2,1,0:T(8,128)(2,1)S(1)}, bf16[2,512,384]{2,1,0:T(8,128)(2,1)S(1)}, u32[]{:S(2)}, u32[]{:S(2)}) %collective-permute-start.2) | collective-permute-done | bytes 786464 | tf_op jit(solution)/shard_map/ppermute | solution.py:446
  18.2 0.9 %collective-permute-done.1.a_ref = bf16[2,512,384]{2,1,0:T(8,128)(2,1)S(1)} collective-permute-done((bf16[2,512,384]{2,1,0:T(8,128)(2,1)S(1)}, bf16[2,512,384]{2,1,0:T(8,128)(2,1)S(1)}, u32[]{:S(2)}, u32[]{:S(2)}) %collective-permute-start.1) | collective-permute-done | bytes 786464 | tf_op jit(solution)/shard_map/ppermute | solution.py:446
  19.1 2.5 %collective-permute-start.7 = (bf16[2,512,384]{2,1,0:T(8,128)(2,1)S(1)}, bf16[2,512,384]{2,1,0:T(8,128)(2,1)S(1)}, u32[]{:S(2)}, u32[]{:S(2)}) collective-permute-start(bf16[2,512,384]{2,1,0:T(8,128)(2,1)S(1)} %collective-permute-done.3.c_ref), channel_id=1, source_target_pairs={{0,32},{1,33},{2,34},{3,35},{4,36},{5,37},{6,38},{7,39},{8,40},{9,... | collective-permute-start | bytes 2359304 | tf_op jit(solution)/shard_map/ppermute | solution.py:446
  21.6 0.5 collective-permute-start.6
  22.1 0.2 shard_map.32.refs_3_
  22.3 1.0 %collective-permute-start.5 = (bf16[2,512,384]{2,1,0:T(8,128)(2,1)S(1)}, bf16[2,512,384]{2,1,0:T(8,128)(2,1)S(1)}, u32[]{:S(2)}, u32[]{:S(2)}) collective-permute-start(bf16[2,512,384]{2,1,0:T(8,128)(2,1)S(1)} %collective-permute-done.1.a_ref), channel_id=1, source_target_pairs={{0,4},{1,5},{2,6},{3,7},{4,0},{5,1},{6,2},{7,3},{8,12},{9,13},{10,... | collective-permute-start | bytes 2359304 | tf_op jit(solution)/shard_map/ppermute | solution.py:446
  23.4 0.0 collective-permute-start.4
  23.4 2.0 %shard_map.33 = (f32[6,512,128]{2,1,0:T(8,128)S(1)}, f32[2,8,512]{2,1,0:T(8,128)S(1)}) custom-call(s32[133]{0:T(256)S(1)} %get-tuple-element.31.refs_0_, s32[133]{0:T(256)S(1)} %get-tuple-element.32.refs_1_, s32[14]{0:T(128)S(1)} %get-tuple-element.33.refs_2_, bf16[6,512,384]{2,1,0:T(8,128)(2,1)S(1)} %shard_map.32.refs_3_, ...), custom_call_target="tpu_custom_call" | custom-call | flops 30000001024 | bytes 8000000 | tf_op jit(solution)/shard_map/pallas_call | solution.py:348
  25.4 2.5 %collective-permute-done.4.refs_5_ = bf16[6,512,384]{2,1,0:T(8,128)(2,1)S(1)} collective-permute-done((bf16[6,512,384]{2,1,0:T(8,128)(2,1)S(1)}, bf16[6,512,384]{2,1,0:T(8,128)(2,1)S(1)}, u32[]{:S(2)}, u32[]{:S(2)}) %collective-permute-start.4) | collective-permute-done | bytes 2359328 | tf_op jit(solution)/shard_map/ppermute | solution.py:441
  27.9 3.6 %shard_map.34 = (f32[6,512,128]{2,1,0:T(8,128)S(1)}, f32[8,8,512]{2,1,0:T(8,128)S(1)}, bf16[8,512,384]{2,1,0:T(8,128)(2,1)S(1)}) custom-call(s32[133]{0:T(256)S(1)} %get-tuple-element.31.refs_0_, s32[133]{0:T(256)S(1)} %get-tuple-element.32.refs_1_, s32[14]{0:T(128)S(1)} %get-tuple-element.33.refs_2_, bf16[6,512,384]{2,1,0:T(8,128)(2,1)S(1)} %shard_map.32.refs_3_, ...), custom_call_target="tpu_custom_call" | custom-call | flops 3000000000 | bytes 8000000 | tf_op jit(solution)/shard_map/pallas_call | solution.py:348
  31.5 0.0 collective-permute-done.7.c_ref
  31.5 2.2 %collective-permute-done.6.b_ref = bf16[2,512,384]{2,1,0:T(8,128)(2,1)S(1)} collective-permute-done((bf16[2,512,384]{2,1,0:T(8,128)(2,1)S(1)}, bf16[2,512,384]{2,1,0:T(8,128)(2,1)S(1)}, u32[]{:S(2)}, u32[]{:S(2)}) %collective-permute-start.6) | collective-permute-done | bytes 786464 | tf_op jit(solution)/shard_map/ppermute | solution.py:446
  33.7 0.0 collective-permute-done.5.a_ref
  33.8 0.2 shard_map.35.refs_3_.refs_5_
  34.0 0.9 %collective-permute-start.9 = (bf16[512,384]{1,0:T(8,128)(2,1)S(1)}, bf16[512,384]{1,0:T(8,128)(2,1)S(1)}, u32[]{:S(2)}, u32[]{:S(2)}) collective-permute-start(bf16[512,384]{1,0:T(8,128)(2,1)S(1)} %slice_bitcast_fusion), channel_id=1, source_target_pairs={{0,4},{1,5},{2,6},{3,7},{4,0},{5,1},{6,2},{7,3},{8,12},{9,13},{10,... | collective-permute-start | bytes 1179656 | tf_op jit(solution)/shard_map/ppermute | solution.py:446
  34.9 0.9 %collective-permute-start.8 = (bf16[512,384]{1,0:T(8,128)(2,1)S(1)}, bf16[512,384]{1,0:T(8,128)(2,1)S(1)}, u32[]{:S(2)}, u32[]{:S(2)}) collective-permute-start(bf16[512,384]{1,0:T(8,128)(2,1)S(1)} %slice_bitcast_fusion.1), channel_id=1, source_target_pairs={{0,32},{1,33},{2,34},{3,35},{4,36},{5,37},{6,38},{7,39},{8,40},{9,... | collective-permute-start | bytes 1179656 | tf_op jit(solution)/shard_map/ppermute | solution.py:446
  35.8 0.0 collective-permute-start.10
  35.8 3.3 %shard_map.36 = (f32[6,512,128]{2,1,0:T(8,128)S(1)}, f32[8,8,512]{2,1,0:T(8,128)S(1)}) custom-call(s32[133]{0:T(256)S(1)} %get-tuple-element.31.refs_0_, s32[133]{0:T(256)S(1)} %get-tuple-element.32.refs_1_, s32[14]{0:T(128)S(1)} %get-tuple-element.33.refs_2_, bf16[6,512,384]{2,1,0:T(8,128)(2,1)S(1)} %shard_map.35.refs_3_.refs_5_, ...), custom_call_target="tpu_custom_call" | custom-call | flops 30000001024 | bytes 8000000 | tf_op jit(solution)/shard_map/pallas_call | solution.py:348
  39.1 1.9 %collective-permute-done.9.refs_4_ = bf16[512,384]{1,0:T(8,128)(2,1)S(1)} collective-permute-done((bf16[512,384]{1,0:T(8,128)(2,1)S(1)}, bf16[512,384]{1,0:T(8,128)(2,1)S(1)}, u32[]{:S(2)}, u32[]{:S(2)}) %collective-permute-start.9) | collective-permute-done | bytes 393248 | tf_op jit(solution)/shard_map/ppermute | solution.py:446
  41.0 1.7 %collective-permute-done.8.refs_3_ = bf16[512,384]{1,0:T(8,128)(2,1)S(1)} collective-permute-done((bf16[512,384]{1,0:T(8,128)(2,1)S(1)}, bf16[512,384]{1,0:T(8,128)(2,1)S(1)}, u32[]{:S(2)}, u32[]{:S(2)}) %collective-permute-start.8) | collective-permute-done | bytes 393248 | tf_op jit(solution)/shard_map/ppermute | solution.py:446
  42.7 0.3 collective-permute-start.12
  43.0 0.2 collective-permute-start.11
  43.2 0.0 collective-permute-done.10.refs_7_
  43.2 2.1 %shard_map.37 = (f32[6,512,128]{2,1,0:T(8,128)S(1)}, f32[2,512,128]{2,1,0:T(8,128)S(1)}, f32[8,8,512]{2,1,0:T(8,128)S(1)}, f32[6,8,512]{2,1,0:T(8,128)S(1)}) custom-call(s32[133]{0:T(256)S(1)} %get-tuple-element.31.refs_0_, s32[133]{0:T(256)S(1)} %get-tuple-element.32.refs_1_, s32[14]{0:T(128)S(1)} %get-tuple-element.33.refs_2_, ...), custom_call_target="tpu_custom_call" | custom-call | flops 5000000000 | bytes 8000000 | tf_op jit(solution)/shard_map/pallas_call | solution.py:348
  45.3 0.0 collective-permute-done.12.refs_6_
  45.4 1.1 %shard_map.38 = (f32[16,512]{1,0:T(8,128)S(1)}, f32[2,512,128]{2,1,0:T(8,128)S(1)}) custom-call(s32[133]{0:T(256)S(1)} %get-tuple-element.31.refs_0_, s32[133]{0:T(256)S(1)} %get-tuple-element.32.refs_1_, s32[14]{0:T(128)S(1)} %get-tuple-element.33.refs_2_, bf16[512,384]{1,0:T(8,128)(2,1)S(1)} %collective-permute-done.8.refs_3_, ...), custom_call_target="tpu_custom_call" | custom-call | flops 500000000 | bytes 8000000 | tf_op jit(solution)/shard_map/pallas_call | solution.py:348
  46.4 3.2 %collective-permute-start.13 = (f32[16,512]{1,0:T(8,128)S(1)}, f32[16,512]{1,0:T(8,128)S(1)}, u32[]{:S(2)}, u32[]{:S(2)}) collective-permute-start(f32[16,512]{1,0:T(8,128)S(1)} %get-tuple-element.55), channel_id=1, source_target_pairs={{0,16},{1,17},{2,18},{3,19},{4,20},{5,21},{6,22},{7,23},{8,24},{9,... | collective-permute-start | bytes 98312 | tf_op jit(solution)/shard_map/ppermute | solution.py:441
  49.6 1.0 %shard_map.39 = (f32[8,512]{1,0:T(8,128)S(1)}, f32[8,512]{1,0:T(8,128)S(1)}) custom-call(f32[6,512,128]{2,1,0:T(8,128)S(1)} %get-tuple-element.39.rows0, f32[6,512,128]{2,1,0:T(8,128)S(1)} %get-tuple-element.45.row_one, f32[6,512,128]{2,1,0:T(8,128)S(1)} %get-tuple-element.49.row_two, f32[2,512,128]{2,1,0:T(8,128)S(1)} %get-tuple-element.53.row_last), custom_call_target="tpu_custom_call" | custom-call | flops 500000000 | bytes 8000000 | tf_op jit(solution)/shard_map/pallas_call | solution.py:348
  50.6 3.5 %collective-permute-start.14 = (f32[8,512]{1,0:T(8,128)S(1)}, f32[8,512]{1,0:T(8,128)S(1)}, u32[]{:S(2)}, u32[]{:S(2)}) collective-permute-start(f32[8,512]{1,0:T(8,128)S(1)} %slice_maximum_fusion), channel_id=1, source_target_pairs={{0,12},{1,13},{2,14},{3,15},{4,8},{5,9},{6,10},{7,11},{8,4},{9,5},... | collective-permute-start | bytes 49160 | tf_op jit(solution)/shard_map/ppermute | solution.py:446
  54.1 1.3 %collective-permute-done.14 = f32[8,512]{1,0:T(8,128)S(1)} collective-permute-done((f32[8,512]{1,0:T(8,128)S(1)}, f32[8,512]{1,0:T(8,128)S(1)}, u32[]{:S(2)}, u32[]{:S(2)}) %collective-permute-start.14) | collective-permute-done | bytes 16416 | tf_op jit(solution)/shard_map/ppermute | solution.py:446
  55.4 0.1 collective-permute-start.15
  55.5 2.5 %collective-permute-done.15 = f32[4,512]{1,0:T(4,128)S(1)} collective-permute-done((f32[4,512]{1,0:T(4,128)S(1)}, f32[4,512]{1,0:T(4,128)S(1)}, u32[]{:S(2)}, u32[]{:S(2)}) %collective-permute-start.15) | collective-permute-done | bytes 8224 | tf_op jit(solution)/shard_map/ppermute | solution.py:446
  58.0 2.0 %collective-permute-start.16 = (f32[2,512]{1,0:T(2,128)S(1)}, f32[2,512]{1,0:T(2,128)S(1)}, u32[]{:S(2)}, u32[]{:S(2)}) collective-permute-start(f32[2,512]{1,0:T(2,128)S(1)} %slice.47), channel_id=1, source_target_pairs={{0,32},{1,33},{2,34},{3,35},{4,36},{5,37},{6,38},{7,39},{8,40},{9,... | collective-permute-start | bytes 12296 | tf_op jit(solution)/shard_map/ppermute | solution.py:446
  60.0 1.7 %collective-permute-done.16 = f32[2,512]{1,0:T(2,128)S(1)} collective-permute-done((f32[2,512]{1,0:T(2,128)S(1)}, f32[2,512]{1,0:T(2,128)S(1)}, u32[]{:S(2)}, u32[]{:S(2)}) %collective-permute-start.16) | collective-permute-done | bytes 4128 | tf_op jit(solution)/shard_map/ppermute | solution.py:446
  61.7 1.6 %collective-permute-start.17 = (f32[512]{0:T(512)S(1)}, f32[512]{0:T(512)S(1)}, u32[]{:S(2)}, u32[]{:S(2)}) collective-permute-start(f32[512]{0:T(512)S(1)} %bitcast.13), channel_id=1, source_target_pairs={{0,16},{1,17},{2,18},{3,19},{4,20},{5,21},{6,22},{7,23},{8,24},{9,... | collective-permute-start | bytes 6152 | tf_op jit(solution)/shard_map/ppermute | solution.py:441
  63.3 0.8 %collective-permute-done.17 = f32[512]{0:T(512)S(1)} collective-permute-done((f32[512]{0:T(512)S(1)}, f32[512]{0:T(512)S(1)}, u32[]{:S(2)}, u32[]{:S(2)}) %collective-permute-start.17) | collective-permute-done | bytes 2080 | tf_op jit(solution)/shard_map/ppermute | solution.py:441
  64.1 0.6 maximum_maximum_fusion
  (14 shorter events, 0.1 us)
Async XLA Ops:
  0.0 9.6 %copy-start.1 = (s32[256]{0:T(256)S(1)}, s32[256]{0:T(256)}, u32[]{:S(2)}) copy-start(s32[256]{0:T(256)} %cluster_ref.3) | copy-start | bytes 3076
  0.0 3.0 %collective-permute-start = (bf16[512,384]{1,0:T(8,128)(2,1)}, bf16[512,384]{1,0:T(8,128)(2,1)S(1)}, u32[]{:S(2)}, u32[]{:S(2)}) collective-permute-start(bf16[512,384]{1,0:T(8,128)(2,1)} %x_ref.1), channel_id=1, source_target_pairs={{0,16},{1,17},{2,18},{3,19},{4,20},{5,21},{6,22},{7,23},{8,24},{9,... | collective-permute-start | bytes 1179656 | tf_op jit(solution)/shard_map/ppermute | solution.py:441
  1.4 1.0 %copy-start = (bf16[512,384]{1,0:T(8,128)(2,1)S(1)}, bf16[512,384]{1,0:T(8,128)(2,1)}, u32[]{:S(2)}) copy-start(bf16[512,384]{1,0:T(8,128)(2,1)} %x_ref.1) | copy-start | bytes 1179652
  3.2 13.3 %collective-permute-start.3 = (bf16[2,512,384]{2,1,0:T(8,128)(2,1)S(1)}, bf16[2,512,384]{2,1,0:T(8,128)(2,1)S(1)}, u32[]{:S(2)}, u32[]{:S(2)}) collective-permute-start(bf16[2,512,384]{2,1,0:T(8,128)(2,1)S(1)} %shard_map.29.unit_ref.refs_4_), channel_id=1, source_target_pairs={{0,12},{1,13},{2,14},{3,15},{4,8},{5,9},{6,10},{7,11},{8,4},{9,5},... | collective-permute-start | bytes 2359304 | tf_op jit(solution)/shard_map/ppermute | solution.py:446
  7.1 11.1 %collective-permute-start.2 = (bf16[2,512,384]{2,1,0:T(8,128)(2,1)S(1)}, bf16[2,512,384]{2,1,0:T(8,128)(2,1)S(1)}, u32[]{:S(2)}, u32[]{:S(2)}) collective-permute-start(bf16[2,512,384]{2,1,0:T(8,128)(2,1)S(1)} %shard_map.29.unit_ref.refs_4_), channel_id=1, source_target_pairs={{0,4},{1,5},{2,6},{3,7},{4,0},{5,1},{6,2},{7,3},{8,12},{9,13},{10,... | collective-permute-start | bytes 2359304 | tf_op jit(solution)/shard_map/ppermute | solution.py:446
  7.1 12.1 %collective-permute-start.1 = (bf16[2,512,384]{2,1,0:T(8,128)(2,1)S(1)}, bf16[2,512,384]{2,1,0:T(8,128)(2,1)S(1)}, u32[]{:S(2)}, u32[]{:S(2)}) collective-permute-start(bf16[2,512,384]{2,1,0:T(8,128)(2,1)S(1)} %shard_map.29.unit_ref.refs_4_), channel_id=1, source_target_pairs={{0,32},{1,33},{2,34},{3,35},{4,36},{5,37},{6,38},{7,39},{8,40},{9,... | collective-permute-start | bytes 2359304 | tf_op jit(solution)/shard_map/ppermute | solution.py:446
  19.1 12.3 %collective-permute-start.7 = (bf16[2,512,384]{2,1,0:T(8,128)(2,1)S(1)}, bf16[2,512,384]{2,1,0:T(8,128)(2,1)S(1)}, u32[]{:S(2)}, u32[]{:S(2)}) collective-permute-start(bf16[2,512,384]{2,1,0:T(8,128)(2,1)S(1)} %collective-permute-done.3.c_ref), channel_id=1, source_target_pairs={{0,32},{1,33},{2,34},{3,35},{4,36},{5,37},{6,38},{7,39},{8,40},{9,... | collective-permute-start | bytes 2359304 | tf_op jit(solution)/shard_map/ppermute | solution.py:446
  21.6 12.1 %collective-permute-start.6 = (bf16[2,512,384]{2,1,0:T(8,128)(2,1)S(1)}, bf16[2,512,384]{2,1,0:T(8,128)(2,1)S(1)}, u32[]{:S(2)}, u32[]{:S(2)}) collective-permute-start(bf16[2,512,384]{2,1,0:T(8,128)(2,1)S(1)} %collective-permute-done.2.b_ref), channel_id=1, source_target_pairs={{0,12},{1,13},{2,14},{3,15},{4,8},{5,9},{6,10},{7,11},{8,4},{9,5},... | collective-permute-start | bytes 2359304 | tf_op jit(solution)/shard_map/ppermute | solution.py:446
  22.3 11.3 %collective-permute-start.5 = (bf16[2,512,384]{2,1,0:T(8,128)(2,1)S(1)}, bf16[2,512,384]{2,1,0:T(8,128)(2,1)S(1)}, u32[]{:S(2)}, u32[]{:S(2)}) collective-permute-start(bf16[2,512,384]{2,1,0:T(8,128)(2,1)S(1)} %collective-permute-done.1.a_ref), channel_id=1, source_target_pairs={{0,4},{1,5},{2,6},{3,7},{4,0},{5,1},{6,2},{7,3},{8,12},{9,13},{10,... | collective-permute-start | bytes 2359304 | tf_op jit(solution)/shard_map/ppermute | solution.py:446
  23.4 4.5 %collective-permute-start.4 = (bf16[6,512,384]{2,1,0:T(8,128)(2,1)S(1)}, bf16[6,512,384]{2,1,0:T(8,128)(2,1)S(1)}, u32[]{:S(2)}, u32[]{:S(2)}) collective-permute-start(bf16[6,512,384]{2,1,0:T(8,128)(2,1)S(1)} %shard_map.32.refs_3_), channel_id=1, source_target_pairs={{0,16},{1,17},{2,18},{3,19},{4,20},{5,21},{6,22},{7,23},{8,24},{9,... | collective-permute-start | bytes 7077896 | tf_op jit(solution)/shard_map/ppermute | solution.py:441
  34.0 7.0 %collective-permute-start.9 = (bf16[512,384]{1,0:T(8,128)(2,1)S(1)}, bf16[512,384]{1,0:T(8,128)(2,1)S(1)}, u32[]{:S(2)}, u32[]{:S(2)}) collective-permute-start(bf16[512,384]{1,0:T(8,128)(2,1)S(1)} %slice_bitcast_fusion), channel_id=1, source_target_pairs={{0,4},{1,5},{2,6},{3,7},{4,0},{5,1},{6,2},{7,3},{8,12},{9,13},{10,... | collective-permute-start | bytes 1179656 | tf_op jit(solution)/shard_map/ppermute | solution.py:446
  34.9 7.8 %collective-permute-start.8 = (bf16[512,384]{1,0:T(8,128)(2,1)S(1)}, bf16[512,384]{1,0:T(8,128)(2,1)S(1)}, u32[]{:S(2)}, u32[]{:S(2)}) collective-permute-start(bf16[512,384]{1,0:T(8,128)(2,1)S(1)} %slice_bitcast_fusion.1), channel_id=1, source_target_pairs={{0,32},{1,33},{2,34},{3,35},{4,36},{5,37},{6,38},{7,39},{8,40},{9,... | collective-permute-start | bytes 1179656 | tf_op jit(solution)/shard_map/ppermute | solution.py:446
  35.8 7.4 %collective-permute-start.10 = (bf16[6,512,384]{2,1,0:T(8,128)(2,1)S(1)}, bf16[6,512,384]{2,1,0:T(8,128)(2,1)S(1)}, u32[]{:S(2)}, u32[]{:S(2)}) collective-permute-start(bf16[6,512,384]{2,1,0:T(8,128)(2,1)S(1)} %shard_map.35.refs_3_.refs_5_), channel_id=1, source_target_pairs={{0,16},{1,17},{2,18},{3,19},{4,20},{5,21},{6,22},{7,23},{8,24},{9,... | collective-permute-start | bytes 7077896 | tf_op jit(solution)/shard_map/ppermute | solution.py:441
  42.7 2.6 %collective-permute-start.12 = (bf16[512,384]{1,0:T(8,128)(2,1)S(1)}, bf16[512,384]{1,0:T(8,128)(2,1)S(1)}, u32[]{:S(2)}, u32[]{:S(2)}) collective-permute-start(bf16[512,384]{1,0:T(8,128)(2,1)S(1)} %collective-permute-done.9.refs_4_), channel_id=1, source_target_pairs={{0,16},{1,17},{2,18},{3,19},{4,20},{5,21},{6,22},{7,23},{8,24},{9,... | collective-permute-start | bytes 1179656 | tf_op jit(solution)/shard_map/ppermute | solution.py:441
  43.0 2.3 %collective-permute-start.11 = (bf16[512,384]{1,0:T(8,128)(2,1)S(1)}, bf16[512,384]{1,0:T(8,128)(2,1)S(1)}, u32[]{:S(2)}, u32[]{:S(2)}) collective-permute-start(bf16[512,384]{1,0:T(8,128)(2,1)S(1)} %collective-permute-done.8.refs_3_), channel_id=1, source_target_pairs={{0,16},{1,17},{2,18},{3,19},{4,20},{5,21},{6,22},{7,23},{8,24},{9,... | collective-permute-start | bytes 1179656 | tf_op jit(solution)/shard_map/ppermute | solution.py:441
  46.4 4.2 %collective-permute-start.13 = (f32[16,512]{1,0:T(8,128)S(1)}, f32[16,512]{1,0:T(8,128)S(1)}, u32[]{:S(2)}, u32[]{:S(2)}) collective-permute-start(f32[16,512]{1,0:T(8,128)S(1)} %get-tuple-element.55), channel_id=1, source_target_pairs={{0,16},{1,17},{2,18},{3,19},{4,20},{5,21},{6,22},{7,23},{8,24},{9,... | collective-permute-start | bytes 98312 | tf_op jit(solution)/shard_map/ppermute | solution.py:441
  50.6 4.7 %collective-permute-start.14 = (f32[8,512]{1,0:T(8,128)S(1)}, f32[8,512]{1,0:T(8,128)S(1)}, u32[]{:S(2)}, u32[]{:S(2)}) collective-permute-start(f32[8,512]{1,0:T(8,128)S(1)} %slice_maximum_fusion), channel_id=1, source_target_pairs={{0,12},{1,13},{2,14},{3,15},{4,8},{5,9},{6,10},{7,11},{8,4},{9,5},... | collective-permute-start | bytes 49160 | tf_op jit(solution)/shard_map/ppermute | solution.py:446
  55.4 2.6 %collective-permute-start.15 = (f32[4,512]{1,0:T(4,128)S(1)}, f32[4,512]{1,0:T(4,128)S(1)}, u32[]{:S(2)}, u32[]{:S(2)}) collective-permute-start(f32[4,512]{1,0:T(4,128)S(1)} %slice.45), channel_id=1, source_target_pairs={{0,4},{1,5},{2,6},{3,7},{4,0},{5,1},{6,2},{7,3},{8,12},{9,13},{10,... | collective-permute-start | bytes 24584 | tf_op jit(solution)/shard_map/ppermute | solution.py:446
  58.0 3.7 %collective-permute-start.16 = (f32[2,512]{1,0:T(2,128)S(1)}, f32[2,512]{1,0:T(2,128)S(1)}, u32[]{:S(2)}, u32[]{:S(2)}) collective-permute-start(f32[2,512]{1,0:T(2,128)S(1)} %slice.47), channel_id=1, source_target_pairs={{0,32},{1,33},{2,34},{3,35},{4,36},{5,37},{6,38},{7,39},{8,40},{9,... | collective-permute-start | bytes 12296 | tf_op jit(solution)/shard_map/ppermute | solution.py:446
  61.7 2.4 %collective-permute-start.17 = (f32[512]{0:T(512)S(1)}, f32[512]{0:T(512)S(1)}, u32[]{:S(2)}, u32[]{:S(2)}) collective-permute-start(f32[512]{0:T(512)S(1)} %bitcast.13), channel_id=1, source_target_pairs={{0,16},{1,17},{2,18},{3,19},{4,20},{5,21},{6,22},{7,23},{8,24},{9,... | collective-permute-start | bytes 6152 | tf_op jit(solution)/shard_map/ppermute | solution.py:441
